TPU v7x, 32 devices: a whole 2x2x4 slice. The times are simulated.
32 devices in a mesh: lon: 8 (over z, x), lat: 4 (over y, core).
Axes of the slice: x: 2, y: 2, z: 4, core: 2. Of those that a mesh axis runs over, the one named last changes fastest.
Arguments:
- features: bfloat16 [180, 360, 192], P('lat', 'lon'), may hold values from -6 to 6
- params: float32 [306176], P(('lon', 'lat')), may hold values from -1.5 to 1.5
- langevin_noise: float32 [306176], P(('lon', 'lat')), may hold values from -6 to 6
- upstream: bfloat16 [180, 360, 192], P('lat', 'lon'), may hold values from -6 to 6
Outputs:
- output: bfloat16 [180, 360, 192], P('lat', 'lon')
- field_grad: bfloat16 [180, 360, 192], P('lat', 'lon')
- new_params: float32 [306176], P(('lon', 'lat'))
All inputs are finite; a program needn't handle non-finite values.
Results may differ from a plain program's by a relative error of at most 0.0085.
Values may be sent and summed in bfloat16 or wider, within the bound.
No kernel may reach another device: no remote copies, remote signals or barrier semaphores. Data moves between devices by JAX's collectives and lax.ppermute only.
A program may use at most 64 MiB of HBM per device.

v0:
```python
import math

import jax
import jax.numpy as jnp
from jax import lax
from jax.sharding import PartitionSpec as P

C = 192
H = 768
KS = 7


EPSILON = 1e-06
STEP_SIZE = 0.003
NOISE_COEF = 0.08


def padded_2(block, sides, width, periodic):
    for axis, dim in sides:
        count = lax.axis_size(axis)
        forward = [(i, i + 1) for i in range(count - 1)]
        if periodic:
            forward.append((count - 1, 0))
        backward = [(target, source) for source, target in forward]
        low = lax.ppermute(
            lax.slice_in_dim(block, block.shape[dim] - width, None, axis=dim), axis, forward
        )
        high = lax.ppermute(lax.slice_in_dim(block, 0, width, axis=dim), axis, backward)
        block = jnp.concatenate([low, block, high], axis=dim)
    return block


def unpack(weights):
    layouts = [(C, H), (H, C), (KS, KS, C), (C,), (C,), (C,), (H,), (C,), (C,)]
    pieces = []
    offset = 0
    for layout in layouts:
        length = math.prod(layout)
        pieces.append(weights[offset : offset + length].reshape(layout))
        offset = offset + length
    return pieces


def gelu_tanh(values):
    return jax.nn.gelu(values, approximate=True)


def depthwise(padded, kernel, conv_bias, lat_rows, lon_cols):
    summed = jnp.zeros((lat_rows, lon_cols, padded.shape[2]), jnp.float32) + conv_bias
    for row_off in range(KS):
        for col_off in range(KS):
            window = padded[row_off : row_off + lat_rows, col_off : col_off + lon_cols]
            summed = summed + kernel[row_off, col_off] * window.astype(jnp.float32)
    return summed


def transposed(grad_padded, kernel, lat_rows, lon_cols):
    span = KS - 1
    summed = jnp.zeros((lat_rows, lon_cols, grad_padded.shape[2]), jnp.float32)
    for row_off in range(KS):
        for col_off in range(KS):
            window = grad_padded[
                span - row_off : span - row_off + lat_rows,
                span - col_off : span - col_off + lon_cols,
            ]
            summed = summed + kernel[row_off, col_off] * window.astype(jnp.float32)
    return summed


def kernel_grad(grad_conv, padded, lat_rows, lon_cols):
    sums = []
    for row_off in range(KS):
        for col_off in range(KS):
            window = padded[row_off : row_off + lat_rows, col_off : col_off + lon_cols]
            sums.append(
                jnp.sum(grad_conv.astype(jnp.float32) * window.astype(jnp.float32), axis=(0, 1))
            )
    return jnp.stack(sums).reshape(KS, KS, -1)


def layer_pass(convolved, features, upstream, unpacked):
    w_in, w_out, kernel, conv_bias, ln_gain, ln_bias, bias_in, bias_out, layer_scale = unpacked
    mean_val = jnp.mean(convolved, axis=-1, keepdims=True)
    centred = convolved - mean_val
    inv_std = lax.rsqrt(jnp.mean(centred * centred, axis=-1, keepdims=True) + EPSILON)
    standard = centred * inv_std
    normed = (standard * ln_gain + ln_bias).astype(jnp.bfloat16)
    pre_act = jnp.einsum("ijc,ch->ijh", normed, w_in, preferred_element_type=jnp.float32) + bias_in
    activated, pullback = jax.vjp(gelu_tanh, pre_act)
    act_rounded = activated.astype(jnp.bfloat16)
    branch = (
        jnp.einsum("ijh,hc->ijc", act_rounded, w_out, preferred_element_type=jnp.float32) + bias_out
    )
    output = (features.astype(jnp.float32) + layer_scale * branch).astype(jnp.bfloat16)
    upstream_f32 = upstream.astype(jnp.float32)
    grad_branch = (layer_scale * upstream_f32).astype(jnp.bfloat16)
    grad_act = jnp.einsum("ijc,hc->ijh", grad_branch, w_out, preferred_element_type=jnp.float32)
    grad_pre = pullback(grad_act)[0].astype(jnp.bfloat16)
    grad_normed = jnp.einsum("ijh,ch->ijc", grad_pre, w_in, preferred_element_type=jnp.float32)
    scaled = grad_normed * ln_gain
    grad_conv = (
        (
            scaled
            - jnp.mean(scaled, axis=-1, keepdims=True)
            - standard * jnp.mean(scaled * standard, axis=-1, keepdims=True)
        )
        * inv_std
    ).astype(jnp.bfloat16)
    grad_in_proj = jnp.einsum("ijc,ijh->ch", normed, grad_pre, preferred_element_type=jnp.float32)
    grad_out_proj = jnp.einsum(
        "ijh,ijc->hc", act_rounded, grad_branch, preferred_element_type=jnp.float32
    )
    grad_gain = jnp.sum(grad_normed * standard, axis=(0, 1))
    grad_shift = jnp.sum(grad_normed, axis=(0, 1))
    grad_bias_in = jnp.sum(grad_pre.astype(jnp.float32), axis=(0, 1))
    grad_bias_out = jnp.sum(grad_branch.astype(jnp.float32), axis=(0, 1))
    grad_scale = jnp.sum(branch * upstream_f32, axis=(0, 1))
    layer_grads = (
        grad_in_proj,
        grad_out_proj,
        grad_gain,
        grad_shift,
        grad_bias_in,
        grad_bias_out,
        grad_scale,
    )
    return (output, grad_conv, layer_grads)


def body(features, params, langevin_noise, upstream):
    lat_rows = features.shape[0]
    lon_cols = features.shape[1]
    half_side = KS // 2
    rounded = params.astype(jnp.bfloat16)
    weights = lax.all_gather(rounded, ("lon", "lat"), axis=0, tiled=True)
    segments = unpack(weights)
    unpacked = [segments[0], segments[1]] + [
        segment.astype(jnp.float32) for segment in segments[2:]
    ]
    kernel = unpacked[2]
    conv_bias = unpacked[3]
    lon_padded = padded_2(features, (("lon", 1),), half_side, True)
    padded = padded_2(lon_padded, (("lat", 0),), half_side, False)
    convolved = depthwise(padded, kernel, conv_bias, lat_rows, lon_cols)
    output, grad_conv, layer_grads = layer_pass(convolved, features, upstream, unpacked)
    grad_kernel = kernel_grad(grad_conv, padded, lat_rows, lon_cols)
    grad_conv_bias = jnp.sum(grad_conv.astype(jnp.float32), axis=(0, 1))
    grad_lon = padded_2(grad_conv, (("lon", 1),), half_side, True)
    grad_padded = padded_2(grad_lon, (("lat", 0),), half_side, False)
    field_grad = (
        upstream.astype(jnp.float32) + transposed(grad_padded, kernel, lat_rows, lon_cols)
    ).astype(jnp.bfloat16)
    grad_in_proj, grad_out_proj, grad_gain, grad_shift, grad_bias_in, grad_bias_out, grad_scale = (
        layer_grads
    )
    flat_grads = jnp.concatenate(
        [
            grad_in_proj.reshape(-1),
            grad_out_proj.reshape(-1),
            grad_kernel.reshape(-1),
            grad_conv_bias,
            grad_gain,
            grad_shift,
            grad_bias_in,
            grad_bias_out,
            grad_scale,
        ]
    )
    full_length = params.shape[0] * lax.axis_size("lon") * lax.axis_size("lat")
    flat_grads = jnp.pad(flat_grads, (0, full_length - flat_grads.shape[0]))
    summed = lax.psum_scatter(flat_grads, ("lon", "lat"), scatter_dimension=0, tiled=True)
    new_params = params - STEP_SIZE * summed + NOISE_COEF * langevin_noise
    return (output, field_grad, new_params)


def solution(mesh):
    return jax.shard_map(
        body,
        mesh=mesh,
        in_specs=(
            P("lat", "lon", None),
            P(("lon", "lat")),
            P(("lon", "lat")),
            P("lat", "lon", None),
        ),
        out_specs=(P("lat", "lon", None), P("lat", "lon", None), P(("lon", "lat"))),
        check_vma=False,
    )
```

profile of v0, /device:TPU:0, one launch (start us, length us, event | category | flops | bytes accessed | tf_op | source)
XLA Modules:
  0.0 374.4 jit_solution(3708644306277143507)
XLA Ops:
  7.2 0.0 all-reduce.6.cloned.1.call-start
  7.2 1.1 fusion.153
  8.3 3.0 collective-permute-start
  11.3 3.1 collective-permute-start.1
  14.4 0.8 convert_element_type.455
  15.2 1.9 collective-permute-done
  17.1 0.7 collective-permute-done.1
  17.8 1.0 pad_maximum_fusion.11
  18.8 1.3 collective-permute-start.2
  20.1 1.3 collective-permute-start.3
  21.5 0.5 dynamic-update-slice
  21.9 0.0 copy-start.5
  22.0 0.8 copy-done.5
  22.8 0.0 all-reduce.6.cloned.1.call-update
  22.8 0.0 all-reduce.8.cloned.1.call-start
  22.9 0.0 copy-start.15
  22.9 0.6 copy-done.15
  23.5 1.7 collective-permute-done.3
  25.2 2.4 maximum_maximum_fusion
  27.6 126.3 %all-reduce.6.cloned.1.call-done = bf16[306176]{0:T(1024)(128)(2,1)} async-done(((bf16[306176]{0:T(1024)(128)(2,1)}), bf16[306176]{0:T(1024)(128)(2,1)}) %all-reduce.6.cloned.1.call-update) | async-done | bytes 612368
  153.9 0.7 slice_convert_fusion
  154.7 0.1 reshape.51
  155.2 0.6 fusion.157
  155.8 1.5 slice_convert_fusion.6
  157.3 20.6 %fusion.150 = (f32[45,45]{1,0:T(8,128)S(1)}, f32[45,45,192]{2,1,0:T(8,128)S(1)}) fusion(bf16[48,51,192]{2,1,0:T(8,128)(2,1)S(1)} %get-tuple-element.78, f32[192]{0:T(256)S(1)} %bitcast.120, f32[192]{0:T(256)S(1)} %bitcast.122, f32[192]{0:T(256)S(1)} %bitcast.124, f32[192]{0:T(256)S(1)} %bitcast.126, f32[192]{0:T(256)S(1)} %bitcast.128, ...), kind=kLoop, calls=%fused_computation.300 | loop fusion | flops 64538776 | bytes 35142180 | tf_op jit(solution)/shard_map/reduce_sum | solution.py:83
  178.3 1.4 copy-done.2
  179.6 0.7 multiply_reduce_fusion.2
  180.3 0.6 add_rsqrt_fusion
  181.0 1.0 reshape.54
  182.0 1.0 reshape.48
  183.0 0.7 slice_convert_fusion.1
  183.7 4.5 %multiply_convert_fusion = (bf16[45,45,768]{2,1,0:T(8,128)(2,1)S(1)}, f32[45,45,768]{2,1,0:T(8,128)S(1)}) fusion(f32[768]{0:T(1024)S(1)} %slice_convert_fusion.1, bf16[192,768,1]{1,0,2:T(8,128)(2,1)} %reshape.54, f32[45,45,192]{2,1,0:T(8,128)} %copy-done.2, f32[192]{0:T(256)} %get-tuple-element.86, f32[192]{0:T(256)} %get-tuple-element.87, ...), kind=kOutput, calls=%fused_computation.61 | convolution fusion | flops 614692800 | bytes 11202120 | tf_op jit(solution)/shard_map/ijc,ch->ijh/dot_general | solution.py:88
  188.3 0.0 copy-start.12
  188.3 0.0 copy-start.14
  188.3 6.1 %convert_reduce_fusion.1 = (f32[768]{0:T(1024)}, bf16[45,45,768]{2,1,0:T(8,128)(2,1)S(1)}) fusion(f32[45,45,768]{2,1,0:T(8,128)S(1)} %get-tuple-element.142, f32[768]{0:T(1024)S(1)} %slice_convert_fusion.1, bf16[768,192]{1,0:T(8,128)(2,1)S(1)} %copy-done.11, bf16[45,45,192]{2,1,0:T(8,128)(2,1)S(1)} %copy-done.6, f32[192]{0:T(256)S(1)} %copy-done.124), kind=kOutput, calls=%fused_computation.60 | convolution fusion | flops 634132032 | bytes 10410624 | tf_op jit(solution)/shard_map/ijc,hc->ijh/dot_general | solution.py:97
  194.5 2.4 multiply_reduce_fusion
  196.8 2.5 convolution_bitcast_fusion.1
  199.3 7.4 %fusion.133 = (f32[192]{0:T(256)S(1)}, f32[192]{0:T(256)S(1)}, f32[192]{0:T(256)S(1)}, f32[192]{0:T(256)S(1)}, f32[192]{0:T(256)S(1)}, /*index=5*/f32[192]{0:T(2...) fusion(bf16[48,51,192]{2,1,0:T(8,128)(2,1)S(1)} %get-tuple-elem, ...), kind=kLoop, calls=%fused_computation.241 | loop fusion | flops 24490944 | bytes 17931792 | tf_op jit(solution)/shard_map/reduce_sum | solution.py:76
  206.8 0.0 copy-start
  206.8 7.2 %fusion.105 = (f32[192]{0:T(256)}, f32[192]{0:T(256)}, f32[192]{0:T(256)}, f32[192]{0:T(256)}, f32[192]{0:T(256)}, /*index=5*/f32[192]{0:T(256)}, f32[192]{0:T(2...) fusion(bf16[45,45,192]{2,1,0:T(8,128)(2,1)S(1)} %get-tuple-elem, ...), kind=kLoop, calls=%fused_computation.213 | loop fusion | flops 21769152 | bytes 14788992 | tf_op jit(solution)/shard_map/reduce_sum | solution.py:76
  214.1 0.1 fusion.152
  214.1 0.0 copy-start.4
  214.1 2.0 convolution_bitcast_fusion
  216.2 1.4 collective-permute-start.4
  217.6 3.3 collective-permute-start.5
  220.9 4.8 %fusion.132 = (f32[192]{0:T(256)}, f32[192]{0:T(256)}, f32[192]{0:T(256)}, f32[192]{0:T(256)}, f32[192]{0:T(256)}, /*index=5*/f32[192]{0:T(256)}, f32[192]{0:T(256)}, f32[192]{0:T(256)}, f32[192]{0:T(256)}, f32[192]{0:T(256)}) fusion(bf16[45,45,192]{2,1,0:T(8,128)(2,1)S(1)} %get-tuple-element.69, bf16[48,51,192]{2,1,0:T(8,128)(2,1)S(1)} %get-tuple-element.78, ...), kind=kLoop, calls=%fused_computation.240 | loop fusion | flops 19049280 | bytes 3999360 | tf_op jit(solution)/shard_map/reduce_sum | solution.py:76
  225.7 2.5 fusion.59
  228.2 0.1 pad_maximum_fusion.8
  228.3 1.3 collective-permute-start.6
  229.9 3.2 collective-permute-start.7
  233.1 1.2 fusion.88
  234.3 0.0 copy-start.122
  234.6 0.2 stack.199
  234.7 0.1 reshape_reshape.3
  234.9 0.4 reshape.50
  235.4 0.8 concatenate.133
  236.1 1.1 pad.4
  237.3 0.0 all-reduce.8.cloned.1.call-update
  237.7 0.1 copy-done.1
  237.8 1.3 pad_maximum_fusion.1
  239.5 0.0 copy-start.13
  239.5 19.4 %fusion.58 = bf16[45,45,192]{2,1,0:T(8,128)(2,1)} fusion(bf16[45,45,192]{2,1,0:T(8,128)(2,1)S(1)} %copy-done.7, bf16[45,45,192]{2,1,0:T(8,128)(2,1)S(1)} %copy-done.1, bf16[45,3,192]{2,1,0:T(4,128)(2,1)S(1)} %collective-permute-done.4, bf16[45,3,192]{2,1,0:T(4,128)(2,1)S(1)} %collective-permute-done.5, bf16[48,51,192]{2,1,0:T(8,128)(2,1)S(1)} %get-tuple-element.74, ...), kind=kLoop, calls=%fused_computation.166 | loop fusion | flops 64929600 | bytes 35133312 | tf_op jit(solution)/shard_map/convert_element_type | solution.py:152
  258.9 107.2 %all-reduce.8.cloned.1.call-done = f32[306176]{0:T(1024)} async-done(((f32[306176]{0:T(1024)}), f32[306176]{0:T(1024)}) %all-reduce.8.cloned.1.call-update) | async-done | bytes 1224720
  366.1 1.5 fusion.148
  (254 shorter events, 0.7 us)
Async XLA Ops:
  7.2 146.8 %all-reduce.6.cloned.1.call-start = ((), (), s32[]{:S(2)}) async-start(), calls=%async_computation | async-start | bytes 1224704
  8.3 8.8 %collective-permute-start = (bf16[45,3,192]{2,1,0:T(4,128)(2,1)S(1)}, bf16[45,3,192]{2,1,0:T(4,128)(2,1)S(1)}, u32[]{:S(2)}, u32[]{:S(2)}) collective-permute-start(bf16[45,3,192]{2,1,0:T(4,128)(2,1)S(1)} %get-tuple-element.83), channel_id=1, source_target_pairs={{0,4},{4,8},{8,12},{12,16},{16,20},{20,24},{24,28},{28,0},{1,5},{5... | collective-permute-start | bytes 155528 | tf_op jit(solution)/shard_map/ppermute | solution.py:25
  11.3 6.5 %collective-permute-start.1 = (bf16[45,3,192]{2,1,0:T(4,128)(2,1)S(1)}, bf16[45,3,192]{2,1,0:T(4,128)(2,1)S(1)}, u32[]{:S(2)}, u32[]{:S(2)}) collective-permute-start(bf16[45,3,192]{2,1,0:T(4,128)(2,1)S(1)} %get-tuple-element.84), channel_id=1, source_target_pairs={{4,0},{8,4},{12,8},{16,12},{20,16},{24,20},{28,24},{0,28},{5,1},{9... | collective-permute-start | bytes 155528 | tf_op jit(solution)/shard_map/ppermute | solution.py:28
  18.8 4.0 %collective-permute-start.2 = (bf16[3,51,192]{2,1,0:T(8,128)(2,1)S(1)}, bf16[3,51,192]{2,1,0:T(8,128)(2,1)S(1)}, u32[]{:S(2)}, u32[]{:S(2)}) collective-permute-start(bf16[3,51,192]{2,1,0:T(8,128)(2,1)S(1)} %get-tuple-element.79), channel_id=1, source_target_pairs={{0,1},{1,2},{2,3},{4,5},{5,6},{6,7},{8,9},{9,10},{10,11},{12,13},{... | collective-permute-start | bytes 176264 | tf_op jit(solution)/shard_map/ppermute | solution.py:25
  20.1 5.1 %collective-permute-start.3 = (bf16[3,51,192]{2,1,0:T(8,128)(2,1)S(1)}, bf16[3,51,192]{2,1,0:T(8,128)(2,1)}, u32[]{:S(2)}, u32[]{:S(2)}) collective-permute-start(bf16[3,51,192]{2,1,0:T(8,128)(2,1)S(1)} %get-tuple-element.80), channel_id=1, source_target_pairs={{1,0},{2,1},{3,2},{5,4},{6,5},{7,6},{9,8},{10,9},{11,10},{13,12},{... | collective-permute-start | bytes 176264 | tf_op jit(solution)/shard_map/ppermute | solution.py:28
  22.8 343.3 %all-reduce.8.cloned.1.call-start = ((), (), s32[]{:S(2)}) async-start(), calls=%async_computation.1 | async-start | bytes 2449408
  154.8 23.1 %copy-start.17 = (f32[1,1,192]{2,1,0:T(1,128)}, f32[1,1,192]{2,1,0:T(1,128)S(1)}, u32[]{:S(2)}) copy-start(f32[1,1,192]{2,1,0:T(1,128)S(1)} %get-tuple-element.92) | copy-start | bytes 2308
  154.8 23.1 %copy-start.19 = (f32[1,1,192]{2,1,0:T(1,128)}, f32[1,1,192]{2,1,0:T(1,128)S(1)}, u32[]{:S(2)}) copy-start(f32[1,1,192]{2,1,0:T(1,128)S(1)} %get-tuple-element.93) | copy-start | bytes 2308
  154.8 23.1 %copy-start.21 = (f32[1,1,192]{2,1,0:T(1,128)}, f32[1,1,192]{2,1,0:T(1,128)S(1)}, u32[]{:S(2)}) copy-start(f32[1,1,192]{2,1,0:T(1,128)S(1)} %get-tuple-element.94) | copy-start | bytes 2308
  154.8 23.1 %copy-start.23 = (f32[1,1,192]{2,1,0:T(1,128)}, f32[1,1,192]{2,1,0:T(1,128)S(1)}, u32[]{:S(2)}) copy-start(f32[1,1,192]{2,1,0:T(1,128)S(1)} %get-tuple-element.95) | copy-start | bytes 2308
  154.8 23.1 %copy-start.25 = (f32[1,1,192]{2,1,0:T(1,128)}, f32[1,1,192]{2,1,0:T(1,128)S(1)}, u32[]{:S(2)}) copy-start(f32[1,1,192]{2,1,0:T(1,128)S(1)} %get-tuple-element.96) | copy-start | bytes 2308
  154.8 23.1 %copy-start.27 = (f32[1,1,192]{2,1,0:T(1,128)}, f32[1,1,192]{2,1,0:T(1,128)S(1)}, u32[]{:S(2)}) copy-start(f32[1,1,192]{2,1,0:T(1,128)S(1)} %get-tuple-element.97) | copy-start | bytes 2308
  154.8 23.1 %copy-start.29 = (f32[1,1,192]{2,1,0:T(1,128)}, f32[1,1,192]{2,1,0:T(1,128)S(1)}, u32[]{:S(2)}) copy-start(f32[1,1,192]{2,1,0:T(1,128)S(1)} %get-tuple-element.98) | copy-start | bytes 2308
  154.8 23.1 %copy-start.31 = (f32[1,1,192]{2,1,0:T(1,128)}, f32[1,1,192]{2,1,0:T(1,128)S(1)}, u32[]{:S(2)}) copy-start(f32[1,1,192]{2,1,0:T(1,128)S(1)} %get-tuple-element.99) | copy-start | bytes 2308
  154.9 23.1 %copy-start.33 = (f32[1,1,192]{2,1,0:T(1,128)}, f32[1,1,192]{2,1,0:T(1,128)S(1)}, u32[]{:S(2)}) copy-start(f32[1,1,192]{2,1,0:T(1,128)S(1)} %get-tuple-element.100) | copy-start | bytes 2308
  154.9 23.1 %copy-start.35 = (f32[1,1,192]{2,1,0:T(1,128)}, f32[1,1,192]{2,1,0:T(1,128)S(1)}, u32[]{:S(2)}) copy-start(f32[1,1,192]{2,1,0:T(1,128)S(1)} %get-tuple-element.101) | copy-start | bytes 2308
  154.9 23.1 %copy-start.37 = (f32[1,1,192]{2,1,0:T(1,128)}, f32[1,1,192]{2,1,0:T(1,128)S(1)}, u32[]{:S(2)}) copy-start(f32[1,1,192]{2,1,0:T(1,128)S(1)} %get-tuple-element.102) | copy-start | bytes 2308
  154.9 23.1 %copy-start.39 = (f32[1,1,192]{2,1,0:T(1,128)}, f32[1,1,192]{2,1,0:T(1,128)S(1)}, u32[]{:S(2)}) copy-start(f32[1,1,192]{2,1,0:T(1,128)S(1)} %get-tuple-element.103) | copy-start | bytes 2308
  154.9 23.1 %copy-start.41 = (f32[1,1,192]{2,1,0:T(1,128)}, f32[1,1,192]{2,1,0:T(1,128)S(1)}, u32[]{:S(2)}) copy-start(f32[1,1,192]{2,1,0:T(1,128)S(1)} %get-tuple-element.104) | copy-start | bytes 2308
  154.9 23.1 %copy-start.43 = (f32[1,1,192]{2,1,0:T(1,128)}, f32[1,1,192]{2,1,0:T(1,128)S(1)}, u32[]{:S(2)}) copy-start(f32[1,1,192]{2,1,0:T(1,128)S(1)} %get-tuple-element.105) | copy-start | bytes 2308
  154.9 23.1 %copy-start.45 = (f32[1,1,192]{2,1,0:T(1,128)}, f32[1,1,192]{2,1,0:T(1,128)S(1)}, u32[]{:S(2)}) copy-start(f32[1,1,192]{2,1,0:T(1,128)S(1)} %get-tuple-element.106) | copy-start | bytes 2308
  154.9 23.1 %copy-start.47 = (f32[1,1,192]{2,1,0:T(1,128)}, f32[1,1,192]{2,1,0:T(1,128)S(1)}, u32[]{:S(2)}) copy-start(f32[1,1,192]{2,1,0:T(1,128)S(1)} %get-tuple-element.107) | copy-start | bytes 2308
  154.9 23.1 %copy-start.49 = (f32[1,1,192]{2,1,0:T(1,128)}, f32[1,1,192]{2,1,0:T(1,128)S(1)}, u32[]{:S(2)}) copy-start(f32[1,1,192]{2,1,0:T(1,128)S(1)} %get-tuple-element.108) | copy-start | bytes 2308
  154.9 23.1 %copy-start.51 = (f32[1,1,192]{2,1,0:T(1,128)}, f32[1,1,192]{2,1,0:T(1,128)S(1)}, u32[]{:S(2)}) copy-start(f32[1,1,192]{2,1,0:T(1,128)S(1)} %get-tuple-element.109) | copy-start | bytes 2308
  155.0 23.1 %copy-start.53 = (f32[1,1,192]{2,1,0:T(1,128)}, f32[1,1,192]{2,1,0:T(1,128)S(1)}, u32[]{:S(2)}) copy-start(f32[1,1,192]{2,1,0:T(1,128)S(1)} %get-tuple-element.110) | copy-start | bytes 2308
  155.0 23.1 %copy-start.55 = (f32[1,1,192]{2,1,0:T(1,128)}, f32[1,1,192]{2,1,0:T(1,128)S(1)}, u32[]{:S(2)}) copy-start(f32[1,1,192]{2,1,0:T(1,128)S(1)} %get-tuple-element.111) | copy-start | bytes 2308
  155.0 23.1 %copy-start.57 = (f32[1,1,192]{2,1,0:T(1,128)}, f32[1,1,192]{2,1,0:T(1,128)S(1)}, u32[]{:S(2)}) copy-start(f32[1,1,192]{2,1,0:T(1,128)S(1)} %get-tuple-element.112) | copy-start | bytes 2308
  155.0 23.1 %copy-start.59 = (f32[1,1,192]{2,1,0:T(1,128)}, f32[1,1,192]{2,1,0:T(1,128)S(1)}, u32[]{:S(2)}) copy-start(f32[1,1,192]{2,1,0:T(1,128)S(1)} %get-tuple-element.113) | copy-start | bytes 2308
  155.0 23.1 %copy-start.61 = (f32[1,1,192]{2,1,0:T(1,128)}, f32[1,1,192]{2,1,0:T(1,128)S(1)}, u32[]{:S(2)}) copy-start(f32[1,1,192]{2,1,0:T(1,128)S(1)} %get-tuple-element.114) | copy-start | bytes 2308
  155.0 23.1 %copy-start.63 = (f32[1,1,192]{2,1,0:T(1,128)}, f32[1,1,192]{2,1,0:T(1,128)S(1)}, u32[]{:S(2)}) copy-start(f32[1,1,192]{2,1,0:T(1,128)S(1)} %get-tuple-element.115) | copy-start | bytes 2308
  155.0 23.1 %copy-start.65 = (f32[1,1,192]{2,1,0:T(1,128)}, f32[1,1,192]{2,1,0:T(1,128)S(1)}, u32[]{:S(2)}) copy-start(f32[1,1,192]{2,1,0:T(1,128)S(1)} %get-tuple-element.116) | copy-start | bytes 2308
  155.1 23.1 %copy-start.67 = (f32[1,1,192]{2,1,0:T(1,128)}, f32[1,1,192]{2,1,0:T(1,128)S(1)}, u32[]{:S(2)}) copy-start(f32[1,1,192]{2,1,0:T(1,128)S(1)} %get-tuple-element.117) | copy-start | bytes 2308
  155.1 23.1 %copy-start.69 = (f32[1,1,192]{2,1,0:T(1,128)}, f32[1,1,192]{2,1,0:T(1,128)S(1)}, u32[]{:S(2)}) copy-start(f32[1,1,192]{2,1,0:T(1,128)S(1)} %get-tuple-element.118) | copy-start | bytes 2308
  155.1 23.1 %copy-start.71 = (f32[1,1,192]{2,1,0:T(1,128)}, f32[1,1,192]{2,1,0:T(1,128)S(1)}, u32[]{:S(2)}) copy-start(f32[1,1,192]{2,1,0:T(1,128)S(1)} %get-tuple-element.119) | copy-start | bytes 2308
  155.1 23.1 %copy-start.73 = (f32[1,1,192]{2,1,0:T(1,128)}, f32[1,1,192]{2,1,0:T(1,128)S(1)}, u32[]{:S(2)}) copy-start(f32[1,1,192]{2,1,0:T(1,128)S(1)} %get-tuple-element.120) | copy-start | bytes 2308
  155.1 23.1 %copy-start.75 = (f32[1,1,192]{2,1,0:T(1,128)}, f32[1,1,192]{2,1,0:T(1,128)S(1)}, u32[]{:S(2)}) copy-start(f32[1,1,192]{2,1,0:T(1,128)S(1)} %get-tuple-element.121) | copy-start | bytes 2308
  155.1 23.1 %copy-start.77 = (f32[1,1,192]{2,1,0:T(1,128)}, f32[1,1,192]{2,1,0:T(1,128)S(1)}, u32[]{:S(2)}) copy-start(f32[1,1,192]{2,1,0:T(1,128)S(1)} %get-tuple-element.122) | copy-start | bytes 2308
  155.1 23.1 %copy-start.79 = (f32[1,1,192]{2,1,0:T(1,128)}, f32[1,1,192]{2,1,0:T(1,128)S(1)}, u32[]{:S(2)}) copy-start(f32[1,1,192]{2,1,0:T(1,128)S(1)} %get-tuple-element.123) | copy-start | bytes 2308
  155.1 23.1 %copy-start.81 = (f32[1,1,192]{2,1,0:T(1,128)}, f32[1,1,192]{2,1,0:T(1,128)S(1)}, u32[]{:S(2)}) copy-start(f32[1,1,192]{2,1,0:T(1,128)S(1)} %get-tuple-element.124) | copy-start | bytes 2308
  155.1 23.1 %copy-start.83 = (f32[1,1,192]{2,1,0:T(1,128)}, f32[1,1,192]{2,1,0:T(1,128)S(1)}, u32[]{:S(2)}) copy-start(f32[1,1,192]{2,1,0:T(1,128)S(1)} %get-tuple-element.125) | copy-start | bytes 2308
  155.1 23.1 %copy-start.85 = (f32[1,1,192]{2,1,0:T(1,128)}, f32[1,1,192]{2,1,0:T(1,128)S(1)}, u32[]{:S(2)}) copy-start(f32[1,1,192]{2,1,0:T(1,128)S(1)} %get-tuple-element.126) | copy-start | bytes 2308
  155.2 23.1 %copy-start.87 = (f32[1,1,192]{2,1,0:T(1,128)}, f32[1,1,192]{2,1,0:T(1,128)S(1)}, u32[]{:S(2)}) copy-start(f32[1,1,192]{2,1,0:T(1,128)S(1)} %get-tuple-element.127) | copy-start | bytes 2308
  155.2 23.1 %copy-start.89 = (f32[1,1,192]{2,1,0:T(1,128)}, f32[1,1,192]{2,1,0:T(1,128)S(1)}, u32[]{:S(2)}) copy-start(f32[1,1,192]{2,1,0:T(1,128)S(1)} %get-tuple-element.128) | copy-start | bytes 2308
  155.2 23.1 %copy-start.90 = (f32[1,1,192]{2,1,0:T(1,128)}, f32[1,1,192]{2,1,0:T(1,128)S(1)}, u32[]{:S(2)}) copy-start(f32[1,1,192]{2,1,0:T(1,128)S(1)} %get-tuple-element.129) | copy-start | bytes 2308
  188.2 6.2 %copy-start.3 = (f32[45,45,192]{2,1,0:T(8,128)S(1)}, f32[45,45,192]{2,1,0:T(8,128)}, u32[]{:S(2)}) copy-start(f32[45,45,192]{2,1,0:T(8,128)} %copy-done.2) | copy-start | bytes 4665604
  188.3 6.2 %copy-start.12 = (bf16[192,768,1]{1,0,2:T(8,128)(2,1)S(1)}, bf16[192,768,1]{1,0,2:T(8,128)(2,1)}, u32[]{:S(2)}) copy-start(bf16[192,768,1]{1,0,2:T(8,128)(2,1)} %reshape.54) | copy-start | bytes 884740
  188.3 6.2 %copy-start.14 = (f32[45,45]{1,0:T(8,128)S(1)}, f32[45,45]{1,0:T(8,128)}, u32[]{:S(2)}) copy-start(f32[45,45]{1,0:T(8,128)} %add_rsqrt_fusion) | copy-start | bytes 24304
  188.3 6.2 %copy-start.121 = (f32[192]{0:T(256)S(1)}, f32[192]{0:T(256)}, u32[]{:S(2)}) copy-start(f32[192]{0:T(256)} %get-tuple-element.87) | copy-start | bytes 2308
  206.8 26.3 %copy-start = (bf16[45,45,192]{2,1,0:T(8,128)(2,1)}, bf16[45,45,192]{2,1,0:T(8,128)(2,1)S(1)}, u32[]{:S(2)}) copy-start(bf16[45,45,192]{2,1,0:T(8,128)(2,1)S(1)} %get-tuple-element.69) | copy-start | bytes 2332804
  214.1 6.8 %copy-start.4 = (bf16[45,45,192]{2,1,0:T(8,128)(2,1)S(1)}, bf16[45,45,192]{2,1,0:T(8,128)(2,1)}, u32[]{:S(2)}) copy-start(bf16[45,45,192]{2,1,0:T(8,128)(2,1)} %param.4) | copy-start | bytes 2332804
  216.2 12.1 %collective-permute-start.4 = (bf16[45,3,192]{2,1,0:T(4,128)(2,1)S(1)}, bf16[45,3,192]{2,1,0:T(4,128)(2,1)S(1)}, u32[]{:S(2)}, u32[]{:S(2)}) collective-permute-start(bf16[45,3,192]{2,1,0:T(4,128)(2,1)S(1)} %get-tuple-element.82), channel_id=1, source_target_pairs={{0,4},{4,8},{8,12},{12,16},{16,20},{20,24},{24,28},{28,0},{1,5},{5... | collective-permute-start | bytes 155528 | tf_op jit(solution)/shard_map/ppermute | solution.py:25
  217.6 8.1 %copy-start.125 = (f32[192]{0:T(256)S(1)}, f32[192]{0:T(256)}, u32[]{:S(2)}) copy-start(f32[192]{0:T(256)} %get-tuple-element.89) | copy-start | bytes 2308
  217.6 10.6 %collective-permute-start.5 = (bf16[45,3,192]{2,1,0:T(4,128)(2,1)S(1)}, bf16[45,3,192]{2,1,0:T(4,128)(2,1)S(1)}, u32[]{:S(2)}, u32[]{:S(2)}) collective-permute-start(bf16[45,3,192]{2,1,0:T(4,128)(2,1)S(1)} %get-tuple-element.81), channel_id=1, source_target_pairs={{4,0},{8,4},{12,8},{16,12},{20,16},{24,20},{28,24},{0,28},{5,1},{9... | collective-permute-start | bytes 155528 | tf_op jit(solution)/shard_map/ppermute | solution.py:28
  228.3 9.4 %collective-permute-start.6 = (bf16[3,51,192]{2,1,0:T(8,128)(2,1)S(1)}, bf16[3,51,192]{2,1,0:T(8,128)(2,1)S(1)}, u32[]{:S(2)}, u32[]{:S(2)}) collective-permute-start(bf16[3,51,192]{2,1,0:T(8,128)(2,1)S(1)} %get-tuple-element.75), channel_id=1, source_target_pairs={{1,0},{2,1},{3,2},{5,4},{6,5},{7,6},{9,8},{10,9},{11,10},{13,12},{... | collective-permute-start | bytes 176264 | tf_op jit(solution)/shard_map/ppermute | solution.py:28
  229.6 4.7 %copy-start.93 = (f32[192]{0:T(256)S(1)}, f32[192]{0:T(256)}, u32[]{:S(2)}) copy-start(f32[192]{0:T(256)} %get-tuple-element.26) | copy-start | bytes 2308
  229.6 4.7 %copy-start.94 = (f32[192]{0:T(256)S(1)}, f32[192]{0:T(256)}, u32[]{:S(2)}) copy-start(f32[192]{0:T(256)} %get-tuple-element.27) | copy-start | bytes 2308
  229.6 4.7 %copy-start.95 = (f32[192]{0:T(256)S(1)}, f32[192]{0:T(256)}, u32[]{:S(2)}) copy-start(f32[192]{0:T(256)} %get-tuple-element.28) | copy-start | bytes 2308
  229.6 4.7 %copy-start.96 = (f32[192]{0:T(256)S(1)}, f32[192]{0:T(256)}, u32[]{:S(2)}) copy-start(f32[192]{0:T(256)} %get-tuple-element.29) | copy-start | bytes 2308
  229.6 4.7 %copy-start.97 = (f32[192]{0:T(256)S(1)}, f32[192]{0:T(256)}, u32[]{:S(2)}) copy-start(f32[192]{0:T(256)} %get-tuple-element.30) | copy-start | bytes 2308
  229.9 5.0 %copy-start.10 = (f32[192,768]{1,0:T(8,128)S(1)}, f32[192,768]{1,0:T(8,128)}, u32[]{:S(2)}) copy-start(f32[192,768]{1,0:T(8,128)} %convolution_bitcast_fusion.1) | copy-start | bytes 1769476
  229.9 5.0 %copy-start.8 = (f32[768,192]{1,0:T(8,128)S(1)}, f32[768,192]{1,0:T(8,128)}, u32[]{:S(2)}) copy-start(f32[768,192]{1,0:T(8,128)} %convolution_bitcast_fusion) | copy-start | bytes 1769476
  229.9 7.8 %collective-permute-start.7 = (bf16[3,51,192]{2,1,0:T(8,128)(2,1)S(1)}, bf16[3,51,192]{2,1,0:T(8,128)(2,1)S(1)}, u32[]{:S(2)}, u32[]{:S(2)}) collective-permute-start(bf16[3,51,192]{2,1,0:T(8,128)(2,1)S(1)} %get-tuple-element.76), channel_id=1, source_target_pairs={{0,1},{1,2},{2,3},{4,5},{5,6},{6,7},{8,9},{9,10},{10,11},{12,13},{... | collective-permute-start | bytes 176264 | tf_op jit(solution)/shard_map/ppermute | solution.py:25
  239.5 126.6 %copy-start.13 = (f32[9568]{0:T(1024)S(1)}, f32[9568]{0:T(1024)}, u32[]{:S(2)}) copy-start(f32[9568]{0:T(1024)} %param.5) | copy-start | bytes 114820
  239.5 126.6 %copy-start.16 = (f32[9568]{0:T(1024)S(1)}, f32[9568]{0:T(1024)}, u32[]{:S(2)}) copy-start(f32[9568]{0:T(1024)} %param.6) | copy-start | bytes 114820
  (73 other events, 202.3 us)
Sparse Core Ops, SparseCore 0:
  22.9 130.9 all-reduce.5
  237.4 128.6 all-reduce.7
where the time goes:
time: 375 us; the launch traced here: 374 us
  waiting for transfers between devices  238 us (63%)
  other arithmetic  71.8 us (19%)
  matrix products  20.1 us (5%)
  starting transfers between devices  17.9 us (5%)
  between operations  16.1 us (4%)
  local copies, waits for them, and re-layouts  10.6 us (3%)
    unnamed x4, waiting for transfers between devices  234 us
    reduce_sum x4, other arithmetic, kernel_grad(): jnp.sum(grad_conv.astype(jnp.float32) * window.astype(jnp.float32), axis=...  20.7 us
    reduce_sum x1, other arithmetic, layer_pass(): mean_val = jnp.mean(convolved, axis=-1, keepdims=True)  20.6 us
    convert_element_type x1, other arithmetic, body(): field_grad = (upstream.astype(jnp.float32) + transposed(grad_padded, kern...  19.4 us
    ppermute x4, starting transfers between devices, padded_2(): lax.ppermute(lax.slice_in_dim(block, 0, width, axis=dim), axis, backward)  8.96 us
    ppermute x4, starting transfers between devices, padded_2(): lax.ppermute(lax.slice_in_dim(block, block.shape[dim] - width, None, axis...  8.9 us
  transfers between devices with their start and end apart: 10, of which 5 were waited for; matrix products, arithmetic and copies ran while one was open for 9% of the time, Pallas kernels for 0%

commit v1 on v0

--- a/solution.py
+++ b/solution.py
@@ -28,6 +28,48 @@
         high = lax.ppermute(lax.slice_in_dim(block, 0, width, axis=dim), axis, backward)
         block = jnp.concatenate([low, block, high], axis=dim)
     return block
+
+
+def exchange_bits(axes):
+    steps = []
+    for axis in axes:
+        bit = lax.axis_size(axis) // 2
+        while bit:
+            steps.append((axis, bit))
+            bit //= 2
+    return steps
+
+
+def swap(values, axis, bit):
+    return lax.ppermute(values, axis, [(i, i ^ bit) for i in range(lax.axis_size(axis))])
+
+
+def gather_flat(share, axes):
+    steps = exchange_bits(axes)
+    length = share.shape[0]
+    for axis, bit in steps:
+        other = swap(share, axis, bit)
+        upper = (lax.axis_index(axis) & bit) != 0
+        share = jnp.concatenate([jnp.where(upper, other, share), jnp.where(upper, share, other)])
+    return reverse_bits(share, len(steps), length)
+
+
+def reverse_bits(values, count, length):
+    blocks = values.reshape((2,) * count + (length,))
+    return blocks.transpose(tuple(range(count))[::-1] + (count,)).reshape(-1)
+
+
+def scatter_sum(values, axes):
+    steps = exchange_bits(axes)
+    values = reverse_bits(values, len(steps), values.shape[0] >> len(steps))
+    for axis, bit in steps[::-1]:
+        half = values.shape[0] // 2
+        upper = (lax.axis_index(axis) & bit) != 0
+        low, high = values[:half], values[half:]
+        sent = jnp.where(upper, low, high).astype(jnp.bfloat16)
+        kept = jnp.where(upper, high, low)
+        values = kept + swap(sent, axis, bit).astype(jnp.float32)
+    return values
 
 
 def unpack(weights):
@@ -132,7 +174,7 @@
     lon_cols = features.shape[1]
     half_side = KS // 2
     rounded = params.astype(jnp.bfloat16)
-    weights = lax.all_gather(rounded, ("lon", "lat"), axis=0, tiled=True)
+    weights = gather_flat(rounded, ("lon", "lat"))
     segments = unpack(weights)
     unpacked = [segments[0], segments[1]] + [
         segment.astype(jnp.float32) for segment in segments[2:]
@@ -168,7 +210,7 @@
     )
     full_length = params.shape[0] * lax.axis_size("lon") * lax.axis_size("lat")
     flat_grads = jnp.pad(flat_grads, (0, full_length - flat_grads.shape[0]))
-    summed = lax.psum_scatter(flat_grads, ("lon", "lat"), scatter_dimension=0, tiled=True)
+    summed = scatter_sum(flat_grads, ("lon", "lat"))
     new_params = params - STEP_SIZE * summed + NOISE_COEF * langevin_noise
     return (output, field_grad, new_params)
 

time: 375 us -> 170 us (0.45)
  waiting for transfers between devices: 238 us -> 13.6 us
  starting transfers between devices: 17.9 us -> 33.2 us
  between operations: 16.1 us -> 3.01 us
  other arithmetic: 71.8 us -> 81 us
  local copies, waits for them, and re-layouts: 10.6 us -> 18 us
    unnamed x4 -> x0, waiting for transfers between devices: 234 us -> none
    ppermute x0 -> x10, starting transfers between devices: none -> 16.7 us  [swap(): lax.ppermute(values, axis, [(i, i ^ bit) for i in range(lax.axis_size(axi...]
    ppermute x0 -> x10, waiting for transfers between devices: none -> 7.4 us  [swap(): lax.ppermute(values, axis, [(i, i ^ bit) for i in range(lax.axis_size(axi...]
    reduce_sum x4, other arithmetic: 20.7 us -> 26.4 us  [kernel_grad(): jnp.sum(grad_conv.astype(jnp.float32) * window.astype(jnp.float32), axis=...]
    ppermute x4, starting transfers between devices: 8.9 us -> 4.5 us  [padded_2(): lax.ppermute(lax.slice_in_dim(block, block.shape[dim] - width, None, axis...]
    ppermute x4, waiting for transfers between devices: 1.93 us -> 6.16 us  [padded_2(): lax.ppermute(lax.slice_in_dim(block, block.shape[dim] - width, None, axis...]
  transfers between devices with their start and end apart: 10 -> 18, of which waited for: 5 -> 8; matrix products, arithmetic and copies ran while one was open for 9% -> 16% of each run, Pallas kernels for 0% -> 0%
where the time goes in v1:
time: 170 us; the launch traced here: 169 us
  other arithmetic  81 us (48%)
  starting transfers between devices  33.2 us (20%)
  matrix products  20.2 us (12%)
  local copies, waits for them, and re-layouts  18 us (11%)
  waiting for transfers between devices  13.6 us (8%)
  between operations  3.01 us (2%)
    reduce_sum x4, other arithmetic, kernel_grad(): jnp.sum(grad_conv.astype(jnp.float32) * window.astype(jnp.float32), axis=...  26.4 us
    reduce_sum x1, other arithmetic, layer_pass(): mean_val = jnp.mean(convolved, axis=-1, keepdims=True)  20.7 us
    convert_element_type x1, other arithmetic, body(): field_grad = (upstream.astype(jnp.float32) + transposed(grad_padded, kern...  19.2 us
    ppermute x10, starting transfers between devices, swap(): lax.ppermute(values, axis, [(i, i ^ bit) for i in range(lax.axis_size(axi...  16.7 us
    ppermute x4, starting transfers between devices, padded_2(): lax.ppermute(lax.slice_in_dim(block, 0, width, axis=dim), axis, backward)  12 us
    ppermute x10, waiting for transfers between devices, swap(): lax.ppermute(values, axis, [(i, i ^ bit) for i in range(lax.axis_size(axi...  7.4 us
    dot_general x1, matrix products, layer_pass(): jnp.einsum('ijc,hc->ijh', grad_branch, w_out, preferred_element_type=jnp....  6.19 us
    ppermute x4, waiting for transfers between devices, padded_2(): lax.ppermute(lax.slice_in_dim(block, block.shape[dim] - width, None, axis...  6.16 us
  transfers between devices with their start and end apart: 18, of which 8 were waited for; matrix products, arithmetic and copies ran while one was open for 16% of the time, Pallas kernels for 0%

profile of v1, /device:TPU:0, one launch (start us, length us, event | category | flops | bytes accessed | tf_op | source)
XLA Modules:
  0.0 169.0 jit_solution(12880333635125058354)
XLA Ops:
  0.6 0.9 convert_element_type.488
  1.5 4.0 %collective-permute-start = (bf16[9568]{0:T(1024)(128)(2,1)S(1)}, bf16[9568]{0:T(1024)(128)(2,1)S(1)}, u32[]{:S(2)}, u32[]{:S(2)}) collective-permute-start(bf16[9568]{0:T(1024)(128)(2,1)S(1)} %convert_element_type.488), channel_id=1, source_target_pairs={{0,16},{4,20},{8,24},{12,28},{16,0},{20,4},{24,8},{28,12},{1,17},{... | collective-permute-start | bytes 57416 | tf_op jit(solution)/shard_map/ppermute | solution.py:44
  5.6 1.8 %collective-permute-done = bf16[9568]{0:T(1024)(128)(2,1)S(1)} collective-permute-done((bf16[9568]{0:T(1024)(128)(2,1)S(1)}, bf16[9568]{0:T(1024)(128)(2,1)S(1)}, u32[]{:S(2)}, u32[]{:S(2)}) %collective-permute-start) | collective-permute-done | bytes 19168 | tf_op jit(solution)/shard_map/ppermute | solution.py:44
  7.3 0.8 broadcast_select_fusion.11
  8.2 1.9 %collective-permute-start.1 = (bf16[19136]{0:T(1024)(128)(2,1)S(1)}, bf16[19136]{0:T(1024)(128)(2,1)S(1)}, u32[]{:S(2)}, u32[]{:S(2)}) collective-permute-start(bf16[19136]{0:T(1024)(128)(2,1)S(1)} %pad_maximum_fusion.15), channel_id=1, source_target_pairs={{0,8},{4,12},{8,0},{12,4},{16,24},{20,28},{24,16},{28,20},{1,9},{5... | collective-permute-start | bytes 114824 | tf_op jit(solution)/shard_map/ppermute | solution.py:44
  10.1 2.1 %collective-permute-done.1 = bf16[19136]{0:T(1024)(128)(2,1)S(1)} collective-permute-done((bf16[19136]{0:T(1024)(128)(2,1)S(1)}, bf16[19136]{0:T(1024)(128)(2,1)S(1)}, u32[]{:S(2)}, u32[]{:S(2)}) %collective-permute-start.1) | collective-permute-done | bytes 38304 | tf_op jit(solution)/shard_map/ppermute | solution.py:44
  12.4 2.0 %collective-permute-start.2 = (bf16[38272]{0:T(1024)(128)(2,1)S(1)}, bf16[38272]{0:T(1024)(128)(2,1)S(1)}, u32[]{:S(2)}, u32[]{:S(2)}) collective-permute-start(bf16[38272]{0:T(1024)(128)(2,1)S(1)} %pad_maximum_fusion.14), channel_id=1, source_target_pairs={{0,4},{4,0},{8,12},{12,8},{16,20},{20,16},{24,28},{28,24},{1,5},{5... | collective-permute-start | bytes 229640 | tf_op jit(solution)/shard_map/ppermute | solution.py:44
  14.4 1.1 fusion.152
  15.6 4.6 %collective-permute-start.6 = (bf16[45,3,192]{2,1,0:T(4,128)(2,1)S(1)}, bf16[45,3,192]{2,1,0:T(4,128)(2,1)S(1)}, u32[]{:S(2)}, u32[]{:S(2)}) collective-permute-start(bf16[45,3,192]{2,1,0:T(4,128)(2,1)S(1)} %get-tuple-element.84), channel_id=1, source_target_pairs={{4,0},{8,4},{12,8},{16,12},{20,16},{24,20},{28,24},{0,28},{5,1},{9... | collective-permute-start | bytes 155528 | tf_op jit(solution)/shard_map/ppermute | solution.py:28
  20.4 1.6 collective-permute-start.3
  21.9 0.8 collective-permute-done.5
  22.8 1.3 collective-permute-start.7
  24.1 1.3 collective-permute-start.8
  25.4 0.2 collective-permute-done.3
  25.7 0.8 pad_maximum_fusion.6
  26.5 2.7 %collective-permute-start.4 = (bf16[153088]{0:T(1024)(128)(2,1)}, bf16[153088]{0:T(1024)(128)(2,1)}, u32[]{:S(2)}, u32[]{:S(2)}) collective-permute-start(bf16[153088]{0:T(1024)(128)(2,1)} %pad_maximum_fusion.6), channel_id=1, source_target_pairs={{0,1},{1,0},{2,3},{3,2},{4,5},{5,4},{6,7},{7,6},{8,9},{9,8},{10,11... | collective-permute-start | bytes 918536 | tf_op jit(solution)/shard_map/ppermute | solution.py:44
  29.2 2.4 %maximum_maximum_fusion = (bf16[48,51,192]{2,1,0:T(8,128)(2,1)S(1)}, bf16[48,51,192]{2,1,0:T(8,128)(2,1)S(1)}) fusion(bf16[45,3,192]{2,1,0:T(4,128)(2,1)S(1)} %collective-permute-done.6, bf16[45,45,192]{2,1,0:T(8,128)(2,1)} %param.4, bf16[45,3,192]{2,1,0:T(4,128)(2,1)S(1)} %collective-permute-done.5, bf16[3,51,192]{2,1,0:T(8,128)(2,1)S(1)} %collective-permute-done.7, ...), kind=kLoop, calls=%fused_computation.258 | loop fusion | flops 7520256 | bytes 2878848 | tf_op jit(solution)/shard_map/concatenate | solution.py:29
  31.6 1.9 %broadcast_select_fusion.3 = (bf16[153088]{0:T(1024)(128)(2,1)}, bf16[153088]{0:T(1024)(128)(2,1)}) fusion(bf16[153088]{0:T(1024)(128)(2,1)} %collective-permute-done.4, pred[]{:T(512)S(6)} %ne.20, bf16[76544]{0:T(1024)(128)(2,1)S(1)} %get-tuple-element.95, bf16[76544]{0:T(1024)(128)(2,1)S(1)} %get-tuple-element.94), kind=kLoop, calls=%fused_computation.288 | loop fusion | flops 918528 | bytes 1224705 | tf_op jit(solution)/shard_map/jit(_where)/select_n | solution.py:53
  33.5 1.4 concatenate.147
  34.9 1.4 concatenate.148
  36.2 0.9 maximum_bitcast_fusion
  37.1 1.3 copy.10
  38.4 1.6 reshape.64
  40.1 0.6 slice_convert_fusion.1
  40.7 0.7 slice_convert_fusion.6
  41.3 0.6 slice_convert_fusion
  42.0 0.8 fusion.153
  42.8 0.9 reshape.70
  44.0 0.6 fusion.154
  44.7 1.2 reshape.66
  46.0 2.1 %reshape.71 = bf16[192,768,1]{1,0,2:T(8,128)(2,1)} reshape(bf16[147456]{0:T(1024)(128)(2,1)} %get-tuple-element.93) | data formatting | bytes 589824 | tf_op jit(solution)/shard_map/reshape | solution.py:81
  48.1 20.7 %fusion.149 = (f32[45,45]{1,0:T(8,128)S(1)}, f32[45,45,192]{2,1,0:T(8,128)S(1)}) fusion(bf16[48,51,192]{2,1,0:T(8,128)(2,1)S(1)} %get-tuple-element.78, f32[192]{0:T(256)S(1)} %bitcast.185, f32[192]{0:T(256)S(1)} %bitcast.187, f32[192]{0:T(256)S(1)} %bitcast.189, f32[192]{0:T(256)S(1)} %bitcast.191, f32[192]{0:T(256)S(1)} %bitcast.193, ...), kind=kLoop, calls=%fused_computation.324 | loop fusion | flops 64538776 | bytes 35142180 | tf_op jit(solution)/shard_map/reduce_sum | solution.py:125
  69.2 0.7 multiply_reduce_fusion.2
  70.1 4.3 %multiply_convert_fusion = (bf16[45,45,768]{2,1,0:T(8,128)(2,1)}, f32[45,45,768]{2,1,0:T(8,128)S(1)}) fusion(f32[768]{0:T(1024)S(1)} %copy-done.128, bf16[192,768,1]{1,0,2:T(8,128)(2,1)S(1)} %copy-done.10, f32[45,45,192]{2,1,0:T(8,128)S(1)} %get-tuple-element.71, f32[192]{0:T(256)S(1)} %copy-done.134, f32[192]{0:T(256)S(1)} %copy-done.127, ...), kind=kOutput, calls=%fused_computation.61 | convolution fusion | flops 614692800 | bytes 11202120 | tf_op jit(solution)/shard_map/ijc,ch->ijh/dot_general | solution.py:130
  74.4 6.2 %convert_reduce_fusion.1 = (f32[768]{0:T(1024)}, bf16[45,45,768]{2,1,0:T(8,128)(2,1)S(1)}) fusion(f32[45,45,768]{2,1,0:T(8,128)S(1)} %get-tuple-element.152, f32[768]{0:T(1024)S(1)} %copy-done.128, bf16[768,192]{1,0:T(8,128)(2,1)S(1)} %reshape.66, bf16[45,45,192]{2,1,0:T(8,128)(2,1)S(1)} %copy-done.4, f32[192]{0:T(256)S(1)} %copy-done.131), kind=kOutput, calls=%fused_computation.60 | convolution fusion | flops 634132032 | bytes 10410624 | tf_op jit(solution)/shard_map/ijc,hc->ijh/dot_general | solution.py:139
  80.6 1.7 convolution_bitcast_fusion.1
  82.3 2.4 %multiply_reduce_fusion = (f32[192]{0:T(256)}, f32[45,45]{1,0:T(8,128)S(1)}, f32[45,45]{1,0:T(8,128)S(1)}, f32[192]{0:T(256)}, f32[45,45,192]{2,1,0:T(8,128)S(1)}) fusion(f32[45,45,192]{2,1,0:T(8,128)S(1)} %get-tuple-element.71, f32[45,45]{1,0:T(8,128)S(1)} %add_rsqrt_fusion, f32[45,45]{1,0:T(8,128)S(1)} %broadcast_multiply_fusion.2, ...), kind=kOutput, calls=%fused_computation.243 | convolution fusion | flops 600691520 | bytes 6550416 | tf_op jit(solution)/shard_map/ijh,ch->ijc/dot_general | solution.py:141
  84.7 8.1 %fusion.133 = (f32[192]{0:T(256)}, f32[192]{0:T(256)}, f32[192]{0:T(256)}, f32[192]{0:T(256)}, f32[192]{0:T(256)}, /*index=5*/f32[192]{0:T(256)}, f32[192]{0:T(2...) fusion(bf16[48,51,192]{2,1,0:T(8,128)(2,1)S(1)} %get-tuple-elem, ...), kind=kLoop, calls=%fused_computation.241 | loop fusion | flops 24490944 | bytes 17931792 | tf_op jit(solution)/shard_map/reduce_sum | solution.py:118
  92.8 1.8 %fusion.88 = (f32[192]{0:T(256)}, f32[192]{0:T(256)}, f32[192]{0:T(256)}) fusion(bf16[45,45,192]{2,1,0:T(8,128)(2,1)S(1)} %get-tuple-element.69, bf16[48,51,192]{2,1,0:T(8,128)(2,1)S(1)} %get-tuple-element.77), kind=kLoop, calls=%fused_computation.196 | loop fusion | flops 3887424 | bytes 3112704 | tf_op jit(solution)/shard_map/reduce_sum | solution.py:118
  94.5 7.0 %fusion.105 = (f32[192]{0:T(256)}, f32[192]{0:T(256)}, f32[192]{0:T(256)}, f32[192]{0:T(256)}, f32[192]{0:T(256)}, /*index=5*/f32[192]{0:T(256)}, f32[192]{0:T(2...) fusion(bf16[45,45,192]{2,1,0:T(8,128)(2,1)S(1)} %get-tuple-elem, ...), kind=kLoop, calls=%fused_computation.213 | loop fusion | flops 21769152 | bytes 14788992 | tf_op jit(solution)/shard_map/reduce_sum | solution.py:118
  102.0 9.5 %fusion.132 = (f32[192]{0:T(256)S(1)}, f32[192]{0:T(256)S(1)}, f32[192]{0:T(256)S(1)}, f32[192]{0:T(256)S(1)}, f32[192]{0:T(256)S(1)}, /*index=5*/f32[192]{0:T(2...) fusion(bf16[45,45,192]{2,1,0:T(8,128)(2,1)} %copy-done, ...), kind=kLoop, calls=%fused_computation.240 | loop fusion | flops 19049280 | bytes 3999360 | tf_op jit(solution)/shard_map/reduce_sum | solution.py:118
  112.2 3.2 %convolution_bitcast_fusion = f32[768,192]{1,0:T(8,128)S(1)} fusion(bf16[45,45,768]{2,1,0:T(8,128)(2,1)} %get-tuple-element.151, bf16[45,45,192]{2,1,0:T(8,128)(2,1)S(1)} %copy-done.5, f32[192]{0:T(256)} %get-tuple-element.87), kind=kOutput, calls=%fused_computation.262 | convolution fusion | flops 598363200 | bytes 4478592 | tf_op jit(solution)/shard_map/ijh,ijc->hc/dot_general | solution.py:152
  115.6 2.4 %fusion.59 = (f32[192]{0:T(256)S(1)}, f32[192]{0:T(256)S(1)}, bf16[45,45,192]{2,1,0:T(8,128)(2,1)}) fusion(bf16[45,45,192]{2,1,0:T(8,128)(2,1)S(1)} %copy-done.5, f32[192]{0:T(256)S(1)} %copy-done.133, f32[192]{0:T(256)S(1)} %copy-done.132, bf16[45,45,192]{2,1,0:T(8,128)(2,1)S(1)} %copy-done.3, bf16[45,45,768]{2,1,0:T(8,128)(2,1)S(1)} %copy-done.135, ...), kind=kOutput, calls=%fused_computation.167 | convolution fusion | flops 601862016 | bytes 5741184 | tf_op jit(solution)/shard_map/ijh,hc->ijc/dot_general | solution.py:134
  118.0 0.4 reshape.68
  118.5 1.0 concatenate.160
  119.6 1.1 reshape.69
  120.7 0.9 fusion.144
  121.6 0.3 copy.15
  121.9 0.4 convert_element_type.605
  122.3 3.2 %collective-permute-start.13 = (bf16[153088]{0:T(1024)(128)(2,1)S(1)}, bf16[153088]{0:T(1024)(128)(2,1)S(1)}, u32[]{:S(2)}, u32[]{:S(2)}) collective-permute-start(bf16[153088]{0:T(1024)(128)(2,1)S(1)} %convert_element_type.605), channel_id=1, source_target_pairs={{0,1},{1,0},{2,3},{3,2},{4,5},{5,4},{6,7},{7,6},{8,9},{9,8},{10,11... | collective-permute-start | bytes 918536 | tf_op jit(solution)/shard_map/ppermute | solution.py:44
  125.4 0.6 broadcast_select_fusion.1
  126.1 0.3 copy.14
  126.4 0.6 select_n.133
  127.4 4.8 %collective-permute-start.10 = (bf16[45,3,192]{2,1,0:T(4,128)(2,1)S(1)}, bf16[45,3,192]{2,1,0:T(4,128)(2,1)S(1)}, u32[]{:S(2)}, u32[]{:S(2)}) collective-permute-start(bf16[45,3,192]{2,1,0:T(4,128)(2,1)S(1)} %get-tuple-element.81), channel_id=1, source_target_pairs={{4,0},{8,4},{12,8},{16,12},{20,16},{24,20},{28,24},{0,28},{5,1},{9... | collective-permute-start | bytes 155528 | tf_op jit(solution)/shard_map/ppermute | solution.py:28
  132.2 0.9 collective-permute-done.14
  133.2 1.2 collective-permute-start.15
  134.4 5.1 %collective-permute-done.9 = bf16[45,3,192]{2,1,0:T(4,128)(2,1)S(1)} collective-permute-done((bf16[45,3,192]{2,1,0:T(4,128)(2,1)S(1)}, bf16[45,3,192]{2,1,0:T(4,128)(2,1)S(1)}, u32[]{:S(2)}, u32[]{:S(2)}) %collective-permute-start.9) | collective-permute-done | bytes 51872 | tf_op jit(solution)/shard_map/ppermute | solution.py:25
  139.5 1.3 collective-permute-start.11
  140.8 3.0 %collective-permute-start.12 = (bf16[3,51,192]{2,1,0:T(8,128)(2,1)S(1)}, bf16[3,51,192]{2,1,0:T(8,128)(2,1)S(1)}, u32[]{:S(2)}, u32[]{:S(2)}) collective-permute-start(bf16[3,51,192]{2,1,0:T(8,128)(2,1)S(1)} %get-tuple-element.76), channel_id=1, source_target_pairs={{0,1},{1,2},{2,3},{4,5},{5,6},{6,7},{8,9},{9,10},{10,11},{12,13},{... | collective-permute-start | bytes 176264 | tf_op jit(solution)/shard_map/ppermute | solution.py:25
  144.5 0.3 collective-permute-done.12
  144.8 1.3 pad_maximum_fusion.1
  146.1 2.4 %collective-permute-done.16 = bf16[19136]{0:T(1024)(128)(2,1)S(1)} collective-permute-done((bf16[19136]{0:T(1024)(128)(2,1)S(1)}, bf16[19136]{0:T(1024)(128)(2,1)S(1)}, u32[]{:S(2)}, u32[]{:S(2)}) %collective-permute-start.16) | collective-permute-done | bytes 38304 | tf_op jit(solution)/shard_map/ppermute | solution.py:44
  149.1 19.2 %fusion.58 = bf16[45,45,192]{2,1,0:T(8,128)(2,1)} fusion(bf16[45,45,192]{2,1,0:T(8,128)(2,1)S(1)} %copy-done.6, bf16[45,45,192]{2,1,0:T(8,128)(2,1)S(1)} %copy-done.1, bf16[45,3,192]{2,1,0:T(4,128)(2,1)S(1)} %collective-permute-done.9, bf16[45,3,192]{2,1,0:T(4,128)(2,1)S(1)} %collective-permute-done.10, bf16[48,51,192]{2,1,0:T(8,128)(2,1)S(1)} %get-tuple-element.74, ...), kind=kLoop, calls=%fused_computation.166 | loop fusion | flops 64929600 | bytes 35133312 | tf_op jit(solution)/shard_map/convert_element_type | solution.py:194
  168.3 0.7 multiply_add_fusion
  (313 shorter events, 3.0 us)
Async XLA Ops:
  0.6 22.1 %copy-start.2 = (bf16[45,45,192]{2,1,0:T(8,128)(2,1)S(1)}, bf16[45,45,192]{2,1,0:T(8,128)(2,1)}, u32[]{:S(2)}) copy-start(bf16[45,45,192]{2,1,0:T(8,128)(2,1)} %param.4) | copy-start | bytes 2332804
  1.5 5.8 %collective-permute-start = (bf16[9568]{0:T(1024)(128)(2,1)S(1)}, bf16[9568]{0:T(1024)(128)(2,1)S(1)}, u32[]{:S(2)}, u32[]{:S(2)}) collective-permute-start(bf16[9568]{0:T(1024)(128)(2,1)S(1)} %convert_element_type.488), channel_id=1, source_target_pairs={{0,16},{4,20},{8,24},{12,28},{16,0},{20,4},{24,8},{28,12},{1,17},{... | collective-permute-start | bytes 57416 | tf_op jit(solution)/shard_map/ppermute | solution.py:44
  8.2 4.0 %collective-permute-start.1 = (bf16[19136]{0:T(1024)(128)(2,1)S(1)}, bf16[19136]{0:T(1024)(128)(2,1)S(1)}, u32[]{:S(2)}, u32[]{:S(2)}) collective-permute-start(bf16[19136]{0:T(1024)(128)(2,1)S(1)} %pad_maximum_fusion.15), channel_id=1, source_target_pairs={{0,8},{4,12},{8,0},{12,4},{16,24},{20,28},{24,16},{28,20},{1,9},{5... | collective-permute-start | bytes 114824 | tf_op jit(solution)/shard_map/ppermute | solution.py:44
  12.4 7.8 %collective-permute-start.2 = (bf16[38272]{0:T(1024)(128)(2,1)S(1)}, bf16[38272]{0:T(1024)(128)(2,1)S(1)}, u32[]{:S(2)}, u32[]{:S(2)}) collective-permute-start(bf16[38272]{0:T(1024)(128)(2,1)S(1)} %pad_maximum_fusion.14), channel_id=1, source_target_pairs={{0,4},{4,0},{8,12},{12,8},{16,20},{20,16},{24,28},{28,24},{1,5},{5... | collective-permute-start | bytes 229640 | tf_op jit(solution)/shard_map/ppermute | solution.py:44
  15.4 7.3 %collective-permute-start.5 = (bf16[45,3,192]{2,1,0:T(4,128)(2,1)S(1)}, bf16[45,3,192]{2,1,0:T(4,128)(2,1)S(1)}, u32[]{:S(2)}, u32[]{:S(2)}) collective-permute-start(bf16[45,3,192]{2,1,0:T(4,128)(2,1)S(1)} %get-tuple-element.83), channel_id=1, source_target_pairs={{0,4},{4,8},{8,12},{12,16},{16,20},{20,24},{24,28},{28,0},{1,5},{5... | collective-permute-start | bytes 155528 | tf_op jit(solution)/shard_map/ppermute | solution.py:25
  15.6 7.1 %collective-permute-start.6 = (bf16[45,3,192]{2,1,0:T(4,128)(2,1)S(1)}, bf16[45,3,192]{2,1,0:T(4,128)(2,1)S(1)}, u32[]{:S(2)}, u32[]{:S(2)}) collective-permute-start(bf16[45,3,192]{2,1,0:T(4,128)(2,1)S(1)} %get-tuple-element.84), channel_id=1, source_target_pairs={{4,0},{8,4},{12,8},{16,12},{20,16},{24,20},{28,24},{0,28},{5,1},{9... | collective-permute-start | bytes 155528 | tf_op jit(solution)/shard_map/ppermute | solution.py:28
  20.4 5.3 %collective-permute-start.3 = (bf16[76544]{0:T(1024)(128)(2,1)S(1)}, bf16[76544]{0:T(1024)(128)(2,1)S(1)}, u32[]{:S(2)}, u32[]{:S(2)}) collective-permute-start(bf16[76544]{0:T(1024)(128)(2,1)S(1)} %pad_maximum_fusion.7), channel_id=1, source_target_pairs={{0,2},{1,3},{2,0},{3,1},{4,6},{5,7},{6,4},{7,5},{8,10},{9,11},{10,... | collective-permute-start | bytes 459272 | tf_op jit(solution)/shard_map/ppermute | solution.py:44
  22.8 6.3 %collective-permute-start.7 = (bf16[3,51,192]{2,1,0:T(8,128)(2,1)S(1)}, bf16[3,51,192]{2,1,0:T(8,128)(2,1)S(1)}, u32[]{:S(2)}, u32[]{:S(2)}) collective-permute-start(bf16[3,51,192]{2,1,0:T(8,128)(2,1)S(1)} %get-tuple-element.79), channel_id=1, source_target_pairs={{0,1},{1,2},{2,3},{4,5},{5,6},{6,7},{8,9},{9,10},{10,11},{12,13},{... | collective-permute-start | bytes 176264 | tf_op jit(solution)/shard_map/ppermute | solution.py:25
  24.1 5.1 %collective-permute-start.8 = (bf16[3,51,192]{2,1,0:T(8,128)(2,1)S(1)}, bf16[3,51,192]{2,1,0:T(8,128)(2,1)}, u32[]{:S(2)}, u32[]{:S(2)}) collective-permute-start(bf16[3,51,192]{2,1,0:T(8,128)(2,1)S(1)} %get-tuple-element.80), channel_id=1, source_target_pairs={{1,0},{2,1},{3,2},{5,4},{6,5},{7,6},{9,8},{10,9},{11,10},{13,12},{... | collective-permute-start | bytes 176264 | tf_op jit(solution)/shard_map/ppermute | solution.py:28
  26.5 5.1 %collective-permute-start.4 = (bf16[153088]{0:T(1024)(128)(2,1)}, bf16[153088]{0:T(1024)(128)(2,1)}, u32[]{:S(2)}, u32[]{:S(2)}) collective-permute-start(bf16[153088]{0:T(1024)(128)(2,1)} %pad_maximum_fusion.6), channel_id=1, source_target_pairs={{0,1},{1,0},{2,3},{3,2},{4,5},{5,4},{6,7},{7,6},{8,9},{9,8},{10,11... | collective-permute-start | bytes 918536 | tf_op jit(solution)/shard_map/ppermute | solution.py:44
  43.7 25.1 %copy-start.12 = (f32[1,1,192]{2,1,0:T(1,128)}, f32[1,1,192]{2,1,0:T(1,128)S(1)}, u32[]{:S(2)}) copy-start(f32[1,1,192]{2,1,0:T(1,128)S(1)} %get-tuple-element.138) | copy-start | bytes 2308
  43.7 25.1 %copy-start.14 = (f32[1,1,192]{2,1,0:T(1,128)}, f32[1,1,192]{2,1,0:T(1,128)S(1)}, u32[]{:S(2)}) copy-start(f32[1,1,192]{2,1,0:T(1,128)S(1)} %get-tuple-element.139) | copy-start | bytes 2308
  43.7 25.1 %copy-start.16 = (f32[1,1,192]{2,1,0:T(1,128)}, f32[1,1,192]{2,1,0:T(1,128)S(1)}, u32[]{:S(2)}) copy-start(f32[1,1,192]{2,1,0:T(1,128)S(1)} %get-tuple-element.140) | copy-start | bytes 2308
  43.7 25.1 %copy-start.18 = (f32[1,1,192]{2,1,0:T(1,128)}, f32[1,1,192]{2,1,0:T(1,128)S(1)}, u32[]{:S(2)}) copy-start(f32[1,1,192]{2,1,0:T(1,128)S(1)} %get-tuple-element.141) | copy-start | bytes 2308
  43.7 25.1 %copy-start.20 = (f32[1,1,192]{2,1,0:T(1,128)}, f32[1,1,192]{2,1,0:T(1,128)S(1)}, u32[]{:S(2)}) copy-start(f32[1,1,192]{2,1,0:T(1,128)S(1)} %get-tuple-element.142) | copy-start | bytes 2308
  43.7 25.1 %copy-start.22 = (f32[1,1,192]{2,1,0:T(1,128)}, f32[1,1,192]{2,1,0:T(1,128)S(1)}, u32[]{:S(2)}) copy-start(f32[1,1,192]{2,1,0:T(1,128)S(1)} %get-tuple-element.143) | copy-start | bytes 2308
  43.7 25.1 %copy-start.24 = (f32[1,1,192]{2,1,0:T(1,128)}, f32[1,1,192]{2,1,0:T(1,128)S(1)}, u32[]{:S(2)}) copy-start(f32[1,1,192]{2,1,0:T(1,128)S(1)} %get-tuple-element.144) | copy-start | bytes 2308
  43.7 25.1 %copy-start.26 = (f32[1,1,192]{2,1,0:T(1,128)}, f32[1,1,192]{2,1,0:T(1,128)S(1)}, u32[]{:S(2)}) copy-start(f32[1,1,192]{2,1,0:T(1,128)S(1)} %get-tuple-element.145) | copy-start | bytes 2308
  43.8 25.1 %copy-start.28 = (f32[1,1,192]{2,1,0:T(1,128)}, f32[1,1,192]{2,1,0:T(1,128)S(1)}, u32[]{:S(2)}) copy-start(f32[1,1,192]{2,1,0:T(1,128)S(1)} %get-tuple-element.146) | copy-start | bytes 2308
  43.8 25.1 %copy-start.30 = (f32[1,1,192]{2,1,0:T(1,128)}, f32[1,1,192]{2,1,0:T(1,128)S(1)}, u32[]{:S(2)}) copy-start(f32[1,1,192]{2,1,0:T(1,128)S(1)} %get-tuple-element.147) | copy-start | bytes 2308
  43.8 25.1 %copy-start.32 = (f32[1,1,192]{2,1,0:T(1,128)}, f32[1,1,192]{2,1,0:T(1,128)S(1)}, u32[]{:S(2)}) copy-start(f32[1,1,192]{2,1,0:T(1,128)S(1)} %get-tuple-element.148) | copy-start | bytes 2308
  43.8 25.0 %copy-start.34 = (f32[1,1,192]{2,1,0:T(1,128)}, f32[1,1,192]{2,1,0:T(1,128)S(1)}, u32[]{:S(2)}) copy-start(f32[1,1,192]{2,1,0:T(1,128)S(1)} %get-tuple-element.119) | copy-start | bytes 2308
  43.8 25.0 %copy-start.36 = (f32[1,1,192]{2,1,0:T(1,128)}, f32[1,1,192]{2,1,0:T(1,128)S(1)}, u32[]{:S(2)}) copy-start(f32[1,1,192]{2,1,0:T(1,128)S(1)} %get-tuple-element.120) | copy-start | bytes 2308
  43.8 25.0 %copy-start.38 = (f32[1,1,192]{2,1,0:T(1,128)}, f32[1,1,192]{2,1,0:T(1,128)S(1)}, u32[]{:S(2)}) copy-start(f32[1,1,192]{2,1,0:T(1,128)S(1)} %get-tuple-element.121) | copy-start | bytes 2308
  43.8 25.0 %copy-start.40 = (f32[1,1,192]{2,1,0:T(1,128)}, f32[1,1,192]{2,1,0:T(1,128)S(1)}, u32[]{:S(2)}) copy-start(f32[1,1,192]{2,1,0:T(1,128)S(1)} %get-tuple-element.122) | copy-start | bytes 2308
  43.8 25.0 %copy-start.42 = (f32[1,1,192]{2,1,0:T(1,128)}, f32[1,1,192]{2,1,0:T(1,128)S(1)}, u32[]{:S(2)}) copy-start(f32[1,1,192]{2,1,0:T(1,128)S(1)} %get-tuple-element.123) | copy-start | bytes 2308
  43.9 25.0 %copy-start.44 = (f32[1,1,192]{2,1,0:T(1,128)}, f32[1,1,192]{2,1,0:T(1,128)S(1)}, u32[]{:S(2)}) copy-start(f32[1,1,192]{2,1,0:T(1,128)S(1)} %get-tuple-element.124) | copy-start | bytes 2308
  43.9 25.0 %copy-start.46 = (f32[1,1,192]{2,1,0:T(1,128)}, f32[1,1,192]{2,1,0:T(1,128)S(1)}, u32[]{:S(2)}) copy-start(f32[1,1,192]{2,1,0:T(1,128)S(1)} %get-tuple-element.125) | copy-start | bytes 2308
  43.9 25.0 %copy-start.48 = (f32[1,1,192]{2,1,0:T(1,128)}, f32[1,1,192]{2,1,0:T(1,128)S(1)}, u32[]{:S(2)}) copy-start(f32[1,1,192]{2,1,0:T(1,128)S(1)} %get-tuple-element.126) | copy-start | bytes 2308
  43.9 25.0 %copy-start.50 = (f32[1,1,192]{2,1,0:T(1,128)}, f32[1,1,192]{2,1,0:T(1,128)S(1)}, u32[]{:S(2)}) copy-start(f32[1,1,192]{2,1,0:T(1,128)S(1)} %get-tuple-element.127) | copy-start | bytes 2308
  43.9 25.0 %copy-start.52 = (f32[1,1,192]{2,1,0:T(1,128)}, f32[1,1,192]{2,1,0:T(1,128)S(1)}, u32[]{:S(2)}) copy-start(f32[1,1,192]{2,1,0:T(1,128)S(1)} %get-tuple-element.128) | copy-start | bytes 2308
  43.9 25.0 %copy-start.54 = (f32[1,1,192]{2,1,0:T(1,128)}, f32[1,1,192]{2,1,0:T(1,128)S(1)}, u32[]{:S(2)}) copy-start(f32[1,1,192]{2,1,0:T(1,128)S(1)} %get-tuple-element.129) | copy-start | bytes 2308
  43.9 25.0 %copy-start.56 = (f32[1,1,192]{2,1,0:T(1,128)}, f32[1,1,192]{2,1,0:T(1,128)S(1)}, u32[]{:S(2)}) copy-start(f32[1,1,192]{2,1,0:T(1,128)S(1)} %get-tuple-element.130) | copy-start | bytes 2308
  43.9 25.0 %copy-start.58 = (f32[1,1,192]{2,1,0:T(1,128)}, f32[1,1,192]{2,1,0:T(1,128)S(1)}, u32[]{:S(2)}) copy-start(f32[1,1,192]{2,1,0:T(1,128)S(1)} %get-tuple-element.131) | copy-start | bytes 2308
  43.9 25.0 %copy-start.60 = (f32[1,1,192]{2,1,0:T(1,128)}, f32[1,1,192]{2,1,0:T(1,128)S(1)}, u32[]{:S(2)}) copy-start(f32[1,1,192]{2,1,0:T(1,128)S(1)} %get-tuple-element.132) | copy-start | bytes 2308
  43.9 25.0 %copy-start.62 = (f32[1,1,192]{2,1,0:T(1,128)}, f32[1,1,192]{2,1,0:T(1,128)S(1)}, u32[]{:S(2)}) copy-start(f32[1,1,192]{2,1,0:T(1,128)S(1)} %get-tuple-element.133) | copy-start | bytes 2308
  44.0 25.0 %copy-start.64 = (f32[1,1,192]{2,1,0:T(1,128)}, f32[1,1,192]{2,1,0:T(1,128)S(1)}, u32[]{:S(2)}) copy-start(f32[1,1,192]{2,1,0:T(1,128)S(1)} %get-tuple-element.134) | copy-start | bytes 2308
  44.0 25.0 %copy-start.66 = (f32[1,1,192]{2,1,0:T(1,128)}, f32[1,1,192]{2,1,0:T(1,128)S(1)}, u32[]{:S(2)}) copy-start(f32[1,1,192]{2,1,0:T(1,128)S(1)} %get-tuple-element.135) | copy-start | bytes 2308
  44.0 25.0 %copy-start.68 = (f32[1,1,192]{2,1,0:T(1,128)}, f32[1,1,192]{2,1,0:T(1,128)S(1)}, u32[]{:S(2)}) copy-start(f32[1,1,192]{2,1,0:T(1,128)S(1)} %get-tuple-element.136) | copy-start | bytes 2308
  44.0 25.0 %copy-start.70 = (f32[1,1,192]{2,1,0:T(1,128)}, f32[1,1,192]{2,1,0:T(1,128)S(1)}, u32[]{:S(2)}) copy-start(f32[1,1,192]{2,1,0:T(1,128)S(1)} %get-tuple-element.137) | copy-start | bytes 2308
  44.6 24.4 %copy-start.72 = (f32[1,1,192]{2,1,0:T(1,128)}, f32[1,1,192]{2,1,0:T(1,128)S(1)}, u32[]{:S(2)}) copy-start(f32[1,1,192]{2,1,0:T(1,128)S(1)} %get-tuple-element.100) | copy-start | bytes 2308
  44.6 24.4 %copy-start.74 = (f32[1,1,192]{2,1,0:T(1,128)}, f32[1,1,192]{2,1,0:T(1,128)S(1)}, u32[]{:S(2)}) copy-start(f32[1,1,192]{2,1,0:T(1,128)S(1)} %get-tuple-element.101) | copy-start | bytes 2308
  44.7 24.4 %copy-start.76 = (f32[1,1,192]{2,1,0:T(1,128)}, f32[1,1,192]{2,1,0:T(1,128)S(1)}, u32[]{:S(2)}) copy-start(f32[1,1,192]{2,1,0:T(1,128)S(1)} %get-tuple-element.102) | copy-start | bytes 2308
  44.7 24.4 %copy-start.78 = (f32[1,1,192]{2,1,0:T(1,128)}, f32[1,1,192]{2,1,0:T(1,128)S(1)}, u32[]{:S(2)}) copy-start(f32[1,1,192]{2,1,0:T(1,128)S(1)} %get-tuple-element.103) | copy-start | bytes 2308
  44.7 24.4 %copy-start.80 = (f32[1,1,192]{2,1,0:T(1,128)}, f32[1,1,192]{2,1,0:T(1,128)S(1)}, u32[]{:S(2)}) copy-start(f32[1,1,192]{2,1,0:T(1,128)S(1)} %get-tuple-element.104) | copy-start | bytes 2308
  44.7 24.4 %copy-start.82 = (f32[1,1,192]{2,1,0:T(1,128)}, f32[1,1,192]{2,1,0:T(1,128)S(1)}, u32[]{:S(2)}) copy-start(f32[1,1,192]{2,1,0:T(1,128)S(1)} %get-tuple-element.105) | copy-start | bytes 2308
  44.7 24.4 %copy-start.84 = (f32[1,1,192]{2,1,0:T(1,128)}, f32[1,1,192]{2,1,0:T(1,128)S(1)}, u32[]{:S(2)}) copy-start(f32[1,1,192]{2,1,0:T(1,128)S(1)} %get-tuple-element.106) | copy-start | bytes 2308
  44.7 24.4 %copy-start.86 = (f32[1,1,192]{2,1,0:T(1,128)}, f32[1,1,192]{2,1,0:T(1,128)S(1)}, u32[]{:S(2)}) copy-start(f32[1,1,192]{2,1,0:T(1,128)S(1)} %get-tuple-element.107) | copy-start | bytes 2308
  46.0 28.4 %copy-start.7 = (bf16[768,192]{1,0:T(8,128)(2,1)}, bf16[768,192]{1,0:T(8,128)(2,1)S(1)}, u32[]{:S(2)}) copy-start(bf16[768,192]{1,0:T(8,128)(2,1)S(1)} %reshape.66) | copy-start | bytes 884740
  101.6 9.9 %copy-start.88 = (f32[192]{0:T(256)S(1)}, f32[192]{0:T(256)}, u32[]{:S(2)}) copy-start(f32[192]{0:T(256)} %get-tuple-element.5) | copy-start | bytes 2308
  101.6 9.9 %copy-start.89 = (f32[192]{0:T(256)S(1)}, f32[192]{0:T(256)}, u32[]{:S(2)}) copy-start(f32[192]{0:T(256)} %get-tuple-element.6) | copy-start | bytes 2308
  101.7 9.9 %copy-start.90 = (f32[192]{0:T(256)S(1)}, f32[192]{0:T(256)}, u32[]{:S(2)}) copy-start(f32[192]{0:T(256)} %get-tuple-element.7) | copy-start | bytes 2308
  102.0 10.1 %copy-start.5 = (bf16[45,45,192]{2,1,0:T(8,128)(2,1)S(1)}, bf16[45,45,192]{2,1,0:T(8,128)(2,1)}, u32[]{:S(2)}) copy-start(bf16[45,45,192]{2,1,0:T(8,128)(2,1)} %param.7) | copy-start | bytes 2332804
  122.3 4.7 %collective-permute-start.13 = (bf16[153088]{0:T(1024)(128)(2,1)S(1)}, bf16[153088]{0:T(1024)(128)(2,1)S(1)}, u32[]{:S(2)}, u32[]{:S(2)}) collective-permute-start(bf16[153088]{0:T(1024)(128)(2,1)S(1)} %convert_element_type.605), channel_id=1, source_target_pairs={{0,1},{1,0},{2,3},{3,2},{4,5},{5,4},{6,7},{7,6},{8,9},{9,8},{10,11... | collective-permute-start | bytes 918536 | tf_op jit(solution)/shard_map/ppermute | solution.py:44
  127.1 6.0 %collective-permute-start.14 = (bf16[76544]{0:T(1024)(128)(2,1)S(1)}, bf16[76544]{0:T(1024)(128)(2,1)S(1)}, u32[]{:S(2)}, u32[]{:S(2)}) collective-permute-start(bf16[76544]{0:T(1024)(128)(2,1)S(1)} %select_convert_fusion), channel_id=1, source_target_pairs={{0,2},{1,3},{2,0},{3,1},{4,6},{5,7},{6,4},{7,5},{8,10},{9,11},{10,... | collective-permute-start | bytes 459272 | tf_op jit(solution)/shard_map/ppermute | solution.py:44
  127.4 7.0 %collective-permute-start.10 = (bf16[45,3,192]{2,1,0:T(4,128)(2,1)S(1)}, bf16[45,3,192]{2,1,0:T(4,128)(2,1)S(1)}, u32[]{:S(2)}, u32[]{:S(2)}) collective-permute-start(bf16[45,3,192]{2,1,0:T(4,128)(2,1)S(1)} %get-tuple-element.81), channel_id=1, source_target_pairs={{4,0},{8,4},{12,8},{16,12},{20,16},{24,20},{28,24},{0,28},{5,1},{9... | collective-permute-start | bytes 155528 | tf_op jit(solution)/shard_map/ppermute | solution.py:28
  132.2 7.3 %collective-permute-start.9 = (bf16[45,3,192]{2,1,0:T(4,128)(2,1)S(1)}, bf16[45,3,192]{2,1,0:T(4,128)(2,1)S(1)}, u32[]{:S(2)}, u32[]{:S(2)}) collective-permute-start(bf16[45,3,192]{2,1,0:T(4,128)(2,1)S(1)} %get-tuple-element.82), channel_id=1, source_target_pairs={{0,4},{4,8},{8,12},{12,16},{16,20},{20,24},{24,28},{28,0},{1,5},{5... | collective-permute-start | bytes 155528 | tf_op jit(solution)/shard_map/ppermute | solution.py:25
  133.2 10.7 %collective-permute-start.15 = (bf16[38272]{0:T(1024)(128)(2,1)S(1)}, bf16[38272]{0:T(1024)(128)(2,1)S(1)}, u32[]{:S(2)}, u32[]{:S(2)}) collective-permute-start(bf16[38272]{0:T(1024)(128)(2,1)S(1)} %select_convert_fusion.1), channel_id=1, source_target_pairs={{0,4},{4,0},{8,12},{12,8},{16,20},{20,16},{24,28},{28,24},{1,5},{5... | collective-permute-start | bytes 229640 | tf_op jit(solution)/shard_map/ppermute | solution.py:44
  139.5 4.9 %collective-permute-start.11 = (bf16[3,51,192]{2,1,0:T(8,128)(2,1)S(1)}, bf16[3,51,192]{2,1,0:T(8,128)(2,1)S(1)}, u32[]{:S(2)}, u32[]{:S(2)}) collective-permute-start(bf16[3,51,192]{2,1,0:T(8,128)(2,1)S(1)} %get-tuple-element.75), channel_id=1, source_target_pairs={{1,0},{2,1},{3,2},{5,4},{6,5},{7,6},{9,8},{10,9},{11,10},{13,12},{... | collective-permute-start | bytes 176264 | tf_op jit(solution)/shard_map/ppermute | solution.py:28
  140.8 3.9 %collective-permute-start.12 = (bf16[3,51,192]{2,1,0:T(8,128)(2,1)S(1)}, bf16[3,51,192]{2,1,0:T(8,128)(2,1)S(1)}, u32[]{:S(2)}, u32[]{:S(2)}) collective-permute-start(bf16[3,51,192]{2,1,0:T(8,128)(2,1)S(1)} %get-tuple-element.76), channel_id=1, source_target_pairs={{0,1},{1,2},{2,3},{4,5},{5,6},{6,7},{8,9},{9,10},{10,11},{12,13},{... | collective-permute-start | bytes 176264 | tf_op jit(solution)/shard_map/ppermute | solution.py:25
  144.4 4.0 %collective-permute-start.16 = (bf16[19136]{0:T(1024)(128)(2,1)S(1)}, bf16[19136]{0:T(1024)(128)(2,1)S(1)}, u32[]{:S(2)}, u32[]{:S(2)}) collective-permute-start(bf16[19136]{0:T(1024)(128)(2,1)S(1)} %select_convert_fusion.2), channel_id=1, source_target_pairs={{0,8},{4,12},{8,0},{12,4},{16,24},{20,28},{24,16},{28,20},{1,9},{5... | collective-permute-start | bytes 114824 | tf_op jit(solution)/shard_map/ppermute | solution.py:44
  148.6 19.6 %collective-permute-start.17 = (bf16[9568]{0:T(1024)(128)(2,1)S(1)}, bf16[9568]{0:T(1024)(128)(2,1)S(1)}, u32[]{:S(2)}, u32[]{:S(2)}) collective-permute-start(bf16[9568]{0:T(1024)(128)(2,1)S(1)} %select_convert_fusion.3), channel_id=1, source_target_pairs={{0,16},{4,20},{8,24},{12,28},{16,0},{20,4},{24,8},{28,12},{1,17},{... | collective-permute-start | bytes 57416 | tf_op jit(solution)/shard_map/ppermute | solution.py:44
  149.0 19.2 %copy-start.9 = (f32[9568]{0:T(1024)S(1)}, f32[9568]{0:T(1024)}, u32[]{:S(2)}) copy-start(f32[9568]{0:T(1024)} %param.5) | copy-start | bytes 114820
  149.1 19.2 %copy-start.11 = (f32[9568]{0:T(1024)S(1)}, f32[9568]{0:T(1024)}, u32[]{:S(2)}) copy-start(f32[9568]{0:T(1024)} %param.6) | copy-start | bytes 114820
  (90 other events, 572.8 us)

commit v2 on v0

v2 whole, which is shorter than its diff:
```python
import math

import jax
import jax.numpy as jnp
from jax import lax
from jax.experimental import pallas as pl
from jax.experimental.pallas import tpu as pltpu
from jax.sharding import PartitionSpec as P

C = 192
H = 768
KS = 7
RAD = KS // 2
LANES = 128
CP = 256
TAPS = KS * KS
EPSILON = 1e-06
STEP_SIZE = 0.003
NOISE_COEF = 0.08
GELU_A = math.sqrt(2.0 / math.pi)
GELU_B = GELU_A * 0.044715
F32 = jnp.float32
BF16 = jnp.bfloat16
ROW_OUT = C
ROW_TAPS = 2 * C
ROW_NORM = ROW_TAPS + TAPS // 4
ROW_BIAS_IN = ROW_NORM + 1
ROW_LAST = ROW_NORM + 2
ROWS = ROW_LAST + 1
TILES = H // LANES
WINDOW = 16
VMEM = 56 << 20


def exchange_bits(axes):
    steps = []
    for axis in axes:
        bit = lax.axis_size(axis) // 2
        while bit:
            steps.append((axis, bit))
            bit //= 2
    return steps


def swap(values, axis, bit):
    return lax.ppermute(values, axis, [(i, i ^ bit) for i in range(lax.axis_size(axis))])


def shift_both(low_edge, high_edge, axis, periodic):
    count = lax.axis_size(axis)
    forward = [(i, i + 1) for i in range(count - 1)]
    if periodic:
        forward.append((count - 1, 0))
    backward = [(target, source) for source, target in forward]
    return lax.ppermute(high_edge, axis, forward), lax.ppermute(low_edge, axis, backward)


def reversed_bits(number, count):
    result = 0
    for k in range(count):
        result |= ((number >> k) & 1) << (count - 1 - k)
    return result


def padded_field(block):
    west, east = shift_both(block[:, :RAD], block[:, -RAD:], "lon", True)
    wide = jnp.concatenate([west, block, east], axis=1)
    south, north = shift_both(wide[:RAD], wide[-RAD:], "lat", False)
    return jnp.concatenate([south, wide, north], axis=0)


def up(value, multiple):
    return -(-value // multiple) * multiple


def split_quarter(tiles, quarter):
    lane = lax.broadcasted_iota(jnp.int32, tiles[0].shape, 1)
    low = lane < LANES // 2
    first = 3 * quarter // 2
    if quarter % 2 == 0:
        return tiles[first], jnp.where(low, tiles[first + 1], 0.0)
    left = pltpu.roll(tiles[first], LANES // 2, 1)
    right = pltpu.roll(tiles[first + 1], LANES // 2, 1)
    return jnp.where(low, left, right), jnp.where(low, right, 0.0)


def join_quarters(quarters):
    lane = lax.broadcasted_iota(jnp.int32, quarters[0][0].shape, 1)
    low = lane < LANES // 2
    tiles = []
    for even in (0, 2):
        first, second = quarters[even]
        turned = pltpu.roll(quarters[even + 1][0], LANES // 2, 1)
        last = pltpu.roll(quarters[even + 1][1], LANES // 2, 1)
        tiles += [first, jnp.where(low, second, turned), jnp.where(low, turned, last)]
    return tiles


def depthwise_block(x_ref, k_ref, row, out_rows, lon_regs, store, flip):
    steps = lon_regs // 2

    def body(step, carry):
        tile = step // steps
        lon = pl.multiple_of(step % steps * 16, 16)
        sums = [None] * out_rows
        for offset in range(out_rows + KS - 1):
            for b in range(KS):
                window = x_ref[tile, row + offset, pl.ds(lon + b, 16), :]
                for r in range(out_rows):
                    a = offset - r
                    if 0 <= a < KS:
                        tap = a * KS + b
                        if flip:
                            tap = TAPS - 1 - tap
                        term = window * k_ref[tile, pl.ds(tap, 1), :]
                        sums[r] = term if sums[r] is None else sums[r] + term
        store(tile, lon, sums)
        return carry

    lax.fori_loop(0, 2 * steps, body, 0)


def layer_kernel(order, starts, rows, lon_pad, block_rows,
                 me_ref, gathered_ref, x_ref, feat_ref, up_ref,
                 out_ref, gconv_ref, gin_ref, gout_ref, sums_ref, taps_ref,
                 w_ref, win_ref, wint_ref, wout_ref, woutt_ref, wo32_ref, conv_ref):
    me = me_ref[0]
    w_ref[...] = jnp.zeros_like(w_ref)
    for position, start in zip(order, starts):
        share = gathered_ref[position ^ me].astype(F32)
        for j in range(TILES):
            w_ref[j, pl.ds(start, WINDOW), :] += share[:, j * LANES : (j + 1) * LANES]
    rest = lax.broadcasted_iota(jnp.int32, (CP - C, LANES), 0)
    for j in range(TILES):
        lanes = slice(j * LANES, (j + 1) * LANES)
        main = w_ref[j, pl.ds(0, C), :]
        bias = jnp.where(rest == 0, w_ref[j, pl.ds(ROW_BIAS_IN, 1), :], 0.0)
        whole = jnp.concatenate([main, bias], axis=0)
        win_ref[:, lanes] = whole.astype(BF16)
        wint_ref[lanes, :] = whole.T.astype(BF16)
    for quarter in range(4):
        tiles = [w_ref[j, pl.ds(ROW_OUT, C), :] for j in range(TILES)]
        pair = split_quarter(tiles, quarter)
        tail = split_quarter([w_ref[j, pl.ds(ROW_TAPS, 16), :] for j in range(TILES)], quarter)
        for t in range(2):
            wo32_ref[t, pl.ds(quarter, C, stride=4), :] = pair[t]
            taps_ref[t, pl.ds(quarter, 16, stride=4), :] = tail[t]
    for t in range(2):
        lanes = slice(t * LANES, (t + 1) * LANES)
        whole = wo32_ref[t]
        wout_ref[:, lanes] = whole.astype(BF16)
        woutt_ref[lanes, :] = whole.T.astype(BF16)

    def vector(row, quarter):
        at = (row - ROW_TAPS) * 4 + quarter
        return [taps_ref[t, pl.ds(at, 1), :] for t in range(2)]

    cbias = vector(ROW_NORM, 1)
    gain = vector(ROW_NORM, 2)
    shift = vector(ROW_NORM, 3)
    bias_out = vector(ROW_LAST, 0)
    scale = vector(ROW_LAST, 1)
    lane = lax.broadcasted_iota(jnp.int32, (1, LANES), 1)
    inside = (lane < C - LANES).astype(F32)
    shift[1] = shift[1] + (lane == C - LANES).astype(F32)

    gin_ref[...] = jnp.zeros_like(gin_ref)
    gout_ref[...] = jnp.zeros_like(gout_ref)
    sums_ref[...] = jnp.zeros_like(sums_ref)
    cells = block_rows * lon_pad

    def partial(values):
        return values.reshape(cells // 8, 8, LANES).sum(axis=0)

    def body(block, carry):
        row = block * block_rows

        def store(tile, lon, sums):
            for r in range(block_rows):
                conv_ref[tile, r, pl.ds(lon, 16), :] = sums[r]

        depthwise_block(x_ref, taps_ref, row, block_rows, lon_pad // 8, store, False)
        conv = [conv_ref[t].reshape(cells, LANES) + cbias[t] for t in range(2)]
        mean = jnp.sum(conv[0] + conv[1], axis=1, keepdims=True) * (1.0 / C)
        centred = [conv[0] - mean, (conv[1] - mean) * inside]
        square = centred[0] * centred[0] + centred[1] * centred[1]
        inv_std = lax.rsqrt(jnp.sum(square, axis=1, keepdims=True) * (1.0 / C) + EPSILON)
        standard = [c * inv_std for c in centred]
        normed = jnp.concatenate(
            [(standard[t] * gain[t] + shift[t]).astype(BF16) for t in range(2)], axis=1
        )
        upstream = up_ref[pl.ds(row, block_rows)].reshape(cells, CP)
        ups = [upstream[:, t * LANES : (t + 1) * LANES].astype(F32) for t in range(2)]
        grad_branch = [(scale[t] * ups[t]).astype(BF16) for t in range(2)]
        gbranch = jnp.concatenate(grad_branch, axis=1)
        branch = None
        gnormed = None
        for h in range(0, H, CP):
            hidden = slice(h, h + CP)
            pre = jnp.dot(normed, win_ref[:, hidden], preferred_element_type=F32)
            gact = jnp.dot(gbranch, woutt_ref[:, hidden], preferred_element_type=F32)
            square = pre * pre
            half = 0.5 + 0.5 * jnp.tanh(pre * (GELU_A + GELU_B * square))
            act = pre * half
            slope = half + act * (1.0 - half) * (2.0 * GELU_A + 6.0 * GELU_B * square)
            act = act.astype(BF16)
            gpre = (gact * slope).astype(BF16)
            part = jnp.dot(act, wout_ref[hidden, :], preferred_element_type=F32)
            branch = part if branch is None else branch + part
            part = jnp.dot(gpre, wint_ref[hidden, :], preferred_element_type=F32)
            gnormed = part if gnormed is None else gnormed + part
            over = (((0,), (0,)), ((), ()))
            gin_ref[:, hidden] += lax.dot_general(normed, gpre, over, preferred_element_type=F32)
            gout_ref[:, hidden] += lax.dot_general(gbranch, act, over, preferred_element_type=F32)
        feat = feat_ref[pl.ds(row, block_rows)].reshape(cells, CP)
        outs = []
        gs = []
        gn = []
        for t in range(2):
            lanes = slice(t * LANES, (t + 1) * LANES)
            branch_t = branch[:, lanes] + bias_out[t]
            outs.append((feat[:, lanes].astype(F32) + scale[t] * branch_t).astype(BF16))
            gn.append(gnormed[:, lanes])
            sums_ref[4, t] += partial(branch_t * ups[t])
            sums_ref[3, t] += partial(grad_branch[t].astype(F32))
            sums_ref[1, t] += partial(gn[t] * standard[t])
            sums_ref[2, t] += partial(gn[t])
            gs.append(gn[t] * gain[t])
        mean_g = jnp.sum(gs[0] + gs[1], axis=1, keepdims=True) * (1.0 / C)
        both = gs[0] * standard[0] + gs[1] * standard[1]
        mean_gs = jnp.sum(both, axis=1, keepdims=True) * (1.0 / C)
        gconv = []
        for t in range(2):
            grad = ((gs[t] - mean_g - standard[t] * mean_gs) * inv_std).astype(BF16)
            sums_ref[0, t] += partial(grad.astype(F32))
            gconv.append(grad)
        gconv_ref[pl.ds(row, block_rows)] = jnp.concatenate(gconv, axis=1).reshape(
            block_rows, lon_pad, CP
        )
        out = jnp.concatenate(outs, axis=1).reshape(block_rows, lon_pad, CP)
        out_ref[pl.ds(row, block_rows)] = out[:, : out_ref.shape[1], :C]
        return carry

    lax.fori_loop(0, rows // block_rows, body, 0)


def taps_kernel(order, starts, rows, lon_pad, block_rows,
                me_ref, gconv_ref, x_ref, gin_ref, gout_ref, sums_ref,
                g_ref, rows_ref, acc_ref, wo32_ref, small_ref):
    acc_ref[...] = jnp.zeros_like(acc_ref)

    def body(step, carry):
        tile = step % 2
        row = step // 2 * block_rows
        lanes = pl.ds(pl.multiple_of(tile * LANES, LANES), LANES)
        grads = [gconv_ref[row + r, :, lanes].astype(F32) for r in range(block_rows)]
        for b in range(KS):
            windows = [
                x_ref[tile, row + offset, pl.ds(b, lon_pad), :]
                for offset in range(block_rows + KS - 1)
            ]
            for a in range(KS):
                total = None
                for r in range(block_rows):
                    term = grads[r] * windows[r + a]
                    total = term if total is None else total + term
                acc_ref[tile, a * KS + b] += total.reshape(lon_pad // 8, 8, LANES).sum(axis=0)
        return carry

    lax.fori_loop(0, 2 * (rows // block_rows), body, 0)
    rows_ref[...] = jnp.zeros_like(rows_ref)
    small_ref[...] = jnp.zeros_like(small_ref)
    for t in range(2):
        small_ref[t, pl.ds(0, TAPS), :] = jnp.sum(acc_ref[t], axis=1)
        for at, k in ((TAPS, 0), (TAPS + 1, 1), (TAPS + 2, 2), (TAPS + 7, 3), (TAPS + 8, 4)):
            small_ref[t, pl.ds(at, 1), :] = jnp.sum(sums_ref[k, t], axis=0, keepdims=True)
        wo32_ref[t] = gout_ref[pl.ds(t * LANES, LANES), :].T
    outs = join_quarters(
        [[wo32_ref[t, pl.ds(q, C, stride=4), :] for t in range(2)] for q in range(4)]
    )
    tails = join_quarters(
        [[small_ref[t, pl.ds(q, 16, stride=4), :] for t in range(2)] for q in range(4)]
    )
    for j in range(TILES):
        lanes = slice(j * LANES, (j + 1) * LANES)
        rows_ref[j, pl.ds(0, C), :] = gin_ref[pl.ds(0, C), lanes]
        rows_ref[j, pl.ds(ROW_OUT, C), :] = outs[j]
        rows_ref[j, pl.ds(ROW_TAPS, 16), :] = tails[j]
        rows_ref[j, pl.ds(ROW_BIAS_IN, 1), :] = gin_ref[pl.ds(C, 1), lanes]
    me = me_ref[0]
    for position, start in zip(order, starts):
        share = jnp.concatenate(
            [rows_ref[j, pl.ds(start, WINDOW), :] for j in range(TILES)], axis=1
        )
        g_ref[position ^ me] = share.astype(BF16)


def field_kernel(rows, lon_pad, block_rows, pad_ref, taps_ref, up_ref, out_ref, x_ref):
    for t in range(2):
        x_ref[t] = pad_ref[:, :, t * LANES : (t + 1) * LANES].astype(F32)

    def body(block, carry):
        row = block * block_rows

        def store(tile, lon, sums):
            lanes = pl.ds(pl.multiple_of(tile * LANES, LANES), LANES)
            for r in range(block_rows):
                total = sums[r] + up_ref[row + r, pl.ds(lon, 16), lanes].astype(F32)
                out_ref[row + r, pl.ds(lon, 16), lanes] = total.astype(BF16)

        depthwise_block(x_ref, taps_ref, row, block_rows, lon_pad // 8, store, True)
        return carry

    lax.fori_loop(0, rows // block_rows, body, 0)


def shape(dims, kind):
    return jax.ShapeDtypeStruct(dims, kind)


def whole(count):
    return [pl.BlockSpec(memory_space=pltpu.VMEM)] * count


def body(features, params, langevin_noise, upstream):
    rows, cols = features.shape[:2]
    lon_pad = up(cols, 16)
    lon_wide = up(lon_pad + KS - 1, 8)
    block_rows = max(r for r in range(1, 6) if rows % r == 0)
    axes = ("lon", "lat")
    steps = exchange_bits(axes)
    count = 1 << len(steps)
    lat_size = lax.axis_size("lat")
    length = params.shape[0]
    number = lax.axis_index("lon") * lat_size + lax.axis_index("lat")
    place = jnp.int32(0)
    for k in range(len(steps)):
        place = place | (((number >> k) & 1) << (len(steps) - 1 - k))
    place = place.reshape(1).astype(jnp.int32)
    offset = (number * length) % H
    order = [reversed_bits(s, len(steps)) for s in range(count)]
    starts = [s * length // H for s in range(count)]
    w_rows = up(starts[-1] + WINDOW, 8)

    window = lax.dynamic_update_slice(
        jnp.zeros((WINDOW * H,), BF16), params.astype(BF16), (offset,)
    )
    gathered = window.reshape(1, WINDOW, H)
    for axis, bit in steps:
        gathered = jnp.concatenate([gathered, swap(gathered, axis, bit)], axis=0)

    def widen(field, lons):
        return jnp.pad(field, ((0, 0), (0, lons - field.shape[1]), (0, CP - C)))

    padded = widen(padded_field(features), lon_wide)
    x = padded.astype(F32).reshape(rows + KS - 1, lon_wide, 2, LANES).transpose(2, 0, 1, 3)
    feat = widen(features, lon_pad)
    ups = widen(upstream, lon_pad)

    params_in = pltpu.CompilerParams(vmem_limit_bytes=VMEM)
    smem = [pl.BlockSpec(memory_space=pltpu.SMEM)]
    static = (order, starts, rows, lon_pad, block_rows)
    output, gconv, gin, gout, sums, taps = pl.pallas_call(
        lambda *refs: layer_kernel(*static, *refs),
        out_shape=(
            shape((rows, cols, C), BF16),
            shape((rows, lon_pad, CP), BF16),
            shape((CP, H), F32),
            shape((CP, H), F32),
            shape((5, 2, 8, LANES), F32),
            shape((2, 64, LANES), F32),
        ),
        in_specs=smem + whole(4),
        out_specs=tuple(whole(6)),
        scratch_shapes=[
            pltpu.VMEM((TILES, w_rows, LANES), F32),
            pltpu.VMEM((CP, H), BF16),
            pltpu.VMEM((H, CP), BF16),
            pltpu.VMEM((H, CP), BF16),
            pltpu.VMEM((CP, H), BF16),
            pltpu.VMEM((2, H, LANES), F32),
            pltpu.VMEM((2, block_rows, lon_pad, LANES), F32),
        ],
        compiler_params=params_in,
        name="layer",
    )(place, gathered, x, feat, ups)

    grad_padded = widen(padded_field(gconv[:, :cols, :C]), lon_wide)
    grads = pl.pallas_call(
        lambda *refs: taps_kernel(*static, *refs),
        out_shape=shape((count, WINDOW, H), BF16),
        in_specs=smem + whole(5),
        out_specs=whole(1)[0],
        scratch_shapes=[
            pltpu.VMEM((TILES, w_rows, LANES), F32),
            pltpu.VMEM((2, TAPS, 8, LANES), F32),
            pltpu.VMEM((2, H, LANES), F32),
            pltpu.VMEM((2, 64, LANES), F32),
        ],
        compiler_params=params_in,
        name="taps",
    )(place, gconv, x, gin, gout, sums)

    field = pl.pallas_call(
        lambda *refs: field_kernel(rows, lon_pad, block_rows, *refs),
        out_shape=shape((rows, lon_pad, CP), BF16),
        in_specs=whole(3),
        out_specs=whole(1)[0],
        scratch_shapes=[pltpu.VMEM((2, rows + KS - 1, lon_wide, LANES), F32)],
        compiler_params=params_in,
        name="field",
    )(grad_padded, taps, ups)

    values = grads
    kept = None
    for axis, bit in steps[::-1]:
        half = values.shape[0] // 2
        received = swap(values[half:].astype(BF16), axis, bit)
        values = values[:half].astype(F32) + received.astype(F32)
    summed = lax.dynamic_slice(values.reshape(-1), (offset,), (length,))
    new_params = params - STEP_SIZE * summed + NOISE_COEF * langevin_noise
    return (output, field[:, :cols, :C], new_params)


def solution(mesh):
    return jax.shard_map(
        body,
        mesh=mesh,
        in_specs=(
            P("lat", "lon", None),
            P(("lon", "lat")),
            P(("lon", "lat")),
            P("lat", "lon", None),
        ),
        out_specs=(P("lat", "lon", None), P("lat", "lon", None), P(("lon", "lat"))),
        check_vma=False,
    )
```

time: 375 us -> 121 us (0.32)
  the two profiles are of different devices: /device:TPU:0 before, /device:TPU:1 now
where the time goes in v2:
time: 121 us; the launch traced here: 120 us
  Pallas kernels  50.2 us (41%)
  starting transfers between devices  29.5 us (24%)
  waiting for transfers between devices  22.4 us (19%)
  other arithmetic  8.57 us (7%)
  local copies, waits for them, and re-layouts  8.52 us (7%)
    pallas_call x1, Pallas kernels, body(): pl.pallas_call(lambda *refs: layer_kernel(*static, *refs), out_shape=(sha...  26.4 us
    ppermute x10, waiting for transfers between devices, swap(): lax.ppermute(values, axis, [(i, i ^ bit) for i in range(lax.axis_size(axi...  16.8 us
    pallas_call x1, Pallas kernels, body(): pl.pallas_call(lambda *refs: taps_kernel(*static, *refs), out_shape=shape...  12 us
    pallas_call x1, Pallas kernels, body(): pl.pallas_call(lambda *refs: field_kernel(rows, lon_pad, block_rows, *ref...  11.8 us
    ppermute x4, starting transfers between devices, shift_both(): lax.ppermute(high_edge, axis, forward)  11.2 us
    ppermute x4, starting transfers between devices, shift_both(): lax.ppermute(low_edge, axis, backward)  10.9 us
    ppermute x10, starting transfers between devices, swap(): lax.ppermute(values, axis, [(i, i ^ bit) for i in range(lax.axis_size(axi...  7.37 us
    ppermute x4, waiting for transfers between devices, shift_both(): lax.ppermute(low_edge, axis, backward)  3.75 us
  transfers between devices with their start and end apart: 18, of which 6 were waited for; matrix products, arithmetic and copies ran while one was open for 10% of the time, Pallas kernels for 10%

profile of v2, /device:TPU:1, one launch (start us, length us, event | category | flops | bytes accessed | tf_op | source)
XLA Modules:
  0.0 120.2 jit_solution(12956006603444495584)
XLA Ops:
  0.6 0.0 copy-start.2
  0.7 0.9 convert_element_type.32
  1.5 0.4 dynamic_update_slice.3
  2.0 3.2 %collective-permute-start = (bf16[1,16,768]{2,1,0:T(8,128)(2,1)S(1)}, bf16[1,16,768]{2,1,0:T(8,128)(2,1)S(1)}, u32[]{:S(2)}, u32[]{:S(2)}) collective-permute-start(bf16[1,16,768]{2,1,0:T(8,128)(2,1)S(1)} %reshape.20), channel_id=1, source_target_pairs={{0,16},{4,20},{8,24},{12,28},{16,0},{20,4},{24,8},{28,12},{1,17},{... | collective-permute-start | bytes 73736 | tf_op jit(solution)/shard_map/ppermute | solution.py:46
  5.2 1.1 fusion.30
  6.3 1.3 %collective-permute-start.5 = (bf16[45,3,192]{2,1,0:T(4,128)(2,1)S(1)}, bf16[45,3,192]{2,1,0:T(4,128)(2,1)S(1)}, u32[]{:S(2)}, u32[]{:S(2)}) collective-permute-start(bf16[45,3,192]{2,1,0:T(4,128)(2,1)S(1)} %get-tuple-element.21), channel_id=1, source_target_pairs={{0,4},{4,8},{8,12},{12,16},{16,20},{20,24},{24,28},{28,0},{1,5},{5... | collective-permute-start | bytes 155528 | tf_op jit(solution)/shard_map/ppermute | solution.py:55
  7.6 3.0 %collective-permute-start.6 = (bf16[45,3,192]{2,1,0:T(4,128)(2,1)S(1)}, bf16[45,3,192]{2,1,0:T(4,128)(2,1)S(1)}, u32[]{:S(2)}, u32[]{:S(2)}) collective-permute-start(bf16[45,3,192]{2,1,0:T(4,128)(2,1)S(1)} %get-tuple-element.22), channel_id=1, source_target_pairs={{4,0},{8,4},{12,8},{16,12},{20,16},{24,20},{28,24},{0,28},{5,1},{9... | collective-permute-start | bytes 155528 | tf_op jit(solution)/shard_map/ppermute | solution.py:55
  10.5 0.6 constant_dynamic-update-slice_fusion.4
  11.1 2.4 %pad.15.refs_3_ = bf16[45,48,256]{2,1,0:T(8,128)(2,1)} pad(bf16[45,45,192]{2,1,0:T(8,128)(2,1)} %param.4, bf16[]{:T(256)} %constant.33.clone.1), padding=0_0x0_3x0_64 | pad | bytes 1883522 | tf_op jit(solution)/shard_map/jit(_pad)/pad | solution.py:353
  13.6 0.0 copy-done.2
  13.6 1.2 pad.16.refs_4_.refs_2_
  14.8 0.0 collective-permute-done
  14.8 0.1 collective-permute-start.1
  14.9 0.6 constant_dynamic-update-slice_fusion.3
  15.5 2.3 %collective-permute-done.1 = bf16[2,16,768]{2,1,0:T(8,128)(2,1)S(1)} collective-permute-done((bf16[2,16,768]{2,1,0:T(8,128)(2,1)S(1)}, bf16[2,16,768]{2,1,0:T(8,128)(2,1)S(1)}, u32[]{:S(2)}, u32[]{:S(2)}) %collective-permute-start.1) | collective-permute-done | bytes 49184 | tf_op jit(solution)/shard_map/ppermute | solution.py:46
  17.8 0.1 collective-permute-start.2
  17.9 0.0 collective-permute-done.5
  17.9 0.0 collective-permute-done.6
  17.9 0.0 copy-done.1
  17.9 0.1 pad_maximum_fusion.7
  18.0 5.7 %collective-permute-start.7 = (bf16[3,51,192]{2,1,0:T(8,128)(2,1)S(1)}, bf16[3,51,192]{2,1,0:T(8,128)(2,1)S(1)}, u32[]{:S(2)}, u32[]{:S(2)}) collective-permute-start(bf16[3,51,192]{2,1,0:T(8,128)(2,1)S(1)} %get-tuple-element.17), channel_id=1, source_target_pairs={{0,1},{1,2},{2,3},{4,5},{5,6},{6,7},{8,9},{9,10},{10,11},{12,13},{... | collective-permute-start | bytes 176264 | tf_op jit(solution)/shard_map/ppermute | solution.py:55
  23.7 1.9 %collective-permute-start.8 = (bf16[3,51,192]{2,1,0:T(8,128)(2,1)S(1)}, bf16[3,51,192]{2,1,0:T(8,128)(2,1)S(1)}, u32[]{:S(2)}, u32[]{:S(2)}) collective-permute-start(bf16[3,51,192]{2,1,0:T(8,128)(2,1)S(1)} %get-tuple-element.18), channel_id=1, source_target_pairs={{1,0},{2,1},{3,2},{5,4},{6,5},{7,6},{9,8},{10,9},{11,10},{13,12},{... | collective-permute-start | bytes 176264 | tf_op jit(solution)/shard_map/ppermute | solution.py:55
  25.6 0.0 collective-permute-done.2
  25.6 0.2 collective-permute-start.3
  25.8 0.0 copy-done.6
  25.9 6.4 %collective-permute-done.3 = bf16[8,16,768]{2,1,0:T(8,128)(2,1)S(1)} collective-permute-done((bf16[8,16,768]{2,1,0:T(8,128)(2,1)S(1)}, bf16[8,16,768]{2,1,0:T(8,128)(2,1)S(1)}, u32[]{:S(2)}, u32[]{:S(2)}) %collective-permute-start.3) | collective-permute-done | bytes 196640 | tf_op jit(solution)/shard_map/ppermute | solution.py:46
  32.3 1.7 %collective-permute-start.4 = (bf16[16,16,768]{2,1,0:T(8,128)(2,1)S(1)}, bf16[16,16,768]{2,1,0:T(8,128)(2,1)S(1)}, u32[]{:S(2)}, u32[]{:S(2)}) collective-permute-start(bf16[16,16,768]{2,1,0:T(8,128)(2,1)S(1)} %get-tuple-element.23), channel_id=1, source_target_pairs={{0,1},{1,0},{2,3},{3,2},{4,5},{5,4},{6,7},{7,6},{8,9},{9,8},{10,11... | collective-permute-start | bytes 1179656 | tf_op jit(solution)/shard_map/ppermute | solution.py:46
  34.1 0.0 collective-permute-done.7
  34.1 0.0 collective-permute-done.8
  34.1 2.9 %bitcast_bitcast_fusion.refs_2_ = f32[2,51,56,128]{3,2,1,0:T(8,128)} fusion(bf16[3,51,192]{2,1,0:T(8,128)(2,1)S(1)} %collective-permute-done.8, bf16[3,51,192]{2,1,0:T(8,128)(2,1)S(1)} %collective-permute-done.7, bf16[45,3,192]{2,1,0:T(4,128)(2,1)S(1)} %collective-permute-done.6, bf16[45,45,192]{2,1,0:T(8,128)(2,1)S(1)} %copy-done.1, ...), kind=kLoop, calls=%fused_computation | loop fusion | flops 16816128 | bytes 3923328 | tf_op jit(solution)/shard_map/transpose | solution.py:356
  36.9 0.0 collective-permute-done.4
  37.0 0.0 copy-start.3
  37.0 0.9 copy-done.3
  37.8 26.4 %layer.1 = (bf16[45,45,192]{2,1,0:T(8,128)(2,1)}, bf16[45,48,256]{2,1,0:T(8,128)(2,1)}, f32[256,768]{1,0:T(8,128)}, f32[256,768]{1,0:T(8,128)}, f32[5,2,8,128]{3,2,1,0:T(8,128)}, /*index=5*/f32[2,64,128]{2,1,0:T(8,128)}) custom-call(s32[1]{0:T(128)} %bitcast.refs_0_, bf16[32,16,768]{2,1,0:T(8,128)(2,1)} %copy-done.3, ...), custom_call_target="tpu_custom_call" | custom-call | tf_op jit(solution)/shard_map/layer/pallas_call | solution.py:363
  64.3 12.0 %taps.1 = bf16[32,16,768]{2,1,0:T(8,128)(2,1)} custom-call(s32[1]{0:T(128)} %bitcast.refs_0_, bf16[45,48,256]{2,1,0:T(8,128)(2,1)} %get-tuple-element.10.refs_1_, f32[2,51,56,128]{3,2,1,0:T(8,128)} %bitcast_bitcast_fusion.refs_2_, f32[256,768]{1,0:T(8,128)} %get-tuple-element.12.refs_3_, f32[256,768]{1,0:T(8,128)} %get-tuple-element.13.refs_4_, ...), custom_call_target="tpu_custom_call" | custom-call | tf_op jit(solution)/shard_map/taps/pallas_call | solution.py:389
  76.3 1.0 slice.88
  77.3 0.0 copy-start
  77.3 0.1 collective-permute-start.13
  77.4 1.7 %collective-permute-done.13 = bf16[16,16,768]{2,1,0:T(8,128)(2,1)S(1)} collective-permute-done((bf16[16,16,768]{2,1,0:T(8,128)(2,1)S(1)}, bf16[16,16,768]{2,1,0:T(8,128)(2,1)S(1)}, u32[]{:S(2)}, u32[]{:S(2)}) %collective-permute-start.13) | collective-permute-done | bytes 393248 | tf_op jit(solution)/shard_map/ppermute | solution.py:46
  79.1 1.1 convert_add_fusion
  80.2 0.1 collective-permute-start.14
  80.3 6.3 %collective-permute-done.14 = bf16[8,16,768]{2,1,0:T(8,128)(2,1)S(1)} collective-permute-done((bf16[8,16,768]{2,1,0:T(8,128)(2,1)S(1)}, bf16[8,16,768]{2,1,0:T(8,128)(2,1)S(1)}, u32[]{:S(2)}, u32[]{:S(2)}) %collective-permute-start.14) | collective-permute-done | bytes 196640 | tf_op jit(solution)/shard_map/ppermute | solution.py:46
  86.7 1.8 %collective-permute-start.15 = (bf16[4,16,768]{2,1,0:T(8,128)(2,1)S(1)}, bf16[4,16,768]{2,1,0:T(8,128)(2,1)S(1)}, u32[]{:S(2)}, u32[]{:S(2)}) collective-permute-start(bf16[4,16,768]{2,1,0:T(8,128)(2,1)S(1)} %slice.107), channel_id=1, source_target_pairs={{0,4},{4,0},{8,12},{12,8},{16,20},{20,16},{24,28},{28,24},{1,5},{5... | collective-permute-start | bytes 294920 | tf_op jit(solution)/shard_map/ppermute | solution.py:46
  88.5 0.0 copy-done
  88.5 0.1 fusion.29
  88.5 0.1 collective-permute-start.9
  88.6 4.1 %collective-permute-start.10 = (bf16[45,3,192]{2,1,0:T(4,128)(2,1)S(1)}, bf16[45,3,192]{2,1,0:T(4,128)(2,1)S(1)}, u32[]{:S(2)}, u32[]{:S(2)}) collective-permute-start(bf16[45,3,192]{2,1,0:T(4,128)(2,1)S(1)} %get-tuple-element.20), channel_id=1, source_target_pairs={{4,0},{8,4},{12,8},{16,12},{20,16},{24,20},{28,24},{0,28},{5,1},{9... | collective-permute-start | bytes 155528 | tf_op jit(solution)/shard_map/ppermute | solution.py:55
  92.8 0.0 collective-permute-done.15
  92.8 0.1 collective-permute-start.16
  92.9 1.9 %collective-permute-done.9 = bf16[45,3,192]{2,1,0:T(4,128)(2,1)S(1)} collective-permute-done((bf16[45,3,192]{2,1,0:T(4,128)(2,1)S(1)}, bf16[45,3,192]{2,1,0:T(4,128)(2,1)S(1)}, u32[]{:S(2)}, u32[]{:S(2)}) %collective-permute-start.9) | collective-permute-done | bytes 51872 | tf_op jit(solution)/shard_map/ppermute | solution.py:55
  94.8 0.0 collective-permute-done.10
  94.8 0.1 pad_maximum_fusion.4
  94.8 4.2 %collective-permute-start.11 = (bf16[3,51,192]{2,1,0:T(8,128)(2,1)S(1)}, bf16[3,51,192]{2,1,0:T(8,128)(2,1)S(1)}, u32[]{:S(2)}, u32[]{:S(2)}) collective-permute-start(bf16[3,51,192]{2,1,0:T(8,128)(2,1)S(1)} %get-tuple-element.15), channel_id=1, source_target_pairs={{0,1},{1,2},{2,3},{4,5},{5,6},{6,7},{8,9},{9,10},{10,11},{12,13},{... | collective-permute-start | bytes 176264 | tf_op jit(solution)/shard_map/ppermute | solution.py:55
  99.0 1.9 %collective-permute-start.12 = (bf16[3,51,192]{2,1,0:T(8,128)(2,1)S(1)}, bf16[3,51,192]{2,1,0:T(8,128)(2,1)S(1)}, u32[]{:S(2)}, u32[]{:S(2)}) collective-permute-start(bf16[3,51,192]{2,1,0:T(8,128)(2,1)S(1)} %get-tuple-element.16), channel_id=1, source_target_pairs={{1,0},{2,1},{3,2},{5,4},{6,5},{7,6},{9,8},{10,9},{11,10},{13,12},{... | collective-permute-start | bytes 176264 | tf_op jit(solution)/shard_map/ppermute | solution.py:55
  100.9 0.0 collective-permute-done.16
  101.0 0.1 collective-permute-start.17
  101.1 0.0 collective-permute-done.11
  101.1 3.7 %collective-permute-done.12 = bf16[3,51,192]{2,1,0:T(8,128)(2,1)S(1)} collective-permute-done((bf16[3,51,192]{2,1,0:T(8,128)(2,1)S(1)}, bf16[3,51,192]{2,1,0:T(8,128)(2,1)S(1)}, u32[]{:S(2)}, u32[]{:S(2)}) %collective-permute-start.12) | collective-permute-done | bytes 58784 | tf_op jit(solution)/shard_map/ppermute | solution.py:55
  104.8 2.8 %fusion.22.refs_0_ = bf16[51,56,256]{2,1,0:T(8,128)(2,1)} fusion(bf16[3,51,192]{2,1,0:T(8,128)(2,1)S(1)} %collective-permute-done.12, bf16[3,51,192]{2,1,0:T(8,128)(2,1)S(1)} %collective-permute-done.11, bf16[45,3,192]{2,1,0:T(4,128)(2,1)S(1)} %collective-permute-done.10, bf16[45,45,192]{2,1,0:T(8,128)(2,1)S(1)} %bitcast.11, ...), kind=kLoop, calls=%fused_computation.26 | loop fusion | flops 16816128 | bytes 2461056 | tf_op jit(solution)/shard_map/concatenate | solution.py:69
  107.6 11.8 %field.1 = bf16[45,48,256]{2,1,0:T(8,128)(2,1)} custom-call(bf16[51,56,256]{2,1,0:T(8,128)(2,1)} %fusion.22.refs_0_, f32[2,64,128]{2,1,0:T(8,128)} %get-tuple-element.11.refs_1_, bf16[45,48,256]{2,1,0:T(8,128)(2,1)} %pad.16.refs_4_.refs_2_), custom_call_target="tpu_custom_call" | custom-call | tf_op jit(solution)/shard_map/field/pallas_call | solution.py:404
  119.4 0.0 collective-permute-done.17
  119.5 0.0 copy-done.4
  119.5 0.0 copy-done.5
  119.5 0.7 multiply_add_fusion
  (22 shorter events, 0.3 us)
Async XLA Ops:
  0.6 12.9 %copy-start.2 = (bf16[45,45,192]{2,1,0:T(8,128)(2,1)S(1)}, bf16[45,45,192]{2,1,0:T(8,128)(2,1)}, u32[]{:S(2)}) copy-start(bf16[45,45,192]{2,1,0:T(8,128)(2,1)} %param.7) | copy-start | bytes 2332804
  2.0 12.8 %collective-permute-start = (bf16[1,16,768]{2,1,0:T(8,128)(2,1)S(1)}, bf16[1,16,768]{2,1,0:T(8,128)(2,1)S(1)}, u32[]{:S(2)}, u32[]{:S(2)}) collective-permute-start(bf16[1,16,768]{2,1,0:T(8,128)(2,1)S(1)} %reshape.20), channel_id=1, source_target_pairs={{0,16},{4,20},{8,24},{12,28},{16,0},{20,4},{24,8},{28,12},{1,17},{... | collective-permute-start | bytes 73736 | tf_op jit(solution)/shard_map/ppermute | solution.py:46
  6.3 11.6 %collective-permute-start.5 = (bf16[45,3,192]{2,1,0:T(4,128)(2,1)S(1)}, bf16[45,3,192]{2,1,0:T(4,128)(2,1)S(1)}, u32[]{:S(2)}, u32[]{:S(2)}) collective-permute-start(bf16[45,3,192]{2,1,0:T(4,128)(2,1)S(1)} %get-tuple-element.21), channel_id=1, source_target_pairs={{0,4},{4,8},{8,12},{12,16},{16,20},{20,24},{24,28},{28,0},{1,5},{5... | collective-permute-start | bytes 155528 | tf_op jit(solution)/shard_map/ppermute | solution.py:55
  7.6 10.3 %collective-permute-start.6 = (bf16[45,3,192]{2,1,0:T(4,128)(2,1)S(1)}, bf16[45,3,192]{2,1,0:T(4,128)(2,1)S(1)}, u32[]{:S(2)}, u32[]{:S(2)}) collective-permute-start(bf16[45,3,192]{2,1,0:T(4,128)(2,1)S(1)} %get-tuple-element.22), channel_id=1, source_target_pairs={{4,0},{8,4},{12,8},{16,12},{20,16},{24,20},{28,24},{0,28},{5,1},{9... | collective-permute-start | bytes 155528 | tf_op jit(solution)/shard_map/ppermute | solution.py:55
  13.6 4.3 %copy-start.1 = (bf16[45,45,192]{2,1,0:T(8,128)(2,1)S(1)}, bf16[45,45,192]{2,1,0:T(8,128)(2,1)}, u32[]{:S(2)}) copy-start(bf16[45,45,192]{2,1,0:T(8,128)(2,1)} %param.4) | copy-start | bytes 2332804
  14.8 3.0 %collective-permute-start.1 = (bf16[2,16,768]{2,1,0:T(8,128)(2,1)S(1)}, bf16[2,16,768]{2,1,0:T(8,128)(2,1)S(1)}, u32[]{:S(2)}, u32[]{:S(2)}) collective-permute-start(bf16[2,16,768]{2,1,0:T(8,128)(2,1)S(1)} %pad_maximum_fusion.8), channel_id=1, source_target_pairs={{0,8},{4,12},{8,0},{12,4},{16,24},{20,28},{24,16},{28,20},{1,9},{5... | collective-permute-start | bytes 147464 | tf_op jit(solution)/shard_map/ppermute | solution.py:46
  15.5 10.4 %copy-start.6 = (bf16[16,16,768]{2,1,0:T(8,128)(2,1)S(1)}, bf16[16,16,768]{2,1,0:T(8,128)(2,1)}, u32[]{:S(2)}) copy-start(bf16[16,16,768]{2,1,0:T(8,128)(2,1)} %get-tuple-element.29) | copy-start | bytes 1179652
  17.8 7.8 %collective-permute-start.2 = (bf16[4,16,768]{2,1,0:T(8,128)(2,1)S(1)}, bf16[4,16,768]{2,1,0:T(8,128)(2,1)S(1)}, u32[]{:S(2)}, u32[]{:S(2)}) collective-permute-start(bf16[4,16,768]{2,1,0:T(8,128)(2,1)S(1)} %pad_maximum_fusion.1), channel_id=1, source_target_pairs={{0,4},{4,0},{8,12},{12,8},{16,20},{20,16},{24,28},{28,24},{1,5},{5... | collective-permute-start | bytes 294920 | tf_op jit(solution)/shard_map/ppermute | solution.py:46
  18.0 16.1 %collective-permute-start.7 = (bf16[3,51,192]{2,1,0:T(8,128)(2,1)S(1)}, bf16[3,51,192]{2,1,0:T(8,128)(2,1)S(1)}, u32[]{:S(2)}, u32[]{:S(2)}) collective-permute-start(bf16[3,51,192]{2,1,0:T(8,128)(2,1)S(1)} %get-tuple-element.17), channel_id=1, source_target_pairs={{0,1},{1,2},{2,3},{4,5},{5,6},{6,7},{8,9},{9,10},{10,11},{12,13},{... | collective-permute-start | bytes 176264 | tf_op jit(solution)/shard_map/ppermute | solution.py:55
  23.7 10.4 %collective-permute-start.8 = (bf16[3,51,192]{2,1,0:T(8,128)(2,1)S(1)}, bf16[3,51,192]{2,1,0:T(8,128)(2,1)S(1)}, u32[]{:S(2)}, u32[]{:S(2)}) collective-permute-start(bf16[3,51,192]{2,1,0:T(8,128)(2,1)S(1)} %get-tuple-element.18), channel_id=1, source_target_pairs={{1,0},{2,1},{3,2},{5,4},{6,5},{7,6},{9,8},{10,9},{11,10},{13,12},{... | collective-permute-start | bytes 176264 | tf_op jit(solution)/shard_map/ppermute | solution.py:55
  25.6 6.6 %collective-permute-start.3 = (bf16[8,16,768]{2,1,0:T(8,128)(2,1)S(1)}, bf16[8,16,768]{2,1,0:T(8,128)(2,1)S(1)}, u32[]{:S(2)}, u32[]{:S(2)}) collective-permute-start(bf16[8,16,768]{2,1,0:T(8,128)(2,1)S(1)} %pad_maximum_fusion), channel_id=1, source_target_pairs={{0,2},{1,3},{2,0},{3,1},{4,6},{5,7},{6,4},{7,5},{8,10},{9,11},{10,... | collective-permute-start | bytes 589832 | tf_op jit(solution)/shard_map/ppermute | solution.py:46
  32.3 4.6 %collective-permute-start.4 = (bf16[16,16,768]{2,1,0:T(8,128)(2,1)S(1)}, bf16[16,16,768]{2,1,0:T(8,128)(2,1)S(1)}, u32[]{:S(2)}, u32[]{:S(2)}) collective-permute-start(bf16[16,16,768]{2,1,0:T(8,128)(2,1)S(1)} %get-tuple-element.23), channel_id=1, source_target_pairs={{0,1},{1,0},{2,3},{3,2},{4,5},{5,4},{6,7},{7,6},{8,9},{9,8},{10,11... | collective-permute-start | bytes 1179656 | tf_op jit(solution)/shard_map/ppermute | solution.py:46
  37.0 0.9 copy-start.3
  77.3 11.2 %copy-start = (bf16[45,48,256]{2,1,0:T(8,128)(2,1)S(1)}, bf16[45,48,256]{2,1,0:T(8,128)(2,1)}, u32[]{:S(2)}) copy-start(bf16[45,48,256]{2,1,0:T(8,128)(2,1)} %get-tuple-element.10.refs_1_) | copy-start | bytes 3317764
  77.3 1.8 %collective-permute-start.13 = (bf16[16,16,768]{2,1,0:T(8,128)(2,1)S(1)}, bf16[16,16,768]{2,1,0:T(8,128)(2,1)S(1)}, u32[]{:S(2)}, u32[]{:S(2)}) collective-permute-start(bf16[16,16,768]{2,1,0:T(8,128)(2,1)S(1)} %slice.88), channel_id=1, source_target_pairs={{0,1},{1,0},{2,3},{3,2},{4,5},{5,4},{6,7},{7,6},{8,9},{9,8},{10,11... | collective-permute-start | bytes 1179656 | tf_op jit(solution)/shard_map/ppermute | solution.py:46
  80.2 6.4 %collective-permute-start.14 = (bf16[8,16,768]{2,1,0:T(8,128)(2,1)S(1)}, bf16[8,16,768]{2,1,0:T(8,128)(2,1)S(1)}, u32[]{:S(2)}, u32[]{:S(2)}) collective-permute-start(bf16[8,16,768]{2,1,0:T(8,128)(2,1)S(1)} %slice.106), channel_id=1, source_target_pairs={{0,2},{1,3},{2,0},{3,1},{4,6},{5,7},{6,4},{7,5},{8,10},{9,11},{10,... | collective-permute-start | bytes 589832 | tf_op jit(solution)/shard_map/ppermute | solution.py:46
  86.7 6.1 %collective-permute-start.15 = (bf16[4,16,768]{2,1,0:T(8,128)(2,1)S(1)}, bf16[4,16,768]{2,1,0:T(8,128)(2,1)S(1)}, u32[]{:S(2)}, u32[]{:S(2)}) collective-permute-start(bf16[4,16,768]{2,1,0:T(8,128)(2,1)S(1)} %slice.107), channel_id=1, source_target_pairs={{0,4},{4,0},{8,12},{12,8},{16,20},{20,16},{24,28},{28,24},{1,5},{5... | collective-permute-start | bytes 294920 | tf_op jit(solution)/shard_map/ppermute | solution.py:46
  88.5 6.2 %collective-permute-start.9 = (bf16[45,3,192]{2,1,0:T(4,128)(2,1)S(1)}, bf16[45,3,192]{2,1,0:T(4,128)(2,1)S(1)}, u32[]{:S(2)}, u32[]{:S(2)}) collective-permute-start(bf16[45,3,192]{2,1,0:T(4,128)(2,1)S(1)} %get-tuple-element.19), channel_id=1, source_target_pairs={{0,4},{4,8},{8,12},{12,16},{16,20},{20,24},{24,28},{28,0},{1,5},{5... | collective-permute-start | bytes 155528 | tf_op jit(solution)/shard_map/ppermute | solution.py:55
  88.6 6.1 %collective-permute-start.10 = (bf16[45,3,192]{2,1,0:T(4,128)(2,1)S(1)}, bf16[45,3,192]{2,1,0:T(4,128)(2,1)S(1)}, u32[]{:S(2)}, u32[]{:S(2)}) collective-permute-start(bf16[45,3,192]{2,1,0:T(4,128)(2,1)S(1)} %get-tuple-element.20), channel_id=1, source_target_pairs={{4,0},{8,4},{12,8},{16,12},{20,16},{24,20},{28,24},{0,28},{5,1},{9... | collective-permute-start | bytes 155528 | tf_op jit(solution)/shard_map/ppermute | solution.py:55
  92.8 8.1 %collective-permute-start.16 = (bf16[2,16,768]{2,1,0:T(8,128)(2,1)S(1)}, bf16[2,16,768]{2,1,0:T(8,128)(2,1)S(1)}, u32[]{:S(2)}, u32[]{:S(2)}) collective-permute-start(bf16[2,16,768]{2,1,0:T(8,128)(2,1)S(1)} %slice.108), channel_id=1, source_target_pairs={{0,8},{4,12},{8,0},{12,4},{16,24},{20,28},{24,16},{28,20},{1,9},{5... | collective-permute-start | bytes 147464 | tf_op jit(solution)/shard_map/ppermute | solution.py:46
  94.8 6.3 %collective-permute-start.11 = (bf16[3,51,192]{2,1,0:T(8,128)(2,1)S(1)}, bf16[3,51,192]{2,1,0:T(8,128)(2,1)S(1)}, u32[]{:S(2)}, u32[]{:S(2)}) collective-permute-start(bf16[3,51,192]{2,1,0:T(8,128)(2,1)S(1)} %get-tuple-element.15), channel_id=1, source_target_pairs={{0,1},{1,2},{2,3},{4,5},{5,6},{6,7},{8,9},{9,10},{10,11},{12,13},{... | collective-permute-start | bytes 176264 | tf_op jit(solution)/shard_map/ppermute | solution.py:55
  99.0 5.8 %collective-permute-start.12 = (bf16[3,51,192]{2,1,0:T(8,128)(2,1)S(1)}, bf16[3,51,192]{2,1,0:T(8,128)(2,1)S(1)}, u32[]{:S(2)}, u32[]{:S(2)}) collective-permute-start(bf16[3,51,192]{2,1,0:T(8,128)(2,1)S(1)} %get-tuple-element.16), channel_id=1, source_target_pairs={{1,0},{2,1},{3,2},{5,4},{6,5},{7,6},{9,8},{10,9},{11,10},{13,12},{... | collective-permute-start | bytes 176264 | tf_op jit(solution)/shard_map/ppermute | solution.py:55
  101.0 18.4 %collective-permute-start.17 = (bf16[1,16,768]{2,1,0:T(8,128)(2,1)S(1)}, bf16[1,16,768]{2,1,0:T(8,128)(2,1)S(1)}, u32[]{:S(2)}, u32[]{:S(2)}) collective-permute-start(bf16[1,16,768]{2,1,0:T(8,128)(2,1)S(1)} %slice.109), channel_id=1, source_target_pairs={{0,16},{4,20},{8,24},{12,28},{16,0},{20,4},{24,8},{28,12},{1,17},{... | collective-permute-start | bytes 73736 | tf_op jit(solution)/shard_map/ppermute | solution.py:46
  107.6 11.8 %copy-start.4 = (f32[9568]{0:T(1024)S(1)}, f32[9568]{0:T(1024)}, u32[]{:S(2)}) copy-start(f32[9568]{0:T(1024)} %param.5) | copy-start | bytes 114820
  107.6 11.9 %copy-start.5 = (f32[9568]{0:T(1024)S(1)}, f32[9568]{0:T(1024)}, u32[]{:S(2)}) copy-start(f32[9568]{0:T(1024)} %param.6) | copy-start | bytes 114820

commit v3 on v2

--- a/solution.py
+++ b/solution.py
@@ -28,7 +28,9 @@
 ROW_LAST = ROW_NORM + 2
 ROWS = ROW_LAST + 1
 TILES = H // LANES
-WINDOW = 16
+SHARE_LANES = 256
+ALL = ((1,), (1,)), ((), ())
+OVER = ((0,), (0,)), ((), ())
 VMEM = 56 << 20
 
 
@@ -60,13 +62,6 @@
     for k in range(count):
         result |= ((number >> k) & 1) << (count - 1 - k)
     return result
-
-
-def padded_field(block):
-    west, east = shift_both(block[:, :RAD], block[:, -RAD:], "lon", True)
-    wide = jnp.concatenate([west, block, east], axis=1)
-    south, north = shift_both(wide[:RAD], wide[-RAD:], "lat", False)
-    return jnp.concatenate([south, wide, north], axis=0)
 
 
 def up(value, multiple):
@@ -94,6 +89,42 @@
         last = pltpu.roll(quarters[even + 1][1], LANES // 2, 1)
         tiles += [first, jnp.where(low, second, turned), jnp.where(low, turned, last)]
     return tiles
+
+
+def get_rows(flat_ref, row, count):
+    return [
+        flat_ref[j % 2, pl.ds(3 * row + j // 2, count, stride=3), :] for j in range(TILES)
+    ]
+
+
+def put_rows(flat_ref, row, tiles):
+    for j in range(TILES):
+        flat_ref[j % 2, pl.ds(3 * row + j // 2, tiles[j].shape[0], stride=3), :] = tiles[j]
+
+
+def assemble(x_ref, first, count, main, west, east, south, north, rows, cols):
+    x_ref[...] = jnp.zeros_like(x_ref)
+    for t in range(2):
+        lanes = slice(t * LANES, min(C, (t + 1) * LANES))
+        width = slice(0, lanes.stop - lanes.start)
+        low = max(0, first - RAD)
+        high = min(rows, first + count - RAD)
+        at = slice(low + RAD - first, high + RAD - first)
+        x_ref[t, at, 0:RAD, width] = west[low:high, :, lanes].astype(F32)
+        x_ref[t, at, RAD : RAD + cols, width] = main[low:high, 0:cols, lanes].astype(F32)
+        x_ref[t, at, RAD + cols : 2 * RAD + cols, width] = east[low:high, :, lanes].astype(F32)
+        if first < RAD:
+            x_ref[t, 0 : RAD - first, 0 : cols + 2 * RAD, width] = south[first:, :, lanes].astype(F32)
+        over = first + count - rows - RAD
+        if over > 0:
+            x_ref[t, count - over : count, 0 : cols + 2 * RAD, width] = north[0:over, :, lanes].astype(F32)
+
+
+def assemble_kernel(rows, cols, feat_ref, west_ref, east_ref, south_ref, north_ref, up_ref,
+                    x_ref, ups_ref):
+    assemble(x_ref, 0, x_ref.shape[1], feat_ref, west_ref, east_ref, south_ref, north_ref, rows, cols)
+    ups_ref[...] = jnp.zeros_like(ups_ref)
+    ups_ref[:, 0:cols, 0:C] = up_ref[...]
 
 
 def depthwise_block(x_ref, k_ref, row, out_rows, lon_regs, store, flip):
@@ -120,36 +151,32 @@
     lax.fori_loop(0, 2 * steps, body, 0)
 
 
-def layer_kernel(order, starts, rows, lon_pad, block_rows,
-                 me_ref, gathered_ref, x_ref, feat_ref, up_ref,
+def layer_kernel(order, starts, rows, lon_pad, block_rows, conv_rows,
+                 me_ref, gathered_ref, x_ref, up_ref,
                  out_ref, gconv_ref, gin_ref, gout_ref, sums_ref, taps_ref,
-                 w_ref, win_ref, wint_ref, wout_ref, woutt_ref, wo32_ref, conv_ref):
+                 w_ref, win_ref, wout_ref, wo32_ref, conv_ref):
     me = me_ref[0]
     w_ref[...] = jnp.zeros_like(w_ref)
+    window = gathered_ref.shape[1]
     for position, start in zip(order, starts):
         share = gathered_ref[position ^ me].astype(F32)
-        for j in range(TILES):
-            w_ref[j, pl.ds(start, WINDOW), :] += share[:, j * LANES : (j + 1) * LANES]
+        for t in range(2):
+            w_ref[t, pl.ds(start, window), :] += share[:, t * LANES : (t + 1) * LANES]
     rest = lax.broadcasted_iota(jnp.int32, (CP - C, LANES), 0)
+    mains = get_rows(w_ref, 0, C)
+    biases = get_rows(w_ref, ROW_BIAS_IN, 1)
     for j in range(TILES):
-        lanes = slice(j * LANES, (j + 1) * LANES)
-        main = w_ref[j, pl.ds(0, C), :]
-        bias = jnp.where(rest == 0, w_ref[j, pl.ds(ROW_BIAS_IN, 1), :], 0.0)
-        whole = jnp.concatenate([main, bias], axis=0)
-        win_ref[:, lanes] = whole.astype(BF16)
-        wint_ref[lanes, :] = whole.T.astype(BF16)
+        bias = jnp.where(rest == 0, biases[j], 0.0)
+        whole = jnp.concatenate([mains[j], bias], axis=0)
+        win_ref[:, j * LANES : (j + 1) * LANES] = whole.astype(BF16)
     for quarter in range(4):
-        tiles = [w_ref[j, pl.ds(ROW_OUT, C), :] for j in range(TILES)]
-        pair = split_quarter(tiles, quarter)
-        tail = split_quarter([w_ref[j, pl.ds(ROW_TAPS, 16), :] for j in range(TILES)], quarter)
+        pair = split_quarter(get_rows(w_ref, ROW_OUT, C), quarter)
+        tail = split_quarter(get_rows(w_ref, ROW_TAPS, 16), quarter)
         for t in range(2):
             wo32_ref[t, pl.ds(quarter, C, stride=4), :] = pair[t]
             taps_ref[t, pl.ds(quarter, 16, stride=4), :] = tail[t]
     for t in range(2):
-        lanes = slice(t * LANES, (t + 1) * LANES)
-        whole = wo32_ref[t]
-        wout_ref[:, lanes] = whole.astype(BF16)
-        woutt_ref[lanes, :] = whole.T.astype(BF16)
+        wout_ref[:, t * LANES : (t + 1) * LANES] = wo32_ref[t].astype(BF16)
 
     def vector(row, quarter):
         at = (row - ROW_TAPS) * 4 + quarter
@@ -175,11 +202,17 @@
     def body(block, carry):
         row = block * block_rows
 
-        def store(tile, lon, sums):
-            for r in range(block_rows):
-                conv_ref[tile, r, pl.ds(lon, 16), :] = sums[r]
-
-        depthwise_block(x_ref, taps_ref, row, block_rows, lon_pad // 8, store, False)
+        def conv_step(part, carry):
+            at = part * conv_rows
+
+            def store(tile, lon, sums):
+                for r in range(conv_rows):
+                    conv_ref[tile, at + r, pl.ds(lon, 16), :] = sums[r]
+
+            depthwise_block(x_ref, taps_ref, row + at, conv_rows, lon_pad // 8, store, False)
+            return carry
+
+        lax.fori_loop(0, block_rows // conv_rows, conv_step, 0)
         conv = [conv_ref[t].reshape(cells, LANES) + cbias[t] for t in range(2)]
         mean = jnp.sum(conv[0] + conv[1], axis=1, keepdims=True) * (1.0 / C)
         centred = [conv[0] - mean, (conv[1] - mean) * inside]
@@ -198,7 +231,7 @@
         for h in range(0, H, CP):
             hidden = slice(h, h + CP)
             pre = jnp.dot(normed, win_ref[:, hidden], preferred_element_type=F32)
-            gact = jnp.dot(gbranch, woutt_ref[:, hidden], preferred_element_type=F32)
+            gact = lax.dot_general(gbranch, wout_ref[hidden, :], ALL, preferred_element_type=F32)
             square = pre * pre
             half = 0.5 + 0.5 * jnp.tanh(pre * (GELU_A + GELU_B * square))
             act = pre * half
@@ -207,19 +240,19 @@
             gpre = (gact * slope).astype(BF16)
             part = jnp.dot(act, wout_ref[hidden, :], preferred_element_type=F32)
             branch = part if branch is None else branch + part
-            part = jnp.dot(gpre, wint_ref[hidden, :], preferred_element_type=F32)
+            part = lax.dot_general(gpre, win_ref[:, hidden], ALL, preferred_element_type=F32)
             gnormed = part if gnormed is None else gnormed + part
-            over = (((0,), (0,)), ((), ()))
-            gin_ref[:, hidden] += lax.dot_general(normed, gpre, over, preferred_element_type=F32)
-            gout_ref[:, hidden] += lax.dot_general(gbranch, act, over, preferred_element_type=F32)
-        feat = feat_ref[pl.ds(row, block_rows)].reshape(cells, CP)
+            gin_ref[:, hidden] += lax.dot_general(normed, gpre, OVER, preferred_element_type=F32)
+            gout_ref[:, hidden] += lax.dot_general(gbranch, act, OVER, preferred_element_type=F32)
         outs = []
         gs = []
         gn = []
         for t in range(2):
             lanes = slice(t * LANES, (t + 1) * LANES)
             branch_t = branch[:, lanes] + bias_out[t]
-            outs.append((feat[:, lanes].astype(F32) + scale[t] * branch_t).astype(BF16))
+            feat = x_ref[t, pl.ds(row + RAD, block_rows), pl.ds(RAD, lon_pad), :]
+            feat = feat.reshape(cells, LANES)
+            outs.append((feat + scale[t] * branch_t).astype(BF16))
             gn.append(gnormed[:, lanes])
             sums_ref[4, t] += partial(branch_t * ups[t])
             sums_ref[3, t] += partial(grad_branch[t].astype(F32))
@@ -244,30 +277,30 @@
     lax.fori_loop(0, rows // block_rows, body, 0)
 
 
-def taps_kernel(order, starts, rows, lon_pad, block_rows,
+def taps_kernel(order, starts, rows, lon_pad, block_rows, conv_rows,
                 me_ref, gconv_ref, x_ref, gin_ref, gout_ref, sums_ref,
                 g_ref, rows_ref, acc_ref, wo32_ref, small_ref):
     acc_ref[...] = jnp.zeros_like(acc_ref)
 
     def body(step, carry):
         tile = step % 2
-        row = step // 2 * block_rows
+        row = step // 2 * conv_rows
         lanes = pl.ds(pl.multiple_of(tile * LANES, LANES), LANES)
-        grads = [gconv_ref[row + r, :, lanes].astype(F32) for r in range(block_rows)]
+        grads = [gconv_ref[row + r, :, lanes].astype(F32) for r in range(conv_rows)]
         for b in range(KS):
             windows = [
                 x_ref[tile, row + offset, pl.ds(b, lon_pad), :]
-                for offset in range(block_rows + KS - 1)
+                for offset in range(conv_rows + KS - 1)
             ]
             for a in range(KS):
                 total = None
-                for r in range(block_rows):
+                for r in range(conv_rows):
                     term = grads[r] * windows[r + a]
                     total = term if total is None else total + term
                 acc_ref[tile, a * KS + b] += total.reshape(lon_pad // 8, 8, LANES).sum(axis=0)
         return carry
 
-    lax.fori_loop(0, 2 * (rows // block_rows), body, 0)
+    lax.fori_loop(0, 2 * (rows // conv_rows), body, 0)
     rows_ref[...] = jnp.zeros_like(rows_ref)
     small_ref[...] = jnp.zeros_like(small_ref)
     for t in range(2):
@@ -281,37 +314,40 @@
     tails = join_quarters(
         [[small_ref[t, pl.ds(q, 16, stride=4), :] for t in range(2)] for q in range(4)]
     )
-    for j in range(TILES):
-        lanes = slice(j * LANES, (j + 1) * LANES)
-        rows_ref[j, pl.ds(0, C), :] = gin_ref[pl.ds(0, C), lanes]
-        rows_ref[j, pl.ds(ROW_OUT, C), :] = outs[j]
-        rows_ref[j, pl.ds(ROW_TAPS, 16), :] = tails[j]
-        rows_ref[j, pl.ds(ROW_BIAS_IN, 1), :] = gin_ref[pl.ds(C, 1), lanes]
+    put_rows(rows_ref, 0, [gin_ref[pl.ds(0, C), j * LANES : (j + 1) * LANES] for j in range(TILES)])
+    put_rows(rows_ref, ROW_OUT, outs)
+    put_rows(rows_ref, ROW_TAPS, tails)
+    put_rows(
+        rows_ref,
+        ROW_BIAS_IN,
+        [gin_ref[pl.ds(C, 1), j * LANES : (j + 1) * LANES] for j in range(TILES)],
+    )
     me = me_ref[0]
+    window = g_ref.shape[1]
     for position, start in zip(order, starts):
-        share = jnp.concatenate(
-            [rows_ref[j, pl.ds(start, WINDOW), :] for j in range(TILES)], axis=1
-        )
-        g_ref[position ^ me] = share.astype(BF16)
-
-
-def field_kernel(rows, lon_pad, block_rows, pad_ref, taps_ref, up_ref, out_ref, x_ref):
-    for t in range(2):
-        x_ref[t] = pad_ref[:, :, t * LANES : (t + 1) * LANES].astype(F32)
+        share = [rows_ref[t, pl.ds(start, window), :] for t in range(2)]
+        g_ref[position ^ me] = jnp.concatenate(share, axis=1).astype(BF16)
+
+
+def field_kernel(first, count, rows, cols, lon_pad, conv_rows,
+                 taps_ref, up_ref, main_ref, west_ref, east_ref, south_ref, north_ref, *rest):
+    out_ref, x_ref, sum_ref = rest[-3:]
+    assemble(x_ref, first, count + KS - 1, main_ref, west_ref, east_ref, south_ref, north_ref, rows, cols)
 
     def body(block, carry):
-        row = block * block_rows
+        row = block * conv_rows
 
         def store(tile, lon, sums):
             lanes = pl.ds(pl.multiple_of(tile * LANES, LANES), LANES)
-            for r in range(block_rows):
+            for r in range(conv_rows):
                 total = sums[r] + up_ref[row + r, pl.ds(lon, 16), lanes].astype(F32)
-                out_ref[row + r, pl.ds(lon, 16), lanes] = total.astype(BF16)
-
-        depthwise_block(x_ref, taps_ref, row, block_rows, lon_pad // 8, store, True)
+                sum_ref[row + r, pl.ds(lon, 16), lanes] = total.astype(BF16)
+
+        depthwise_block(x_ref, taps_ref, row, conv_rows, lon_pad // 8, store, True)
         return carry
 
-    lax.fori_loop(0, rows // block_rows, body, 0)
+    lax.fori_loop(0, count // conv_rows, body, 0)
+    out_ref[...] = sum_ref[:, 0 : out_ref.shape[1], 0:C]
 
 
 def shape(dims, kind):
@@ -320,13 +356,28 @@
 
 def whole(count):
     return [pl.BlockSpec(memory_space=pltpu.VMEM)] * count
+
+
+def halos(block, cols):
+    west, east = shift_both(block[:, :RAD, :C], block[:, cols - RAD : cols, :C], "lon", True)
+
+    def wide(rows):
+        return jnp.concatenate([west[rows], block[rows, :cols, :C], east[rows]], axis=1)
+
+    south, north = shift_both(wide(slice(0, RAD)), wide(slice(-RAD, None)), "lat", False)
+    return west, east, south, north
+
+
+def cost(micros):
+    return pl.CostEstimate(flops=int(micros * 1.1e9), bytes_accessed=0, transcendentals=0)
 
 
 def body(features, params, langevin_noise, upstream):
     rows, cols = features.shape[:2]
     lon_pad = up(cols, 16)
     lon_wide = up(lon_pad + KS - 1, 8)
-    block_rows = max(r for r in range(1, 6) if rows % r == 0)
+    conv_rows = max(r for r in range(1, 6) if rows % r == 0)
+    block_rows = max(r for r in range(1, 16) if rows % r == 0 and r % conv_rows == 0)
     axes = ("lon", "lat")
     steps = exchange_bits(axes)
     count = 1 << len(steps)
@@ -337,29 +388,39 @@
     for k in range(len(steps)):
         place = place | (((number >> k) & 1) << (len(steps) - 1 - k))
     place = place.reshape(1).astype(jnp.int32)
-    offset = (number * length) % H
+    offset = (number * length) % SHARE_LANES
     order = [reversed_bits(s, len(steps)) for s in range(count)]
-    starts = [s * length // H for s in range(count)]
-    w_rows = up(starts[-1] + WINDOW, 8)
-
-    window = lax.dynamic_update_slice(
-        jnp.zeros((WINDOW * H,), BF16), params.astype(BF16), (offset,)
+    starts = [s * length // SHARE_LANES for s in range(count)]
+    spill = SHARE_LANES - math.gcd(SHARE_LANES, length)
+    window = up(-(-(length + spill) // SHARE_LANES), 8)
+    flat_rows = up(max(starts[-1] + window, 3 * (ROWS + 1)), 8)
+
+    share = lax.dynamic_update_slice(
+        jnp.zeros((window * SHARE_LANES,), BF16), params.astype(BF16), (offset,)
     )
-    gathered = window.reshape(1, WINDOW, H)
-    for axis, bit in steps:
+    gathered = share.reshape(1, window, SHARE_LANES)
+    feature_halos = halos(features, cols)
+    for k, (axis, bit) in enumerate(steps):
+        if k == len(steps) - 2:
+            gathered, upstream = lax.optimization_barrier((gathered, upstream))
         gathered = jnp.concatenate([gathered, swap(gathered, axis, bit)], axis=0)
 
-    def widen(field, lons):
-        return jnp.pad(field, ((0, 0), (0, lons - field.shape[1]), (0, CP - C)))
-
-    padded = widen(padded_field(features), lon_wide)
-    x = padded.astype(F32).reshape(rows + KS - 1, lon_wide, 2, LANES).transpose(2, 0, 1, 3)
-    feat = widen(features, lon_pad)
-    ups = widen(upstream, lon_pad)
-
-    params_in = pltpu.CompilerParams(vmem_limit_bytes=VMEM)
+    compiler_params = pltpu.CompilerParams(vmem_limit_bytes=VMEM)
     smem = [pl.BlockSpec(memory_space=pltpu.SMEM)]
-    static = (order, starts, rows, lon_pad, block_rows)
+    x, ups = pl.pallas_call(
+        lambda *refs: assemble_kernel(rows, cols, *refs),
+        out_shape=(
+            shape((2, rows + KS - 1, lon_wide, LANES), F32),
+            shape((rows, lon_pad, CP), BF16),
+        ),
+        in_specs=whole(6),
+        out_specs=tuple(whole(2)),
+        compiler_params=compiler_params,
+        cost_estimate=cost(3),
+        name="assemble",
+    )(features, *feature_halos, upstream)
+
+    static = (order, starts, rows, lon_pad, block_rows, conv_rows)
     output, gconv, gin, gout, sums, taps = pl.pallas_call(
         lambda *refs: layer_kernel(*static, *refs),
         out_shape=(
@@ -370,56 +431,72 @@
             shape((5, 2, 8, LANES), F32),
             shape((2, 64, LANES), F32),
         ),
-        in_specs=smem + whole(4),
+        in_specs=smem + whole(3),
         out_specs=tuple(whole(6)),
         scratch_shapes=[
-            pltpu.VMEM((TILES, w_rows, LANES), F32),
+            pltpu.VMEM((2, flat_rows, LANES), F32),
             pltpu.VMEM((CP, H), BF16),
             pltpu.VMEM((H, CP), BF16),
-            pltpu.VMEM((H, CP), BF16),
-            pltpu.VMEM((CP, H), BF16),
             pltpu.VMEM((2, H, LANES), F32),
             pltpu.VMEM((2, block_rows, lon_pad, LANES), F32),
         ],
-        compiler_params=params_in,
+        compiler_params=compiler_params,
+        cost_estimate=cost(22),
         name="layer",
-    )(place, gathered, x, feat, ups)
-
-    grad_padded = widen(padded_field(gconv[:, :cols, :C]), lon_wide)
-    grads = pl.pallas_call(
+    )(place, gathered, x, ups)
+
+    grad_halos = halos(gconv, cols)
+    values = pl.pallas_call(
         lambda *refs: taps_kernel(*static, *refs),
-        out_shape=shape((count, WINDOW, H), BF16),
+        out_shape=shape((count, window, SHARE_LANES), BF16),
         in_specs=smem + whole(5),
         out_specs=whole(1)[0],
         scratch_shapes=[
-            pltpu.VMEM((TILES, w_rows, LANES), F32),
+            pltpu.VMEM((2, flat_rows, LANES), F32),
             pltpu.VMEM((2, TAPS, 8, LANES), F32),
             pltpu.VMEM((2, H, LANES), F32),
             pltpu.VMEM((2, 64, LANES), F32),
         ],
-        compiler_params=params_in,
+        compiler_params=compiler_params,
+        cost_estimate=cost(11),
         name="taps",
     )(place, gconv, x, gin, gout, sums)
 
-    field = pl.pallas_call(
-        lambda *refs: field_kernel(rows, lon_pad, block_rows, *refs),
-        out_shape=shape((rows, lon_pad, CP), BF16),
-        in_specs=whole(3),
-        out_specs=whole(1)[0],
-        scratch_shapes=[pltpu.VMEM((2, rows + KS - 1, lon_wide, LANES), F32)],
-        compiler_params=params_in,
-        name="field",
-    )(grad_padded, taps, ups)
-
-    values = grads
-    kept = None
+    pieces = 3 if rows % (3 * conv_rows) == 0 else 1
+    piece_rows = rows // pieces
+    field = None
+    for piece in range(pieces):
+        before = [] if field is None else [field]
+        held = [pl.BlockSpec(memory_space=pl.ANY)] * len(before)
+        at = lambda i, piece=piece: (piece, 0, 0)
+        field = pl.pallas_call(
+            lambda *refs, piece=piece: field_kernel(
+                piece * piece_rows, piece_rows, rows, cols, lon_pad, conv_rows, *refs
+            ),
+            grid=(1,),
+            out_shape=shape((rows, cols, C), BF16),
+            in_specs=whole(1)
+            + [pl.BlockSpec((piece_rows, lon_pad, CP), at)]
+            + whole(5)
+            + held,
+            out_specs=pl.BlockSpec((piece_rows, cols, C), at),
+            scratch_shapes=[
+                pltpu.VMEM((2, piece_rows + KS - 1, lon_wide, LANES), F32),
+                pltpu.VMEM((piece_rows, lon_pad, CP), BF16),
+            ],
+            input_output_aliases={7: 0} if before else {},
+            compiler_params=compiler_params,
+            cost_estimate=cost(12 / pieces),
+            name="field",
+        )(taps, ups, gconv, *grad_halos, *before)
+
     for axis, bit in steps[::-1]:
         half = values.shape[0] // 2
         received = swap(values[half:].astype(BF16), axis, bit)
         values = values[:half].astype(F32) + received.astype(F32)
     summed = lax.dynamic_slice(values.reshape(-1), (offset,), (length,))
     new_params = params - STEP_SIZE * summed + NOISE_COEF * langevin_noise
-    return (output, field[:, :cols, :C], new_params)
+    return (output, field, new_params)
 
 
 def solution(mesh):

time: 121 us -> 109 us (0.901)
  the two profiles are of different devices: /device:TPU:1 before, /device:TPU:0 now
where the time goes in v3:
time: 109 us
  Pallas kernels  54.4 us (50%)
  starting transfers between devices  32 us (29%)
  waiting for transfers between devices  10.8 us (10%)
  local copies, waits for them, and re-layouts  6.82 us (6%)
  other arithmetic  3.73 us (3%)
    pallas_call x1, Pallas kernels, body(): pl.pallas_call(lambda *refs: layer_kernel(*static, *refs), out_shape=(sha...  22.3 us
    ppermute x10, starting transfers between devices, swap(): lax.ppermute(values, axis, [(i, i ^ bit) for i in range(lax.axis_size(axi...  20.3 us
    pallas_call x3, Pallas kernels, body(): pl.pallas_call(lambda *refs, piece=piece: field_kernel(piece * piece_rows...  16 us
    pallas_call x1, Pallas kernels, body(): pl.pallas_call(lambda *refs: taps_kernel(*static, *refs), out_shape=shape...  11.9 us
    ppermute x10, waiting for transfers between devices, swap(): lax.ppermute(values, axis, [(i, i ^ bit) for i in range(lax.axis_size(axi...  10 us
    ppermute x4, starting transfers between devices, shift_both(): lax.ppermute(low_edge, axis, backward)  8.57 us
    pallas_call x1, Pallas kernels, body(): pl.pallas_call(lambda *refs: assemble_kernel(rows, cols, *refs), out_shap...  4.13 us
    ppermute x4, starting transfers between devices, shift_both(): lax.ppermute(high_edge, axis, forward)  3.14 us
  transfers between devices with their start and end apart: 18, of which 7 were waited for; matrix products, arithmetic and copies ran while one was open for 3% of the time, Pallas kernels for 30%

profile of v3, /device:TPU:0, one launch (start us, length us, event | category | flops | bytes accessed | tf_op | source)
XLA Modules:
  0.0 108.7 jit_solution(6849902965969700642)
XLA Ops:
  0.6 0.8 convert_element_type.25
  1.4 0.4 dynamic_update_slice.3
  1.8 4.1 %collective-permute-start = (bf16[1,40,256]{2,1,0:T(8,128)(2,1)S(1)}, bf16[1,40,256]{2,1,0:T(8,128)(2,1)S(1)}, u32[]{:S(2)}, u32[]{:S(2)}) collective-permute-start(bf16[1,40,256]{2,1,0:T(8,128)(2,1)S(1)} %reshape.16), channel_id=1, source_target_pairs={{0,16},{4,20},{8,24},{12,28},{16,0},{20,4},{24,8},{28,12},{1,17},{... | collective-permute-start | bytes 61448 | tf_op jit(solution)/shard_map/ppermute | solution.py:48
  5.9 1.1 %fusion.4 = (bf16[45,3,192]{2,1,0:T(4,128)(2,1)S(1)}, bf16[45,3,192]{2,1,0:T(4,128)(2,1)S(1)}) fusion(bf16[45,45,192]{2,1,0:T(8,128)(2,1)} %refs_0_.1), kind=kLoop, calls=%fused_computation.23 | loop fusion | bytes 207360 | tf_op jit(solution)/shard_map/slice | solution.py:362
  7.0 2.3 %collective-permute-start.6 = (bf16[45,3,192]{2,1,0:T(4,128)(2,1)S(1)}, bf16[45,3,192]{2,1,0:T(4,128)(2,1)S(1)}, u32[]{:S(2)}, u32[]{:S(2)}) collective-permute-start(bf16[45,3,192]{2,1,0:T(4,128)(2,1)S(1)} %get-tuple-element.29), channel_id=1, source_target_pairs={{4,0},{8,4},{12,8},{16,12},{20,16},{24,20},{28,24},{0,28},{5,1},{9... | collective-permute-start | bytes 155528 | tf_op jit(solution)/shard_map/ppermute | solution.py:57
  9.3 0.0 collective-permute-start.5
  9.3 0.9 fusion.3
  10.3 0.0 collective-permute-done
  10.3 1.4 %collective-permute-start.1 = (bf16[2,40,256]{2,1,0:T(8,128)(2,1)S(1)}, bf16[2,40,256]{2,1,0:T(8,128)(2,1)S(1)}, u32[]{:S(2)}, u32[]{:S(2)}) collective-permute-start(bf16[2,40,256]{2,1,0:T(8,128)(2,1)S(1)} %pad_maximum_fusion.8), channel_id=1, source_target_pairs={{0,8},{4,12},{8,0},{12,4},{16,24},{20,28},{24,16},{28,20},{1,9},{5... | collective-permute-start | bytes 122888 | tf_op jit(solution)/shard_map/ppermute | solution.py:48
  11.7 0.2 collective-permute-done.6.refs_2_
  11.9 2.5 %collective-permute-done.1 = bf16[2,40,256]{2,1,0:T(8,128)(2,1)S(1)} collective-permute-done((bf16[2,40,256]{2,1,0:T(8,128)(2,1)S(1)}, bf16[2,40,256]{2,1,0:T(8,128)(2,1)S(1)}, u32[]{:S(2)}, u32[]{:S(2)}) %collective-permute-start.1) | collective-permute-done | bytes 40992 | tf_op jit(solution)/shard_map/ppermute | solution.py:48
  14.4 3.2 %collective-permute-start.2 = (bf16[4,40,256]{2,1,0:T(8,128)(2,1)S(1)}, bf16[4,40,256]{2,1,0:T(8,128)(2,1)S(1)}, u32[]{:S(2)}, u32[]{:S(2)}) collective-permute-start(bf16[4,40,256]{2,1,0:T(8,128)(2,1)S(1)} %pad_maximum_fusion.7), channel_id=1, source_target_pairs={{0,4},{4,0},{8,12},{12,8},{16,20},{20,16},{24,28},{28,24},{1,5},{5... | collective-permute-start | bytes 245768 | tf_op jit(solution)/shard_map/ppermute | solution.py:48
  17.6 0.0 collective-permute-done.5.refs_1_
  17.6 2.4 %collective-permute-done.2 = bf16[4,40,256]{2,1,0:T(8,128)(2,1)S(1)} collective-permute-done((bf16[4,40,256]{2,1,0:T(8,128)(2,1)S(1)}, bf16[4,40,256]{2,1,0:T(8,128)(2,1)S(1)}, u32[]{:S(2)}, u32[]{:S(2)}) %collective-permute-start.2) | collective-permute-done | bytes 81952 | tf_op jit(solution)/shard_map/ppermute | solution.py:48
  20.0 1.6 %collective-permute-start.3 = (bf16[8,40,256]{2,1,0:T(8,128)(2,1)S(1)}, bf16[8,40,256]{2,1,0:T(8,128)(2,1)S(1)}, u32[]{:S(2)}, u32[]{:S(2)}) collective-permute-start(bf16[8,40,256]{2,1,0:T(8,128)(2,1)S(1)} %pad_maximum_fusion.2), channel_id=1, source_target_pairs={{0,2},{1,3},{2,0},{3,1},{4,6},{5,7},{6,4},{7,5},{8,10},{9,11},{10,... | collective-permute-start | bytes 491528 | tf_op jit(solution)/shard_map/ppermute | solution.py:48
  21.6 1.3 %collective-permute-start.7 = (bf16[3,51,192]{2,1,0:T(8,128)(2,1)S(1)}, bf16[3,51,192]{2,1,0:T(8,128)(2,1)S(1)}, u32[]{:S(2)}, u32[]{:S(2)}) collective-permute-start(bf16[3,51,192]{2,1,0:T(8,128)(2,1)S(1)} %pad_maximum_fusion.3), channel_id=1, source_target_pairs={{0,1},{1,2},{2,3},{4,5},{5,6},{6,7},{8,9},{9,10},{10,11},{12,13},{... | collective-permute-start | bytes 176264 | tf_op jit(solution)/shard_map/ppermute | solution.py:57
  23.0 1.3 %collective-permute-start.8 = (bf16[3,51,192]{2,1,0:T(8,128)(2,1)S(1)}, bf16[3,51,192]{2,1,0:T(8,128)(2,1)S(1)}, u32[]{:S(2)}, u32[]{:S(2)}) collective-permute-start(bf16[3,51,192]{2,1,0:T(8,128)(2,1)S(1)} %pad_maximum_fusion.4), channel_id=1, source_target_pairs={{1,0},{2,1},{3,2},{5,4},{6,5},{7,6},{9,8},{10,9},{11,10},{13,12},{... | collective-permute-start | bytes 176264 | tf_op jit(solution)/shard_map/ppermute | solution.py:57
  24.3 1.1 %collective-permute-done.3 = bf16[8,40,256]{2,1,0:T(8,128)(2,1)S(1)} collective-permute-done((bf16[8,40,256]{2,1,0:T(8,128)(2,1)S(1)}, bf16[8,40,256]{2,1,0:T(8,128)(2,1)S(1)}, u32[]{:S(2)}, u32[]{:S(2)}) %collective-permute-start.3) | collective-permute-done | bytes 163872 | tf_op jit(solution)/shard_map/ppermute | solution.py:48
  25.4 0.8 collective-permute-start.4
  26.3 0.0 collective-permute-done.7.refs_3_
  26.3 0.6 collective-permute-done.8.refs_4_
  26.9 0.0 copy-done.2
  26.9 0.0 copy-done.3
  26.9 0.0 copy-done.6
  26.9 0.0 copy-start.7
  26.9 0.6 copy-done.7
  27.6 4.1 %assemble.1 = (f32[2,51,56,128]{3,2,1,0:T(8,128)}, bf16[45,48,256]{2,1,0:T(8,128)(2,1)}) custom-call(bf16[45,45,192]{2,1,0:T(8,128)(2,1)} %refs_0_.1, bf16[45,3,192]{2,1,0:T(4,128)(2,1)} %copy-done.3, bf16[45,3,192]{2,1,0:T(4,128)(2,1)} %copy-done.2, bf16[3,51,192]{2,1,0:T(8,128)(2,1)} %copy-done.6, bf16[3,51,192]{2,1,0:T(8,128)(2,1)} %copy-done.7, ...), custom_call_target="tpu_custom_call" | custom-call | flops 3300000000 | tf_op jit(solution)/shard_map/assemble/pallas_call | solution.py:410
  31.7 0.0 collective-permute-done.4
  31.7 0.9 pad_maximum_fusion.refs_1_
  32.6 22.3 %layer.1 = (bf16[45,45,192]{2,1,0:T(8,128)(2,1)}, bf16[45,48,256]{2,1,0:T(8,128)(2,1)}, f32[256,768]{1,0:T(8,128)}, f32[256,768]{1,0:T(8,128)}, f32[5,2,8,128]{3,2,1,0:T(8,128)}, /*index=5*/f32[2,64,128]{2,1,0:T(8,128)}) custom-call(s32[1]{0:T(128)} %bitcast.refs_0_, bf16[32,40,256]{2,1,0:T(8,128)(2,1)} %pad_maximum_fusion.refs_1_, ...), custom_call_target="tpu_custom_call" | custom-call | flops 24199999488 | tf_op jit(solution)/shard_map/layer/pallas_call | solution.py:424
  54.9 0.9 fusion.1
  55.8 1.1 %fusion.2 = (bf16[45,3,192]{2,1,0:T(4,128)(2,1)S(1)}, bf16[45,3,192]{2,1,0:T(4,128)(2,1)S(1)}) fusion(bf16[45,48,256]{2,1,0:T(8,128)(2,1)} %get-tuple-element.19.refs_2_.refs_1_), kind=kLoop, calls=%fused_computation.21 | loop fusion | bytes 207360 | tf_op jit(solution)/shard_map/slice | solution.py:362
  56.9 3.7 %collective-permute-start.10 = (bf16[45,3,192]{2,1,0:T(4,128)(2,1)S(1)}, bf16[45,3,192]{2,1,0:T(4,128)(2,1)S(1)}, u32[]{:S(2)}, u32[]{:S(2)}) collective-permute-start(bf16[45,3,192]{2,1,0:T(4,128)(2,1)S(1)} %get-tuple-element.25), channel_id=1, source_target_pairs={{4,0},{8,4},{12,8},{16,12},{20,16},{24,20},{28,24},{0,28},{5,1},{9... | collective-permute-start | bytes 155528 | tf_op jit(solution)/shard_map/ppermute | solution.py:57
  60.6 0.0 collective-permute-start.9
  60.6 11.9 %taps.1 = bf16[32,40,256]{2,1,0:T(8,128)(2,1)} custom-call(s32[1]{0:T(128)} %bitcast.refs_0_, bf16[45,48,256]{2,1,0:T(8,128)(2,1)} %get-tuple-element.19.refs_2_.refs_1_, f32[2,51,56,128]{3,2,1,0:T(8,128)} %get-tuple-element.15.refs_2_, f32[256,768]{1,0:T(8,128)} %get-tuple-element.20.refs_3_, f32[256,768]{1,0:T(8,128)} %get-tuple-element.21.refs_4_, ...), custom_call_target="tpu_custom_call" | custom-call | flops 12099999744 | tf_op jit(solution)/shard_map/taps/pallas_call | solution.py:449
  72.5 1.0 slice.117
  73.5 2.9 %collective-permute-start.13 = (bf16[16,40,256]{2,1,0:T(8,128)(2,1)S(1)}, bf16[16,40,256]{2,1,0:T(8,128)(2,1)S(1)}, u32[]{:S(2)}, u32[]{:S(2)}) collective-permute-start(bf16[16,40,256]{2,1,0:T(8,128)(2,1)S(1)} %slice.117), channel_id=1, source_target_pairs={{0,1},{1,0},{2,3},{3,2},{4,5},{5,4},{6,7},{7,6},{8,9},{9,8},{10,11... | collective-permute-start | bytes 983048 | tf_op jit(solution)/shard_map/ppermute | solution.py:48
  76.4 0.0 collective-permute-done.10.refs_4_
  76.4 0.0 collective-permute-done.9.refs_3_
  76.5 0.0 copy-start.5
  76.5 1.2 %collective-permute-done.13 = bf16[16,40,256]{2,1,0:T(8,128)(2,1)S(1)} collective-permute-done((bf16[16,40,256]{2,1,0:T(8,128)(2,1)S(1)}, bf16[16,40,256]{2,1,0:T(8,128)(2,1)S(1)}, u32[]{:S(2)}, u32[]{:S(2)}) %collective-permute-start.13) | collective-permute-done | bytes 327712 | tf_op jit(solution)/shard_map/ppermute | solution.py:48
  77.7 1.1 convert_add_fusion
  78.8 0.5 collective-permute-start.14
  79.3 1.8 %collective-permute-start.11 = (bf16[3,51,192]{2,1,0:T(8,128)(2,1)S(1)}, bf16[3,51,192]{2,1,0:T(8,128)(2,1)S(1)}, u32[]{:S(2)}, u32[]{:S(2)}) collective-permute-start(bf16[3,51,192]{2,1,0:T(8,128)(2,1)S(1)} %pad_maximum_fusion.5), channel_id=1, source_target_pairs={{0,1},{1,2},{2,3},{4,5},{5,6},{6,7},{8,9},{9,10},{10,11},{12,13},{... | collective-permute-start | bytes 176264 | tf_op jit(solution)/shard_map/ppermute | solution.py:57
  81.2 1.3 %collective-permute-start.12 = (bf16[3,51,192]{2,1,0:T(8,128)(2,1)S(1)}, bf16[3,51,192]{2,1,0:T(8,128)(2,1)S(1)}, u32[]{:S(2)}, u32[]{:S(2)}) collective-permute-start(bf16[3,51,192]{2,1,0:T(8,128)(2,1)S(1)} %pad_maximum_fusion.6), channel_id=1, source_target_pairs={{1,0},{2,1},{3,2},{5,4},{6,5},{7,6},{9,8},{10,9},{11,10},{13,12},{... | collective-permute-start | bytes 176264 | tf_op jit(solution)/shard_map/ppermute | solution.py:57
  82.5 2.8 %collective-permute-done.14 = bf16[8,40,256]{2,1,0:T(8,128)(2,1)S(1)} collective-permute-done((bf16[8,40,256]{2,1,0:T(8,128)(2,1)S(1)}, bf16[8,40,256]{2,1,0:T(8,128)(2,1)S(1)}, u32[]{:S(2)}, u32[]{:S(2)}) %collective-permute-start.14) | collective-permute-done | bytes 163872 | tf_op jit(solution)/shard_map/ppermute | solution.py:48
  85.3 0.0 copy-done.4
  85.4 0.0 copy-done.5
  85.4 1.1 %collective-permute-start.15 = (bf16[4,40,256]{2,1,0:T(8,128)(2,1)S(1)}, bf16[4,40,256]{2,1,0:T(8,128)(2,1)S(1)}, u32[]{:S(2)}, u32[]{:S(2)}) collective-permute-start(bf16[4,40,256]{2,1,0:T(8,128)(2,1)S(1)} %slice.138), channel_id=1, source_target_pairs={{0,4},{4,0},{8,12},{12,8},{16,20},{20,16},{24,28},{28,24},{1,5},{5... | collective-permute-start | bytes 245768 | tf_op jit(solution)/shard_map/ppermute | solution.py:48
  86.5 0.0 collective-permute-done.11.refs_5_
  86.5 0.0 collective-permute-done.12.refs_6_
  86.5 0.6 copy-done.8
  87.1 0.0 copy-done.9
  87.2 5.3 %field.3.refs_7_ = bf16[45,45,192]{2,1,0:T(8,128)(2,1)} custom-call(f32[2,64,128]{2,1,0:T(8,128)} %get-tuple-element.18.refs_0_, bf16[45,48,256]{2,1,0:T(8,128)(2,1)} %get-tuple-element.16.refs_3_.refs_1_, bf16[45,48,256]{2,1,0:T(8,128)(2,1)} %get-tuple-element.19.refs_2_.refs_1_, bf16[45,3,192]{2,1,0:T(4,128)(2,1)} %copy-done.5, ...), custom_call_target="tpu_custom_call" | custom-call | flops 4400000000 | tf_op jit(solution)/shard_map/field/pallas_call | solution.py:472
  92.5 0.0 collective-permute-done.15
  92.6 0.7 collective-permute-start.16
  93.2 5.4 %field.4.refs_7_ = bf16[45,45,192]{2,1,0:T(8,128)(2,1)} custom-call(f32[2,64,128]{2,1,0:T(8,128)} %get-tuple-element.18.refs_0_, bf16[45,48,256]{2,1,0:T(8,128)(2,1)} %get-tuple-element.16.refs_3_.refs_1_, bf16[45,48,256]{2,1,0:T(8,128)(2,1)} %get-tuple-element.19.refs_2_.refs_1_, bf16[45,3,192]{2,1,0:T(4,128)(2,1)} %copy-done.5, ...), custom_call_target="tpu_custom_call", output_to_operand_aliasing={{}: (7, {})} | custom-call | flops 4400000000 | tf_op jit(solution)/shard_map/field/pallas_call | solution.py:472
  98.6 0.0 collective-permute-done.16
  98.6 0.0 copy-start
  98.6 0.0 copy-start.1
  98.6 4.0 %collective-permute-start.17 = (bf16[1,40,256]{2,1,0:T(8,128)(2,1)S(1)}, bf16[1,40,256]{2,1,0:T(8,128)(2,1)S(1)}, u32[]{:S(2)}, u32[]{:S(2)}) collective-permute-start(bf16[1,40,256]{2,1,0:T(8,128)(2,1)S(1)} %slice.140), channel_id=1, source_target_pairs={{0,16},{4,20},{8,24},{12,28},{16,0},{20,4},{24,8},{28,12},{1,17},{... | collective-permute-start | bytes 61448 | tf_op jit(solution)/shard_map/ppermute | solution.py:48
  102.6 5.3 %field.5 = bf16[45,45,192]{2,1,0:T(8,128)(2,1)} custom-call(f32[2,64,128]{2,1,0:T(8,128)} %get-tuple-element.18.refs_0_, bf16[45,48,256]{2,1,0:T(8,128)(2,1)} %get-tuple-element.16.refs_3_.refs_1_, bf16[45,48,256]{2,1,0:T(8,128)(2,1)} %get-tuple-element.19.refs_2_.refs_1_, bf16[45,3,192]{2,1,0:T(4,128)(2,1)} %copy-done.5, ...), custom_call_target="tpu_custom_call", output_to_operand_aliasing={{}: (7, {})} | custom-call | flops 4400000000 | tf_op jit(solution)/shard_map/field/pallas_call | solution.py:472
  108.0 0.0 collective-permute-done.17
  108.0 0.7 multiply_add_fusion
  (31 shorter events, 0.4 us)
Async XLA Ops:
  1.8 8.5 %collective-permute-start = (bf16[1,40,256]{2,1,0:T(8,128)(2,1)S(1)}, bf16[1,40,256]{2,1,0:T(8,128)(2,1)S(1)}, u32[]{:S(2)}, u32[]{:S(2)}) collective-permute-start(bf16[1,40,256]{2,1,0:T(8,128)(2,1)S(1)} %reshape.16), channel_id=1, source_target_pairs={{0,16},{4,20},{8,24},{12,28},{16,0},{20,4},{24,8},{28,12},{1,17},{... | collective-permute-start | bytes 61448 | tf_op jit(solution)/shard_map/ppermute | solution.py:48
  7.0 4.8 %collective-permute-start.6 = (bf16[45,3,192]{2,1,0:T(4,128)(2,1)S(1)}, bf16[45,3,192]{2,1,0:T(4,128)(2,1)S(1)}, u32[]{:S(2)}, u32[]{:S(2)}) collective-permute-start(bf16[45,3,192]{2,1,0:T(4,128)(2,1)S(1)} %get-tuple-element.29), channel_id=1, source_target_pairs={{4,0},{8,4},{12,8},{16,12},{20,16},{24,20},{28,24},{0,28},{5,1},{9... | collective-permute-start | bytes 155528 | tf_op jit(solution)/shard_map/ppermute | solution.py:57
  9.3 8.2 %collective-permute-start.5 = (bf16[45,3,192]{2,1,0:T(4,128)(2,1)S(1)}, bf16[45,3,192]{2,1,0:T(4,128)(2,1)S(1)}, u32[]{:S(2)}, u32[]{:S(2)}) collective-permute-start(bf16[45,3,192]{2,1,0:T(4,128)(2,1)S(1)} %get-tuple-element.30), channel_id=1, source_target_pairs={{0,4},{4,8},{8,12},{12,16},{16,20},{20,24},{24,28},{28,0},{1,5},{5... | collective-permute-start | bytes 155528 | tf_op jit(solution)/shard_map/ppermute | solution.py:57
  10.3 4.1 %collective-permute-start.1 = (bf16[2,40,256]{2,1,0:T(8,128)(2,1)S(1)}, bf16[2,40,256]{2,1,0:T(8,128)(2,1)S(1)}, u32[]{:S(2)}, u32[]{:S(2)}) collective-permute-start(bf16[2,40,256]{2,1,0:T(8,128)(2,1)S(1)} %pad_maximum_fusion.8), channel_id=1, source_target_pairs={{0,8},{4,12},{8,0},{12,4},{16,24},{20,28},{24,16},{28,20},{1,9},{5... | collective-permute-start | bytes 122888 | tf_op jit(solution)/shard_map/ppermute | solution.py:48
  11.9 15.1 %copy-start.2 = (bf16[45,3,192]{2,1,0:T(4,128)(2,1)}, bf16[45,3,192]{2,1,0:T(4,128)(2,1)S(1)}, u32[]{:S(2)}) copy-start(bf16[45,3,192]{2,1,0:T(4,128)(2,1)S(1)} %collective-permute-done.6.refs_2_) | copy-start | bytes 155524
  14.4 5.6 %collective-permute-start.2 = (bf16[4,40,256]{2,1,0:T(8,128)(2,1)S(1)}, bf16[4,40,256]{2,1,0:T(8,128)(2,1)S(1)}, u32[]{:S(2)}, u32[]{:S(2)}) collective-permute-start(bf16[4,40,256]{2,1,0:T(8,128)(2,1)S(1)} %pad_maximum_fusion.7), channel_id=1, source_target_pairs={{0,4},{4,0},{8,12},{12,8},{16,20},{20,16},{24,28},{28,24},{1,5},{5... | collective-permute-start | bytes 245768 | tf_op jit(solution)/shard_map/ppermute | solution.py:48
  17.6 9.3 %copy-start.3 = (bf16[45,3,192]{2,1,0:T(4,128)(2,1)}, bf16[45,3,192]{2,1,0:T(4,128)(2,1)S(1)}, u32[]{:S(2)}) copy-start(bf16[45,3,192]{2,1,0:T(4,128)(2,1)S(1)} %collective-permute-done.5.refs_1_) | copy-start | bytes 155524
  20.0 5.4 %collective-permute-start.3 = (bf16[8,40,256]{2,1,0:T(8,128)(2,1)S(1)}, bf16[8,40,256]{2,1,0:T(8,128)(2,1)S(1)}, u32[]{:S(2)}, u32[]{:S(2)}) collective-permute-start(bf16[8,40,256]{2,1,0:T(8,128)(2,1)S(1)} %pad_maximum_fusion.2), channel_id=1, source_target_pairs={{0,2},{1,3},{2,0},{3,1},{4,6},{5,7},{6,4},{7,5},{8,10},{9,11},{10,... | collective-permute-start | bytes 491528 | tf_op jit(solution)/shard_map/ppermute | solution.py:48
  21.6 4.6 %collective-permute-start.7 = (bf16[3,51,192]{2,1,0:T(8,128)(2,1)S(1)}, bf16[3,51,192]{2,1,0:T(8,128)(2,1)S(1)}, u32[]{:S(2)}, u32[]{:S(2)}) collective-permute-start(bf16[3,51,192]{2,1,0:T(8,128)(2,1)S(1)} %pad_maximum_fusion.3), channel_id=1, source_target_pairs={{0,1},{1,2},{2,3},{4,5},{5,6},{6,7},{8,9},{9,10},{10,11},{12,13},{... | collective-permute-start | bytes 176264 | tf_op jit(solution)/shard_map/ppermute | solution.py:57
  23.0 3.9 %collective-permute-start.8 = (bf16[3,51,192]{2,1,0:T(8,128)(2,1)S(1)}, bf16[3,51,192]{2,1,0:T(8,128)(2,1)S(1)}, u32[]{:S(2)}, u32[]{:S(2)}) collective-permute-start(bf16[3,51,192]{2,1,0:T(8,128)(2,1)S(1)} %pad_maximum_fusion.4), channel_id=1, source_target_pairs={{1,0},{2,1},{3,2},{5,4},{6,5},{7,6},{9,8},{10,9},{11,10},{13,12},{... | collective-permute-start | bytes 176264 | tf_op jit(solution)/shard_map/ppermute | solution.py:57
  25.4 6.2 %collective-permute-start.4 = (bf16[16,40,256]{2,1,0:T(8,128)(2,1)S(1)}, bf16[16,40,256]{2,1,0:T(8,128)(2,1)S(1)}, u32[]{:S(2)}, u32[]{:S(2)}) collective-permute-start(bf16[16,40,256]{2,1,0:T(8,128)(2,1)S(1)} %pad_maximum_fusion.1), channel_id=1, source_target_pairs={{0,1},{1,0},{2,3},{3,2},{4,5},{5,4},{6,7},{7,6},{8,9},{9,8},{10,11... | collective-permute-start | bytes 983048 | tf_op jit(solution)/shard_map/ppermute | solution.py:48
  26.3 0.6 copy-start.6
  26.9 0.6 copy-start.7
  56.9 19.5 %collective-permute-start.10 = (bf16[45,3,192]{2,1,0:T(4,128)(2,1)S(1)}, bf16[45,3,192]{2,1,0:T(4,128)(2,1)S(1)}, u32[]{:S(2)}, u32[]{:S(2)}) collective-permute-start(bf16[45,3,192]{2,1,0:T(4,128)(2,1)S(1)} %get-tuple-element.25), channel_id=1, source_target_pairs={{4,0},{8,4},{12,8},{16,12},{20,16},{24,20},{28,24},{0,28},{5,1},{9... | collective-permute-start | bytes 155528 | tf_op jit(solution)/shard_map/ppermute | solution.py:57
  60.6 15.9 %collective-permute-start.9 = (bf16[45,3,192]{2,1,0:T(4,128)(2,1)S(1)}, bf16[45,3,192]{2,1,0:T(4,128)(2,1)S(1)}, u32[]{:S(2)}, u32[]{:S(2)}) collective-permute-start(bf16[45,3,192]{2,1,0:T(4,128)(2,1)S(1)} %get-tuple-element.26), channel_id=1, source_target_pairs={{0,4},{4,8},{8,12},{12,16},{16,20},{20,24},{24,28},{28,0},{1,5},{5... | collective-permute-start | bytes 155528 | tf_op jit(solution)/shard_map/ppermute | solution.py:57
  73.5 4.2 %collective-permute-start.13 = (bf16[16,40,256]{2,1,0:T(8,128)(2,1)S(1)}, bf16[16,40,256]{2,1,0:T(8,128)(2,1)S(1)}, u32[]{:S(2)}, u32[]{:S(2)}) collective-permute-start(bf16[16,40,256]{2,1,0:T(8,128)(2,1)S(1)} %slice.117), channel_id=1, source_target_pairs={{0,1},{1,0},{2,3},{3,2},{4,5},{5,4},{6,7},{7,6},{8,9},{9,8},{10,11... | collective-permute-start | bytes 983048 | tf_op jit(solution)/shard_map/ppermute | solution.py:48
  76.4 8.9 %copy-start.4 = (bf16[45,3,192]{2,1,0:T(4,128)(2,1)}, bf16[45,3,192]{2,1,0:T(4,128)(2,1)S(1)}, u32[]{:S(2)}) copy-start(bf16[45,3,192]{2,1,0:T(4,128)(2,1)S(1)} %collective-permute-done.10.refs_4_) | copy-start | bytes 155524
  76.5 8.9 %copy-start.5 = (bf16[45,3,192]{2,1,0:T(4,128)(2,1)}, bf16[45,3,192]{2,1,0:T(4,128)(2,1)S(1)}, u32[]{:S(2)}) copy-start(bf16[45,3,192]{2,1,0:T(4,128)(2,1)S(1)} %collective-permute-done.9.refs_3_) | copy-start | bytes 155524
  78.8 6.5 %collective-permute-start.14 = (bf16[8,40,256]{2,1,0:T(8,128)(2,1)S(1)}, bf16[8,40,256]{2,1,0:T(8,128)(2,1)S(1)}, u32[]{:S(2)}, u32[]{:S(2)}) collective-permute-start(bf16[8,40,256]{2,1,0:T(8,128)(2,1)S(1)} %slice.137), channel_id=1, source_target_pairs={{0,2},{1,3},{2,0},{3,1},{4,6},{5,7},{6,4},{7,5},{8,10},{9,11},{10,... | collective-permute-start | bytes 491528 | tf_op jit(solution)/shard_map/ppermute | solution.py:48
  79.3 7.2 %collective-permute-start.11 = (bf16[3,51,192]{2,1,0:T(8,128)(2,1)S(1)}, bf16[3,51,192]{2,1,0:T(8,128)(2,1)S(1)}, u32[]{:S(2)}, u32[]{:S(2)}) collective-permute-start(bf16[3,51,192]{2,1,0:T(8,128)(2,1)S(1)} %pad_maximum_fusion.5), channel_id=1, source_target_pairs={{0,1},{1,2},{2,3},{4,5},{5,6},{6,7},{8,9},{9,10},{10,11},{12,13},{... | collective-permute-start | bytes 176264 | tf_op jit(solution)/shard_map/ppermute | solution.py:57
  81.2 5.3 %collective-permute-start.12 = (bf16[3,51,192]{2,1,0:T(8,128)(2,1)S(1)}, bf16[3,51,192]{2,1,0:T(8,128)(2,1)S(1)}, u32[]{:S(2)}, u32[]{:S(2)}) collective-permute-start(bf16[3,51,192]{2,1,0:T(8,128)(2,1)S(1)} %pad_maximum_fusion.6), channel_id=1, source_target_pairs={{1,0},{2,1},{3,2},{5,4},{6,5},{7,6},{9,8},{10,9},{11,10},{13,12},{... | collective-permute-start | bytes 176264 | tf_op jit(solution)/shard_map/ppermute | solution.py:57
  85.4 7.1 %collective-permute-start.15 = (bf16[4,40,256]{2,1,0:T(8,128)(2,1)S(1)}, bf16[4,40,256]{2,1,0:T(8,128)(2,1)S(1)}, u32[]{:S(2)}, u32[]{:S(2)}) collective-permute-start(bf16[4,40,256]{2,1,0:T(8,128)(2,1)S(1)} %slice.138), channel_id=1, source_target_pairs={{0,4},{4,0},{8,12},{12,8},{16,20},{20,16},{24,28},{28,24},{1,5},{5... | collective-permute-start | bytes 245768 | tf_op jit(solution)/shard_map/ppermute | solution.py:48
  86.5 0.6 copy-start.8
  86.5 0.7 copy-start.9
  92.6 6.0 %collective-permute-start.16 = (bf16[2,40,256]{2,1,0:T(8,128)(2,1)S(1)}, bf16[2,40,256]{2,1,0:T(8,128)(2,1)S(1)}, u32[]{:S(2)}, u32[]{:S(2)}) collective-permute-start(bf16[2,40,256]{2,1,0:T(8,128)(2,1)S(1)} %slice.139), channel_id=1, source_target_pairs={{0,8},{4,12},{8,0},{12,4},{16,24},{20,28},{24,16},{28,20},{1,9},{5... | collective-permute-start | bytes 122888 | tf_op jit(solution)/shard_map/ppermute | solution.py:48
  98.6 9.4 %copy-start = (f32[9568]{0:T(1024)S(1)}, f32[9568]{0:T(1024)}, u32[]{:S(2)}) copy-start(f32[9568]{0:T(1024)} %param.5) | copy-start | bytes 114820
  98.6 9.4 %copy-start.1 = (f32[9568]{0:T(1024)S(1)}, f32[9568]{0:T(1024)}, u32[]{:S(2)}) copy-start(f32[9568]{0:T(1024)} %param.6) | copy-start | bytes 114820
  98.6 9.3 %collective-permute-start.17 = (bf16[1,40,256]{2,1,0:T(8,128)(2,1)S(1)}, bf16[1,40,256]{2,1,0:T(8,128)(2,1)S(1)}, u32[]{:S(2)}, u32[]{:S(2)}) collective-permute-start(bf16[1,40,256]{2,1,0:T(8,128)(2,1)S(1)} %slice.140), channel_id=1, source_target_pairs={{0,16},{4,20},{8,24},{12,28},{16,0},{20,4},{24,8},{28,12},{1,17},{... | collective-permute-start | bytes 61448 | tf_op jit(solution)/shard_map/ppermute | solution.py:48

commit v4 on v3

--- a/solution.py
+++ b/solution.py
@@ -31,7 +31,7 @@
 SHARE_LANES = 256
 ALL = ((1,), (1,)), ((), ())
 OVER = ((0,), (0,)), ((), ())
-VMEM = 56 << 20
+VMEM = 28 << 20
 
 
 def exchange_bits(axes):

time: 109 us -> 90.5 us (0.83)
  Pallas kernels: 54.4 us -> 40.1 us
  local copies, waits for them, and re-layouts: 6.82 us -> 2.62 us
  starting transfers between devices: 32 us -> 33.1 us
    pallas_call x3, Pallas kernels: 16 us -> 11.8 us  [body(): pl.pallas_call(lambda *refs, piece=piece: field_kernel(piece * piece_rows...]
    pallas_call x1, Pallas kernels: 11.9 us -> 8.39 us  [body(): pl.pallas_call(lambda *refs: taps_kernel(*static, *refs), out_shape=shape...]
    pallas_call x1, Pallas kernels: 4.13 us -> 0.62 us  [body(): pl.pallas_call(lambda *refs: assemble_kernel(rows, cols, *refs), out_shap...]
    pallas_call x1, Pallas kernels: 22.3 us -> 19.4 us  [body(): pl.pallas_call(lambda *refs: layer_kernel(*static, *refs), out_shape=(sha...]
    unnamed x21 -> x9, local copies, waits for them, and re-layouts: 1.34 us -> 0.05 us
    concatenate x4, other arithmetic: 0.13 us -> 1.4 us  [wide(): jnp.concatenate([west[rows], block[rows, :cols, :C], east[rows]], axis=1)]
    ppermute x10, waiting for transfers between devices: 10 us -> 8.9 us  [swap(): lax.ppermute(values, axis, [(i, i ^ bit) for i in range(lax.axis_size(axi...]
  transfers between devices with their start and end apart: 18 -> 18, of which waited for: 7 -> 6; matrix products, arithmetic and copies ran while one was open for 3% -> 4% of each run, Pallas kernels for 30% -> 23%
where the time goes in v4:
time: 90.5 us; the launch traced here: 90.1 us
  Pallas kernels  40.1 us (44%)
  starting transfers between devices  33.1 us (37%)
  waiting for transfers between devices  10.1 us (11%)
  other arithmetic  3.17 us (4%)
  local copies, waits for them, and re-layouts  2.62 us (3%)
  between operations  0.94 us (1%)
    ppermute x10, starting transfers between devices, swap(): lax.ppermute(values, axis, [(i, i ^ bit) for i in range(lax.axis_size(axi...  21.1 us
    pallas_call x1, Pallas kernels, body(): pl.pallas_call(lambda *refs: layer_kernel(*static, *refs), out_shape=(sha...  19.4 us
    pallas_call x3, Pallas kernels, body(): pl.pallas_call(lambda *refs, piece=piece: field_kernel(piece * piece_rows...  11.8 us
    ppermute x4, starting transfers between devices, shift_both(): lax.ppermute(low_edge, axis, backward)  9 us
    ppermute x10, waiting for transfers between devices, swap(): lax.ppermute(values, axis, [(i, i ^ bit) for i in range(lax.axis_size(axi...  8.9 us
    pallas_call x1, Pallas kernels, body(): pl.pallas_call(lambda *refs: taps_kernel(*static, *refs), out_shape=shape...  8.39 us
    ppermute x4, starting transfers between devices, shift_both(): lax.ppermute(high_edge, axis, forward)  3.05 us
  transfers between devices with their start and end apart: 18, of which 6 were waited for; matrix products, arithmetic and copies ran while one was open for 4% of the time, Pallas kernels for 23%

profile of v4, /device:TPU:0, one launch (start us, length us, event | category | flops | bytes accessed | tf_op | source)
XLA Modules:
  0.0 90.1 jit_solution(5780786528898766254)
XLA Ops:
  0.6 0.8 convert_element_type.25
  1.4 0.4 dynamic_update_slice.3
  1.8 0.0 copy-start
  1.8 0.0 copy-start.1
  1.8 4.1 %collective-permute-start = (bf16[1,40,256]{2,1,0:T(8,128)(2,1)S(1)}, bf16[1,40,256]{2,1,0:T(8,128)(2,1)S(1)}, u32[]{:S(2)}, u32[]{:S(2)}) collective-permute-start(bf16[1,40,256]{2,1,0:T(8,128)(2,1)S(1)} %reshape.16), channel_id=1, source_target_pairs={{0,16},{4,20},{8,24},{12,28},{16,0},{20,4},{24,8},{28,12},{1,17},{... | collective-permute-start | bytes 61448 | tf_op jit(solution)/shard_map/ppermute | solution.py:48
  6.0 1.1 %fusion.4 = (bf16[45,3,192]{2,1,0:T(4,128)(2,1)S(1)}, bf16[45,3,192]{2,1,0:T(4,128)(2,1)S(1)}) fusion(bf16[45,45,192]{2,1,0:T(8,128)(2,1)} %refs_0_.1), kind=kLoop, calls=%fused_computation.23 | loop fusion | bytes 207360 | tf_op jit(solution)/shard_map/slice | solution.py:362
  7.0 2.5 %collective-permute-start.6 = (bf16[45,3,192]{2,1,0:T(4,128)(2,1)S(1)}, bf16[45,3,192]{2,1,0:T(4,128)(2,1)S(1)}, u32[]{:S(2)}, u32[]{:S(2)}) collective-permute-start(bf16[45,3,192]{2,1,0:T(4,128)(2,1)S(1)} %get-tuple-element.29), channel_id=1, source_target_pairs={{4,0},{8,4},{12,8},{16,12},{20,16},{24,20},{28,24},{0,28},{5,1},{9... | collective-permute-start | bytes 155528 | tf_op jit(solution)/shard_map/ppermute | solution.py:57
  9.6 0.0 collective-permute-start.5
  9.6 0.9 %fusion.3 = (bf16[3,45,192]{2,1,0:T(8,128)(2,1)S(1)}, bf16[3,45,192]{2,1,0:T(8,128)(2,1)S(1)}) fusion(bf16[45,45,192]{2,1,0:T(8,128)(2,1)} %refs_0_.1), kind=kLoop, calls=%fused_computation.22 | loop fusion | bytes 207360 | tf_op jit(solution)/shard_map/slice | solution.py:365
  10.5 0.0 collective-permute-done
  10.5 1.2 %collective-permute-start.1 = (bf16[2,40,256]{2,1,0:T(8,128)(2,1)S(1)}, bf16[2,40,256]{2,1,0:T(8,128)(2,1)S(1)}, u32[]{:S(2)}, u32[]{:S(2)}) collective-permute-start(bf16[2,40,256]{2,1,0:T(8,128)(2,1)S(1)} %pad_maximum_fusion.8), channel_id=1, source_target_pairs={{0,8},{4,12},{8,0},{12,4},{16,24},{20,28},{24,16},{28,20},{1,9},{5... | collective-permute-start | bytes 122888 | tf_op jit(solution)/shard_map/ppermute | solution.py:48
  11.7 0.4 collective-permute-done.6.refs_2_
  12.1 2.5 %collective-permute-done.1 = bf16[2,40,256]{2,1,0:T(8,128)(2,1)S(1)} collective-permute-done((bf16[2,40,256]{2,1,0:T(8,128)(2,1)S(1)}, bf16[2,40,256]{2,1,0:T(8,128)(2,1)S(1)}, u32[]{:S(2)}, u32[]{:S(2)}) %collective-permute-start.1) | collective-permute-done | bytes 40992 | tf_op jit(solution)/shard_map/ppermute | solution.py:48
  14.6 3.0 %collective-permute-start.2 = (bf16[4,40,256]{2,1,0:T(8,128)(2,1)S(1)}, bf16[4,40,256]{2,1,0:T(8,128)(2,1)S(1)}, u32[]{:S(2)}, u32[]{:S(2)}) collective-permute-start(bf16[4,40,256]{2,1,0:T(8,128)(2,1)S(1)} %pad_maximum_fusion.7), channel_id=1, source_target_pairs={{0,4},{4,0},{8,12},{12,8},{16,20},{20,16},{24,28},{28,24},{1,5},{5... | collective-permute-start | bytes 245768 | tf_op jit(solution)/shard_map/ppermute | solution.py:48
  17.6 0.0 collective-permute-done.5.refs_1_
  17.6 2.4 %collective-permute-done.2 = bf16[4,40,256]{2,1,0:T(8,128)(2,1)S(1)} collective-permute-done((bf16[4,40,256]{2,1,0:T(8,128)(2,1)S(1)}, bf16[4,40,256]{2,1,0:T(8,128)(2,1)S(1)}, u32[]{:S(2)}, u32[]{:S(2)}) %collective-permute-start.2) | collective-permute-done | bytes 81952 | tf_op jit(solution)/shard_map/ppermute | solution.py:48
  20.0 1.6 %collective-permute-start.3 = (bf16[8,40,256]{2,1,0:T(8,128)(2,1)S(1)}, bf16[8,40,256]{2,1,0:T(8,128)(2,1)S(1)}, u32[]{:S(2)}, u32[]{:S(2)}) collective-permute-start(bf16[8,40,256]{2,1,0:T(8,128)(2,1)S(1)} %pad_maximum_fusion.2), channel_id=1, source_target_pairs={{0,2},{1,3},{2,0},{3,1},{4,6},{5,7},{6,4},{7,5},{8,10},{9,11},{10,... | collective-permute-start | bytes 491528 | tf_op jit(solution)/shard_map/ppermute | solution.py:48
  21.6 0.7 pad_maximum_fusion.3
  22.3 1.3 %collective-permute-start.7 = (bf16[3,51,192]{2,1,0:T(8,128)(2,1)}, bf16[3,51,192]{2,1,0:T(8,128)(2,1)S(1)}, u32[]{:S(2)}, u32[]{:S(2)}) collective-permute-start(bf16[3,51,192]{2,1,0:T(8,128)(2,1)} %pad_maximum_fusion.3), channel_id=1, source_target_pairs={{0,1},{1,2},{2,3},{4,5},{5,6},{6,7},{8,9},{9,10},{10,11},{12,13},{... | collective-permute-start | bytes 176264 | tf_op jit(solution)/shard_map/ppermute | solution.py:57
  23.6 0.7 pad_maximum_fusion.4
  24.3 1.3 %collective-permute-start.8 = (bf16[3,51,192]{2,1,0:T(8,128)(2,1)}, bf16[3,51,192]{2,1,0:T(8,128)(2,1)S(1)}, u32[]{:S(2)}, u32[]{:S(2)}) collective-permute-start(bf16[3,51,192]{2,1,0:T(8,128)(2,1)} %pad_maximum_fusion.4), channel_id=1, source_target_pairs={{1,0},{2,1},{3,2},{5,4},{6,5},{7,6},{9,8},{10,9},{11,10},{13,12},{... | collective-permute-start | bytes 176264 | tf_op jit(solution)/shard_map/ppermute | solution.py:57
  25.5 0.0 collective-permute-done.3
  25.6 1.9 %collective-permute-start.4 = (bf16[16,40,256]{2,1,0:T(8,128)(2,1)S(1)}, bf16[16,40,256]{2,1,0:T(8,128)(2,1)S(1)}, u32[]{:S(2)}, u32[]{:S(2)}) collective-permute-start(bf16[16,40,256]{2,1,0:T(8,128)(2,1)S(1)} %pad_maximum_fusion.1), channel_id=1, source_target_pairs={{0,1},{1,0},{2,3},{3,2},{4,5},{5,4},{6,7},{7,6},{8,9},{9,8},{10,11... | collective-permute-start | bytes 983048 | tf_op jit(solution)/shard_map/ppermute | solution.py:48
  27.5 0.0 collective-permute-done.7.refs_3_
  27.5 0.8 collective-permute-done.8.refs_4_
  28.4 0.0 copy-done
  28.4 0.0 copy-done.1
  28.4 0.6 assemble.1
  29.0 0.0 collective-permute-done.4
  29.0 0.1 pad_maximum_fusion.refs_1_
  29.1 19.4 %layer.1 = (bf16[45,45,192]{2,1,0:T(8,128)(2,1)}, bf16[45,48,256]{2,1,0:T(8,128)(2,1)S(1)}, f32[256,768]{1,0:T(8,128)S(1)}, f32[256,768]{1,0:T(8,128)S(1)}, f32[...) custom-call(s32[1]{0:T(128)} %bitcast.refs_0_, bf16[32,40,256]{2,1,0:T(8,128)(2,1)S(1)} %pad_maximum_fusion.refs_1_, ...), custom_call_target="tpu_custom_call" | custom-call | flops 24199999488 | tf_op jit(solution)/shard_map/layer/pallas_call | solution.py:424
  48.5 0.1 fusion.2
  48.5 3.9 %collective-permute-start.10 = (bf16[45,3,192]{2,1,0:T(4,128)(2,1)S(1)}, bf16[45,3,192]{2,1,0:T(4,128)(2,1)S(1)}, u32[]{:S(2)}, u32[]{:S(2)}) collective-permute-start(bf16[45,3,192]{2,1,0:T(4,128)(2,1)S(1)} %get-tuple-element.25), channel_id=1, source_target_pairs={{4,0},{8,4},{12,8},{16,12},{20,16},{24,20},{28,24},{0,28},{5,1},{9... | collective-permute-start | bytes 155528 | tf_op jit(solution)/shard_map/ppermute | solution.py:57
  52.4 0.0 collective-permute-start.9
  52.4 8.4 %taps.1 = bf16[32,40,256]{2,1,0:T(8,128)(2,1)S(1)} custom-call(s32[1]{0:T(128)} %bitcast.refs_0_, bf16[45,48,256]{2,1,0:T(8,128)(2,1)S(1)} %get-tuple-element.19.refs_2_.refs_1_, f32[2,51,56,128]{3,2,1,0:T(8,128)S(1)} %get-tuple-element.15.refs_2_, f32[256,768]{1,0:T(8,128)S(1)} %get-tuple-element.20.refs_3_, f32[256,768]{1,0:T(8,128)S(1)} %get-tuple-element.21.refs_4_, ...), custom_call_target="tpu_custom_call" | custom-call | flops 12099999744 | tf_op jit(solution)/shard_map/taps/pallas_call | solution.py:449
  60.9 2.9 %collective-permute-start.13 = (bf16[16,40,256]{2,1,0:T(8,128)(2,1)S(1)}, bf16[16,40,256]{2,1,0:T(8,128)(2,1)S(1)}, u32[]{:S(2)}, u32[]{:S(2)}) collective-permute-start(bf16[16,40,256]{2,1,0:T(8,128)(2,1)S(1)} %slice.117), channel_id=1, source_target_pairs={{0,1},{1,0},{2,3},{3,2},{4,5},{5,4},{6,7},{7,6},{8,9},{9,8},{10,11... | collective-permute-start | bytes 983048 | tf_op jit(solution)/shard_map/ppermute | solution.py:48
  63.8 0.0 collective-permute-done.10.refs_4_
  63.8 0.0 collective-permute-done.9.refs_3_
  63.8 1.2 %collective-permute-done.13 = bf16[16,40,256]{2,1,0:T(8,128)(2,1)S(1)} collective-permute-done((bf16[16,40,256]{2,1,0:T(8,128)(2,1)S(1)}, bf16[16,40,256]{2,1,0:T(8,128)(2,1)S(1)}, u32[]{:S(2)}, u32[]{:S(2)}) %collective-permute-start.13) | collective-permute-done | bytes 327712 | tf_op jit(solution)/shard_map/ppermute | solution.py:48
  65.0 0.1 convert_add_fusion
  65.1 0.6 collective-permute-start.14
  65.8 1.8 %collective-permute-start.11 = (bf16[3,51,192]{2,1,0:T(8,128)(2,1)S(1)}, bf16[3,51,192]{2,1,0:T(8,128)(2,1)S(1)}, u32[]{:S(2)}, u32[]{:S(2)}) collective-permute-start(bf16[3,51,192]{2,1,0:T(8,128)(2,1)S(1)} %pad_maximum_fusion.5), channel_id=1, source_target_pairs={{0,1},{1,2},{2,3},{4,5},{5,6},{6,7},{8,9},{9,10},{10,11},{12,13},{... | collective-permute-start | bytes 176264 | tf_op jit(solution)/shard_map/ppermute | solution.py:57
  67.6 1.3 %collective-permute-start.12 = (bf16[3,51,192]{2,1,0:T(8,128)(2,1)S(1)}, bf16[3,51,192]{2,1,0:T(8,128)(2,1)S(1)}, u32[]{:S(2)}, u32[]{:S(2)}) collective-permute-start(bf16[3,51,192]{2,1,0:T(8,128)(2,1)S(1)} %pad_maximum_fusion.6), channel_id=1, source_target_pairs={{1,0},{2,1},{3,2},{5,4},{6,5},{7,6},{9,8},{10,9},{11,10},{13,12},{... | collective-permute-start | bytes 176264 | tf_op jit(solution)/shard_map/ppermute | solution.py:57
  68.9 2.8 %collective-permute-done.14 = bf16[8,40,256]{2,1,0:T(8,128)(2,1)S(1)} collective-permute-done((bf16[8,40,256]{2,1,0:T(8,128)(2,1)S(1)}, bf16[8,40,256]{2,1,0:T(8,128)(2,1)S(1)}, u32[]{:S(2)}, u32[]{:S(2)}) %collective-permute-start.14) | collective-permute-done | bytes 163872 | tf_op jit(solution)/shard_map/ppermute | solution.py:48
  71.7 0.9 collective-permute-start.15
  72.6 0.0 collective-permute-done.11.refs_5_
  72.6 0.0 collective-permute-done.12.refs_6_
  72.6 3.9 %field.3.refs_7_ = bf16[45,45,192]{2,1,0:T(8,128)(2,1)} custom-call(f32[2,64,128]{2,1,0:T(8,128)S(1)} %get-tuple-element.18.refs_0_, bf16[45,48,256]{2,1,0:T(8,128)(2,1)S(1)} %get-tuple-element.16.refs_3_.refs_1_, bf16[45,48,256]{2,1,0:T(8,128)(2,1)S(1)} %get-tuple-element.19.refs_2_.refs_1_, bf16[45,3,192]{2,1,0:T(4,128)(2,1)S(1)} %collective-permute-done.9.refs_3_, ...), custom_call_target="tpu_custom_call" | custom-call | flops 4400000000 | tf_op jit(solution)/shard_map/field/pallas_call | solution.py:472
  76.5 0.0 collective-permute-done.15
  76.6 0.6 collective-permute-start.16
  77.2 3.9 %field.4.refs_7_ = bf16[45,45,192]{2,1,0:T(8,128)(2,1)} custom-call(f32[2,64,128]{2,1,0:T(8,128)S(1)} %get-tuple-element.18.refs_0_, bf16[45,48,256]{2,1,0:T(8,128)(2,1)S(1)} %get-tuple-element.16.refs_3_.refs_1_, bf16[45,48,256]{2,1,0:T(8,128)(2,1)S(1)} %get-tuple-element.19.refs_2_.refs_1_, ...), custom_call_target="tpu_custom_call", output_to_operand_aliasing={{}: (7, {})} | custom-call | flops 4400000000 | tf_op jit(solution)/shard_map/field/pallas_call | solution.py:472
  81.2 0.0 collective-permute-done.16
  81.2 0.0 copy-start.2
  81.2 0.0 copy-start.3
  81.2 4.2 %collective-permute-start.17 = (bf16[1,40,256]{2,1,0:T(8,128)(2,1)S(1)}, bf16[1,40,256]{2,1,0:T(8,128)(2,1)S(1)}, u32[]{:S(2)}, u32[]{:S(2)}) collective-permute-start(bf16[1,40,256]{2,1,0:T(8,128)(2,1)S(1)} %slice.140), channel_id=1, source_target_pairs={{0,16},{4,20},{8,24},{12,28},{16,0},{20,4},{24,8},{28,12},{1,17},{... | collective-permute-start | bytes 61448 | tf_op jit(solution)/shard_map/ppermute | solution.py:48
  85.4 3.9 %field.5 = bf16[45,45,192]{2,1,0:T(8,128)(2,1)} custom-call(f32[2,64,128]{2,1,0:T(8,128)S(1)} %get-tuple-element.18.refs_0_, bf16[45,48,256]{2,1,0:T(8,128)(2,1)S(1)} %get-tuple-element.16.refs_3_.refs_1_, bf16[45,48,256]{2,1,0:T(8,128)(2,1)S(1)} %get-tuple-element.19.refs_2_.refs_1_, ...), custom_call_target="tpu_custom_call", output_to_operand_aliasing={{}: (7, {})} | custom-call | flops 4400000000 | tf_op jit(solution)/shard_map/field/pallas_call | solution.py:472
  89.4 0.0 collective-permute-done.17
  89.4 0.0 copy-done.2
  89.4 0.0 copy-done.3
  89.4 0.7 multiply_add_fusion
  (23 shorter events, 0.4 us)
Async XLA Ops:
  1.8 26.6 %copy-start = (bf16[45,45,192]{2,1,0:T(8,128)(2,1)S(1)}, bf16[45,45,192]{2,1,0:T(8,128)(2,1)}, u32[]{:S(2)}) copy-start(bf16[45,45,192]{2,1,0:T(8,128)(2,1)} %refs_0_.1) | copy-start | bytes 2332804
  1.8 26.5 %copy-start.1 = (bf16[45,45,192]{2,1,0:T(8,128)(2,1)S(1)}, bf16[45,45,192]{2,1,0:T(8,128)(2,1)}, u32[]{:S(2)}) copy-start(bf16[45,45,192]{2,1,0:T(8,128)(2,1)} %refs_5_) | copy-start | bytes 2332804
  1.8 8.7 %collective-permute-start = (bf16[1,40,256]{2,1,0:T(8,128)(2,1)S(1)}, bf16[1,40,256]{2,1,0:T(8,128)(2,1)S(1)}, u32[]{:S(2)}, u32[]{:S(2)}) collective-permute-start(bf16[1,40,256]{2,1,0:T(8,128)(2,1)S(1)} %reshape.16), channel_id=1, source_target_pairs={{0,16},{4,20},{8,24},{12,28},{16,0},{20,4},{24,8},{28,12},{1,17},{... | collective-permute-start | bytes 61448 | tf_op jit(solution)/shard_map/ppermute | solution.py:48
  7.0 5.0 %collective-permute-start.6 = (bf16[45,3,192]{2,1,0:T(4,128)(2,1)S(1)}, bf16[45,3,192]{2,1,0:T(4,128)(2,1)S(1)}, u32[]{:S(2)}, u32[]{:S(2)}) collective-permute-start(bf16[45,3,192]{2,1,0:T(4,128)(2,1)S(1)} %get-tuple-element.29), channel_id=1, source_target_pairs={{4,0},{8,4},{12,8},{16,12},{20,16},{24,20},{28,24},{0,28},{5,1},{9... | collective-permute-start | bytes 155528 | tf_op jit(solution)/shard_map/ppermute | solution.py:57
  9.6 8.0 %collective-permute-start.5 = (bf16[45,3,192]{2,1,0:T(4,128)(2,1)S(1)}, bf16[45,3,192]{2,1,0:T(4,128)(2,1)S(1)}, u32[]{:S(2)}, u32[]{:S(2)}) collective-permute-start(bf16[45,3,192]{2,1,0:T(4,128)(2,1)S(1)} %get-tuple-element.30), channel_id=1, source_target_pairs={{0,4},{4,8},{8,12},{12,16},{16,20},{20,24},{24,28},{28,0},{1,5},{5... | collective-permute-start | bytes 155528 | tf_op jit(solution)/shard_map/ppermute | solution.py:57
  10.5 4.1 %collective-permute-start.1 = (bf16[2,40,256]{2,1,0:T(8,128)(2,1)S(1)}, bf16[2,40,256]{2,1,0:T(8,128)(2,1)S(1)}, u32[]{:S(2)}, u32[]{:S(2)}) collective-permute-start(bf16[2,40,256]{2,1,0:T(8,128)(2,1)S(1)} %pad_maximum_fusion.8), channel_id=1, source_target_pairs={{0,8},{4,12},{8,0},{12,4},{16,24},{20,28},{24,16},{28,20},{1,9},{5... | collective-permute-start | bytes 122888 | tf_op jit(solution)/shard_map/ppermute | solution.py:48
  14.6 5.4 %collective-permute-start.2 = (bf16[4,40,256]{2,1,0:T(8,128)(2,1)S(1)}, bf16[4,40,256]{2,1,0:T(8,128)(2,1)S(1)}, u32[]{:S(2)}, u32[]{:S(2)}) collective-permute-start(bf16[4,40,256]{2,1,0:T(8,128)(2,1)S(1)} %pad_maximum_fusion.7), channel_id=1, source_target_pairs={{0,4},{4,0},{8,12},{12,8},{16,20},{20,16},{24,28},{28,24},{1,5},{5... | collective-permute-start | bytes 245768 | tf_op jit(solution)/shard_map/ppermute | solution.py:48
  20.0 5.5 %collective-permute-start.3 = (bf16[8,40,256]{2,1,0:T(8,128)(2,1)S(1)}, bf16[8,40,256]{2,1,0:T(8,128)(2,1)S(1)}, u32[]{:S(2)}, u32[]{:S(2)}) collective-permute-start(bf16[8,40,256]{2,1,0:T(8,128)(2,1)S(1)} %pad_maximum_fusion.2), channel_id=1, source_target_pairs={{0,2},{1,3},{2,0},{3,1},{4,6},{5,7},{6,4},{7,5},{8,10},{9,11},{10,... | collective-permute-start | bytes 491528 | tf_op jit(solution)/shard_map/ppermute | solution.py:48
  22.3 5.2 %collective-permute-start.7 = (bf16[3,51,192]{2,1,0:T(8,128)(2,1)}, bf16[3,51,192]{2,1,0:T(8,128)(2,1)S(1)}, u32[]{:S(2)}, u32[]{:S(2)}) collective-permute-start(bf16[3,51,192]{2,1,0:T(8,128)(2,1)} %pad_maximum_fusion.3), channel_id=1, source_target_pairs={{0,1},{1,2},{2,3},{4,5},{5,6},{6,7},{8,9},{9,10},{10,11},{12,13},{... | collective-permute-start | bytes 176264 | tf_op jit(solution)/shard_map/ppermute | solution.py:57
  24.3 4.1 %collective-permute-start.8 = (bf16[3,51,192]{2,1,0:T(8,128)(2,1)}, bf16[3,51,192]{2,1,0:T(8,128)(2,1)S(1)}, u32[]{:S(2)}, u32[]{:S(2)}) collective-permute-start(bf16[3,51,192]{2,1,0:T(8,128)(2,1)} %pad_maximum_fusion.4), channel_id=1, source_target_pairs={{1,0},{2,1},{3,2},{5,4},{6,5},{7,6},{9,8},{10,9},{11,10},{13,12},{... | collective-permute-start | bytes 176264 | tf_op jit(solution)/shard_map/ppermute | solution.py:57
  25.6 3.4 %collective-permute-start.4 = (bf16[16,40,256]{2,1,0:T(8,128)(2,1)S(1)}, bf16[16,40,256]{2,1,0:T(8,128)(2,1)S(1)}, u32[]{:S(2)}, u32[]{:S(2)}) collective-permute-start(bf16[16,40,256]{2,1,0:T(8,128)(2,1)S(1)} %pad_maximum_fusion.1), channel_id=1, source_target_pairs={{0,1},{1,0},{2,3},{3,2},{4,5},{5,4},{6,7},{7,6},{8,9},{9,8},{10,11... | collective-permute-start | bytes 983048 | tf_op jit(solution)/shard_map/ppermute | solution.py:48
  48.5 15.2 %collective-permute-start.10 = (bf16[45,3,192]{2,1,0:T(4,128)(2,1)S(1)}, bf16[45,3,192]{2,1,0:T(4,128)(2,1)S(1)}, u32[]{:S(2)}, u32[]{:S(2)}) collective-permute-start(bf16[45,3,192]{2,1,0:T(4,128)(2,1)S(1)} %get-tuple-element.25), channel_id=1, source_target_pairs={{4,0},{8,4},{12,8},{16,12},{20,16},{24,20},{28,24},{0,28},{5,1},{9... | collective-permute-start | bytes 155528 | tf_op jit(solution)/shard_map/ppermute | solution.py:57
  52.4 11.4 %collective-permute-start.9 = (bf16[45,3,192]{2,1,0:T(4,128)(2,1)S(1)}, bf16[45,3,192]{2,1,0:T(4,128)(2,1)S(1)}, u32[]{:S(2)}, u32[]{:S(2)}) collective-permute-start(bf16[45,3,192]{2,1,0:T(4,128)(2,1)S(1)} %get-tuple-element.26), channel_id=1, source_target_pairs={{0,4},{4,8},{8,12},{12,16},{16,20},{20,24},{24,28},{28,0},{1,5},{5... | collective-permute-start | bytes 155528 | tf_op jit(solution)/shard_map/ppermute | solution.py:57
  60.9 4.2 %collective-permute-start.13 = (bf16[16,40,256]{2,1,0:T(8,128)(2,1)S(1)}, bf16[16,40,256]{2,1,0:T(8,128)(2,1)S(1)}, u32[]{:S(2)}, u32[]{:S(2)}) collective-permute-start(bf16[16,40,256]{2,1,0:T(8,128)(2,1)S(1)} %slice.117), channel_id=1, source_target_pairs={{0,1},{1,0},{2,3},{3,2},{4,5},{5,4},{6,7},{7,6},{8,9},{9,8},{10,11... | collective-permute-start | bytes 983048 | tf_op jit(solution)/shard_map/ppermute | solution.py:48
  65.1 6.5 %collective-permute-start.14 = (bf16[8,40,256]{2,1,0:T(8,128)(2,1)S(1)}, bf16[8,40,256]{2,1,0:T(8,128)(2,1)S(1)}, u32[]{:S(2)}, u32[]{:S(2)}) collective-permute-start(bf16[8,40,256]{2,1,0:T(8,128)(2,1)S(1)} %slice.137), channel_id=1, source_target_pairs={{0,2},{1,3},{2,0},{3,1},{4,6},{5,7},{6,4},{7,5},{8,10},{9,11},{10,... | collective-permute-start | bytes 491528 | tf_op jit(solution)/shard_map/ppermute | solution.py:48
  65.8 6.8 %collective-permute-start.11 = (bf16[3,51,192]{2,1,0:T(8,128)(2,1)S(1)}, bf16[3,51,192]{2,1,0:T(8,128)(2,1)S(1)}, u32[]{:S(2)}, u32[]{:S(2)}) collective-permute-start(bf16[3,51,192]{2,1,0:T(8,128)(2,1)S(1)} %pad_maximum_fusion.5), channel_id=1, source_target_pairs={{0,1},{1,2},{2,3},{4,5},{5,6},{6,7},{8,9},{9,10},{10,11},{12,13},{... | collective-permute-start | bytes 176264 | tf_op jit(solution)/shard_map/ppermute | solution.py:57
  67.6 5.0 %collective-permute-start.12 = (bf16[3,51,192]{2,1,0:T(8,128)(2,1)S(1)}, bf16[3,51,192]{2,1,0:T(8,128)(2,1)S(1)}, u32[]{:S(2)}, u32[]{:S(2)}) collective-permute-start(bf16[3,51,192]{2,1,0:T(8,128)(2,1)S(1)} %pad_maximum_fusion.6), channel_id=1, source_target_pairs={{1,0},{2,1},{3,2},{5,4},{6,5},{7,6},{9,8},{10,9},{11,10},{13,12},{... | collective-permute-start | bytes 176264 | tf_op jit(solution)/shard_map/ppermute | solution.py:57
  71.7 4.8 %collective-permute-start.15 = (bf16[4,40,256]{2,1,0:T(8,128)(2,1)S(1)}, bf16[4,40,256]{2,1,0:T(8,128)(2,1)S(1)}, u32[]{:S(2)}, u32[]{:S(2)}) collective-permute-start(bf16[4,40,256]{2,1,0:T(8,128)(2,1)S(1)} %slice.138), channel_id=1, source_target_pairs={{0,4},{4,0},{8,12},{12,8},{16,20},{20,16},{24,28},{28,24},{1,5},{5... | collective-permute-start | bytes 245768 | tf_op jit(solution)/shard_map/ppermute | solution.py:48
  76.6 4.6 %collective-permute-start.16 = (bf16[2,40,256]{2,1,0:T(8,128)(2,1)S(1)}, bf16[2,40,256]{2,1,0:T(8,128)(2,1)S(1)}, u32[]{:S(2)}, u32[]{:S(2)}) collective-permute-start(bf16[2,40,256]{2,1,0:T(8,128)(2,1)S(1)} %slice.139), channel_id=1, source_target_pairs={{0,8},{4,12},{8,0},{12,4},{16,24},{20,28},{24,16},{28,20},{1,9},{5... | collective-permute-start | bytes 122888 | tf_op jit(solution)/shard_map/ppermute | solution.py:48
  81.2 8.2 %copy-start.2 = (f32[9568]{0:T(1024)S(1)}, f32[9568]{0:T(1024)}, u32[]{:S(2)}) copy-start(f32[9568]{0:T(1024)} %param.5) | copy-start | bytes 114820
  81.2 8.2 %copy-start.3 = (f32[9568]{0:T(1024)S(1)}, f32[9568]{0:T(1024)}, u32[]{:S(2)}) copy-start(f32[9568]{0:T(1024)} %param.6) | copy-start | bytes 114820
  81.2 8.1 %collective-permute-start.17 = (bf16[1,40,256]{2,1,0:T(8,128)(2,1)S(1)}, bf16[1,40,256]{2,1,0:T(8,128)(2,1)S(1)}, u32[]{:S(2)}, u32[]{:S(2)}) collective-permute-start(bf16[1,40,256]{2,1,0:T(8,128)(2,1)S(1)} %slice.140), channel_id=1, source_target_pairs={{0,16},{4,20},{8,24},{12,28},{16,0},{20,4},{24,8},{28,12},{1,17},{... | collective-permute-start | bytes 61448 | tf_op jit(solution)/shard_map/ppermute | solution.py:48

commit v5 on v4

--- a/solution.py
+++ b/solution.py
@@ -120,41 +120,132 @@
             x_ref[t, count - over : count, 0 : cols + 2 * RAD, width] = north[0:over, :, lanes].astype(F32)
 
 
-def assemble_kernel(rows, cols, feat_ref, west_ref, east_ref, south_ref, north_ref, up_ref,
-                    x_ref, ups_ref):
+def assemble_kernel(rows, cols, conv_rows, feat_ref, west_ref, east_ref, south_ref, north_ref, up_ref,
+                    v_ref, feats_ref, ups_ref, x_ref):
     assemble(x_ref, 0, x_ref.shape[1], feat_ref, west_ref, east_ref, south_ref, north_ref, rows, cols)
+    write_points(x_ref, v_ref, rows // conv_rows, conv_rows)
+    feats_ref[...] = jnp.zeros_like(feats_ref)
+    feats_ref[:, 0:cols, 0:C] = feat_ref[...]
     ups_ref[...] = jnp.zeros_like(ups_ref)
     ups_ref[:, 0:cols, 0:C] = up_ref[...]
 
 
-def depthwise_block(x_ref, k_ref, row, out_rows, lon_regs, store, flip):
-    steps = lon_regs // 2
+def points_for(out_rows):
+    pairs = [1.0, 0.5, 2.0, 1.5, 0.75][: (out_rows + KS - 2) // 2]
+    points = [0.0] + [sign * p for p in pairs for sign in (1.0, -1.0)]
+    filters = []
+    for k, point in enumerate(points):
+        scale = math.prod(point - other for i, other in enumerate(points) if i != k)
+        filters.append([point**a / scale for a in range(KS)])
+    return pairs, filters
+
+
+def polynomial(roots):
+    coefs = [1.0]
+    for root in roots:
+        coefs = [
+            (coefs[i - 1] if i else 0.0) - (root * coefs[i] if i < len(coefs) else 0.0)
+            for i in range(len(coefs) + 1)
+        ]
+    return coefs
+
+
+def weighted(coefs, values):
+    total = None
+    for coef, value in zip(coefs, values):
+        if coef == 0.0:
+            continue
+        term = value if coef == 1.0 else value * coef
+        total = term if total is None else total + term
+    return total
+
+
+def data_points(pairs, rows):
+    squares = [p * p for p in pairs]
+    values = [weighted(polynomial(squares), rows[0::2])]
+    for p in pairs:
+        coefs = polynomial([q for q in squares if q != p * p])
+        even = weighted(coefs, rows[2::2])
+        odd = weighted([p * c for c in coefs], rows[1::2])
+        values += [even + odd, even - odd]
+    return values
+
+
+def grad_points(pairs, rows):
+    values = [rows[0]]
+    for p in pairs:
+        even = weighted([p ** (2 * i) for i in range(len(rows[0::2]))], rows[0::2])
+        odd = weighted([p ** (2 * i + 1) for i in range(len(rows[1::2]))], rows[1::2])
+        values += [even + odd, even - odd] if odd is not None else [even, even]
+    return values
+
+
+def write_points(x_ref, v_ref, blocks, out_rows):
+    pairs, filters = points_for(out_rows)
+    count = len(filters)
+    lon_regs = x_ref.shape[2] // 8
 
     def body(step, carry):
-        tile = step // steps
-        lon = pl.multiple_of(step % steps * 16, 16)
+        tile = step // lon_regs
+        lon = pl.ds(pl.multiple_of(step % lon_regs * 8, 8), 8)
+
+        def block(k, carry):
+            rows = [x_ref[tile, k * out_rows + r, lon, :] for r in range(count)]
+            for i, value in enumerate(data_points(pairs, rows)):
+                v_ref[tile, k * count + i, lon, :] = value
+            return carry
+
+        return lax.fori_loop(0, blocks, block, carry, unroll=3 if blocks % 3 == 0 else 1)
+
+    lax.fori_loop(0, 2 * lon_regs, body, 0)
+
+
+def filter_points(taps_ref, out_rows, u_ref, flip):
+    for k, coefs in enumerate(points_for(out_rows)[1]):
+        coefs = coefs[::-1] if flip else coefs
+        for t in range(2):
+            u_ref[t, k, 0:KS, :] = weighted(
+                coefs, [taps_ref[t, pl.ds(a * KS, KS), :] for a in range(KS)]
+            )
+
+
+def depthwise_block(v_ref, u_ref, block, out_rows, lon_pad, store, flip):
+    pairs, filters = points_for(out_rows)
+    count = len(filters)
+    chunk = lon_pad // 2 if lon_pad % 16 == 0 else lon_pad
+
+    def body(step, carry):
+        tile = step // (lon_pad // chunk)
+        lon = pl.multiple_of(step % (lon_pad // chunk) * chunk, 8)
+
+        def product(k):
+            total = None
+            for b in range(KS):
+                tap = KS - 1 - b if flip else b
+                term = v_ref[tile, block * count + k, pl.ds(lon + b, chunk), :]
+                term = term * u_ref[tile, k, pl.ds(tap, 1), :]
+                total = term if total is None else total + term
+            return total
+
         sums = [None] * out_rows
-        for offset in range(out_rows + KS - 1):
-            for b in range(KS):
-                window = x_ref[tile, row + offset, pl.ds(lon + b, 16), :]
-                for r in range(out_rows):
-                    a = offset - r
-                    if 0 <= a < KS:
-                        tap = a * KS + b
-                        if flip:
-                            tap = TAPS - 1 - tap
-                        term = window * k_ref[tile, pl.ds(tap, 1), :]
-                        sums[r] = term if sums[r] is None else sums[r] + term
-        store(tile, lon, sums)
+        sums[0] = product(0)
+        for i, p in enumerate(pairs):
+            plus, minus = product(2 * i + 1), product(2 * i + 2)
+            even, odd = plus + minus, plus - minus
+            for r in range(out_rows):
+                term = odd if r % 2 else even
+                term = term if p**r == 1.0 else term * p**r
+                sums[r] = term if sums[r] is None else sums[r] + term
+        store(tile, lon, chunk, sums)
         return carry
 
-    lax.fori_loop(0, 2 * steps, body, 0)
+    lax.fori_loop(0, 2 * (lon_pad // chunk), body, 0)
 
 
 def layer_kernel(order, starts, rows, lon_pad, block_rows, conv_rows,
-                 me_ref, gathered_ref, x_ref, up_ref,
-                 out_ref, gconv_ref, gin_ref, gout_ref, sums_ref, taps_ref,
-                 w_ref, win_ref, wout_ref, wo32_ref, conv_ref):
+                 me_ref, gathered_ref, v_ref, feat_ref, up_ref,
+                 out_ref, gconv_ref, gin_ref, gout_ref, sums_ref, flipped_ref,
+                 u_ref, taps_ref, w_ref, win_ref, wout_ref, wo32_ref, conv_ref):
     me = me_ref[0]
     w_ref[...] = jnp.zeros_like(w_ref)
     window = gathered_ref.shape[1]
@@ -182,6 +273,8 @@
         at = (row - ROW_TAPS) * 4 + quarter
         return [taps_ref[t, pl.ds(at, 1), :] for t in range(2)]
 
+    filter_points(taps_ref, conv_rows, u_ref, False)
+    filter_points(taps_ref, conv_rows, flipped_ref, True)
     cbias = vector(ROW_NORM, 1)
     gain = vector(ROW_NORM, 2)
     shift = vector(ROW_NORM, 3)
@@ -205,11 +298,12 @@
         def conv_step(part, carry):
             at = part * conv_rows
 
-            def store(tile, lon, sums):
+            def store(tile, lon, chunk, sums):
                 for r in range(conv_rows):
-                    conv_ref[tile, at + r, pl.ds(lon, 16), :] = sums[r]
-
-            depthwise_block(x_ref, taps_ref, row + at, conv_rows, lon_pad // 8, store, False)
+                    conv_ref[tile, at + r, pl.ds(lon, chunk), :] = sums[r]
+
+            at_block = block * (block_rows // conv_rows) + part
+            depthwise_block(v_ref, u_ref, at_block, conv_rows, lon_pad, store, False)
             return carry
 
         lax.fori_loop(0, block_rows // conv_rows, conv_step, 0)
@@ -250,8 +344,7 @@
         for t in range(2):
             lanes = slice(t * LANES, (t + 1) * LANES)
             branch_t = branch[:, lanes] + bias_out[t]
-            feat = x_ref[t, pl.ds(row + RAD, block_rows), pl.ds(RAD, lon_pad), :]
-            feat = feat.reshape(cells, LANES)
+            feat = feat_ref[pl.ds(row, block_rows), :, lanes].reshape(cells, LANES).astype(F32)
             outs.append((feat + scale[t] * branch_t).astype(BF16))
             gn.append(gnormed[:, lanes])
             sums_ref[4, t] += partial(branch_t * ups[t])
@@ -278,33 +371,33 @@
 
 
 def taps_kernel(order, starts, rows, lon_pad, block_rows, conv_rows,
-                me_ref, gconv_ref, x_ref, gin_ref, gout_ref, sums_ref,
+                me_ref, gconv_ref, v_ref, gin_ref, gout_ref, sums_ref,
                 g_ref, rows_ref, acc_ref, wo32_ref, small_ref):
     acc_ref[...] = jnp.zeros_like(acc_ref)
+    pairs, filters = points_for(conv_rows)
+    count = len(filters)
 
     def body(step, carry):
         tile = step % 2
-        row = step // 2 * conv_rows
+        block = step // 2
         lanes = pl.ds(pl.multiple_of(tile * LANES, LANES), LANES)
-        grads = [gconv_ref[row + r, :, lanes].astype(F32) for r in range(conv_rows)]
-        for b in range(KS):
-            windows = [
-                x_ref[tile, row + offset, pl.ds(b, lon_pad), :]
-                for offset in range(conv_rows + KS - 1)
-            ]
-            for a in range(KS):
-                total = None
-                for r in range(conv_rows):
-                    term = grads[r] * windows[r + a]
-                    total = term if total is None else total + term
-                acc_ref[tile, a * KS + b] += total.reshape(lon_pad // 8, 8, LANES).sum(axis=0)
+        grads = grad_points(
+            pairs,
+            [gconv_ref[block * conv_rows + r, :, lanes].astype(F32) for r in range(conv_rows)],
+        )
+        for k in range(count):
+            for b in range(KS):
+                term = grads[k] * v_ref[tile, block * count + k, pl.ds(b, lon_pad), :]
+                acc_ref[tile, k, b] += term.reshape(lon_pad // 8, 8, LANES).sum(axis=0)
         return carry
 
     lax.fori_loop(0, 2 * (rows // conv_rows), body, 0)
     rows_ref[...] = jnp.zeros_like(rows_ref)
     small_ref[...] = jnp.zeros_like(small_ref)
     for t in range(2):
-        small_ref[t, pl.ds(0, TAPS), :] = jnp.sum(acc_ref[t], axis=1)
+        totals = [jnp.sum(acc_ref[t, k], axis=1) for k in range(count)]
+        for a in range(KS):
+            small_ref[t, pl.ds(a * KS, KS), :] = weighted([f[a] for f in filters], totals)
         for at, k in ((TAPS, 0), (TAPS + 1, 1), (TAPS + 2, 2), (TAPS + 7, 3), (TAPS + 8, 4)):
             small_ref[t, pl.ds(at, 1), :] = jnp.sum(sums_ref[k, t], axis=0, keepdims=True)
         wo32_ref[t] = gout_ref[pl.ds(t * LANES, LANES), :].T
@@ -330,24 +423,25 @@
 
 
 def field_kernel(first, count, rows, cols, lon_pad, conv_rows,
-                 taps_ref, up_ref, main_ref, west_ref, east_ref, south_ref, north_ref, *rest):
-    out_ref, x_ref, sum_ref = rest[-3:]
+                 u_ref, up_ref, main_ref, west_ref, east_ref, south_ref, north_ref, *rest):
+    out_ref, x_ref, v_ref, sum_ref = rest[-4:]
     assemble(x_ref, first, count + KS - 1, main_ref, west_ref, east_ref, south_ref, north_ref, rows, cols)
+    write_points(x_ref, v_ref, count // conv_rows, conv_rows)
 
     def body(block, carry):
         row = block * conv_rows
 
-        def store(tile, lon, sums):
+        def store(tile, lon, chunk, sums):
             lanes = pl.ds(pl.multiple_of(tile * LANES, LANES), LANES)
             for r in range(conv_rows):
-                total = sums[r] + up_ref[row + r, pl.ds(lon, 16), lanes].astype(F32)
-                sum_ref[row + r, pl.ds(lon, 16), lanes] = total.astype(BF16)
-
-        depthwise_block(x_ref, taps_ref, row, conv_rows, lon_pad // 8, store, True)
+                total = sums[r] + up_ref[row + r, pl.ds(lon, chunk), lanes].astype(F32)
+                sum_ref[row + r, pl.ds(lon, chunk), lanes] = total
+
+        depthwise_block(v_ref, u_ref, block, conv_rows, lon_pad, store, True)
         return carry
 
     lax.fori_loop(0, count // conv_rows, body, 0)
-    out_ref[...] = sum_ref[:, 0 : out_ref.shape[1], 0:C]
+    out_ref[...] = sum_ref[:, 0 : out_ref.shape[1], 0:C].astype(BF16)
 
 
 def shape(dims, kind):
@@ -376,7 +470,9 @@
     rows, cols = features.shape[:2]
     lon_pad = up(cols, 16)
     lon_wide = up(lon_pad + KS - 1, 8)
-    conv_rows = max(r for r in range(1, 6) if rows % r == 0)
+    conv_rows = max(r for r in (1, 3, 5) if rows % r == 0)
+    points = conv_rows + KS - 1
+    blocks = rows // conv_rows
     block_rows = max(r for r in range(1, 16) if rows % r == 0 and r % conv_rows == 0)
     axes = ("lon", "lat")
     steps = exchange_bits(axes)
@@ -407,21 +503,23 @@
 
     compiler_params = pltpu.CompilerParams(vmem_limit_bytes=VMEM)
     smem = [pl.BlockSpec(memory_space=pltpu.SMEM)]
-    x, ups = pl.pallas_call(
-        lambda *refs: assemble_kernel(rows, cols, *refs),
+    data, feats, ups = pl.pallas_call(
+        lambda *refs: assemble_kernel(rows, cols, conv_rows, *refs),
         out_shape=(
-            shape((2, rows + KS - 1, lon_wide, LANES), F32),
+            shape((2, blocks * points, lon_wide, LANES), F32),
+            shape((rows, lon_pad, CP), BF16),
             shape((rows, lon_pad, CP), BF16),
         ),
         in_specs=whole(6),
-        out_specs=tuple(whole(2)),
+        out_specs=tuple(whole(3)),
+        scratch_shapes=[pltpu.VMEM((2, rows + KS - 1, lon_wide, LANES), F32)],
         compiler_params=compiler_params,
         cost_estimate=cost(3),
         name="assemble",
     )(features, *feature_halos, upstream)
 
     static = (order, starts, rows, lon_pad, block_rows, conv_rows)
-    output, gconv, gin, gout, sums, taps = pl.pallas_call(
+    output, gconv, gin, gout, sums, flipped = pl.pallas_call(
         lambda *refs: layer_kernel(*static, *refs),
         out_shape=(
             shape((rows, cols, C), BF16),
@@ -429,11 +527,13 @@
             shape((CP, H), F32),
             shape((CP, H), F32),
             shape((5, 2, 8, LANES), F32),
-            shape((2, 64, LANES), F32),
+            shape((2, points, 8, LANES), F32),
         ),
-        in_specs=smem + whole(3),
+        in_specs=smem + whole(4),
         out_specs=tuple(whole(6)),
         scratch_shapes=[
+            pltpu.VMEM((2, points, 8, LANES), F32),
+            pltpu.VMEM((2, 64, LANES), F32),
             pltpu.VMEM((2, flat_rows, LANES), F32),
             pltpu.VMEM((CP, H), BF16),
             pltpu.VMEM((H, CP), BF16),
@@ -443,7 +543,7 @@
         compiler_params=compiler_params,
         cost_estimate=cost(22),
         name="layer",
-    )(place, gathered, x, ups)
+    )(place, gathered, data, feats, ups)
 
     grad_halos = halos(gconv, cols)
     values = pl.pallas_call(
@@ -453,14 +553,14 @@
         out_specs=whole(1)[0],
         scratch_shapes=[
             pltpu.VMEM((2, flat_rows, LANES), F32),
-            pltpu.VMEM((2, TAPS, 8, LANES), F32),
+            pltpu.VMEM((2, points, KS, 8, LANES), F32),
             pltpu.VMEM((2, H, LANES), F32),
             pltpu.VMEM((2, 64, LANES), F32),
         ],
         compiler_params=compiler_params,
         cost_estimate=cost(11),
         name="taps",
-    )(place, gconv, x, gin, gout, sums)
+    )(place, gconv, data, gin, gout, sums)
 
     pieces = 3 if rows % (3 * conv_rows) == 0 else 1
     piece_rows = rows // pieces
@@ -482,13 +582,14 @@
             out_specs=pl.BlockSpec((piece_rows, cols, C), at),
             scratch_shapes=[
                 pltpu.VMEM((2, piece_rows + KS - 1, lon_wide, LANES), F32),
-                pltpu.VMEM((piece_rows, lon_pad, CP), BF16),
+                pltpu.VMEM((2, piece_rows // conv_rows * points, lon_wide, LANES), F32),
+                pltpu.VMEM((piece_rows, lon_pad, CP), F32),
             ],
             input_output_aliases={7: 0} if before else {},
             compiler_params=compiler_params,
             cost_estimate=cost(12 / pieces),
             name="field",
-        )(taps, ups, gconv, *grad_halos, *before)
+        )(flipped, ups, gconv, *grad_halos, *before)
 
     for axis, bit in steps[::-1]:
         half = values.shape[0] // 2

time: 90.5 us -> 82.5 us (0.912)
  Pallas kernels: 40.1 us -> 32.2 us
    pallas_call x1, Pallas kernels: 8.39 us -> 4.07 us  [body(): pl.pallas_call(lambda *refs: taps_kernel(*static, *refs), out_shape=shape...]
    pallas_call x1, Pallas kernels: 19.4 us -> 15.3 us  [body(): pl.pallas_call(lambda *refs: layer_kernel(*static, *refs), out_shape=(sha...]
    pallas_call x1, Pallas kernels: 0.62 us -> 2.99 us  [body(): pl.pallas_call(lambda *refs: assemble_kernel(rows, cols, conv_rows, *refs...]
    pallas_call x3, Pallas kernels: 11.8 us -> 9.84 us  [body(): pl.pallas_call(lambda *refs, piece=piece: field_kernel(piece * piece_rows...]
  transfers between devices with their start and end apart: 18 -> 18, of which waited for: 6 -> 9; matrix products, arithmetic and copies ran while one was open for 4% -> 4% of each run, Pallas kernels for 23% -> 21%
where the time goes in v5:
time: 82.5 us; the launch traced here: 82.2 us
  starting transfers between devices  32.5 us (39%)
  Pallas kernels  32.2 us (39%)
  waiting for transfers between devices  10.8 us (13%)
  other arithmetic  3.16 us (4%)
  local copies, waits for them, and re-layouts  2.62 us (3%)
  between operations  0.93 us (1%)
    ppermute x10, starting transfers between devices, swap(): lax.ppermute(values, axis, [(i, i ^ bit) for i in range(lax.axis_size(axi...  20.9 us
    pallas_call x1, Pallas kernels, body(): pl.pallas_call(lambda *refs: layer_kernel(*static, *refs), out_shape=(sha...  15.3 us
    pallas_call x3, Pallas kernels, body(): pl.pallas_call(lambda *refs, piece=piece: field_kernel(piece * piece_rows...  9.84 us
    ppermute x10, waiting for transfers between devices, swap(): lax.ppermute(values, axis, [(i, i ^ bit) for i in range(lax.axis_size(axi...  9.35 us
    ppermute x4, starting transfers between devices, shift_both(): lax.ppermute(low_edge, axis, backward)  8.99 us
    pallas_call x1, Pallas kernels, body(): pl.pallas_call(lambda *refs: taps_kernel(*static, *refs), out_shape=shape...  4.07 us
    pallas_call x1, Pallas kernels, body(): pl.pallas_call(lambda *refs: assemble_kernel(rows, cols, conv_rows, *refs...  2.99 us
    ppermute x4, starting transfers between devices, shift_both(): lax.ppermute(high_edge, axis, forward)  2.58 us
  transfers between devices with their start and end apart: 18, of which 9 were waited for; matrix products, arithmetic and copies ran while one was open for 4% of the time, Pallas kernels for 21%

profile of v5, /device:TPU:0, one launch (start us, length us, event | category | flops | bytes accessed | tf_op | source)
XLA Modules:
  0.0 82.2 jit_solution(3424171829779401440)
XLA Ops:
  0.6 0.8 convert_element_type.25
  1.4 0.4 dynamic_update_slice.3
  1.8 0.0 copy-start
  1.8 0.0 copy-start.1
  1.8 4.1 %collective-permute-start = (bf16[1,40,256]{2,1,0:T(8,128)(2,1)S(1)}, bf16[1,40,256]{2,1,0:T(8,128)(2,1)S(1)}, u32[]{:S(2)}, u32[]{:S(2)}) collective-permute-start(bf16[1,40,256]{2,1,0:T(8,128)(2,1)S(1)} %reshape.16), channel_id=1, source_target_pairs={{0,16},{4,20},{8,24},{12,28},{16,0},{20,4},{24,8},{28,12},{1,17},{... | collective-permute-start | bytes 61448 | tf_op jit(solution)/shard_map/ppermute | solution.py:48
  6.0 1.1 %fusion.4 = (bf16[45,3,192]{2,1,0:T(4,128)(2,1)S(1)}, bf16[45,3,192]{2,1,0:T(4,128)(2,1)S(1)}) fusion(bf16[45,45,192]{2,1,0:T(8,128)(2,1)} %refs_0_.1), kind=kLoop, calls=%fused_computation.23 | loop fusion | bytes 207360 | tf_op jit(solution)/shard_map/slice | solution.py:456
  7.0 2.5 %collective-permute-start.6 = (bf16[45,3,192]{2,1,0:T(4,128)(2,1)S(1)}, bf16[45,3,192]{2,1,0:T(4,128)(2,1)S(1)}, u32[]{:S(2)}, u32[]{:S(2)}) collective-permute-start(bf16[45,3,192]{2,1,0:T(4,128)(2,1)S(1)} %get-tuple-element.31), channel_id=1, source_target_pairs={{4,0},{8,4},{12,8},{16,12},{20,16},{24,20},{28,24},{0,28},{5,1},{9... | collective-permute-start | bytes 155528 | tf_op jit(solution)/shard_map/ppermute | solution.py:57
  9.6 0.0 collective-permute-start.5
  9.6 0.9 %fusion.3 = (bf16[3,45,192]{2,1,0:T(8,128)(2,1)S(1)}, bf16[3,45,192]{2,1,0:T(8,128)(2,1)S(1)}) fusion(bf16[45,45,192]{2,1,0:T(8,128)(2,1)} %refs_0_.1), kind=kLoop, calls=%fused_computation.22 | loop fusion | bytes 207360 | tf_op jit(solution)/shard_map/slice | solution.py:459
  10.5 0.0 collective-permute-done
  10.5 1.2 %collective-permute-start.1 = (bf16[2,40,256]{2,1,0:T(8,128)(2,1)S(1)}, bf16[2,40,256]{2,1,0:T(8,128)(2,1)S(1)}, u32[]{:S(2)}, u32[]{:S(2)}) collective-permute-start(bf16[2,40,256]{2,1,0:T(8,128)(2,1)S(1)} %pad_maximum_fusion.8), channel_id=1, source_target_pairs={{0,8},{4,12},{8,0},{12,4},{16,24},{20,28},{24,16},{28,20},{1,9},{5... | collective-permute-start | bytes 122888 | tf_op jit(solution)/shard_map/ppermute | solution.py:48
  11.7 0.4 collective-permute-done.6.refs_2_
  12.1 2.5 %collective-permute-done.1 = bf16[2,40,256]{2,1,0:T(8,128)(2,1)S(1)} collective-permute-done((bf16[2,40,256]{2,1,0:T(8,128)(2,1)S(1)}, bf16[2,40,256]{2,1,0:T(8,128)(2,1)S(1)}, u32[]{:S(2)}, u32[]{:S(2)}) %collective-permute-start.1) | collective-permute-done | bytes 40992 | tf_op jit(solution)/shard_map/ppermute | solution.py:48
  14.6 3.0 %collective-permute-start.2 = (bf16[4,40,256]{2,1,0:T(8,128)(2,1)S(1)}, bf16[4,40,256]{2,1,0:T(8,128)(2,1)S(1)}, u32[]{:S(2)}, u32[]{:S(2)}) collective-permute-start(bf16[4,40,256]{2,1,0:T(8,128)(2,1)S(1)} %pad_maximum_fusion.7), channel_id=1, source_target_pairs={{0,4},{4,0},{8,12},{12,8},{16,20},{20,16},{24,28},{28,24},{1,5},{5... | collective-permute-start | bytes 245768 | tf_op jit(solution)/shard_map/ppermute | solution.py:48
  17.6 0.0 collective-permute-done.5.refs_1_
  17.6 2.4 %collective-permute-done.2 = bf16[4,40,256]{2,1,0:T(8,128)(2,1)S(1)} collective-permute-done((bf16[4,40,256]{2,1,0:T(8,128)(2,1)S(1)}, bf16[4,40,256]{2,1,0:T(8,128)(2,1)S(1)}, u32[]{:S(2)}, u32[]{:S(2)}) %collective-permute-start.2) | collective-permute-done | bytes 81952 | tf_op jit(solution)/shard_map/ppermute | solution.py:48
  20.0 1.6 %collective-permute-start.3 = (bf16[8,40,256]{2,1,0:T(8,128)(2,1)S(1)}, bf16[8,40,256]{2,1,0:T(8,128)(2,1)S(1)}, u32[]{:S(2)}, u32[]{:S(2)}) collective-permute-start(bf16[8,40,256]{2,1,0:T(8,128)(2,1)S(1)} %pad_maximum_fusion.2), channel_id=1, source_target_pairs={{0,2},{1,3},{2,0},{3,1},{4,6},{5,7},{6,4},{7,5},{8,10},{9,11},{10,... | collective-permute-start | bytes 491528 | tf_op jit(solution)/shard_map/ppermute | solution.py:48
  21.6 0.7 pad_maximum_fusion.3
  22.3 1.3 %collective-permute-start.7 = (bf16[3,51,192]{2,1,0:T(8,128)(2,1)}, bf16[3,51,192]{2,1,0:T(8,128)(2,1)S(1)}, u32[]{:S(2)}, u32[]{:S(2)}) collective-permute-start(bf16[3,51,192]{2,1,0:T(8,128)(2,1)} %pad_maximum_fusion.3), channel_id=1, source_target_pairs={{0,1},{1,2},{2,3},{4,5},{5,6},{6,7},{8,9},{9,10},{10,11},{12,13},{... | collective-permute-start | bytes 176264 | tf_op jit(solution)/shard_map/ppermute | solution.py:57
  23.6 0.7 pad_maximum_fusion.4
  24.3 1.3 %collective-permute-start.8 = (bf16[3,51,192]{2,1,0:T(8,128)(2,1)}, bf16[3,51,192]{2,1,0:T(8,128)(2,1)S(1)}, u32[]{:S(2)}, u32[]{:S(2)}) collective-permute-start(bf16[3,51,192]{2,1,0:T(8,128)(2,1)} %pad_maximum_fusion.4), channel_id=1, source_target_pairs={{1,0},{2,1},{3,2},{5,4},{6,5},{7,6},{9,8},{10,9},{11,10},{13,12},{... | collective-permute-start | bytes 176264 | tf_op jit(solution)/shard_map/ppermute | solution.py:57
  25.5 0.0 collective-permute-done.3
  25.6 1.9 %collective-permute-start.4 = (bf16[16,40,256]{2,1,0:T(8,128)(2,1)S(1)}, bf16[16,40,256]{2,1,0:T(8,128)(2,1)S(1)}, u32[]{:S(2)}, u32[]{:S(2)}) collective-permute-start(bf16[16,40,256]{2,1,0:T(8,128)(2,1)S(1)} %pad_maximum_fusion.1), channel_id=1, source_target_pairs={{0,1},{1,0},{2,3},{3,2},{4,5},{5,4},{6,7},{7,6},{8,9},{9,8},{10,11... | collective-permute-start | bytes 983048 | tf_op jit(solution)/shard_map/ppermute | solution.py:48
  27.5 0.0 collective-permute-done.7.refs_3_
  27.5 0.8 %collective-permute-done.8.refs_4_ = bf16[3,51,192]{2,1,0:T(8,128)(2,1)S(1)} collective-permute-done((bf16[3,51,192]{2,1,0:T(8,128)(2,1)}, bf16[3,51,192]{2,1,0:T(8,128)(2,1)S(1)}, u32[]{:S(2)}, u32[]{:S(2)}) %collective-permute-start.8) | collective-permute-done | bytes 58784 | tf_op jit(solution)/shard_map/ppermute | solution.py:57
  28.4 0.0 copy-done
  28.4 0.0 copy-done.1
  28.4 3.0 %assemble.1 = (f32[2,99,56,128]{3,2,1,0:T(8,128)S(1)}, bf16[45,48,256]{2,1,0:T(8,128)(2,1)S(1)}, bf16[45,48,256]{2,1,0:T(8,128)(2,1)S(1)}) custom-call(bf16[45,45,192]{2,1,0:T(8,128)(2,1)S(1)} %copy-done, bf16[45,3,192]{2,1,0:T(4,128)(2,1)S(1)} %collective-permute-done.5.refs_1_, bf16[45,3,192]{2,1,0:T(4,128)(2,1)S(1)} %collective-permute-done.6.refs_2_, ...), custom_call_target="tpu_custom_call" | custom-call | flops 3300000000 | tf_op jit(solution)/shard_map/assemble/pallas_call | solution.py:506
  31.4 0.0 collective-permute-done.4
  31.4 0.1 pad_maximum_fusion.refs_1_
  31.5 15.3 %layer.1 = (bf16[45,45,192]{2,1,0:T(8,128)(2,1)}, bf16[45,48,256]{2,1,0:T(8,128)(2,1)S(1)}, f32[256,768]{1,0:T(8,128)S(1)}, f32[256,768]{1,0:T(8,128)S(1)}, f32[...) custom-call(s32[1]{0:T(128)} %bitcast.refs_0_, bf16[32,40,256]{2,1,0:T(8,128)(2,1)S(1)} %pad_maximum_fusion.refs_1_, ...), custom_call_target="tpu_custom_call" | custom-call | flops 24199999488 | tf_op jit(solution)/shard_map/layer/pallas_call | solution.py:522
  46.8 0.1 fusion.2
  46.8 3.9 %collective-permute-start.10 = (bf16[45,3,192]{2,1,0:T(4,128)(2,1)S(1)}, bf16[45,3,192]{2,1,0:T(4,128)(2,1)S(1)}, u32[]{:S(2)}, u32[]{:S(2)}) collective-permute-start(bf16[45,3,192]{2,1,0:T(4,128)(2,1)S(1)} %get-tuple-element.27), channel_id=1, source_target_pairs={{4,0},{8,4},{12,8},{16,12},{20,16},{24,20},{28,24},{0,28},{5,1},{9... | collective-permute-start | bytes 155528 | tf_op jit(solution)/shard_map/ppermute | solution.py:57
  50.7 0.0 collective-permute-start.9
  50.7 4.1 %taps.1 = bf16[32,40,256]{2,1,0:T(8,128)(2,1)S(1)} custom-call(s32[1]{0:T(128)} %bitcast.refs_0_, bf16[45,48,256]{2,1,0:T(8,128)(2,1)S(1)} %get-tuple-element.21.refs_2_.refs_1_, f32[2,99,56,128]{3,2,1,0:T(8,128)S(1)} %get-tuple-element.16.refs_2_, f32[256,768]{1,0:T(8,128)S(1)} %get-tuple-element.22.refs_3_, f32[256,768]{1,0:T(8,128)S(1)} %get-tuple-element.23.refs_4_, ...), custom_call_target="tpu_custom_call" | custom-call | flops 12099999744 | tf_op jit(solution)/shard_map/taps/pallas_call | solution.py:549
  54.8 2.9 %collective-permute-start.13 = (bf16[16,40,256]{2,1,0:T(8,128)(2,1)S(1)}, bf16[16,40,256]{2,1,0:T(8,128)(2,1)S(1)}, u32[]{:S(2)}, u32[]{:S(2)}) collective-permute-start(bf16[16,40,256]{2,1,0:T(8,128)(2,1)S(1)} %slice.117), channel_id=1, source_target_pairs={{0,1},{1,0},{2,3},{3,2},{4,5},{5,4},{6,7},{7,6},{8,9},{9,8},{10,11... | collective-permute-start | bytes 983048 | tf_op jit(solution)/shard_map/ppermute | solution.py:48
  57.7 0.0 collective-permute-done.10.refs_4_
  57.8 0.2 collective-permute-done.9.refs_3_
  58.0 1.0 %collective-permute-done.13 = bf16[16,40,256]{2,1,0:T(8,128)(2,1)S(1)} collective-permute-done((bf16[16,40,256]{2,1,0:T(8,128)(2,1)S(1)}, bf16[16,40,256]{2,1,0:T(8,128)(2,1)S(1)}, u32[]{:S(2)}, u32[]{:S(2)}) %collective-permute-start.13) | collective-permute-done | bytes 327712 | tf_op jit(solution)/shard_map/ppermute | solution.py:48
  59.0 0.1 convert_add_fusion
  59.1 2.1 %collective-permute-start.14 = (bf16[8,40,256]{2,1,0:T(8,128)(2,1)S(1)}, bf16[8,40,256]{2,1,0:T(8,128)(2,1)S(1)}, u32[]{:S(2)}, u32[]{:S(2)}) collective-permute-start(bf16[8,40,256]{2,1,0:T(8,128)(2,1)S(1)} %slice.137), channel_id=1, source_target_pairs={{0,2},{1,3},{2,0},{3,1},{4,6},{5,7},{6,4},{7,5},{8,10},{9,11},{10,... | collective-permute-start | bytes 491528 | tf_op jit(solution)/shard_map/ppermute | solution.py:48
  61.2 1.3 %collective-permute-start.11 = (bf16[3,51,192]{2,1,0:T(8,128)(2,1)S(1)}, bf16[3,51,192]{2,1,0:T(8,128)(2,1)S(1)}, u32[]{:S(2)}, u32[]{:S(2)}) collective-permute-start(bf16[3,51,192]{2,1,0:T(8,128)(2,1)S(1)} %pad_maximum_fusion.5), channel_id=1, source_target_pairs={{0,1},{1,2},{2,3},{4,5},{5,6},{6,7},{8,9},{9,10},{10,11},{12,13},{... | collective-permute-start | bytes 176264 | tf_op jit(solution)/shard_map/ppermute | solution.py:57
  62.6 1.3 %collective-permute-start.12 = (bf16[3,51,192]{2,1,0:T(8,128)(2,1)S(1)}, bf16[3,51,192]{2,1,0:T(8,128)(2,1)S(1)}, u32[]{:S(2)}, u32[]{:S(2)}) collective-permute-start(bf16[3,51,192]{2,1,0:T(8,128)(2,1)S(1)} %pad_maximum_fusion.6), channel_id=1, source_target_pairs={{1,0},{2,1},{3,2},{5,4},{6,5},{7,6},{9,8},{10,9},{11,10},{13,12},{... | collective-permute-start | bytes 176264 | tf_op jit(solution)/shard_map/ppermute | solution.py:57
  63.9 2.1 %collective-permute-done.14 = bf16[8,40,256]{2,1,0:T(8,128)(2,1)S(1)} collective-permute-done((bf16[8,40,256]{2,1,0:T(8,128)(2,1)S(1)}, bf16[8,40,256]{2,1,0:T(8,128)(2,1)S(1)}, u32[]{:S(2)}, u32[]{:S(2)}) %collective-permute-start.14) | collective-permute-done | bytes 163872 | tf_op jit(solution)/shard_map/ppermute | solution.py:48
  66.0 0.6 collective-permute-start.15
  66.6 0.0 collective-permute-done.11.refs_5_
  66.6 0.0 collective-permute-done.12.refs_6_
  66.6 3.3 %field.3.refs_7_ = bf16[45,45,192]{2,1,0:T(8,128)(2,1)} custom-call(f32[2,11,8,128]{3,2,1,0:T(8,128)S(1)} %get-tuple-element.20.refs_0_, bf16[45,48,256]{2,1,0:T(8,128)(2,1)S(1)} %get-tuple-element.18.refs_4_.refs_1_, bf16[45,48,256]{2,1,0:T(8,128)(2,1)S(1)} %get-tuple-element.21.refs_2_.refs_1_, bf16[45,3,192]{2,1,0:T(4,128)(2,1)S(1)} %collective-permute-done.9.refs_3_, ...), custom_call_target="tpu_custom_call" | custom-call | flops 4400000000 | tf_op jit(solution)/shard_map/field/pallas_call | solution.py:572
  69.9 0.7 collective-permute-done.15
  70.6 0.1 collective-permute-start.16
  70.6 3.3 %field.4.refs_7_ = bf16[45,45,192]{2,1,0:T(8,128)(2,1)} custom-call(f32[2,11,8,128]{3,2,1,0:T(8,128)S(1)} %get-tuple-element.20.refs_0_, bf16[45,48,256]{2,1,0:T(8,128)(2,1)S(1)} %get-tuple-element.18.refs_4_.refs_1_, bf16[45,48,256]{2,1,0:T(8,128)(2,1)S(1)} %get-tuple-element.21.refs_2_.refs_1_, ...), custom_call_target="tpu_custom_call", output_to_operand_aliasing={{}: (7, {})} | custom-call | flops 4400000000 | tf_op jit(solution)/shard_map/field/pallas_call | solution.py:572
  73.9 0.7 collective-permute-done.16
  74.6 0.0 copy-start.2
  74.7 0.0 copy-start.3
  74.7 3.5 %collective-permute-start.17 = (bf16[1,40,256]{2,1,0:T(8,128)(2,1)S(1)}, bf16[1,40,256]{2,1,0:T(8,128)(2,1)S(1)}, u32[]{:S(2)}, u32[]{:S(2)}) collective-permute-start(bf16[1,40,256]{2,1,0:T(8,128)(2,1)S(1)} %slice.140), channel_id=1, source_target_pairs={{0,16},{4,20},{8,24},{12,28},{16,0},{20,4},{24,8},{28,12},{1,17},{... | collective-permute-start | bytes 61448 | tf_op jit(solution)/shard_map/ppermute | solution.py:48
  78.1 3.3 %field.5 = bf16[45,45,192]{2,1,0:T(8,128)(2,1)} custom-call(f32[2,11,8,128]{3,2,1,0:T(8,128)S(1)} %get-tuple-element.20.refs_0_, bf16[45,48,256]{2,1,0:T(8,128)(2,1)S(1)} %get-tuple-element.18.refs_4_.refs_1_, bf16[45,48,256]{2,1,0:T(8,128)(2,1)S(1)} %get-tuple-element.21.refs_2_.refs_1_, ...), custom_call_target="tpu_custom_call", output_to_operand_aliasing={{}: (7, {})} | custom-call | flops 4400000000 | tf_op jit(solution)/shard_map/field/pallas_call | solution.py:572
  81.4 0.0 collective-permute-done.17
  81.4 0.0 copy-done.2
  81.4 0.0 copy-done.3
  81.5 0.7 multiply_add_fusion
  (23 shorter events, 0.3 us)
Async XLA Ops:
  1.8 26.6 %copy-start = (bf16[45,45,192]{2,1,0:T(8,128)(2,1)S(1)}, bf16[45,45,192]{2,1,0:T(8,128)(2,1)}, u32[]{:S(2)}) copy-start(bf16[45,45,192]{2,1,0:T(8,128)(2,1)} %refs_0_.1) | copy-start | bytes 2332804
  1.8 26.5 %copy-start.1 = (bf16[45,45,192]{2,1,0:T(8,128)(2,1)S(1)}, bf16[45,45,192]{2,1,0:T(8,128)(2,1)}, u32[]{:S(2)}) copy-start(bf16[45,45,192]{2,1,0:T(8,128)(2,1)} %refs_5_) | copy-start | bytes 2332804
  1.8 8.7 %collective-permute-start = (bf16[1,40,256]{2,1,0:T(8,128)(2,1)S(1)}, bf16[1,40,256]{2,1,0:T(8,128)(2,1)S(1)}, u32[]{:S(2)}, u32[]{:S(2)}) collective-permute-start(bf16[1,40,256]{2,1,0:T(8,128)(2,1)S(1)} %reshape.16), channel_id=1, source_target_pairs={{0,16},{4,20},{8,24},{12,28},{16,0},{20,4},{24,8},{28,12},{1,17},{... | collective-permute-start | bytes 61448 | tf_op jit(solution)/shard_map/ppermute | solution.py:48
  7.0 5.0 %collective-permute-start.6 = (bf16[45,3,192]{2,1,0:T(4,128)(2,1)S(1)}, bf16[45,3,192]{2,1,0:T(4,128)(2,1)S(1)}, u32[]{:S(2)}, u32[]{:S(2)}) collective-permute-start(bf16[45,3,192]{2,1,0:T(4,128)(2,1)S(1)} %get-tuple-element.31), channel_id=1, source_target_pairs={{4,0},{8,4},{12,8},{16,12},{20,16},{24,20},{28,24},{0,28},{5,1},{9... | collective-permute-start | bytes 155528 | tf_op jit(solution)/shard_map/ppermute | solution.py:57
  9.6 8.0 %collective-permute-start.5 = (bf16[45,3,192]{2,1,0:T(4,128)(2,1)S(1)}, bf16[45,3,192]{2,1,0:T(4,128)(2,1)S(1)}, u32[]{:S(2)}, u32[]{:S(2)}) collective-permute-start(bf16[45,3,192]{2,1,0:T(4,128)(2,1)S(1)} %get-tuple-element.32), channel_id=1, source_target_pairs={{0,4},{4,8},{8,12},{12,16},{16,20},{20,24},{24,28},{28,0},{1,5},{5... | collective-permute-start | bytes 155528 | tf_op jit(solution)/shard_map/ppermute | solution.py:57
  10.5 4.1 %collective-permute-start.1 = (bf16[2,40,256]{2,1,0:T(8,128)(2,1)S(1)}, bf16[2,40,256]{2,1,0:T(8,128)(2,1)S(1)}, u32[]{:S(2)}, u32[]{:S(2)}) collective-permute-start(bf16[2,40,256]{2,1,0:T(8,128)(2,1)S(1)} %pad_maximum_fusion.8), channel_id=1, source_target_pairs={{0,8},{4,12},{8,0},{12,4},{16,24},{20,28},{24,16},{28,20},{1,9},{5... | collective-permute-start | bytes 122888 | tf_op jit(solution)/shard_map/ppermute | solution.py:48
  14.6 5.4 %collective-permute-start.2 = (bf16[4,40,256]{2,1,0:T(8,128)(2,1)S(1)}, bf16[4,40,256]{2,1,0:T(8,128)(2,1)S(1)}, u32[]{:S(2)}, u32[]{:S(2)}) collective-permute-start(bf16[4,40,256]{2,1,0:T(8,128)(2,1)S(1)} %pad_maximum_fusion.7), channel_id=1, source_target_pairs={{0,4},{4,0},{8,12},{12,8},{16,20},{20,16},{24,28},{28,24},{1,5},{5... | collective-permute-start | bytes 245768 | tf_op jit(solution)/shard_map/ppermute | solution.py:48
  20.0 5.5 %collective-permute-start.3 = (bf16[8,40,256]{2,1,0:T(8,128)(2,1)S(1)}, bf16[8,40,256]{2,1,0:T(8,128)(2,1)S(1)}, u32[]{:S(2)}, u32[]{:S(2)}) collective-permute-start(bf16[8,40,256]{2,1,0:T(8,128)(2,1)S(1)} %pad_maximum_fusion.2), channel_id=1, source_target_pairs={{0,2},{1,3},{2,0},{3,1},{4,6},{5,7},{6,4},{7,5},{8,10},{9,11},{10,... | collective-permute-start | bytes 491528 | tf_op jit(solution)/shard_map/ppermute | solution.py:48
  22.3 5.2 %collective-permute-start.7 = (bf16[3,51,192]{2,1,0:T(8,128)(2,1)}, bf16[3,51,192]{2,1,0:T(8,128)(2,1)S(1)}, u32[]{:S(2)}, u32[]{:S(2)}) collective-permute-start(bf16[3,51,192]{2,1,0:T(8,128)(2,1)} %pad_maximum_fusion.3), channel_id=1, source_target_pairs={{0,1},{1,2},{2,3},{4,5},{5,6},{6,7},{8,9},{9,10},{10,11},{12,13},{... | collective-permute-start | bytes 176264 | tf_op jit(solution)/shard_map/ppermute | solution.py:57
  24.3 4.1 %collective-permute-start.8 = (bf16[3,51,192]{2,1,0:T(8,128)(2,1)}, bf16[3,51,192]{2,1,0:T(8,128)(2,1)S(1)}, u32[]{:S(2)}, u32[]{:S(2)}) collective-permute-start(bf16[3,51,192]{2,1,0:T(8,128)(2,1)} %pad_maximum_fusion.4), channel_id=1, source_target_pairs={{1,0},{2,1},{3,2},{5,4},{6,5},{7,6},{9,8},{10,9},{11,10},{13,12},{... | collective-permute-start | bytes 176264 | tf_op jit(solution)/shard_map/ppermute | solution.py:57
  25.6 5.8 %collective-permute-start.4 = (bf16[16,40,256]{2,1,0:T(8,128)(2,1)S(1)}, bf16[16,40,256]{2,1,0:T(8,128)(2,1)S(1)}, u32[]{:S(2)}, u32[]{:S(2)}) collective-permute-start(bf16[16,40,256]{2,1,0:T(8,128)(2,1)S(1)} %pad_maximum_fusion.1), channel_id=1, source_target_pairs={{0,1},{1,0},{2,3},{3,2},{4,5},{5,4},{6,7},{7,6},{8,9},{9,8},{10,11... | collective-permute-start | bytes 983048 | tf_op jit(solution)/shard_map/ppermute | solution.py:48
  46.8 10.9 %collective-permute-start.10 = (bf16[45,3,192]{2,1,0:T(4,128)(2,1)S(1)}, bf16[45,3,192]{2,1,0:T(4,128)(2,1)S(1)}, u32[]{:S(2)}, u32[]{:S(2)}) collective-permute-start(bf16[45,3,192]{2,1,0:T(4,128)(2,1)S(1)} %get-tuple-element.27), channel_id=1, source_target_pairs={{4,0},{8,4},{12,8},{16,12},{20,16},{24,20},{28,24},{0,28},{5,1},{9... | collective-permute-start | bytes 155528 | tf_op jit(solution)/shard_map/ppermute | solution.py:57
  50.7 7.2 %collective-permute-start.9 = (bf16[45,3,192]{2,1,0:T(4,128)(2,1)S(1)}, bf16[45,3,192]{2,1,0:T(4,128)(2,1)S(1)}, u32[]{:S(2)}, u32[]{:S(2)}) collective-permute-start(bf16[45,3,192]{2,1,0:T(4,128)(2,1)S(1)} %get-tuple-element.28), channel_id=1, source_target_pairs={{0,4},{4,8},{8,12},{12,16},{16,20},{20,24},{24,28},{28,0},{1,5},{5... | collective-permute-start | bytes 155528 | tf_op jit(solution)/shard_map/ppermute | solution.py:57
  54.8 4.2 %collective-permute-start.13 = (bf16[16,40,256]{2,1,0:T(8,128)(2,1)S(1)}, bf16[16,40,256]{2,1,0:T(8,128)(2,1)S(1)}, u32[]{:S(2)}, u32[]{:S(2)}) collective-permute-start(bf16[16,40,256]{2,1,0:T(8,128)(2,1)S(1)} %slice.117), channel_id=1, source_target_pairs={{0,1},{1,0},{2,3},{3,2},{4,5},{5,4},{6,7},{7,6},{8,9},{9,8},{10,11... | collective-permute-start | bytes 983048 | tf_op jit(solution)/shard_map/ppermute | solution.py:48
  59.1 6.9 %collective-permute-start.14 = (bf16[8,40,256]{2,1,0:T(8,128)(2,1)S(1)}, bf16[8,40,256]{2,1,0:T(8,128)(2,1)S(1)}, u32[]{:S(2)}, u32[]{:S(2)}) collective-permute-start(bf16[8,40,256]{2,1,0:T(8,128)(2,1)S(1)} %slice.137), channel_id=1, source_target_pairs={{0,2},{1,3},{2,0},{3,1},{4,6},{5,7},{6,4},{7,5},{8,10},{9,11},{10,... | collective-permute-start | bytes 491528 | tf_op jit(solution)/shard_map/ppermute | solution.py:48
  61.2 5.3 %collective-permute-start.11 = (bf16[3,51,192]{2,1,0:T(8,128)(2,1)S(1)}, bf16[3,51,192]{2,1,0:T(8,128)(2,1)S(1)}, u32[]{:S(2)}, u32[]{:S(2)}) collective-permute-start(bf16[3,51,192]{2,1,0:T(8,128)(2,1)S(1)} %pad_maximum_fusion.5), channel_id=1, source_target_pairs={{0,1},{1,2},{2,3},{4,5},{5,6},{6,7},{8,9},{9,10},{10,11},{12,13},{... | collective-permute-start | bytes 176264 | tf_op jit(solution)/shard_map/ppermute | solution.py:57
  62.6 4.0 %collective-permute-start.12 = (bf16[3,51,192]{2,1,0:T(8,128)(2,1)S(1)}, bf16[3,51,192]{2,1,0:T(8,128)(2,1)S(1)}, u32[]{:S(2)}, u32[]{:S(2)}) collective-permute-start(bf16[3,51,192]{2,1,0:T(8,128)(2,1)S(1)} %pad_maximum_fusion.6), channel_id=1, source_target_pairs={{1,0},{2,1},{3,2},{5,4},{6,5},{7,6},{9,8},{10,9},{11,10},{13,12},{... | collective-permute-start | bytes 176264 | tf_op jit(solution)/shard_map/ppermute | solution.py:57
  66.0 4.5 %collective-permute-start.15 = (bf16[4,40,256]{2,1,0:T(8,128)(2,1)S(1)}, bf16[4,40,256]{2,1,0:T(8,128)(2,1)S(1)}, u32[]{:S(2)}, u32[]{:S(2)}) collective-permute-start(bf16[4,40,256]{2,1,0:T(8,128)(2,1)S(1)} %slice.138), channel_id=1, source_target_pairs={{0,4},{4,0},{8,12},{12,8},{16,20},{20,16},{24,28},{28,24},{1,5},{5... | collective-permute-start | bytes 245768 | tf_op jit(solution)/shard_map/ppermute | solution.py:48
  70.6 4.1 %collective-permute-start.16 = (bf16[2,40,256]{2,1,0:T(8,128)(2,1)S(1)}, bf16[2,40,256]{2,1,0:T(8,128)(2,1)S(1)}, u32[]{:S(2)}, u32[]{:S(2)}) collective-permute-start(bf16[2,40,256]{2,1,0:T(8,128)(2,1)S(1)} %slice.139), channel_id=1, source_target_pairs={{0,8},{4,12},{8,0},{12,4},{16,24},{20,28},{24,16},{28,20},{1,9},{5... | collective-permute-start | bytes 122888 | tf_op jit(solution)/shard_map/ppermute | solution.py:48
  74.6 6.8 %copy-start.2 = (f32[9568]{0:T(1024)S(1)}, f32[9568]{0:T(1024)}, u32[]{:S(2)}) copy-start(f32[9568]{0:T(1024)} %param.5) | copy-start | bytes 114820
  74.7 6.8 %copy-start.3 = (f32[9568]{0:T(1024)S(1)}, f32[9568]{0:T(1024)}, u32[]{:S(2)}) copy-start(f32[9568]{0:T(1024)} %param.6) | copy-start | bytes 114820
  74.7 6.7 %collective-permute-start.17 = (bf16[1,40,256]{2,1,0:T(8,128)(2,1)S(1)}, bf16[1,40,256]{2,1,0:T(8,128)(2,1)S(1)}, u32[]{:S(2)}, u32[]{:S(2)}) collective-permute-start(bf16[1,40,256]{2,1,0:T(8,128)(2,1)S(1)} %slice.140), channel_id=1, source_target_pairs={{0,16},{4,20},{8,24},{12,28},{16,0},{20,4},{24,8},{28,12},{1,17},{... | collective-permute-start | bytes 61448 | tf_op jit(solution)/shard_map/ppermute | solution.py:48

commit v6 on v5

--- a/solution.py
+++ b/solution.py
@@ -34,27 +34,44 @@
 VMEM = 28 << 20
 
 
-def exchange_bits(axes):
-    steps = []
-    for axis in axes:
-        bit = lax.axis_size(axis) // 2
-        while bit:
-            steps.append((axis, bit))
-            bit //= 2
-    return steps
-
-
-def swap(values, axis, bit):
-    return lax.ppermute(values, axis, [(i, i ^ bit) for i in range(lax.axis_size(axis))])
+def exchange_groups():
+    lon, lat = lax.axis_size("lon"), lax.axis_size("lat")
+    bits = [(lon >> k, 0) for k in range(1, lon.bit_length())]
+    bits += [(0, lat >> k) for k in range(1, lat.bit_length())]
+    groups = []
+    k = 0
+    while k < len(bits):
+        if k + 1 < len(bits) and bits[k][0] == 1 and bits[k + 1][0] == 0:
+            (lon_bit, _), (_, lat_bit) = bits[k : k + 2]
+            groups.append([(lon_bit, 0), (0, lat_bit), (lon_bit, lat_bit)])
+            k += 2
+        else:
+            groups.append([bits[k]])
+            k += 1
+    return groups, len(bits)
+
+
+def swap(values, mask):
+    lon, lat = lax.axis_size("lon"), lax.axis_size("lat")
+    pairs = [
+        (i * lat + j, (i ^ mask[0]) * lat + (j ^ mask[1])) for i in range(lon) for j in range(lat)
+    ]
+    return lax.ppermute(values, ("lon", "lat"), pairs)
 
 
 def shift_both(low_edge, high_edge, axis, periodic):
     count = lax.axis_size(axis)
-    forward = [(i, i + 1) for i in range(count - 1)]
-    if periodic:
-        forward.append((count - 1, 0))
-    backward = [(target, source) for source, target in forward]
-    return lax.ppermute(high_edge, axis, forward), lax.ppermute(low_edge, axis, backward)
+    if count % 2:
+        forward = [(i, (i + 1) % count) for i in range(count if periodic else count - 1)]
+        backward = [(target, source) for source, target in forward]
+        return lax.ppermute(high_edge, axis, forward), lax.ppermute(low_edge, axis, backward)
+    even = lax.axis_index(axis) % 2 == 0
+    near = [(i, i ^ 1) for i in range(count)]
+    odds = [(i, (i + 1) % count) for i in range(1, count if periodic else count - 1, 2)]
+    far = odds + [(target, source) for source, target in odds]
+    near = lax.ppermute(jnp.where(even, high_edge, low_edge), axis, near)
+    far = lax.ppermute(jnp.where(even, low_edge, high_edge), axis, far)
+    return jnp.where(even, far, near), jnp.where(even, near, far)
 
 
 def reversed_bits(number, count):
@@ -120,6 +137,20 @@
             x_ref[t, count - over : count, 0 : cols + 2 * RAD, width] = north[0:over, :, lanes].astype(F32)
 
 
+def edge_kernel(cols, field_hbm, west_ref, east_ref, field_ref):
+    pltpu.sync_copy(field_hbm, field_ref)
+    west_ref[...] = field_ref[:, 0:RAD, :]
+    east_ref[...] = field_ref[:, cols - RAD : cols, :]
+
+
+def wide_kernel(rows, cols, field_ref, west_ref, east_ref, south_ref, north_ref):
+    for out_ref, first in ((south_ref, 0), (north_ref, rows - RAD)):
+        at = slice(first, first + RAD)
+        out_ref[:, 0:RAD, :] = west_ref[at]
+        out_ref[:, RAD : RAD + cols, :] = field_ref[at, 0:cols, :]
+        out_ref[:, RAD + cols : 2 * RAD + cols, :] = east_ref[at]
+
+
 def assemble_kernel(rows, cols, conv_rows, feat_ref, west_ref, east_ref, south_ref, north_ref, up_ref,
                     v_ref, feats_ref, ups_ref, x_ref):
     assemble(x_ref, 0, x_ref.shape[1], feat_ref, west_ref, east_ref, south_ref, north_ref, rows, cols)
@@ -244,8 +275,8 @@
 
 def layer_kernel(order, starts, rows, lon_pad, block_rows, conv_rows,
                  me_ref, gathered_ref, v_ref, feat_ref, up_ref,
-                 out_ref, gconv_ref, gin_ref, gout_ref, sums_ref, flipped_ref,
-                 u_ref, taps_ref, w_ref, win_ref, wout_ref, wo32_ref, conv_ref):
+                 out_hbm, gconv_ref, gin_ref, gout_ref, sums_ref, flipped_ref,
+                 out_ref, out_sem, u_ref, taps_ref, w_ref, win_ref, wout_ref, wo32_ref, conv_ref):
     me = me_ref[0]
     w_ref[...] = jnp.zeros_like(w_ref)
     window = gathered_ref.shape[1]
@@ -365,9 +396,16 @@
         )
         out = jnp.concatenate(outs, axis=1).reshape(block_rows, lon_pad, CP)
         out_ref[pl.ds(row, block_rows)] = out[:, : out_ref.shape[1], :C]
+        out_copy(block).start()
         return carry
 
+    def out_copy(block):
+        at = pl.ds(block * block_rows, block_rows)
+        return pltpu.make_async_copy(out_ref.at[at], out_hbm.at[at], out_sem.at[block])
+
     lax.fori_loop(0, rows // block_rows, body, 0)
+    for block in range(rows // block_rows):
+        out_copy(block).wait()
 
 
 def taps_kernel(order, starts, rows, lon_pad, block_rows, conv_rows,
@@ -424,7 +462,7 @@
 
 def field_kernel(first, count, rows, cols, lon_pad, conv_rows,
                  u_ref, up_ref, main_ref, west_ref, east_ref, south_ref, north_ref, *rest):
-    out_ref, x_ref, v_ref, sum_ref = rest[-4:]
+    out_hbm, x_ref, v_ref, sum_ref, out_ref, out_sem = rest[-6:]
     assemble(x_ref, first, count + KS - 1, main_ref, west_ref, east_ref, south_ref, north_ref, rows, cols)
     write_points(x_ref, v_ref, count // conv_rows, conv_rows)
 
@@ -434,14 +472,25 @@
         def store(tile, lon, chunk, sums):
             lanes = pl.ds(pl.multiple_of(tile * LANES, LANES), LANES)
             for r in range(conv_rows):
-                total = sums[r] + up_ref[row + r, pl.ds(lon, chunk), lanes].astype(F32)
-                sum_ref[row + r, pl.ds(lon, chunk), lanes] = total
+                total = sums[r] + up_ref[first + row + r, pl.ds(lon, chunk), lanes].astype(F32)
+                sum_ref[r, pl.ds(lon, chunk), lanes] = total
 
         depthwise_block(v_ref, u_ref, block, conv_rows, lon_pad, store, True)
+        out_ref[pl.ds(row, conv_rows)] = sum_ref[:, 0:cols, 0:C].astype(BF16)
+        out_copy(block).start()
         return carry
 
+    def out_copy(block):
+        row = block * conv_rows
+        return pltpu.make_async_copy(
+            out_ref.at[pl.ds(row, conv_rows)],
+            out_hbm.at[pl.ds(first + row, conv_rows)],
+            out_sem.at[block],
+        )
+
     lax.fori_loop(0, count // conv_rows, body, 0)
-    out_ref[...] = sum_ref[:, 0 : out_ref.shape[1], 0:C].astype(BF16)
+    for block in range(count // conv_rows):
+        out_copy(block).wait()
 
 
 def shape(dims, kind):
@@ -450,16 +499,6 @@
 
 def whole(count):
     return [pl.BlockSpec(memory_space=pltpu.VMEM)] * count
-
-
-def halos(block, cols):
-    west, east = shift_both(block[:, :RAD, :C], block[:, cols - RAD : cols, :C], "lon", True)
-
-    def wide(rows):
-        return jnp.concatenate([west[rows], block[rows, :cols, :C], east[rows]], axis=1)
-
-    south, north = shift_both(wide(slice(0, RAD)), wide(slice(-RAD, None)), "lat", False)
-    return west, east, south, north
 
 
 def cost(micros):
@@ -474,18 +513,17 @@
     points = conv_rows + KS - 1
     blocks = rows // conv_rows
     block_rows = max(r for r in range(1, 16) if rows % r == 0 and r % conv_rows == 0)
-    axes = ("lon", "lat")
-    steps = exchange_bits(axes)
-    count = 1 << len(steps)
+    groups, bits = exchange_groups()
+    count = 1 << bits
     lat_size = lax.axis_size("lat")
     length = params.shape[0]
     number = lax.axis_index("lon") * lat_size + lax.axis_index("lat")
     place = jnp.int32(0)
-    for k in range(len(steps)):
-        place = place | (((number >> k) & 1) << (len(steps) - 1 - k))
+    for k in range(bits):
+        place = place | (((number >> k) & 1) << (bits - 1 - k))
     place = place.reshape(1).astype(jnp.int32)
     offset = (number * length) % SHARE_LANES
-    order = [reversed_bits(s, len(steps)) for s in range(count)]
+    order = [reversed_bits(s, bits) for s in range(count)]
     starts = [s * length // SHARE_LANES for s in range(count)]
     spill = SHARE_LANES - math.gcd(SHARE_LANES, length)
     window = up(-(-(length + spill) // SHARE_LANES), 8)
@@ -495,13 +533,37 @@
         jnp.zeros((window * SHARE_LANES,), BF16), params.astype(BF16), (offset,)
     )
     gathered = share.reshape(1, window, SHARE_LANES)
-    feature_halos = halos(features, cols)
-    for k, (axis, bit) in enumerate(steps):
-        if k == len(steps) - 2:
+    compiler_params = pltpu.CompilerParams(vmem_limit_bytes=VMEM)
+    edges = pl.pallas_call(
+        lambda *refs: edge_kernel(cols, *refs),
+        out_shape=(shape((rows, RAD, C), BF16),) * 2,
+        in_specs=[pl.BlockSpec(memory_space=pl.ANY)],
+        out_specs=tuple(whole(2)),
+        scratch_shapes=[pltpu.VMEM((rows, cols, C), BF16)],
+        compiler_params=compiler_params,
+        cost_estimate=cost(1),
+        name="edges",
+    )(features)
+    west, east = shift_both(*edges, "lon", True)
+    for k, group in enumerate(groups):
+        parts = [swap(gathered, mask) for mask in group]
+        if k == max(0, len(groups) - 2):
+            west, east, _ = lax.optimization_barrier((west, east, parts[0]))
+            wides = pl.pallas_call(
+                lambda *refs: wide_kernel(rows, cols, *refs),
+                out_shape=(shape((RAD, cols + 2 * RAD, C), BF16),) * 2,
+                in_specs=whole(3),
+                out_specs=tuple(whole(2)),
+                compiler_params=compiler_params,
+                cost_estimate=cost(1),
+                name="wides",
+            )(features, west, east)
+            south, north = shift_both(*wides, "lat", False)
+        gathered = jnp.concatenate([gathered, *parts], axis=0)
+        if k == max(0, len(groups) - 2):
             gathered, upstream = lax.optimization_barrier((gathered, upstream))
-        gathered = jnp.concatenate([gathered, swap(gathered, axis, bit)], axis=0)
-
-    compiler_params = pltpu.CompilerParams(vmem_limit_bytes=VMEM)
+    feature_halos = (west, east, south, north)
+
     smem = [pl.BlockSpec(memory_space=pltpu.SMEM)]
     data, feats, ups = pl.pallas_call(
         lambda *refs: assemble_kernel(rows, cols, conv_rows, *refs),
@@ -530,8 +592,10 @@
             shape((2, points, 8, LANES), F32),
         ),
         in_specs=smem + whole(4),
-        out_specs=tuple(whole(6)),
+        out_specs=(pl.BlockSpec(memory_space=pl.ANY), *whole(5)),
         scratch_shapes=[
+            pltpu.VMEM((rows, cols, C), BF16),
+            pltpu.SemaphoreType.DMA((rows // block_rows,)),
             pltpu.VMEM((2, points, 8, LANES), F32),
             pltpu.VMEM((2, 64, LANES), F32),
             pltpu.VMEM((2, flat_rows, LANES), F32),
@@ -545,7 +609,6 @@
         name="layer",
     )(place, gathered, data, feats, ups)
 
-    grad_halos = halos(gconv, cols)
     values = pl.pallas_call(
         lambda *refs: taps_kernel(*static, *refs),
         out_shape=shape((count, window, SHARE_LANES), BF16),
@@ -562,39 +625,58 @@
         name="taps",
     )(place, gconv, data, gin, gout, sums)
 
+    west, east = shift_both(gconv[:, :RAD, :C], gconv[:, cols - RAD : cols, :C], "lon", True)
     pieces = 3 if rows % (3 * conv_rows) == 0 else 1
     piece_rows = rows // pieces
     field = None
-    for piece in range(pieces):
+
+    def field_piece(piece, south, north, field):
         before = [] if field is None else [field]
         held = [pl.BlockSpec(memory_space=pl.ANY)] * len(before)
-        at = lambda i, piece=piece: (piece, 0, 0)
-        field = pl.pallas_call(
-            lambda *refs, piece=piece: field_kernel(
+        return pl.pallas_call(
+            lambda *refs: field_kernel(
                 piece * piece_rows, piece_rows, rows, cols, lon_pad, conv_rows, *refs
             ),
-            grid=(1,),
             out_shape=shape((rows, cols, C), BF16),
-            in_specs=whole(1)
-            + [pl.BlockSpec((piece_rows, lon_pad, CP), at)]
-            + whole(5)
-            + held,
-            out_specs=pl.BlockSpec((piece_rows, cols, C), at),
+            in_specs=whole(7) + held,
+            out_specs=pl.BlockSpec(memory_space=pl.ANY),
             scratch_shapes=[
                 pltpu.VMEM((2, piece_rows + KS - 1, lon_wide, LANES), F32),
                 pltpu.VMEM((2, piece_rows // conv_rows * points, lon_wide, LANES), F32),
-                pltpu.VMEM((piece_rows, lon_pad, CP), F32),
+                pltpu.VMEM((conv_rows, lon_pad, CP), F32),
+                pltpu.VMEM((piece_rows, cols, C), BF16),
+                pltpu.SemaphoreType.DMA((piece_rows // conv_rows,)),
             ],
             input_output_aliases={7: 0} if before else {},
             compiler_params=compiler_params,
-            cost_estimate=cost(12 / pieces),
+            cost_estimate=cost(10 / pieces),
             name="field",
-        )(flipped, ups, gconv, *grad_halos, *before)
-
-    for axis, bit in steps[::-1]:
-        half = values.shape[0] // 2
-        received = swap(values[half:].astype(BF16), axis, bit)
-        values = values[:half].astype(F32) + received.astype(F32)
+        )(flipped, ups, gconv, west, east, south, north, *before)
+
+    for k, group in enumerate(groups[::-1]):
+        if k == min(1, len(groups) - 1):
+            values, west, east = lax.optimization_barrier((values, west, east))
+        part = values.shape[0] // (len(group) + 1)
+        received = [
+            swap(values[(i + 1) * part : (i + 2) * part].astype(BF16), mask)
+            for i, mask in enumerate(group)
+        ]
+        if k == min(1, len(groups) - 1):
+            def wide(at):
+                return jnp.concatenate([west[at], gconv[at, :cols, :C], east[at]], axis=1)
+
+            wides = (wide(slice(0, RAD)), wide(slice(rows - RAD, rows)))
+            if pieces == 3:
+                field = field_piece(1, *wides, None)
+        if k == min(2, len(groups) - 1):
+            south, north = shift_both(*wides, "lat", False)
+            for piece in ([0, 2] if pieces == 3 else [0]):
+                field = field_piece(piece, south, north, field)
+        values = values[:part].astype(F32)
+        for other in received:
+            values = values + other.astype(F32)
+        if k == 1 and len(groups) > 2:
+            values, wides = lax.optimization_barrier((values, wides))
     summed = lax.dynamic_slice(values.reshape(-1), (offset,), (length,))
     new_params = params - STEP_SIZE * summed + NOISE_COEF * langevin_noise
     return (output, field, new_params)

time: 82.5 us -> 75.4 us (0.914); the launches traced: 82.2 us -> 74 us
  starting transfers between devices: 32.5 us -> 25.7 us
  other arithmetic: 3.16 us -> 2.2 us
  local copies, waits for them, and re-layouts: 2.62 us -> 1.78 us
    ppermute x18 -> x20, starting transfers between devices: 32.5 us -> 25.7 us  [the longest x12 18.5 us: swap(): return lax.ppermute(values, ('lon', 'lat'), pairs)]
    slice x13 -> x6, local copies, waits for them, and re-layouts: 2.2 us -> 0.08 us  [the longest x4 0.05 us: body(): values[(i + 1) * part:(i + 2) * part].astype(BF16)]
    concatenate x9 -> x4, other arithmetic: 1.54 us -> 0.13 us  [the longest x2 0.07 us: wide(): return jnp.concatenate([west[at], gconv[at, :cols, :C], east[at]], axis=1)]
    unnamed x9 -> x15, local copies, waits for them, and re-layouts: 0.05 us -> 1.31 us
    ppermute x18 -> x20, waiting for transfers between devices: 10.8 us -> 11.5 us  [the longest x12 11.4 us: swap(): return lax.ppermute(values, ('lon', 'lat'), pairs)]
    pallas_call x3 -> x5, Pallas kernels: 9.84 us -> 9.93 us  [the longest x3 9.65 us: field_piece(): pl.pallas_call(lambda *refs: field_kernel(piece * piece_rows, piece_rows,...]
  transfers between devices with their start and end apart: 18 -> 20, of which waited for: 9 -> 7; matrix products, arithmetic and copies ran while one was open for 4% -> 1% of each run, Pallas kernels for 21% -> 23%
where the time goes in v6:
time: 75.4 us; the launch traced here: 74 us
  Pallas kernels  31.8 us (42%)
  starting transfers between devices  25.7 us (34%)
  waiting for transfers between devices  11.5 us (15%)
  other arithmetic  2.2 us (3%)
  local copies, waits for them, and re-layouts  1.78 us (2%)
  between operations  1.06 us (1%)
    ppermute x12, starting transfers between devices, swap(): return lax.ppermute(values, ('lon', 'lat'), pairs)  18.5 us
    pallas_call x1, Pallas kernels, body(): pl.pallas_call(lambda *refs: layer_kernel(*static, *refs), out_shape=(sha...  14.9 us
    ppermute x12, waiting for transfers between devices, swap(): return lax.ppermute(values, ('lon', 'lat'), pairs)  11.4 us
    pallas_call x3, Pallas kernels, field_piece(): pl.pallas_call(lambda *refs: field_kernel(piece * piece_rows, piece_rows,...  9.65 us
    pallas_call x1, Pallas kernels, body(): pl.pallas_call(lambda *refs: taps_kernel(*static, *refs), out_shape=shape...  4.06 us
    ppermute x4, starting transfers between devices, shift_both(): near = lax.ppermute(jnp.where(even, high_edge, low_edge), axis, near)  3.69 us
    ppermute x4, starting transfers between devices, shift_both(): far = lax.ppermute(jnp.where(even, low_edge, high_edge), axis, far)  3.58 us
    pallas_call x1, Pallas kernels, body(): pl.pallas_call(lambda *refs: assemble_kernel(rows, cols, conv_rows, *refs...  2.99 us
  transfers between devices with their start and end apart: 20, of which 7 were waited for; matrix products, arithmetic and copies ran while one was open for 1% of the time, Pallas kernels for 23%

profile of v6, /device:TPU:0, one launch (start us, length us, event | category | flops | bytes accessed | tf_op | source)
XLA Modules:
  0.0 74.0 jit_solution(13250919391651537172)
XLA Ops:
  0.7 0.8 %convert_element_type.29 = bf16[9568]{0:T(1024)(128)(2,1)S(1)} convert(f32[9568]{0:T(1024)} %param.5) | non-fusion elementwise | flops 9568 | bytes 57408 | tf_op jit(solution)/shard_map/convert_element_type | solution.py:533
  1.4 0.4 dynamic_update_slice.3
  1.8 4.1 %collective-permute-start = (bf16[1,40,256]{2,1,0:T(8,128)(2,1)S(1)}, bf16[1,40,256]{2,1,0:T(8,128)(2,1)S(1)}, u32[]{:S(2)}, u32[]{:S(2)}) collective-permute-start(bf16[1,40,256]{2,1,0:T(8,128)(2,1)S(1)} %reshape.16), channel_id=1, source_target_pairs={{0,16},{1,17},{2,18},{3,19},{4,20},{5,21},{6,22},{7,23},{8,24},{9,... | collective-permute-start | bytes 61448 | tf_op jit(solution)/shard_map/ppermute | solution.py:59
  5.9 1.2 %copy-done = bf16[45,45,192]{2,1,0:T(8,128)(2,1)S(1)} copy-done((bf16[45,45,192]{2,1,0:T(8,128)(2,1)S(1)}, bf16[45,45,192]{2,1,0:T(8,128)(2,1)}, u32[]{:S(2)}) %copy-start) | copy-done | bytes 777624
  7.2 0.2 edges.1
  7.4 0.0 copy-start.1
  7.4 0.1 broadcast_select_fusion.6
  7.5 1.6 %collective-permute-start.7 = (bf16[45,3,192]{2,1,0:T(4,128)(2,1)S(1)}, bf16[45,3,192]{2,1,0:T(4,128)(2,1)S(1)}, u32[]{:S(2)}, u32[]{:S(2)}) collective-permute-start(bf16[45,3,192]{2,1,0:T(4,128)(2,1)S(1)} %get-tuple-element.60), channel_id=1, source_target_pairs={{0,4},{4,0},{8,12},{12,8},{16,20},{20,16},{24,28},{28,24},{1,5},{5... | collective-permute-start | bytes 155528 | tf_op jit(solution)/shard_map/ppermute | solution.py:72
  9.1 1.3 %collective-permute-start.6 = (bf16[45,3,192]{2,1,0:T(4,128)(2,1)S(1)}, bf16[45,3,192]{2,1,0:T(4,128)(2,1)S(1)}, u32[]{:S(2)}, u32[]{:S(2)}) collective-permute-start(bf16[45,3,192]{2,1,0:T(4,128)(2,1)S(1)} %get-tuple-element.61), channel_id=1, source_target_pairs={{4,8},{12,16},{20,24},{28,0},{8,4},{16,12},{24,20},{0,28},{5,9},{1... | collective-permute-start | bytes 155528 | tf_op jit(solution)/shard_map/ppermute | solution.py:73
  10.4 0.0 collective-permute-done
  10.4 0.7 %collective-permute-start.1 = (bf16[2,40,256]{2,1,0:T(8,128)(2,1)S(1)}, bf16[2,40,256]{2,1,0:T(8,128)(2,1)S(1)}, u32[]{:S(2)}, u32[]{:S(2)}) collective-permute-start(bf16[2,40,256]{2,1,0:T(8,128)(2,1)S(1)} %pad_maximum_fusion.3), channel_id=1, source_target_pairs={{0,8},{1,9},{2,10},{3,11},{4,12},{5,13},{6,14},{7,15},{8,0},{9,1},... | collective-permute-start | bytes 122888 | tf_op jit(solution)/shard_map/ppermute | solution.py:59
  11.2 3.3 %collective-permute-done.1 = bf16[2,40,256]{2,1,0:T(8,128)(2,1)S(1)} collective-permute-done((bf16[2,40,256]{2,1,0:T(8,128)(2,1)S(1)}, bf16[2,40,256]{2,1,0:T(8,128)(2,1)S(1)}, u32[]{:S(2)}, u32[]{:S(2)}) %collective-permute-start.1) | collective-permute-done | bytes 40992 | tf_op jit(solution)/shard_map/ppermute | solution.py:59
  14.5 2.7 %collective-permute-start.2 = (bf16[4,40,256]{2,1,0:T(8,128)(2,1)S(1)}, bf16[4,40,256]{2,1,0:T(8,128)(2,1)S(1)}, u32[]{:S(2)}, u32[]{:S(2)}) collective-permute-start(bf16[4,40,256]{2,1,0:T(8,128)(2,1)S(1)} %get-tuple-element.74), channel_id=1, source_target_pairs={{0,4},{1,5},{2,6},{3,7},{4,0},{5,1},{6,2},{7,3},{8,12},{9,13},{10,... | collective-permute-start | bytes 245768 | tf_op jit(solution)/shard_map/ppermute | solution.py:59
  17.2 0.0 collective-permute-done.7
  17.2 0.0 collective-permute-done.6
  17.2 0.1 broadcast_select_fusion.4
  17.3 1.0 %collective-permute-start.4 = (bf16[4,40,256]{2,1,0:T(8,128)(2,1)S(1)}, bf16[4,40,256]{2,1,0:T(8,128)(2,1)S(1)}, u32[]{:S(2)}, u32[]{:S(2)}) collective-permute-start(bf16[4,40,256]{2,1,0:T(8,128)(2,1)S(1)} %get-tuple-element.74), channel_id=1, source_target_pairs={{0,6},{1,7},{2,4},{3,5},{4,2},{5,3},{6,0},{7,1},{8,14},{9,15},{10,... | collective-permute-start | bytes 245768 | tf_op jit(solution)/shard_map/ppermute | solution.py:59
  18.3 0.6 collective-permute-start.3
  18.9 1.0 %collective-permute-done.2 = bf16[4,40,256]{2,1,0:T(8,128)(2,1)S(1)} collective-permute-done((bf16[4,40,256]{2,1,0:T(8,128)(2,1)S(1)}, bf16[4,40,256]{2,1,0:T(8,128)(2,1)S(1)}, u32[]{:S(2)}, u32[]{:S(2)}) %collective-permute-start.2) | collective-permute-done | bytes 81952 | tf_op jit(solution)/shard_map/ppermute | solution.py:59
  19.9 0.0 copy-done.1
  20.0 0.0 copy-start.2
  20.0 0.1 collective-permute-start.9
  20.1 0.8 %collective-permute-start.8 = (bf16[3,51,192]{2,1,0:T(8,128)(2,1)S(1)}, bf16[3,51,192]{2,1,0:T(8,128)(2,1)S(1)}, u32[]{:S(2)}, u32[]{:S(2)}) collective-permute-start(bf16[3,51,192]{2,1,0:T(8,128)(2,1)S(1)} %get-tuple-element.69), channel_id=1, source_target_pairs={{1,2},{2,1},{5,6},{6,5},{9,10},{10,9},{13,14},{14,13},{17,18},{18,... | collective-permute-start | bytes 176264 | tf_op jit(solution)/shard_map/ppermute | solution.py:73
  20.9 2.7 %collective-permute-done.3 = bf16[4,40,256]{2,1,0:T(8,128)(2,1)S(1)} collective-permute-done((bf16[4,40,256]{2,1,0:T(8,128)(2,1)S(1)}, bf16[4,40,256]{2,1,0:T(8,128)(2,1)S(1)}, u32[]{:S(2)}, u32[]{:S(2)}) %collective-permute-start.3) | collective-permute-done | bytes 81952 | tf_op jit(solution)/shard_map/ppermute | solution.py:59
  23.6 0.0 collective-permute-done.4
  23.6 0.1 collective-permute-start.5
  23.7 0.0 collective-permute-done.9
  23.7 0.0 collective-permute-done.8
  23.7 0.0 copy-done.2
  23.7 3.0 %assemble.1 = (f32[2,99,56,128]{3,2,1,0:T(8,128)S(1)}, bf16[45,48,256]{2,1,0:T(8,128)(2,1)S(1)}, bf16[45,48,256]{2,1,0:T(8,128)(2,1)S(1)}) custom-call(bf16[45,45,192]{2,1,0:T(8,128)(2,1)S(1)} %copy-done.1, bf16[45,3,192]{2,1,0:T(4,128)(2,1)S(1)} %get-tuple-element.29.refs_1_, bf16[45,3,192]{2,1,0:T(4,128)(2,1)S(1)} %get-tuple-element.30.refs_2_, ...), custom_call_target="tpu_custom_call" | custom-call | flops 3300000000 | tf_op jit(solution)/shard_map/assemble/pallas_call | solution.py:568
  26.7 0.0 collective-permute-done.5
  26.7 0.1 pad_maximum_fusion.refs_1_
  26.8 14.9 %layer.1 = (bf16[45,45,192]{2,1,0:T(8,128)(2,1)}, bf16[45,48,256]{2,1,0:T(8,128)(2,1)S(1)}, f32[256,768]{1,0:T(8,128)S(1)}, f32[256,768]{1,0:T(8,128)S(1)}, f32[...) custom-call(s32[1]{0:T(128)} %bitcast.refs_0_, bf16[32,40,256]{2,1,0:T(8,128)(2,1)S(1)} %pad_maximum_fusion.refs_1_, ...), custom_call_target="tpu_custom_call" | custom-call | flops 24199999488 | tf_op jit(solution)/shard_map/layer/pallas_call | solution.py:584
  41.7 0.1 broadcast_select_fusion.2
  41.8 2.0 %collective-permute-start.12 = (bf16[45,3,192]{2,1,0:T(4,128)(2,1)S(1)}, bf16[45,3,192]{2,1,0:T(4,128)(2,1)S(1)}, u32[]{:S(2)}, u32[]{:S(2)}) collective-permute-start(bf16[45,3,192]{2,1,0:T(4,128)(2,1)S(1)} %get-tuple-element.51), channel_id=1, source_target_pairs={{0,4},{4,0},{8,12},{12,8},{16,20},{20,16},{24,28},{28,24},{1,5},{5... | collective-permute-start | bytes 155528 | tf_op jit(solution)/shard_map/ppermute | solution.py:72
  43.8 0.8 %collective-permute-start.11 = (bf16[45,3,192]{2,1,0:T(4,128)(2,1)S(1)}, bf16[45,3,192]{2,1,0:T(4,128)(2,1)S(1)}, u32[]{:S(2)}, u32[]{:S(2)}) collective-permute-start(bf16[45,3,192]{2,1,0:T(4,128)(2,1)S(1)} %get-tuple-element.52), channel_id=1, source_target_pairs={{4,8},{12,16},{20,24},{28,0},{8,4},{16,12},{24,20},{0,28},{5,9},{1... | collective-permute-start | bytes 155528 | tf_op jit(solution)/shard_map/ppermute | solution.py:73
  44.6 4.1 %taps.1 = bf16[32,40,256]{2,1,0:T(8,128)(2,1)S(1)} custom-call(s32[1]{0:T(128)} %bitcast.refs_0_, bf16[45,48,256]{2,1,0:T(8,128)(2,1)S(1)} %get-tuple-element.39.refs_1_.refs_2_, f32[2,99,56,128]{3,2,1,0:T(8,128)S(1)} %get-tuple-element.34.refs_2_, f32[256,768]{1,0:T(8,128)S(1)} %get-tuple-element.40.refs_3_, f32[256,768]{1,0:T(8,128)S(1)} %get-tuple-element.41.refs_4_, ...), custom_call_target="tpu_custom_call" | custom-call | flops 12099999744 | tf_op jit(solution)/shard_map/taps/pallas_call | solution.py:612
  48.7 2.6 %collective-permute-start.10 = (bf16[16,40,256]{2,1,0:T(8,128)(2,1)S(1)}, bf16[16,40,256]{2,1,0:T(8,128)(2,1)S(1)}, u32[]{:S(2)}, u32[]{:S(2)}) collective-permute-start(bf16[16,40,256]{2,1,0:T(8,128)(2,1)S(1)} %slice.78), channel_id=1, source_target_pairs={{0,1},{1,0},{2,3},{3,2},{4,5},{5,4},{6,7},{7,6},{8,9},{9,8},{10,11... | collective-permute-start | bytes 983048 | tf_op jit(solution)/shard_map/ppermute | solution.py:59
  51.3 0.0 collective-permute-done.12
  51.3 0.0 collective-permute-done.11
  51.3 0.1 broadcast_select_fusion
  51.4 1.1 %collective-permute-done.10 = bf16[16,40,256]{2,1,0:T(8,128)(2,1)S(1)} collective-permute-done((bf16[16,40,256]{2,1,0:T(8,128)(2,1)S(1)}, bf16[16,40,256]{2,1,0:T(8,128)(2,1)S(1)}, u32[]{:S(2)}, u32[]{:S(2)}) %collective-permute-start.10) | collective-permute-done | bytes 327712 | tf_op jit(solution)/shard_map/ppermute | solution.py:59
  52.6 0.1 convert_add_fusion
  52.7 0.1 collective-permute-start.13
  52.8 3.6 %collective-permute-start.15 = (bf16[4,40,256]{2,1,0:T(8,128)(2,1)S(1)}, bf16[4,40,256]{2,1,0:T(8,128)(2,1)S(1)}, u32[]{:S(2)}, u32[]{:S(2)}) collective-permute-start(bf16[4,40,256]{2,1,0:T(8,128)(2,1)S(1)} %get-tuple-element.54), channel_id=1, source_target_pairs={{0,6},{1,7},{2,4},{3,5},{4,2},{5,3},{6,0},{7,1},{8,14},{9,15},{10,... | collective-permute-start | bytes 245768 | tf_op jit(solution)/shard_map/ppermute | solution.py:59
  56.4 0.0 collective-permute-start.14
  56.5 3.2 %field.3.refs_7_ = bf16[45,45,192]{2,1,0:T(8,128)(2,1)} custom-call(f32[2,11,8,128]{3,2,1,0:T(8,128)S(1)} %get-tuple-element.38.refs_0_, bf16[45,48,256]{2,1,0:T(8,128)(2,1)S(1)} %get-tuple-element.36.refs_4_.refs_1_, bf16[45,48,256]{2,1,0:T(8,128)(2,1)S(1)} %get-tuple-element.39.refs_1_.refs_2_, bf16[45,3,192]{2,1,0:T(4,128)(2,1)S(1)} %get-tuple-element.43.refs_3_, ...), custom_call_target="tpu_custom_call" | custom-call | flops 3666666752 | tf_op jit(solution)/shard_map/field/pallas_call | solution.py:636
  59.8 0.0 collective-permute-done.13
  59.8 0.1 collective-permute-done.15
  59.9 1.0 %collective-permute-done.14 = bf16[4,40,256]{2,1,0:T(8,128)(2,1)S(1)} collective-permute-done((bf16[4,40,256]{2,1,0:T(8,128)(2,1)S(1)}, bf16[4,40,256]{2,1,0:T(8,128)(2,1)S(1)}, u32[]{:S(2)}, u32[]{:S(2)}) %collective-permute-start.14) | collective-permute-done | bytes 81952 | tf_op jit(solution)/shard_map/ppermute | solution.py:59
  60.9 1.0 %collective-permute-start.18 = (bf16[2,40,256]{2,1,0:T(8,128)(2,1)S(1)}, bf16[2,40,256]{2,1,0:T(8,128)(2,1)S(1)}, u32[]{:S(2)}, u32[]{:S(2)}) collective-permute-start(bf16[2,40,256]{2,1,0:T(8,128)(2,1)S(1)} %slice.97), channel_id=1, source_target_pairs={{0,8},{1,9},{2,10},{3,11},{4,12},{5,13},{6,14},{7,15},{8,0},{9,1},... | collective-permute-start | bytes 122888 | tf_op jit(solution)/shard_map/ppermute | solution.py:59
  62.0 0.1 collective-permute-start.17
  62.0 0.7 collective-permute-start.16
  62.7 2.3 %collective-permute-done.18 = bf16[2,40,256]{2,1,0:T(8,128)(2,1)S(1)} collective-permute-done((bf16[2,40,256]{2,1,0:T(8,128)(2,1)S(1)}, bf16[2,40,256]{2,1,0:T(8,128)(2,1)S(1)}, u32[]{:S(2)}, u32[]{:S(2)}) %collective-permute-start.18) | collective-permute-done | bytes 40992 | tf_op jit(solution)/shard_map/ppermute | solution.py:59
  65.0 1.8 %collective-permute-start.19 = (bf16[1,40,256]{2,1,0:T(8,128)(2,1)S(1)}, bf16[1,40,256]{2,1,0:T(8,128)(2,1)S(1)}, u32[]{:S(2)}, u32[]{:S(2)}) collective-permute-start(bf16[1,40,256]{2,1,0:T(8,128)(2,1)S(1)} %slice.98), channel_id=1, source_target_pairs={{0,16},{1,17},{2,18},{3,19},{4,20},{5,21},{6,22},{7,23},{8,24},{9,... | collective-permute-start | bytes 61448 | tf_op jit(solution)/shard_map/ppermute | solution.py:59
  66.8 0.0 collective-permute-done.17
  66.8 0.0 collective-permute-done.16
  66.8 3.2 %field.4.refs_7_ = bf16[45,45,192]{2,1,0:T(8,128)(2,1)} custom-call(f32[2,11,8,128]{3,2,1,0:T(8,128)S(1)} %get-tuple-element.38.refs_0_, bf16[45,48,256]{2,1,0:T(8,128)(2,1)S(1)} %get-tuple-element.36.refs_4_.refs_1_, bf16[45,48,256]{2,1,0:T(8,128)(2,1)S(1)} %get-tuple-element.39.refs_1_.refs_2_, ...), custom_call_target="tpu_custom_call", output_to_operand_aliasing={{}: (7, {})} | custom-call | flops 3666666752 | tf_op jit(solution)/shard_map/field/pallas_call | solution.py:636
  70.0 0.0 copy-start.3
  70.0 0.0 copy-start.4
  70.0 3.2 %field.5 = bf16[45,45,192]{2,1,0:T(8,128)(2,1)} custom-call(f32[2,11,8,128]{3,2,1,0:T(8,128)S(1)} %get-tuple-element.38.refs_0_, bf16[45,48,256]{2,1,0:T(8,128)(2,1)S(1)} %get-tuple-element.36.refs_4_.refs_1_, bf16[45,48,256]{2,1,0:T(8,128)(2,1)S(1)} %get-tuple-element.39.refs_1_.refs_2_, ...), custom_call_target="tpu_custom_call", output_to_operand_aliasing={{}: (7, {})} | custom-call | flops 3666666752 | tf_op jit(solution)/shard_map/field/pallas_call | solution.py:636
  73.3 0.0 collective-permute-done.19
  73.3 0.0 copy-done.3
  73.3 0.7 multiply_add_fusion
  (29 shorter events, 0.4 us)
Async XLA Ops:
  1.8 8.6 %collective-permute-start = (bf16[1,40,256]{2,1,0:T(8,128)(2,1)S(1)}, bf16[1,40,256]{2,1,0:T(8,128)(2,1)S(1)}, u32[]{:S(2)}, u32[]{:S(2)}) collective-permute-start(bf16[1,40,256]{2,1,0:T(8,128)(2,1)S(1)} %reshape.16), channel_id=1, source_target_pairs={{0,16},{1,17},{2,18},{3,19},{4,20},{5,21},{6,22},{7,23},{8,24},{9,... | collective-permute-start | bytes 61448 | tf_op jit(solution)/shard_map/ppermute | solution.py:59
  5.9 1.2 %copy-start = (bf16[45,45,192]{2,1,0:T(8,128)(2,1)S(1)}, bf16[45,45,192]{2,1,0:T(8,128)(2,1)}, u32[]{:S(2)}) copy-start(bf16[45,45,192]{2,1,0:T(8,128)(2,1)} %refs_0_.5) | copy-start | bytes 2332804
  7.4 12.5 %copy-start.1 = (bf16[45,45,192]{2,1,0:T(8,128)(2,1)S(1)}, bf16[45,45,192]{2,1,0:T(8,128)(2,1)}, u32[]{:S(2)}) copy-start(bf16[45,45,192]{2,1,0:T(8,128)(2,1)} %refs_0_.5) | copy-start | bytes 2332804
  7.5 9.7 %collective-permute-start.7 = (bf16[45,3,192]{2,1,0:T(4,128)(2,1)S(1)}, bf16[45,3,192]{2,1,0:T(4,128)(2,1)S(1)}, u32[]{:S(2)}, u32[]{:S(2)}) collective-permute-start(bf16[45,3,192]{2,1,0:T(4,128)(2,1)S(1)} %get-tuple-element.60), channel_id=1, source_target_pairs={{0,4},{4,0},{8,12},{12,8},{16,20},{20,16},{24,28},{28,24},{1,5},{5... | collective-permute-start | bytes 155528 | tf_op jit(solution)/shard_map/ppermute | solution.py:72
  9.1 8.1 %collective-permute-start.6 = (bf16[45,3,192]{2,1,0:T(4,128)(2,1)S(1)}, bf16[45,3,192]{2,1,0:T(4,128)(2,1)S(1)}, u32[]{:S(2)}, u32[]{:S(2)}) collective-permute-start(bf16[45,3,192]{2,1,0:T(4,128)(2,1)S(1)} %get-tuple-element.61), channel_id=1, source_target_pairs={{4,8},{12,16},{20,24},{28,0},{8,4},{16,12},{24,20},{0,28},{5,9},{1... | collective-permute-start | bytes 155528 | tf_op jit(solution)/shard_map/ppermute | solution.py:73
  10.4 4.1 %collective-permute-start.1 = (bf16[2,40,256]{2,1,0:T(8,128)(2,1)S(1)}, bf16[2,40,256]{2,1,0:T(8,128)(2,1)S(1)}, u32[]{:S(2)}, u32[]{:S(2)}) collective-permute-start(bf16[2,40,256]{2,1,0:T(8,128)(2,1)S(1)} %pad_maximum_fusion.3), channel_id=1, source_target_pairs={{0,8},{1,9},{2,10},{3,11},{4,12},{5,13},{6,14},{7,15},{8,0},{9,1},... | collective-permute-start | bytes 122888 | tf_op jit(solution)/shard_map/ppermute | solution.py:59
  14.5 5.4 %collective-permute-start.2 = (bf16[4,40,256]{2,1,0:T(8,128)(2,1)S(1)}, bf16[4,40,256]{2,1,0:T(8,128)(2,1)S(1)}, u32[]{:S(2)}, u32[]{:S(2)}) collective-permute-start(bf16[4,40,256]{2,1,0:T(8,128)(2,1)S(1)} %get-tuple-element.74), channel_id=1, source_target_pairs={{0,4},{1,5},{2,6},{3,7},{4,0},{5,1},{6,2},{7,3},{8,12},{9,13},{10,... | collective-permute-start | bytes 245768 | tf_op jit(solution)/shard_map/ppermute | solution.py:59
  17.3 6.3 %collective-permute-start.4 = (bf16[4,40,256]{2,1,0:T(8,128)(2,1)S(1)}, bf16[4,40,256]{2,1,0:T(8,128)(2,1)S(1)}, u32[]{:S(2)}, u32[]{:S(2)}) collective-permute-start(bf16[4,40,256]{2,1,0:T(8,128)(2,1)S(1)} %get-tuple-element.74), channel_id=1, source_target_pairs={{0,6},{1,7},{2,4},{3,5},{4,2},{5,3},{6,0},{7,1},{8,14},{9,15},{10,... | collective-permute-start | bytes 245768 | tf_op jit(solution)/shard_map/ppermute | solution.py:59
  18.3 5.2 %collective-permute-start.3 = (bf16[4,40,256]{2,1,0:T(8,128)(2,1)S(1)}, bf16[4,40,256]{2,1,0:T(8,128)(2,1)S(1)}, u32[]{:S(2)}, u32[]{:S(2)}) collective-permute-start(bf16[4,40,256]{2,1,0:T(8,128)(2,1)S(1)} %get-tuple-element.74), channel_id=1, source_target_pairs={{0,2},{1,3},{2,0},{3,1},{4,6},{5,7},{6,4},{7,5},{8,10},{9,11},{10,... | collective-permute-start | bytes 245768 | tf_op jit(solution)/shard_map/ppermute | solution.py:59
  20.0 3.8 %copy-start.2 = (bf16[45,45,192]{2,1,0:T(8,128)(2,1)S(1)}, bf16[45,45,192]{2,1,0:T(8,128)(2,1)}, u32[]{:S(2)}) copy-start(bf16[45,45,192]{2,1,0:T(8,128)(2,1)} %refs_5_) | copy-start | bytes 2332804
  20.0 3.7 %collective-permute-start.9 = (bf16[3,51,192]{2,1,0:T(8,128)(2,1)S(1)}, bf16[3,51,192]{2,1,0:T(8,128)(2,1)S(1)}, u32[]{:S(2)}, u32[]{:S(2)}) collective-permute-start(bf16[3,51,192]{2,1,0:T(8,128)(2,1)S(1)} %get-tuple-element.68), channel_id=1, source_target_pairs={{0,1},{1,0},{2,3},{3,2},{4,5},{5,4},{6,7},{7,6},{8,9},{9,8},{10,11... | collective-permute-start | bytes 176264 | tf_op jit(solution)/shard_map/ppermute | solution.py:72
  20.1 3.6 %collective-permute-start.8 = (bf16[3,51,192]{2,1,0:T(8,128)(2,1)S(1)}, bf16[3,51,192]{2,1,0:T(8,128)(2,1)S(1)}, u32[]{:S(2)}, u32[]{:S(2)}) collective-permute-start(bf16[3,51,192]{2,1,0:T(8,128)(2,1)S(1)} %get-tuple-element.69), channel_id=1, source_target_pairs={{1,2},{2,1},{5,6},{6,5},{9,10},{10,9},{13,14},{14,13},{17,18},{18,... | collective-permute-start | bytes 176264 | tf_op jit(solution)/shard_map/ppermute | solution.py:73
  23.6 3.1 %collective-permute-start.5 = (bf16[16,40,256]{2,1,0:T(8,128)(2,1)S(1)}, bf16[16,40,256]{2,1,0:T(8,128)(2,1)S(1)}, u32[]{:S(2)}, u32[]{:S(2)}) collective-permute-start(bf16[16,40,256]{2,1,0:T(8,128)(2,1)S(1)} %constant_dynamic-update-slice_fusion.3), channel_id=1, source_target_pairs={{0,1},{1,0},{2,3},{3,2},{4,5},{5,4},{6,7},{7,6},{8,9},{9,8},{10,11... | collective-permute-start | bytes 983048 | tf_op jit(solution)/shard_map/ppermute | solution.py:59
  41.8 9.5 %collective-permute-start.12 = (bf16[45,3,192]{2,1,0:T(4,128)(2,1)S(1)}, bf16[45,3,192]{2,1,0:T(4,128)(2,1)S(1)}, u32[]{:S(2)}, u32[]{:S(2)}) collective-permute-start(bf16[45,3,192]{2,1,0:T(4,128)(2,1)S(1)} %get-tuple-element.51), channel_id=1, source_target_pairs={{0,4},{4,0},{8,12},{12,8},{16,20},{20,16},{24,28},{28,24},{1,5},{5... | collective-permute-start | bytes 155528 | tf_op jit(solution)/shard_map/ppermute | solution.py:72
  43.8 7.6 %collective-permute-start.11 = (bf16[45,3,192]{2,1,0:T(4,128)(2,1)S(1)}, bf16[45,3,192]{2,1,0:T(4,128)(2,1)S(1)}, u32[]{:S(2)}, u32[]{:S(2)}) collective-permute-start(bf16[45,3,192]{2,1,0:T(4,128)(2,1)S(1)} %get-tuple-element.52), channel_id=1, source_target_pairs={{4,8},{12,16},{20,24},{28,0},{8,4},{16,12},{24,20},{0,28},{5,9},{1... | collective-permute-start | bytes 155528 | tf_op jit(solution)/shard_map/ppermute | solution.py:73
  48.7 3.9 %collective-permute-start.10 = (bf16[16,40,256]{2,1,0:T(8,128)(2,1)S(1)}, bf16[16,40,256]{2,1,0:T(8,128)(2,1)S(1)}, u32[]{:S(2)}, u32[]{:S(2)}) collective-permute-start(bf16[16,40,256]{2,1,0:T(8,128)(2,1)S(1)} %slice.78), channel_id=1, source_target_pairs={{0,1},{1,0},{2,3},{3,2},{4,5},{5,4},{6,7},{7,6},{8,9},{9,8},{10,11... | collective-permute-start | bytes 983048 | tf_op jit(solution)/shard_map/ppermute | solution.py:59
  52.7 7.1 %collective-permute-start.13 = (bf16[4,40,256]{2,1,0:T(8,128)(2,1)S(1)}, bf16[4,40,256]{2,1,0:T(8,128)(2,1)S(1)}, u32[]{:S(2)}, u32[]{:S(2)}) collective-permute-start(bf16[4,40,256]{2,1,0:T(8,128)(2,1)S(1)} %get-tuple-element.53), channel_id=1, source_target_pairs={{0,4},{1,5},{2,6},{3,7},{4,0},{5,1},{6,2},{7,3},{8,12},{9,13},{10,... | collective-permute-start | bytes 245768 | tf_op jit(solution)/shard_map/ppermute | solution.py:59
  52.8 7.1 %collective-permute-start.15 = (bf16[4,40,256]{2,1,0:T(8,128)(2,1)S(1)}, bf16[4,40,256]{2,1,0:T(8,128)(2,1)S(1)}, u32[]{:S(2)}, u32[]{:S(2)}) collective-permute-start(bf16[4,40,256]{2,1,0:T(8,128)(2,1)S(1)} %get-tuple-element.54), channel_id=1, source_target_pairs={{0,6},{1,7},{2,4},{3,5},{4,2},{5,3},{6,0},{7,1},{8,14},{9,15},{10,... | collective-permute-start | bytes 245768 | tf_op jit(solution)/shard_map/ppermute | solution.py:59
  56.4 4.4 %collective-permute-start.14 = (bf16[4,40,256]{2,1,0:T(8,128)(2,1)S(1)}, bf16[4,40,256]{2,1,0:T(8,128)(2,1)S(1)}, u32[]{:S(2)}, u32[]{:S(2)}) collective-permute-start(bf16[4,40,256]{2,1,0:T(8,128)(2,1)S(1)} %get-tuple-element.55), channel_id=1, source_target_pairs={{0,2},{1,3},{2,0},{3,1},{4,6},{5,7},{6,4},{7,5},{8,10},{9,11},{10,... | collective-permute-start | bytes 245768 | tf_op jit(solution)/shard_map/ppermute | solution.py:59
  60.9 4.1 %collective-permute-start.18 = (bf16[2,40,256]{2,1,0:T(8,128)(2,1)S(1)}, bf16[2,40,256]{2,1,0:T(8,128)(2,1)S(1)}, u32[]{:S(2)}, u32[]{:S(2)}) collective-permute-start(bf16[2,40,256]{2,1,0:T(8,128)(2,1)S(1)} %slice.97), channel_id=1, source_target_pairs={{0,8},{1,9},{2,10},{3,11},{4,12},{5,13},{6,14},{7,15},{8,0},{9,1},... | collective-permute-start | bytes 122888 | tf_op jit(solution)/shard_map/ppermute | solution.py:59
  62.0 4.8 %collective-permute-start.17 = (bf16[3,51,192]{2,1,0:T(8,128)(2,1)S(1)}, bf16[3,51,192]{2,1,0:T(8,128)(2,1)S(1)}, u32[]{:S(2)}, u32[]{:S(2)}) collective-permute-start(bf16[3,51,192]{2,1,0:T(8,128)(2,1)S(1)} %get-tuple-element.64), channel_id=1, source_target_pairs={{0,1},{1,0},{2,3},{3,2},{4,5},{5,4},{6,7},{7,6},{8,9},{9,8},{10,11... | collective-permute-start | bytes 176264 | tf_op jit(solution)/shard_map/ppermute | solution.py:72
  62.0 4.7 %collective-permute-start.16 = (bf16[3,51,192]{2,1,0:T(8,128)(2,1)S(1)}, bf16[3,51,192]{2,1,0:T(8,128)(2,1)S(1)}, u32[]{:S(2)}, u32[]{:S(2)}) collective-permute-start(bf16[3,51,192]{2,1,0:T(8,128)(2,1)S(1)} %get-tuple-element.65), channel_id=1, source_target_pairs={{1,2},{2,1},{5,6},{6,5},{9,10},{10,9},{13,14},{14,13},{17,18},{18,... | collective-permute-start | bytes 176264 | tf_op jit(solution)/shard_map/ppermute | solution.py:73
  65.0 8.3 %collective-permute-start.19 = (bf16[1,40,256]{2,1,0:T(8,128)(2,1)S(1)}, bf16[1,40,256]{2,1,0:T(8,128)(2,1)S(1)}, u32[]{:S(2)}, u32[]{:S(2)}) collective-permute-start(bf16[1,40,256]{2,1,0:T(8,128)(2,1)S(1)} %slice.98), channel_id=1, source_target_pairs={{0,16},{1,17},{2,18},{3,19},{4,20},{5,21},{6,22},{7,23},{8,24},{9,... | collective-permute-start | bytes 61448 | tf_op jit(solution)/shard_map/ppermute | solution.py:59
  70.0 3.3 %copy-start.3 = (f32[9568]{0:T(1024)S(1)}, f32[9568]{0:T(1024)}, u32[]{:S(2)}) copy-start(f32[9568]{0:T(1024)} %param.5) | copy-start | bytes 114820
  70.0 3.3 %copy-start.4 = (f32[9568]{0:T(1024)S(1)}, f32[9568]{0:T(1024)}, u32[]{:S(2)}) copy-start(f32[9568]{0:T(1024)} %param.6) | copy-start | bytes 114820

commit v7 on v6

--- a/solution.py
+++ b/solution.py
@@ -29,6 +29,7 @@
 ROWS = ROW_LAST + 1
 TILES = H // LANES
 SHARE_LANES = 256
+CHUNK = 256
 ALL = ((1,), (1,)), ((), ())
 OVER = ((0,), (0,)), ((), ())
 VMEM = 28 << 20
@@ -119,22 +120,57 @@
         flat_ref[j % 2, pl.ds(3 * row + j // 2, tiles[j].shape[0], stride=3), :] = tiles[j]
 
 
-def assemble(x_ref, first, count, main, west, east, south, north, rows, cols):
-    x_ref[...] = jnp.zeros_like(x_ref)
+def assemble(x_ref, base, first, count, main, west, east, south, north, rows, cols):
     for t in range(2):
         lanes = slice(t * LANES, min(C, (t + 1) * LANES))
         width = slice(0, lanes.stop - lanes.start)
         low = max(0, first - RAD)
         high = min(rows, first + count - RAD)
-        at = slice(low + RAD - first, high + RAD - first)
+        at = slice(base + low + RAD - first, base + high + RAD - first)
         x_ref[t, at, 0:RAD, width] = west[low:high, :, lanes].astype(F32)
         x_ref[t, at, RAD : RAD + cols, width] = main[low:high, 0:cols, lanes].astype(F32)
         x_ref[t, at, RAD + cols : 2 * RAD + cols, width] = east[low:high, :, lanes].astype(F32)
+        wide = slice(0, cols + 2 * RAD)
         if first < RAD:
-            x_ref[t, 0 : RAD - first, 0 : cols + 2 * RAD, width] = south[first:, :, lanes].astype(F32)
+            at = slice(base, base + RAD - first)
+            x_ref[t, at, wide, width] = south[first:, :, lanes].astype(F32)
         over = first + count - rows - RAD
         if over > 0:
-            x_ref[t, count - over : count, 0 : cols + 2 * RAD, width] = north[0:over, :, lanes].astype(F32)
+            at = slice(base + count - over, base + count)
+            x_ref[t, at, wide, width] = north[0:over, :, lanes].astype(F32)
+
+
+def field_points(ranges, conv_rows, x_ref, v_ref, main, west, east, south, north, rows, cols):
+    x_ref[...] = jnp.zeros_like(x_ref)
+    base = done = 0
+    for first, count in ranges:
+        span = count * conv_rows + KS - 1
+        assemble(
+            x_ref, base, first * conv_rows, span, main, west, east, south, north, rows, cols
+        )
+        write_points(x_ref, base, v_ref, done, count, conv_rows)
+        base += span
+        done += count
+
+
+def padded_rows(ranges, conv_rows):
+    return sum(count * conv_rows + KS - 1 for _, count in ranges)
+
+
+def block_count(ranges):
+    return sum(count for _, count in ranges)
+
+
+def over_blocks(ranges, step):
+    done = 0
+    for first, count in ranges:
+
+        def body(i, carry, done=done, first=first):
+            step(done + i, first + i)
+            return carry
+
+        lax.fori_loop(0, count, body, 0)
+        done += count
 
 
 def edge_kernel(cols, field_hbm, west_ref, east_ref, field_ref):
@@ -151,14 +187,23 @@
         out_ref[:, RAD + cols : 2 * RAD + cols, :] = east_ref[at]
 
 
-def assemble_kernel(rows, cols, conv_rows, feat_ref, west_ref, east_ref, south_ref, north_ref, up_ref,
-                    v_ref, feats_ref, ups_ref, x_ref):
-    assemble(x_ref, 0, x_ref.shape[1], feat_ref, west_ref, east_ref, south_ref, north_ref, rows, cols)
-    write_points(x_ref, v_ref, rows // conv_rows, conv_rows)
+def inner_kernel(ranges, rows, cols, conv_rows, feat_ref, west_ref, east_ref, up_ref,
+                 v_ref, feats_ref, ups_ref, x_ref):
+    field_points(
+        ranges, conv_rows, x_ref, v_ref, feat_ref, west_ref, east_ref, None, None, rows, cols
+    )
     feats_ref[...] = jnp.zeros_like(feats_ref)
     feats_ref[:, 0:cols, 0:C] = feat_ref[...]
     ups_ref[...] = jnp.zeros_like(ups_ref)
     ups_ref[:, 0:cols, 0:C] = up_ref[...]
+
+
+def outer_kernel(ranges, rows, cols, conv_rows, feat_ref, west_ref, east_ref, south_ref, north_ref,
+                 v_ref, x_ref):
+    field_points(
+        ranges, conv_rows, x_ref, v_ref, feat_ref, west_ref, east_ref, south_ref, north_ref, rows,
+        cols,
+    )
 
 
 def points_for(out_rows):
@@ -211,7 +256,7 @@
     return values
 
 
-def write_points(x_ref, v_ref, blocks, out_rows):
+def write_points(x_ref, base, v_ref, done, blocks, out_rows):
     pairs, filters = points_for(out_rows)
     count = len(filters)
     lon_regs = x_ref.shape[2] // 8
@@ -221,12 +266,12 @@
         lon = pl.ds(pl.multiple_of(step % lon_regs * 8, 8), 8)
 
         def block(k, carry):
-            rows = [x_ref[tile, k * out_rows + r, lon, :] for r in range(count)]
+            rows = [x_ref[tile, base + k * out_rows + r, lon, :] for r in range(count)]
             for i, value in enumerate(data_points(pairs, rows)):
-                v_ref[tile, k * count + i, lon, :] = value
+                v_ref[tile, (done + k) * count + i, lon, :] = value
             return carry
 
-        return lax.fori_loop(0, blocks, block, carry, unroll=3 if blocks % 3 == 0 else 1)
+        return lax.fori_loop(0, blocks, block, carry, unroll=blocks <= 4)
 
     lax.fori_loop(0, 2 * lon_regs, body, 0)
 
@@ -243,7 +288,7 @@
 def depthwise_block(v_ref, u_ref, block, out_rows, lon_pad, store, flip):
     pairs, filters = points_for(out_rows)
     count = len(filters)
-    chunk = lon_pad // 2 if lon_pad % 16 == 0 else lon_pad
+    chunk = lon_pad
 
     def body(step, carry):
         tile = step // (lon_pad // chunk)
@@ -273,10 +318,10 @@
     lax.fori_loop(0, 2 * (lon_pad // chunk), body, 0)
 
 
-def layer_kernel(order, starts, rows, lon_pad, block_rows, conv_rows,
-                 me_ref, gathered_ref, v_ref, feat_ref, up_ref,
-                 out_hbm, gconv_ref, gin_ref, gout_ref, sums_ref, flipped_ref,
-                 out_ref, out_sem, u_ref, taps_ref, w_ref, win_ref, wout_ref, wo32_ref, conv_ref):
+def layer_kernel(order, starts, rows, lon_pad, block_rows, conv_rows, inner, outer,
+                 me_ref, gathered_ref, inner_ref, outer_ref, feat_ref, up_ref,
+                 out_ref, gconv_ref, gin_ref, gout_ref, sums_ref, flipped_ref,
+                 u_ref, taps_ref, w_ref, win_ref, wout_ref, wo32_ref, conv_ref, act_ref, gpre_ref):
     me = me_ref[0]
     w_ref[...] = jnp.zeros_like(w_ref)
     window = gathered_ref.shape[1]
@@ -323,22 +368,22 @@
     def partial(values):
         return values.reshape(cells // 8, 8, LANES).sum(axis=0)
 
+    for v_ref, ranges in ((inner_ref, inner), (outer_ref, outer)):
+
+        def conv_step(place, block, v_ref=v_ref):
+            def store(tile, lon, chunk, sums):
+                for r in range(conv_rows):
+                    conv_ref[tile, block * conv_rows + r, pl.ds(lon, chunk), :] = sums[r]
+
+            depthwise_block(v_ref, u_ref, place, conv_rows, lon_pad, store, False)
+
+        over_blocks(ranges, conv_step)
+
     def body(block, carry):
         row = block * block_rows
-
-        def conv_step(part, carry):
-            at = part * conv_rows
-
-            def store(tile, lon, chunk, sums):
-                for r in range(conv_rows):
-                    conv_ref[tile, at + r, pl.ds(lon, chunk), :] = sums[r]
-
-            at_block = block * (block_rows // conv_rows) + part
-            depthwise_block(v_ref, u_ref, at_block, conv_rows, lon_pad, store, False)
-            return carry
-
-        lax.fori_loop(0, block_rows // conv_rows, conv_step, 0)
-        conv = [conv_ref[t].reshape(cells, LANES) + cbias[t] for t in range(2)]
+        conv = [
+            conv_ref[t, pl.ds(row, block_rows)].reshape(cells, LANES) + cbias[t] for t in range(2)
+        ]
         mean = jnp.sum(conv[0] + conv[1], axis=1, keepdims=True) * (1.0 / C)
         centred = [conv[0] - mean, (conv[1] - mean) * inside]
         square = centred[0] * centred[0] + centred[1] * centred[1]
@@ -351,24 +396,22 @@
         ups = [upstream[:, t * LANES : (t + 1) * LANES].astype(F32) for t in range(2)]
         grad_branch = [(scale[t] * ups[t]).astype(BF16) for t in range(2)]
         gbranch = jnp.concatenate(grad_branch, axis=1)
-        branch = None
-        gnormed = None
-        for h in range(0, H, CP):
-            hidden = slice(h, h + CP)
+        for h in range(0, H, CHUNK):
+            hidden = slice(h, h + CHUNK)
             pre = jnp.dot(normed, win_ref[:, hidden], preferred_element_type=F32)
             gact = lax.dot_general(gbranch, wout_ref[hidden, :], ALL, preferred_element_type=F32)
             square = pre * pre
             half = 0.5 + 0.5 * jnp.tanh(pre * (GELU_A + GELU_B * square))
             act = pre * half
             slope = half + act * (1.0 - half) * (2.0 * GELU_A + 6.0 * GELU_B * square)
-            act = act.astype(BF16)
-            gpre = (gact * slope).astype(BF16)
-            part = jnp.dot(act, wout_ref[hidden, :], preferred_element_type=F32)
-            branch = part if branch is None else branch + part
-            part = lax.dot_general(gpre, win_ref[:, hidden], ALL, preferred_element_type=F32)
-            gnormed = part if gnormed is None else gnormed + part
-            gin_ref[:, hidden] += lax.dot_general(normed, gpre, OVER, preferred_element_type=F32)
-            gout_ref[:, hidden] += lax.dot_general(gbranch, act, OVER, preferred_element_type=F32)
+            act_ref[:, hidden] = act.astype(BF16)
+            gpre_ref[:, hidden] = (gact * slope).astype(BF16)
+        act = act_ref[...]
+        gpre = gpre_ref[...]
+        branch = jnp.dot(act, wout_ref[...], preferred_element_type=F32)
+        gnormed = lax.dot_general(gpre, win_ref[...], ALL, preferred_element_type=F32)
+        gin_ref[...] += lax.dot_general(normed, gpre, OVER, preferred_element_type=F32)
+        gout_ref[...] += lax.dot_general(gbranch, act, OVER, preferred_element_type=F32)
         outs = []
         gs = []
         gn = []
@@ -396,40 +439,42 @@
         )
         out = jnp.concatenate(outs, axis=1).reshape(block_rows, lon_pad, CP)
         out_ref[pl.ds(row, block_rows)] = out[:, : out_ref.shape[1], :C]
-        out_copy(block).start()
         return carry
 
-    def out_copy(block):
-        at = pl.ds(block * block_rows, block_rows)
-        return pltpu.make_async_copy(out_ref.at[at], out_hbm.at[at], out_sem.at[block])
-
     lax.fori_loop(0, rows // block_rows, body, 0)
-    for block in range(rows // block_rows):
-        out_copy(block).wait()
-
-
-def taps_kernel(order, starts, rows, lon_pad, block_rows, conv_rows,
-                me_ref, gconv_ref, v_ref, gin_ref, gout_ref, sums_ref,
-                g_ref, rows_ref, acc_ref, wo32_ref, small_ref):
+
+
+def taps_kernel(order, starts, rows, lon_pad, block_rows, conv_rows, inner, outer,
+                me_ref, gconv_ref, inner_ref, outer_ref, gin_ref, gout_ref, sums_ref, done_ref,
+                g_ref, done_hbm, rows_ref, acc_ref, wo32_ref, small_ref, done_sem):
+    done_copy = pltpu.make_async_copy(done_ref, done_hbm, done_sem)
+    done_copy.start()
     acc_ref[...] = jnp.zeros_like(acc_ref)
     pairs, filters = points_for(conv_rows)
     count = len(filters)
 
-    def body(step, carry):
-        tile = step % 2
-        block = step // 2
-        lanes = pl.ds(pl.multiple_of(tile * LANES, LANES), LANES)
-        grads = grad_points(
-            pairs,
-            [gconv_ref[block * conv_rows + r, :, lanes].astype(F32) for r in range(conv_rows)],
-        )
-        for k in range(count):
-            for b in range(KS):
-                term = grads[k] * v_ref[tile, block * count + k, pl.ds(b, lon_pad), :]
-                acc_ref[tile, k, b] += term.reshape(lon_pad // 8, 8, LANES).sum(axis=0)
-        return carry
-
-    lax.fori_loop(0, 2 * (rows // conv_rows), body, 0)
+    for v_ref, ranges in ((inner_ref, inner), (outer_ref, outer)):
+
+        def step(place, block, v_ref=v_ref):
+            def side(tile, carry):
+                lanes = pl.ds(pl.multiple_of(tile * LANES, LANES), LANES)
+                grads = grad_points(
+                    pairs,
+                    [
+                        gconv_ref[block * conv_rows + r, :, lanes].astype(F32)
+                        for r in range(conv_rows)
+                    ],
+                )
+                for k in range(count):
+                    for b in range(KS):
+                        term = grads[k] * v_ref[tile, place * count + k, pl.ds(b, lon_pad), :]
+                        acc_ref[tile, k, b] += term.reshape(lon_pad // 8, 8, LANES).sum(axis=0)
+                return carry
+
+            lax.fori_loop(0, 2, side, 0)
+
+        over_blocks(ranges, step)
+
     rows_ref[...] = jnp.zeros_like(rows_ref)
     small_ref[...] = jnp.zeros_like(small_ref)
     for t in range(2):
@@ -458,39 +503,54 @@
     for position, start in zip(order, starts):
         share = [rows_ref[t, pl.ds(start, window), :] for t in range(2)]
         g_ref[position ^ me] = jnp.concatenate(share, axis=1).astype(BF16)
-
-
-def field_kernel(first, count, rows, cols, lon_pad, conv_rows,
-                 u_ref, up_ref, main_ref, west_ref, east_ref, south_ref, north_ref, *rest):
-    out_hbm, x_ref, v_ref, sum_ref, out_ref, out_sem = rest[-6:]
-    assemble(x_ref, first, count + KS - 1, main_ref, west_ref, east_ref, south_ref, north_ref, rows, cols)
-    write_points(x_ref, v_ref, count // conv_rows, conv_rows)
-
-    def body(block, carry):
+    done_copy.wait()
+
+
+def field_kernel(ranges, rows, cols, lon_pad, conv_rows, lat_halos, before, last, begun,
+                 u_ref, up_ref, main_ref, west_ref, east_ref, *rest):
+    rest = list(rest)
+    south_ref, north_ref = (rest.pop(0), rest.pop(0)) if lat_halos else (None, None)
+    before_ref = rest.pop(0) if before else None
+    if begun:
+        rest.pop(0)
+    out_hbm = rest.pop(0) if before or last else None
+    out_ref = None if last else rest.pop(0)
+    x_ref, v_ref, sum_ref, before_sem, out_sem, own_ref = rest
+    out_ref = own_ref if last else out_ref
+    if before:
+        before_copy = pltpu.make_async_copy(before_ref, out_hbm.at[pl.ds(*before)], before_sem)
+        before_copy.start()
+    field_points(
+        ranges, conv_rows, x_ref, v_ref, main_ref, west_ref, east_ref, south_ref, north_ref, rows,
+        cols,
+    )
+
+    def step(place, block):
         row = block * conv_rows
 
         def store(tile, lon, chunk, sums):
             lanes = pl.ds(pl.multiple_of(tile * LANES, LANES), LANES)
             for r in range(conv_rows):
-                total = sums[r] + up_ref[first + row + r, pl.ds(lon, chunk), lanes].astype(F32)
+                total = sums[r] + up_ref[row + r, pl.ds(lon, chunk), lanes].astype(F32)
                 sum_ref[r, pl.ds(lon, chunk), lanes] = total
 
-        depthwise_block(v_ref, u_ref, block, conv_rows, lon_pad, store, True)
-        out_ref[pl.ds(row, conv_rows)] = sum_ref[:, 0:cols, 0:C].astype(BF16)
-        out_copy(block).start()
-        return carry
-
-    def out_copy(block):
-        row = block * conv_rows
+        depthwise_block(v_ref, u_ref, place, conv_rows, lon_pad, store, True)
+        out_ref[pl.ds(place * conv_rows, conv_rows)] = sum_ref[:, 0:cols, 0:C].astype(BF16)
+        if last:
+            out_copy(place, block).start()
+
+    def out_copy(place, block):
         return pltpu.make_async_copy(
-            out_ref.at[pl.ds(row, conv_rows)],
-            out_hbm.at[pl.ds(first + row, conv_rows)],
-            out_sem.at[block],
+            out_ref.at[pl.ds(place * conv_rows, conv_rows)],
+            out_hbm.at[pl.ds(block * conv_rows, conv_rows)],
+            out_sem.at[place],
         )
 
-    lax.fori_loop(0, count // conv_rows, body, 0)
-    for block in range(count // conv_rows):
-        out_copy(block).wait()
+    over_blocks(ranges, step)
+    if last:
+        over_blocks(ranges, lambda place, block: out_copy(place, block).wait())
+    if before:
+        before_copy.wait()
 
 
 def shape(dims, kind):
@@ -529,15 +589,18 @@
     window = up(-(-(length + spill) // SHARE_LANES), 8)
     flat_rows = up(max(starts[-1] + window, 3 * (ROWS + 1)), 8)
 
-    share = lax.dynamic_update_slice(
-        jnp.zeros((window * SHARE_LANES,), BF16), params.astype(BF16), (offset,)
-    )
+    share = jnp.pad(params, (SHARE_LANES, window * SHARE_LANES - length))
+    share = lax.dynamic_slice(share, (SHARE_LANES - offset,), (window * SHARE_LANES,)).astype(BF16)
     gathered = share.reshape(1, window, SHARE_LANES)
     compiler_params = pltpu.CompilerParams(vmem_limit_bytes=VMEM)
+    smem = [pl.BlockSpec(memory_space=pltpu.SMEM)]
+    margin = -(-RAD // conv_rows)
+    inner = [(margin, blocks - 2 * margin)]
+    outer = [(0, margin), (blocks - margin, margin)]
     edges = pl.pallas_call(
         lambda *refs: edge_kernel(cols, *refs),
         out_shape=(shape((rows, RAD, C), BF16),) * 2,
-        in_specs=[pl.BlockSpec(memory_space=pl.ANY)],
+        in_specs=[pl.BlockSpec(memory_space=pltpu.HBM)],
         out_specs=tuple(whole(2)),
         scratch_shapes=[pltpu.VMEM((rows, cols, C), BF16)],
         compiler_params=compiler_params,
@@ -548,7 +611,7 @@
     for k, group in enumerate(groups):
         parts = [swap(gathered, mask) for mask in group]
         if k == max(0, len(groups) - 2):
-            west, east, _ = lax.optimization_barrier((west, east, parts[0]))
+            west, east, _, upstream = lax.optimization_barrier((west, east, parts[0], upstream))
             wides = pl.pallas_call(
                 lambda *refs: wide_kernel(rows, cols, *refs),
                 out_shape=(shape((RAD, cols + 2 * RAD, C), BF16),) * 2,
@@ -559,28 +622,36 @@
                 name="wides",
             )(features, west, east)
             south, north = shift_both(*wides, "lat", False)
+            inner_data, feats, ups = pl.pallas_call(
+                lambda *refs: inner_kernel(inner, rows, cols, conv_rows, *refs),
+                out_shape=(
+                    shape((2, block_count(inner) * points, lon_wide, LANES), F32),
+                    shape((rows, lon_pad, CP), BF16),
+                    shape((rows, lon_pad, CP), BF16),
+                ),
+                in_specs=whole(4),
+                out_specs=tuple(whole(3)),
+                scratch_shapes=[pltpu.VMEM((2, padded_rows(inner, conv_rows), lon_wide, LANES), F32)],
+                compiler_params=compiler_params,
+                cost_estimate=cost(2.5),
+                name="inner",
+            )(features, west, east, upstream)
         gathered = jnp.concatenate([gathered, *parts], axis=0)
         if k == max(0, len(groups) - 2):
-            gathered, upstream = lax.optimization_barrier((gathered, upstream))
-    feature_halos = (west, east, south, north)
-
-    smem = [pl.BlockSpec(memory_space=pltpu.SMEM)]
-    data, feats, ups = pl.pallas_call(
-        lambda *refs: assemble_kernel(rows, cols, conv_rows, *refs),
-        out_shape=(
-            shape((2, blocks * points, lon_wide, LANES), F32),
-            shape((rows, lon_pad, CP), BF16),
-            shape((rows, lon_pad, CP), BF16),
-        ),
-        in_specs=whole(6),
-        out_specs=tuple(whole(3)),
-        scratch_shapes=[pltpu.VMEM((2, rows + KS - 1, lon_wide, LANES), F32)],
+            gathered, inner_data = lax.optimization_barrier((gathered, inner_data))
+
+    outer_data = pl.pallas_call(
+        lambda *refs: outer_kernel(outer, rows, cols, conv_rows, *refs),
+        out_shape=shape((2, block_count(outer) * points, lon_wide, LANES), F32),
+        in_specs=whole(5),
+        out_specs=whole(1)[0],
+        scratch_shapes=[pltpu.VMEM((2, padded_rows(outer, conv_rows), lon_wide, LANES), F32)],
         compiler_params=compiler_params,
-        cost_estimate=cost(3),
-        name="assemble",
-    )(features, *feature_halos, upstream)
-
-    static = (order, starts, rows, lon_pad, block_rows, conv_rows)
+        cost_estimate=cost(1),
+        name="outer",
+    )(features, west, east, south, north)
+
+    static = (order, starts, rows, lon_pad, block_rows, conv_rows, inner, outer)
     output, gconv, gin, gout, sums, flipped = pl.pallas_call(
         lambda *refs: layer_kernel(*static, *refs),
         out_shape=(
@@ -591,68 +662,92 @@
             shape((5, 2, 8, LANES), F32),
             shape((2, points, 8, LANES), F32),
         ),
-        in_specs=smem + whole(4),
-        out_specs=(pl.BlockSpec(memory_space=pl.ANY), *whole(5)),
+        in_specs=smem + whole(5),
+        out_specs=tuple(whole(6)),
         scratch_shapes=[
-            pltpu.VMEM((rows, cols, C), BF16),
-            pltpu.SemaphoreType.DMA((rows // block_rows,)),
             pltpu.VMEM((2, points, 8, LANES), F32),
             pltpu.VMEM((2, 64, LANES), F32),
             pltpu.VMEM((2, flat_rows, LANES), F32),
             pltpu.VMEM((CP, H), BF16),
             pltpu.VMEM((H, CP), BF16),
             pltpu.VMEM((2, H, LANES), F32),
-            pltpu.VMEM((2, block_rows, lon_pad, LANES), F32),
+            pltpu.VMEM((2, rows, lon_pad, LANES), F32),
+            pltpu.VMEM((block_rows * lon_pad, H), BF16),
+            pltpu.VMEM((block_rows * lon_pad, H), BF16),
         ],
         compiler_params=compiler_params,
         cost_estimate=cost(22),
         name="layer",
-    )(place, gathered, data, feats, ups)
-
-    values = pl.pallas_call(
+    )(place, gathered, inner_data, outer_data, feats, ups)
+
+    values, output = pl.pallas_call(
         lambda *refs: taps_kernel(*static, *refs),
-        out_shape=shape((count, window, SHARE_LANES), BF16),
-        in_specs=smem + whole(5),
-        out_specs=whole(1)[0],
+        out_shape=(
+            shape((count, window, SHARE_LANES), BF16),
+            shape((rows, cols, C), BF16),
+        ),
+        in_specs=smem + whole(7),
+        out_specs=(*whole(1), pl.BlockSpec(memory_space=pl.ANY)),
         scratch_shapes=[
             pltpu.VMEM((2, flat_rows, LANES), F32),
             pltpu.VMEM((2, points, KS, 8, LANES), F32),
             pltpu.VMEM((2, H, LANES), F32),
             pltpu.VMEM((2, 64, LANES), F32),
+            pltpu.SemaphoreType.DMA(()),
         ],
         compiler_params=compiler_params,
         cost_estimate=cost(11),
         name="taps",
-    )(place, gconv, data, gin, gout, sums)
+    )(place, gconv, inner_data, outer_data, gin, gout, sums, output)
 
     west, east = shift_both(gconv[:, :RAD, :C], gconv[:, cols - RAD : cols, :C], "lon", True)
-    pieces = 3 if rows % (3 * conv_rows) == 0 else 1
-    piece_rows = rows // pieces
     field = None
 
-    def field_piece(piece, south, north, field):
-        before = [] if field is None else [field]
-        held = [pl.BlockSpec(memory_space=pl.ANY)] * len(before)
-        return pl.pallas_call(
+    def field_piece(ranges, lat_halos, before, field, last):
+        count = block_count(ranges)
+        own = shape((count * conv_rows, cols, C), BF16)
+        operands = [flipped, ups, gconv, west, east, *lat_halos]
+        in_specs = whole(len(operands))
+        span = None
+        if before is not None:
+            span = (before[0], before[1].shape[0])
+            operands.append(before[1])
+            in_specs += whole(1)
+        if field is not None:
+            operands.append(field)
+            in_specs.append(pl.BlockSpec(memory_space=pl.ANY))
+        out_shape = []
+        out_specs = []
+        if before is not None or last:
+            out_shape.append(shape((rows, cols, C), BF16))
+            out_specs.append(pl.BlockSpec(memory_space=pl.ANY))
+        if not last:
+            out_shape.append(own)
+            out_specs += whole(1)
+        results = pl.pallas_call(
             lambda *refs: field_kernel(
-                piece * piece_rows, piece_rows, rows, cols, lon_pad, conv_rows, *refs
+                ranges, rows, cols, lon_pad, conv_rows, bool(lat_halos), span, last,
+                field is not None, *refs
             ),
-            out_shape=shape((rows, cols, C), BF16),
-            in_specs=whole(7) + held,
-            out_specs=pl.BlockSpec(memory_space=pl.ANY),
+            out_shape=tuple(out_shape),
+            in_specs=in_specs,
+            out_specs=tuple(out_specs),
             scratch_shapes=[
-                pltpu.VMEM((2, piece_rows + KS - 1, lon_wide, LANES), F32),
-                pltpu.VMEM((2, piece_rows // conv_rows * points, lon_wide, LANES), F32),
+                pltpu.VMEM((2, padded_rows(ranges, conv_rows), lon_wide, LANES), F32),
+                pltpu.VMEM((2, count * points, lon_wide, LANES), F32),
                 pltpu.VMEM((conv_rows, lon_pad, CP), F32),
-                pltpu.VMEM((piece_rows, cols, C), BF16),
-                pltpu.SemaphoreType.DMA((piece_rows // conv_rows,)),
+                pltpu.SemaphoreType.DMA(()),
+                pltpu.SemaphoreType.DMA((count,)),
+                pltpu.VMEM(own.shape if last else (8, LANES), BF16),
             ],
-            input_output_aliases={7: 0} if before else {},
+            input_output_aliases={} if field is None else {len(operands) - 1: 0},
             compiler_params=compiler_params,
-            cost_estimate=cost(10 / pieces),
+            cost_estimate=cost(1.1 * count),
             name="field",
-        )(flipped, ups, gconv, west, east, south, north, *before)
-
+        )(*operands)
+        return (None if last else results[-1]), (results[0] if out_shape[0] is not own else None)
+
+    early = (inner[0][1] + 1) // 2
     for k, group in enumerate(groups[::-1]):
         if k == min(1, len(groups) - 1):
             values, west, east = lax.optimization_barrier((values, west, east))
@@ -666,12 +761,15 @@
                 return jnp.concatenate([west[at], gconv[at, :cols, :C], east[at]], axis=1)
 
             wides = (wide(slice(0, RAD)), wide(slice(rows - RAD, rows)))
-            if pieces == 3:
-                field = field_piece(1, *wides, None)
+            piece, _ = field_piece([(margin, early)], (), None, None, False)
         if k == min(2, len(groups) - 1):
-            south, north = shift_both(*wides, "lat", False)
-            for piece in ([0, 2] if pieces == 3 else [0]):
-                field = field_piece(piece, south, north, field)
+            lat_halos = shift_both(*wides, "lat", False)
+            piece, _ = lax.optimization_barrier((piece, values))
+            at = margin * conv_rows
+            late = [(margin + early, inner[0][1] - early)]
+            piece, field = field_piece(late, (), (at, piece), None, False)
+            at = (margin + early) * conv_rows
+            _, field = field_piece(outer, lat_halos, (at, piece), field, True)
         values = values[:part].astype(F32)
         for other in received:
             values = values + other.astype(F32)

time: 75.4 us -> 70.5 us (0.935)
  the two profiles are of different devices: /device:TPU:0 before, /device:TPU:1 now
where the time goes in v7:
time: 70.5 us; the launch traced here: 70.3 us
  Pallas kernels  30.2 us (43%)
  starting transfers between devices  28.3 us (40%)
  waiting for transfers between devices  7.02 us (10%)
  local copies, waits for them, and re-layouts  2.29 us (3%)
  other arithmetic  1.42 us (2%)
  between operations  1.03 us (1%)
    ppermute x12, starting transfers between devices, swap(): return lax.ppermute(values, ('lon', 'lat'), pairs)  13.3 us
    pallas_call x1, Pallas kernels, body(): pl.pallas_call(lambda *refs: layer_kernel(*static, *refs), out_shape=(sha...  13.3 us
    pallas_call x3, Pallas kernels, field_piece(): pl.pallas_call(lambda *refs: field_kernel(ranges, rows, cols, lon_pad, co...  8.57 us
    ppermute x4, starting transfers between devices, shift_both(): near = lax.ppermute(jnp.where(even, high_edge, low_edge), axis, near)  7.86 us
    ppermute x4, starting transfers between devices, shift_both(): far = lax.ppermute(jnp.where(even, low_edge, high_edge), axis, far)  7.12 us
    ppermute x12, waiting for transfers between devices, swap(): return lax.ppermute(values, ('lon', 'lat'), pairs)  5.56 us
    pallas_call x1, Pallas kernels, body(): pl.pallas_call(lambda *refs: taps_kernel(*static, *refs), out_shape=(shap...  4.11 us
    pallas_call x1, Pallas kernels, body(): pl.pallas_call(lambda *refs: inner_kernel(inner, rows, cols, conv_rows, *...  2.94 us
  transfers between devices with their start and end apart: 20, of which 8 were waited for; matrix products, arithmetic and copies ran while one was open for 1% of the time, Pallas kernels for 24%

profile of v7, /device:TPU:1, one launch (start us, length us, event | category | flops | bytes accessed | tf_op | source)
XLA Modules:
  0.0 70.3 jit_solution(5230253576146324627)
XLA Ops:
  0.7 0.9 %fusion = bf16[10240]{0:T(1024)(128)(2,1)S(1)} fusion(s32[]{:T(128)S(6)} %select_n.98, f32[9568]{0:T(1024)} %param.5), kind=kLoop, calls=%fused_computation.24 | loop fusion | bytes 58756 | tf_op jit(solution)/shard_map/convert_element_type | solution.py:593
  1.5 3.2 %collective-permute-start = (bf16[1,40,256]{2,1,0:T(8,128)(2,1)S(1)}, bf16[1,40,256]{2,1,0:T(8,128)(2,1)S(1)}, u32[]{:S(2)}, u32[]{:S(2)}) collective-permute-start(bf16[1,40,256]{2,1,0:T(8,128)(2,1)S(1)} %reshape.16), channel_id=1, source_target_pairs={{0,16},{1,17},{2,18},{3,19},{4,20},{5,21},{6,22},{7,23},{8,24},{9,... | collective-permute-start | bytes 61448 | tf_op jit(solution)/shard_map/ppermute | solution.py:60
  4.8 1.2 %copy-done.1 = bf16[45,45,192]{2,1,0:T(8,128)(2,1)S(1)} copy-done((bf16[45,45,192]{2,1,0:T(8,128)(2,1)S(1)}, bf16[45,45,192]{2,1,0:T(8,128)(2,1)}, u32[]{:S(2)}) %copy-start.1) | copy-done | bytes 777624
  6.0 0.2 edges.1
  6.2 0.0 copy-start.2
  6.2 0.1 broadcast_select_fusion.6
  6.3 1.3 %collective-permute-start.6 = (bf16[45,3,192]{2,1,0:T(4,128)(2,1)S(1)}, bf16[45,3,192]{2,1,0:T(4,128)(2,1)S(1)}, u32[]{:S(2)}, u32[]{:S(2)}) collective-permute-start(bf16[45,3,192]{2,1,0:T(4,128)(2,1)S(1)} %get-tuple-element.72), channel_id=1, source_target_pairs={{0,4},{4,0},{8,12},{12,8},{16,20},{20,16},{24,28},{28,24},{1,5},{5... | collective-permute-start | bytes 155528 | tf_op jit(solution)/shard_map/ppermute | solution.py:73
  7.6 1.0 %collective-permute-start.5 = (bf16[45,3,192]{2,1,0:T(4,128)(2,1)S(1)}, bf16[45,3,192]{2,1,0:T(4,128)(2,1)S(1)}, u32[]{:S(2)}, u32[]{:S(2)}) collective-permute-start(bf16[45,3,192]{2,1,0:T(4,128)(2,1)S(1)} %get-tuple-element.73), channel_id=1, source_target_pairs={{4,8},{12,16},{20,24},{28,0},{8,4},{16,12},{24,20},{0,28},{5,9},{1... | collective-permute-start | bytes 155528 | tf_op jit(solution)/shard_map/ppermute | solution.py:74
  8.7 0.0 collective-permute-done
  8.7 0.5 collective-permute-start.1
  9.1 2.5 %collective-permute-done.1 = bf16[2,40,256]{2,1,0:T(8,128)(2,1)S(1)} collective-permute-done((bf16[2,40,256]{2,1,0:T(8,128)(2,1)S(1)}, bf16[2,40,256]{2,1,0:T(8,128)(2,1)S(1)}, u32[]{:S(2)}, u32[]{:S(2)}) %collective-permute-start.1) | collective-permute-done | bytes 40992 | tf_op jit(solution)/shard_map/ppermute | solution.py:60
  11.6 1.7 %collective-permute-start.2 = (bf16[4,40,256]{2,1,0:T(8,128)(2,1)S(1)}, bf16[4,40,256]{2,1,0:T(8,128)(2,1)S(1)}, u32[]{:S(2)}, u32[]{:S(2)}) collective-permute-start(bf16[4,40,256]{2,1,0:T(8,128)(2,1)S(1)} %get-tuple-element.86), channel_id=1, source_target_pairs={{0,4},{1,5},{2,6},{3,7},{4,0},{5,1},{6,2},{7,3},{8,12},{9,13},{10,... | collective-permute-start | bytes 245768 | tf_op jit(solution)/shard_map/ppermute | solution.py:60
  13.3 0.0 collective-permute-done.6
  13.3 0.4 collective-permute-done.5
  13.7 0.1 broadcast_select_fusion.4
  13.8 0.7 collective-permute-start.4
  14.5 0.7 %collective-permute-start.3 = (bf16[4,40,256]{2,1,0:T(8,128)(2,1)S(1)}, bf16[4,40,256]{2,1,0:T(8,128)(2,1)S(1)}, u32[]{:S(2)}, u32[]{:S(2)}) collective-permute-start(bf16[4,40,256]{2,1,0:T(8,128)(2,1)S(1)} %get-tuple-element.86), channel_id=1, source_target_pairs={{0,2},{1,3},{2,0},{3,1},{4,6},{5,7},{6,4},{7,5},{8,10},{9,11},{10,... | collective-permute-start | bytes 245768 | tf_op jit(solution)/shard_map/ppermute | solution.py:60
  15.2 1.0 %collective-permute-done.2 = bf16[4,40,256]{2,1,0:T(8,128)(2,1)S(1)} collective-permute-done((bf16[4,40,256]{2,1,0:T(8,128)(2,1)S(1)}, bf16[4,40,256]{2,1,0:T(8,128)(2,1)S(1)}, u32[]{:S(2)}, u32[]{:S(2)}) %collective-permute-start.2) | collective-permute-done | bytes 81952 | tf_op jit(solution)/shard_map/ppermute | solution.py:60
  16.2 0.0 copy-done.2
  16.2 3.6 %collective-permute-start.9 = (bf16[3,51,192]{2,1,0:T(8,128)(2,1)S(1)}, bf16[3,51,192]{2,1,0:T(8,128)(2,1)S(1)}, u32[]{:S(2)}, u32[]{:S(2)}) collective-permute-start(bf16[3,51,192]{2,1,0:T(8,128)(2,1)S(1)} %get-tuple-element.80), channel_id=1, source_target_pairs={{0,1},{1,0},{2,3},{3,2},{4,5},{5,4},{6,7},{7,6},{8,9},{9,8},{10,11... | collective-permute-start | bytes 176264 | tf_op jit(solution)/shard_map/ppermute | solution.py:73
  19.8 2.9 %collective-permute-start.8 = (bf16[3,51,192]{2,1,0:T(8,128)(2,1)S(1)}, bf16[3,51,192]{2,1,0:T(8,128)(2,1)S(1)}, u32[]{:S(2)}, u32[]{:S(2)}) collective-permute-start(bf16[3,51,192]{2,1,0:T(8,128)(2,1)S(1)} %get-tuple-element.81), channel_id=1, source_target_pairs={{1,2},{2,1},{5,6},{6,5},{9,10},{10,9},{13,14},{14,13},{17,18},{18,... | collective-permute-start | bytes 176264 | tf_op jit(solution)/shard_map/ppermute | solution.py:74
  22.7 0.0 copy-done
  22.7 2.9 %inner.1 = (f32[2,77,56,128]{3,2,1,0:T(8,128)S(1)}, bf16[45,48,256]{2,1,0:T(8,128)(2,1)S(1)}, bf16[45,48,256]{2,1,0:T(8,128)(2,1)S(1)}) custom-call(bf16[45,45,192]{2,1,0:T(8,128)(2,1)S(1)} %copy-done.2, bf16[45,3,192]{2,1,0:T(4,128)(2,1)S(1)} %get-tuple-element.34.refs_1_, bf16[45,3,192]{2,1,0:T(4,128)(2,1)S(1)} %get-tuple-element.35.refs_2_, ...), custom_call_target="tpu_custom_call" | custom-call | flops 2750000128 | tf_op jit(solution)/shard_map/inner/pallas_call | solution.py:625
  25.7 0.0 collective-permute-done.3
  25.7 0.0 collective-permute-done.4
  25.7 0.1 collective-permute-start.7
  25.8 0.0 collective-permute-done.9
  25.8 0.0 collective-permute-done.8
  25.9 1.0 %outer.1.refs_3_ = f32[2,22,56,128]{3,2,1,0:T(8,128)S(1)} custom-call(bf16[45,45,192]{2,1,0:T(8,128)(2,1)S(1)} %copy-done.2, bf16[45,3,192]{2,1,0:T(4,128)(2,1)S(1)} %get-tuple-element.34.refs_1_, bf16[45,3,192]{2,1,0:T(4,128)(2,1)S(1)} %get-tuple-element.35.refs_2_, bf16[3,51,192]{2,1,0:T(8,128)(2,1)S(1)} %get-tuple-element.79.refs_3_, ...), custom_call_target="tpu_custom_call" | custom-call | flops 1100000000 | tf_op jit(solution)/shard_map/outer/pallas_call | solution.py:643
  26.9 0.5 collective-permute-done.7
  27.4 0.1 pad_maximum_fusion.refs_1_
  27.5 13.3 %layer.1 = (bf16[45,45,192]{2,1,0:T(8,128)(2,1)S(1)}, bf16[45,48,256]{2,1,0:T(8,128)(2,1)S(1)}, f32[256,768]{1,0:T(8,128)S(1)}, f32[256,768]{1,0:T(8,128)S(1)}, ...) custom-call(s32[1]{0:T(128)} %bitcast.refs_0_, bf16[32,40,256]{2,1,0:T(8,128)(2,1)S(1)} %pad_maximum_fusion.refs_1_, ...), custom_call_target="tpu_custom_call" | custom-call | flops 24199999488 | tf_op jit(solution)/shard_map/layer/pallas_call | solution.py:655
  40.8 0.1 broadcast_select_fusion.2
  40.9 1.8 %collective-permute-start.12 = (bf16[45,3,192]{2,1,0:T(4,128)(2,1)S(1)}, bf16[45,3,192]{2,1,0:T(4,128)(2,1)S(1)}, u32[]{:S(2)}, u32[]{:S(2)}) collective-permute-start(bf16[45,3,192]{2,1,0:T(4,128)(2,1)S(1)} %get-tuple-element.63), channel_id=1, source_target_pairs={{0,4},{4,0},{8,12},{12,8},{16,20},{20,16},{24,28},{28,24},{1,5},{5... | collective-permute-start | bytes 155528 | tf_op jit(solution)/shard_map/ppermute | solution.py:73
  42.7 0.8 %collective-permute-start.11 = (bf16[45,3,192]{2,1,0:T(4,128)(2,1)S(1)}, bf16[45,3,192]{2,1,0:T(4,128)(2,1)S(1)}, u32[]{:S(2)}, u32[]{:S(2)}) collective-permute-start(bf16[45,3,192]{2,1,0:T(4,128)(2,1)S(1)} %get-tuple-element.64), channel_id=1, source_target_pairs={{4,8},{12,16},{20,24},{28,0},{8,4},{16,12},{24,20},{0,28},{5,9},{1... | collective-permute-start | bytes 155528 | tf_op jit(solution)/shard_map/ppermute | solution.py:74
  43.5 4.1 %taps.1 = (bf16[32,40,256]{2,1,0:T(8,128)(2,1)S(1)}, bf16[45,45,192]{2,1,0:T(8,128)(2,1)}) custom-call(s32[1]{0:T(128)} %bitcast.refs_0_, bf16[45,48,256]{2,1,0:T(8,128)(2,1)S(1)} %get-tuple-element.44.refs_1_.refs_2_, f32[2,77,56,128]{3,2,1,0:T(8,128)S(1)} %get-tuple-element.39.refs_2_, f32[2,22,56,128]{3,2,1,0:T(8,128)S(1)} %outer.1.refs_3_, ...), custom_call_target="tpu_custom_call" | custom-call | flops 12099999744 | tf_op jit(solution)/shard_map/taps/pallas_call | solution.py:683
  47.7 0.5 collective-permute-start.10
  48.2 0.0 collective-permute-done.12
  48.2 1.1 %collective-permute-done.11 = bf16[45,3,192]{2,1,0:T(4,128)(2,1)S(1)} collective-permute-done((bf16[45,3,192]{2,1,0:T(4,128)(2,1)S(1)}, bf16[45,3,192]{2,1,0:T(4,128)(2,1)S(1)}, u32[]{:S(2)}, u32[]{:S(2)}) %collective-permute-start.11) | collective-permute-done | bytes 51872 | tf_op jit(solution)/shard_map/ppermute | solution.py:74
  49.2 0.1 broadcast_select_fusion
  49.3 0.1 collective-permute-done.10
  49.4 0.1 convert_add_fusion
  49.6 0.4 collective-permute-start.13
  49.9 2.0 %collective-permute-start.15 = (bf16[4,40,256]{2,1,0:T(8,128)(2,1)S(1)}, bf16[4,40,256]{2,1,0:T(8,128)(2,1)S(1)}, u32[]{:S(2)}, u32[]{:S(2)}) collective-permute-start(bf16[4,40,256]{2,1,0:T(8,128)(2,1)S(1)} %get-tuple-element.66), channel_id=1, source_target_pairs={{0,6},{1,7},{2,4},{3,5},{4,2},{5,3},{6,0},{7,1},{8,14},{9,15},{10,... | collective-permute-start | bytes 245768 | tf_op jit(solution)/shard_map/ppermute | solution.py:60
  51.9 0.3 collective-permute-start.14
  52.3 3.3 %field.3.refs_5_ = bf16[20,45,192]{2,1,0:T(8,128)(2,1)S(1)} custom-call(f32[2,11,8,128]{3,2,1,0:T(8,128)S(1)} %get-tuple-element.50.refs_0_, bf16[45,48,256]{2,1,0:T(8,128)(2,1)S(1)} %get-tuple-element.43.refs_5_.refs_1_, bf16[45,48,256]{2,1,0:T(8,128)(2,1)S(1)} %get-tuple-element.44.refs_1_.refs_2_, bf16[45,3,192]{2,1,0:T(4,128)(2,1)S(1)} %get-tuple-element.52.refs_3_, ...), custom_call_target="tpu_custom_call" | custom-call | flops 4840000000 | tf_op jit(solution)/shard_map/field/pallas_call | solution.py:727
  55.6 0.0 collective-permute-done.13
  55.7 0.2 collective-permute-done.15
  55.8 1.3 %collective-permute-done.14 = bf16[4,40,256]{2,1,0:T(8,128)(2,1)S(1)} collective-permute-done((bf16[4,40,256]{2,1,0:T(8,128)(2,1)S(1)}, bf16[4,40,256]{2,1,0:T(8,128)(2,1)S(1)}, u32[]{:S(2)}, u32[]{:S(2)}) %collective-permute-start.14) | collective-permute-done | bytes 81952 | tf_op jit(solution)/shard_map/ppermute | solution.py:60
  57.2 0.6 collective-permute-start.18
  57.9 1.2 %collective-permute-start.17 = (bf16[3,51,192]{2,1,0:T(8,128)(2,1)S(1)}, bf16[3,51,192]{2,1,0:T(8,128)(2,1)S(1)}, u32[]{:S(2)}, u32[]{:S(2)}) collective-permute-start(bf16[3,51,192]{2,1,0:T(8,128)(2,1)S(1)} %get-tuple-element.76), channel_id=1, source_target_pairs={{0,1},{1,0},{2,3},{3,2},{4,5},{5,4},{6,7},{7,6},{8,9},{9,8},{10,11... | collective-permute-start | bytes 176264 | tf_op jit(solution)/shard_map/ppermute | solution.py:73
  59.0 2.4 %collective-permute-start.16 = (bf16[3,51,192]{2,1,0:T(8,128)(2,1)S(1)}, bf16[3,51,192]{2,1,0:T(8,128)(2,1)S(1)}, u32[]{:S(2)}, u32[]{:S(2)}) collective-permute-start(bf16[3,51,192]{2,1,0:T(8,128)(2,1)S(1)} %get-tuple-element.77), channel_id=1, source_target_pairs={{1,2},{2,1},{5,6},{6,5},{9,10},{10,9},{13,14},{14,13},{17,18},{18,... | collective-permute-start | bytes 176264 | tf_op jit(solution)/shard_map/ppermute | solution.py:74
  61.5 2.6 %field.4 = (bf16[45,45,192]{2,1,0:T(8,128)(2,1)}, bf16[15,45,192]{2,1,0:T(8,128)(2,1)S(1)}) custom-call(f32[2,11,8,128]{3,2,1,0:T(8,128)S(1)} %get-tuple-element.50.refs_0_, bf16[45,48,256]{2,1,0:T(8,128)(2,1)S(1)} %get-tuple-element.43.refs_5_.refs_1_, bf16[45,48,256]{2,1,0:T(8,128)(2,1)S(1)} %get-tuple-element.44.refs_1_.refs_2_, ...), custom_call_target="tpu_custom_call" | custom-call | flops 3630000128 | tf_op jit(solution)/shard_map/field/pallas_call | solution.py:727
  64.1 0.0 collective-permute-done.18
  64.1 2.6 %collective-permute-start.19 = (bf16[1,40,256]{2,1,0:T(8,128)(2,1)S(1)}, bf16[1,40,256]{2,1,0:T(8,128)(2,1)S(1)}, u32[]{:S(2)}, u32[]{:S(2)}) collective-permute-start(bf16[1,40,256]{2,1,0:T(8,128)(2,1)S(1)} %slice.96), channel_id=1, source_target_pairs={{0,16},{1,17},{2,18},{3,19},{4,20},{5,21},{6,22},{7,23},{8,24},{9,... | collective-permute-start | bytes 61448 | tf_op jit(solution)/shard_map/ppermute | solution.py:60
  66.8 0.0 collective-permute-done.17
  66.8 0.0 collective-permute-done.16
  66.8 0.0 copy-start.3
  66.8 0.0 copy-start.4
  66.8 2.7 %field.5 = bf16[45,45,192]{2,1,0:T(8,128)(2,1)} custom-call(f32[2,11,8,128]{3,2,1,0:T(8,128)S(1)} %get-tuple-element.50.refs_0_, bf16[45,48,256]{2,1,0:T(8,128)(2,1)S(1)} %get-tuple-element.43.refs_5_.refs_1_, bf16[45,48,256]{2,1,0:T(8,128)(2,1)S(1)} %get-tuple-element.44.refs_1_.refs_2_, ...), custom_call_target="tpu_custom_call", output_to_operand_aliasing={{}: (8, {})} | custom-call | flops 2420000000 | tf_op jit(solution)/shard_map/field/pallas_call | solution.py:727
  69.5 0.0 collective-permute-done.19
  69.6 0.0 copy-done.3
  69.6 0.0 copy-done.4
  69.6 0.7 %multiply_add_fusion = f32[9568]{0:T(1024)} fusion(f32[9568]{0:T(1024)S(1)} %copy-done.4, f32[9568]{0:T(1024)S(1)} %copy-done.3, f32[10240]{0:T(1024)S(1)} %bitcast.4, s32[]{:T(128)S(6)} %select_n.119), kind=kLoop, calls=%fused_computation.29 | loop fusion | flops 38272 | bytes 153092 | tf_op jit(solution)/shard_map/add | solution.py:779
  (28 shorter events, 0.4 us)
Async XLA Ops:
  1.5 7.1 %collective-permute-start = (bf16[1,40,256]{2,1,0:T(8,128)(2,1)S(1)}, bf16[1,40,256]{2,1,0:T(8,128)(2,1)S(1)}, u32[]{:S(2)}, u32[]{:S(2)}) collective-permute-start(bf16[1,40,256]{2,1,0:T(8,128)(2,1)S(1)} %reshape.16), channel_id=1, source_target_pairs={{0,16},{1,17},{2,18},{3,19},{4,20},{5,21},{6,22},{7,23},{8,24},{9,... | collective-permute-start | bytes 61448 | tf_op jit(solution)/shard_map/ppermute | solution.py:60
  4.8 1.2 %copy-start.1 = (bf16[45,45,192]{2,1,0:T(8,128)(2,1)S(1)}, bf16[45,45,192]{2,1,0:T(8,128)(2,1)}, u32[]{:S(2)}) copy-start(bf16[45,45,192]{2,1,0:T(8,128)(2,1)} %refs_0_.7) | copy-start | bytes 2332804
  6.2 9.9 %copy-start.2 = (bf16[45,45,192]{2,1,0:T(8,128)(2,1)S(1)}, bf16[45,45,192]{2,1,0:T(8,128)(2,1)}, u32[]{:S(2)}) copy-start(bf16[45,45,192]{2,1,0:T(8,128)(2,1)} %refs_0_.7) | copy-start | bytes 2332804
  6.3 7.0 %collective-permute-start.6 = (bf16[45,3,192]{2,1,0:T(4,128)(2,1)S(1)}, bf16[45,3,192]{2,1,0:T(4,128)(2,1)S(1)}, u32[]{:S(2)}, u32[]{:S(2)}) collective-permute-start(bf16[45,3,192]{2,1,0:T(4,128)(2,1)S(1)} %get-tuple-element.72), channel_id=1, source_target_pairs={{0,4},{4,0},{8,12},{12,8},{16,20},{20,16},{24,28},{28,24},{1,5},{5... | collective-permute-start | bytes 155528 | tf_op jit(solution)/shard_map/ppermute | solution.py:73
  7.6 6.1 %collective-permute-start.5 = (bf16[45,3,192]{2,1,0:T(4,128)(2,1)S(1)}, bf16[45,3,192]{2,1,0:T(4,128)(2,1)S(1)}, u32[]{:S(2)}, u32[]{:S(2)}) collective-permute-start(bf16[45,3,192]{2,1,0:T(4,128)(2,1)S(1)} %get-tuple-element.73), channel_id=1, source_target_pairs={{4,8},{12,16},{20,24},{28,0},{8,4},{16,12},{24,20},{0,28},{5,9},{1... | collective-permute-start | bytes 155528 | tf_op jit(solution)/shard_map/ppermute | solution.py:74
  8.7 2.9 %collective-permute-start.1 = (bf16[2,40,256]{2,1,0:T(8,128)(2,1)S(1)}, bf16[2,40,256]{2,1,0:T(8,128)(2,1)S(1)}, u32[]{:S(2)}, u32[]{:S(2)}) collective-permute-start(bf16[2,40,256]{2,1,0:T(8,128)(2,1)S(1)} %pad_maximum_fusion.3), channel_id=1, source_target_pairs={{0,8},{1,9},{2,10},{3,11},{4,12},{5,13},{6,14},{7,15},{8,0},{9,1},... | collective-permute-start | bytes 122888 | tf_op jit(solution)/shard_map/ppermute | solution.py:60
  11.6 4.6 %collective-permute-start.2 = (bf16[4,40,256]{2,1,0:T(8,128)(2,1)S(1)}, bf16[4,40,256]{2,1,0:T(8,128)(2,1)S(1)}, u32[]{:S(2)}, u32[]{:S(2)}) collective-permute-start(bf16[4,40,256]{2,1,0:T(8,128)(2,1)S(1)} %get-tuple-element.86), channel_id=1, source_target_pairs={{0,4},{1,5},{2,6},{3,7},{4,0},{5,1},{6,2},{7,3},{8,12},{9,13},{10,... | collective-permute-start | bytes 245768 | tf_op jit(solution)/shard_map/ppermute | solution.py:60
  13.8 11.9 %collective-permute-start.4 = (bf16[4,40,256]{2,1,0:T(8,128)(2,1)S(1)}, bf16[4,40,256]{2,1,0:T(8,128)(2,1)S(1)}, u32[]{:S(2)}, u32[]{:S(2)}) collective-permute-start(bf16[4,40,256]{2,1,0:T(8,128)(2,1)S(1)} %get-tuple-element.86), channel_id=1, source_target_pairs={{0,6},{1,7},{2,4},{3,5},{4,2},{5,3},{6,0},{7,1},{8,14},{9,15},{10,... | collective-permute-start | bytes 245768 | tf_op jit(solution)/shard_map/ppermute | solution.py:60
  14.5 11.2 %collective-permute-start.3 = (bf16[4,40,256]{2,1,0:T(8,128)(2,1)S(1)}, bf16[4,40,256]{2,1,0:T(8,128)(2,1)S(1)}, u32[]{:S(2)}, u32[]{:S(2)}) collective-permute-start(bf16[4,40,256]{2,1,0:T(8,128)(2,1)S(1)} %get-tuple-element.86), channel_id=1, source_target_pairs={{0,2},{1,3},{2,0},{3,1},{4,6},{5,7},{6,4},{7,5},{8,10},{9,11},{10,... | collective-permute-start | bytes 245768 | tf_op jit(solution)/shard_map/ppermute | solution.py:60
  16.2 6.6 %copy-start = (bf16[45,45,192]{2,1,0:T(8,128)(2,1)S(1)}, bf16[45,45,192]{2,1,0:T(8,128)(2,1)}, u32[]{:S(2)}) copy-start(bf16[45,45,192]{2,1,0:T(8,128)(2,1)} %refs_3_) | copy-start | bytes 2332804
  16.2 9.6 %collective-permute-start.9 = (bf16[3,51,192]{2,1,0:T(8,128)(2,1)S(1)}, bf16[3,51,192]{2,1,0:T(8,128)(2,1)S(1)}, u32[]{:S(2)}, u32[]{:S(2)}) collective-permute-start(bf16[3,51,192]{2,1,0:T(8,128)(2,1)S(1)} %get-tuple-element.80), channel_id=1, source_target_pairs={{0,1},{1,0},{2,3},{3,2},{4,5},{5,4},{6,7},{7,6},{8,9},{9,8},{10,11... | collective-permute-start | bytes 176264 | tf_op jit(solution)/shard_map/ppermute | solution.py:73
  19.8 6.0 %collective-permute-start.8 = (bf16[3,51,192]{2,1,0:T(8,128)(2,1)S(1)}, bf16[3,51,192]{2,1,0:T(8,128)(2,1)S(1)}, u32[]{:S(2)}, u32[]{:S(2)}) collective-permute-start(bf16[3,51,192]{2,1,0:T(8,128)(2,1)S(1)} %get-tuple-element.81), channel_id=1, source_target_pairs={{1,2},{2,1},{5,6},{6,5},{9,10},{10,9},{13,14},{14,13},{17,18},{18,... | collective-permute-start | bytes 176264 | tf_op jit(solution)/shard_map/ppermute | solution.py:74
  25.7 1.7 %collective-permute-start.7 = (bf16[16,40,256]{2,1,0:T(8,128)(2,1)S(1)}, bf16[16,40,256]{2,1,0:T(8,128)(2,1)S(1)}, u32[]{:S(2)}, u32[]{:S(2)}) collective-permute-start(bf16[16,40,256]{2,1,0:T(8,128)(2,1)S(1)} %constant_dynamic-update-slice_fusion.3), channel_id=1, source_target_pairs={{0,1},{1,0},{2,3},{3,2},{4,5},{5,4},{6,7},{7,6},{8,9},{9,8},{10,11... | collective-permute-start | bytes 983048 | tf_op jit(solution)/shard_map/ppermute | solution.py:60
  40.9 7.3 %collective-permute-start.12 = (bf16[45,3,192]{2,1,0:T(4,128)(2,1)S(1)}, bf16[45,3,192]{2,1,0:T(4,128)(2,1)S(1)}, u32[]{:S(2)}, u32[]{:S(2)}) collective-permute-start(bf16[45,3,192]{2,1,0:T(4,128)(2,1)S(1)} %get-tuple-element.63), channel_id=1, source_target_pairs={{0,4},{4,0},{8,12},{12,8},{16,20},{20,16},{24,28},{28,24},{1,5},{5... | collective-permute-start | bytes 155528 | tf_op jit(solution)/shard_map/ppermute | solution.py:73
  42.7 6.5 %collective-permute-start.11 = (bf16[45,3,192]{2,1,0:T(4,128)(2,1)S(1)}, bf16[45,3,192]{2,1,0:T(4,128)(2,1)S(1)}, u32[]{:S(2)}, u32[]{:S(2)}) collective-permute-start(bf16[45,3,192]{2,1,0:T(4,128)(2,1)S(1)} %get-tuple-element.64), channel_id=1, source_target_pairs={{4,8},{12,16},{20,24},{28,0},{8,4},{16,12},{24,20},{0,28},{5,9},{1... | collective-permute-start | bytes 155528 | tf_op jit(solution)/shard_map/ppermute | solution.py:74
  47.7 1.8 %collective-permute-start.10 = (bf16[16,40,256]{2,1,0:T(8,128)(2,1)S(1)}, bf16[16,40,256]{2,1,0:T(8,128)(2,1)S(1)}, u32[]{:S(2)}, u32[]{:S(2)}) collective-permute-start(bf16[16,40,256]{2,1,0:T(8,128)(2,1)S(1)} %slice.60), channel_id=1, source_target_pairs={{0,1},{1,0},{2,3},{3,2},{4,5},{5,4},{6,7},{7,6},{8,9},{9,8},{10,11... | collective-permute-start | bytes 983048 | tf_op jit(solution)/shard_map/ppermute | solution.py:60
  49.6 6.1 %collective-permute-start.13 = (bf16[4,40,256]{2,1,0:T(8,128)(2,1)S(1)}, bf16[4,40,256]{2,1,0:T(8,128)(2,1)S(1)}, u32[]{:S(2)}, u32[]{:S(2)}) collective-permute-start(bf16[4,40,256]{2,1,0:T(8,128)(2,1)S(1)} %get-tuple-element.65), channel_id=1, source_target_pairs={{0,4},{1,5},{2,6},{3,7},{4,0},{5,1},{6,2},{7,3},{8,12},{9,13},{10,... | collective-permute-start | bytes 245768 | tf_op jit(solution)/shard_map/ppermute | solution.py:60
  49.9 5.9 %collective-permute-start.15 = (bf16[4,40,256]{2,1,0:T(8,128)(2,1)S(1)}, bf16[4,40,256]{2,1,0:T(8,128)(2,1)S(1)}, u32[]{:S(2)}, u32[]{:S(2)}) collective-permute-start(bf16[4,40,256]{2,1,0:T(8,128)(2,1)S(1)} %get-tuple-element.66), channel_id=1, source_target_pairs={{0,6},{1,7},{2,4},{3,5},{4,2},{5,3},{6,0},{7,1},{8,14},{9,15},{10,... | collective-permute-start | bytes 245768 | tf_op jit(solution)/shard_map/ppermute | solution.py:60
  51.9 5.2 %collective-permute-start.14 = (bf16[4,40,256]{2,1,0:T(8,128)(2,1)S(1)}, bf16[4,40,256]{2,1,0:T(8,128)(2,1)S(1)}, u32[]{:S(2)}, u32[]{:S(2)}) collective-permute-start(bf16[4,40,256]{2,1,0:T(8,128)(2,1)S(1)} %get-tuple-element.67), channel_id=1, source_target_pairs={{0,2},{1,3},{2,0},{3,1},{4,6},{5,7},{6,4},{7,5},{8,10},{9,11},{10,... | collective-permute-start | bytes 245768 | tf_op jit(solution)/shard_map/ppermute | solution.py:60
  57.2 6.9 %collective-permute-start.18 = (bf16[2,40,256]{2,1,0:T(8,128)(2,1)S(1)}, bf16[2,40,256]{2,1,0:T(8,128)(2,1)S(1)}, u32[]{:S(2)}, u32[]{:S(2)}) collective-permute-start(bf16[2,40,256]{2,1,0:T(8,128)(2,1)S(1)} %slice.95), channel_id=1, source_target_pairs={{0,8},{1,9},{2,10},{3,11},{4,12},{5,13},{6,14},{7,15},{8,0},{9,1},... | collective-permute-start | bytes 122888 | tf_op jit(solution)/shard_map/ppermute | solution.py:60
  57.9 8.9 %collective-permute-start.17 = (bf16[3,51,192]{2,1,0:T(8,128)(2,1)S(1)}, bf16[3,51,192]{2,1,0:T(8,128)(2,1)S(1)}, u32[]{:S(2)}, u32[]{:S(2)}) collective-permute-start(bf16[3,51,192]{2,1,0:T(8,128)(2,1)S(1)} %get-tuple-element.76), channel_id=1, source_target_pairs={{0,1},{1,0},{2,3},{3,2},{4,5},{5,4},{6,7},{7,6},{8,9},{9,8},{10,11... | collective-permute-start | bytes 176264 | tf_op jit(solution)/shard_map/ppermute | solution.py:73
  59.0 7.7 %collective-permute-start.16 = (bf16[3,51,192]{2,1,0:T(8,128)(2,1)S(1)}, bf16[3,51,192]{2,1,0:T(8,128)(2,1)S(1)}, u32[]{:S(2)}, u32[]{:S(2)}) collective-permute-start(bf16[3,51,192]{2,1,0:T(8,128)(2,1)S(1)} %get-tuple-element.77), channel_id=1, source_target_pairs={{1,2},{2,1},{5,6},{6,5},{9,10},{10,9},{13,14},{14,13},{17,18},{18,... | collective-permute-start | bytes 176264 | tf_op jit(solution)/shard_map/ppermute | solution.py:74
  64.1 5.4 %collective-permute-start.19 = (bf16[1,40,256]{2,1,0:T(8,128)(2,1)S(1)}, bf16[1,40,256]{2,1,0:T(8,128)(2,1)S(1)}, u32[]{:S(2)}, u32[]{:S(2)}) collective-permute-start(bf16[1,40,256]{2,1,0:T(8,128)(2,1)S(1)} %slice.96), channel_id=1, source_target_pairs={{0,16},{1,17},{2,18},{3,19},{4,20},{5,21},{6,22},{7,23},{8,24},{9,... | collective-permute-start | bytes 61448 | tf_op jit(solution)/shard_map/ppermute | solution.py:60
  66.8 2.8 %copy-start.3 = (f32[9568]{0:T(1024)S(1)}, f32[9568]{0:T(1024)}, u32[]{:S(2)}) copy-start(f32[9568]{0:T(1024)} %param.5) | copy-start | bytes 114820
  66.8 2.8 %copy-start.4 = (f32[9568]{0:T(1024)S(1)}, f32[9568]{0:T(1024)}, u32[]{:S(2)}) copy-start(f32[9568]{0:T(1024)} %param.6) | copy-start | bytes 114820

commit v8 on v7

--- a/solution.py
+++ b/solution.py
@@ -60,19 +60,24 @@
     return lax.ppermute(values, ("lon", "lat"), pairs)
 
 
-def shift_both(low_edge, high_edge, axis, periodic):
+def send_edges(low_edge, high_edge, axis, periodic):
     count = lax.axis_size(axis)
-    if count % 2:
-        forward = [(i, (i + 1) % count) for i in range(count if periodic else count - 1)]
-        backward = [(target, source) for source, target in forward]
-        return lax.ppermute(high_edge, axis, forward), lax.ppermute(low_edge, axis, backward)
     even = lax.axis_index(axis) % 2 == 0
     near = [(i, i ^ 1) for i in range(count)]
     odds = [(i, (i + 1) % count) for i in range(1, count if periodic else count - 1, 2)]
     far = odds + [(target, source) for source, target in odds]
     near = lax.ppermute(jnp.where(even, high_edge, low_edge), axis, near)
     far = lax.ppermute(jnp.where(even, low_edge, high_edge), axis, far)
+    return near, far
+
+
+def edges_from(near, far, axis):
+    even = lax.axis_index(axis) % 2 == 0
     return jnp.where(even, far, near), jnp.where(even, near, far)
+
+
+def shift_both(low_edge, high_edge, axis, periodic):
+    return edges_from(*send_edges(low_edge, high_edge, axis, periodic), axis)
 
 
 def reversed_bits(number, count):
@@ -127,21 +132,32 @@
         low = max(0, first - RAD)
         high = min(rows, first + count - RAD)
         at = slice(base + low + RAD - first, base + high + RAD - first)
+        if main.shape[2] == CP:
+            span = slice(RAD, RAD + main.shape[1])
+            x_ref[t, at, span, :] = main[low:high, :, t * LANES : (t + 1) * LANES].astype(F32)
+        else:
+            x_ref[t, at, RAD : RAD + cols, width] = main[low:high, 0:cols, lanes].astype(F32)
         x_ref[t, at, 0:RAD, width] = west[low:high, :, lanes].astype(F32)
-        x_ref[t, at, RAD : RAD + cols, width] = main[low:high, 0:cols, lanes].astype(F32)
         x_ref[t, at, RAD + cols : 2 * RAD + cols, width] = east[low:high, :, lanes].astype(F32)
         wide = slice(0, cols + 2 * RAD)
         if first < RAD:
             at = slice(base, base + RAD - first)
+            x_ref[t, at] = jnp.zeros_like(x_ref[t, at])
             x_ref[t, at, wide, width] = south[first:, :, lanes].astype(F32)
         over = first + count - rows - RAD
         if over > 0:
             at = slice(base + count - over, base + count)
+            x_ref[t, at] = jnp.zeros_like(x_ref[t, at])
             x_ref[t, at, wide, width] = north[0:over, :, lanes].astype(F32)
 
 
 def field_points(ranges, conv_rows, x_ref, v_ref, main, west, east, south, north, rows, cols):
-    x_ref[...] = jnp.zeros_like(x_ref)
+    if main.shape[1:] == (x_ref.shape[2] - 8, CP):
+        for t in range(2):
+            for lon in (0, x_ref.shape[2] - 8):
+                x_ref[t, :, lon : lon + 8, :] = jnp.zeros_like(x_ref[t, :, lon : lon + 8, :])
+    else:
+        x_ref[...] = jnp.zeros_like(x_ref)
     base = done = 0
     for first, count in ranges:
         span = count * conv_rows + KS - 1
@@ -323,12 +339,16 @@
                  out_ref, gconv_ref, gin_ref, gout_ref, sums_ref, flipped_ref,
                  u_ref, taps_ref, w_ref, win_ref, wout_ref, wo32_ref, conv_ref, act_ref, gpre_ref):
     me = me_ref[0]
-    w_ref[...] = jnp.zeros_like(w_ref)
     window = gathered_ref.shape[1]
+    w_ref[:, 0:8, :] = jnp.zeros_like(w_ref[:, 0:8, :])
+    w_ref[:, starts[-1] :, :] = jnp.zeros_like(w_ref[:, starts[-1] :, :])
     for position, start in zip(order, starts):
         share = gathered_ref[position ^ me].astype(F32)
         for t in range(2):
-            w_ref[t, pl.ds(start, window), :] += share[:, t * LANES : (t + 1) * LANES]
+            part = share[:, t * LANES : (t + 1) * LANES]
+            first = w_ref[t, pl.ds(start, 1), :] + part[0:1]
+            w_ref[t, pl.ds(start, window), :] = part
+            w_ref[t, pl.ds(start, 1), :] = first
     rest = lax.broadcasted_iota(jnp.int32, (CP - C, LANES), 0)
     mains = get_rows(w_ref, 0, C)
     biases = get_rows(w_ref, ROW_BIAS_IN, 1)
@@ -336,9 +356,11 @@
         bias = jnp.where(rest == 0, biases[j], 0.0)
         whole = jnp.concatenate([mains[j], bias], axis=0)
         win_ref[:, j * LANES : (j + 1) * LANES] = whole.astype(BF16)
+    out_rows = get_rows(w_ref, ROW_OUT, C)
+    tail_rows = get_rows(w_ref, ROW_TAPS, 16)
     for quarter in range(4):
-        pair = split_quarter(get_rows(w_ref, ROW_OUT, C), quarter)
-        tail = split_quarter(get_rows(w_ref, ROW_TAPS, 16), quarter)
+        pair = split_quarter(out_rows, quarter)
+        tail = split_quarter(tail_rows, quarter)
         for t in range(2):
             wo32_ref[t, pl.ds(quarter, C, stride=4), :] = pair[t]
             taps_ref[t, pl.ds(quarter, 16, stride=4), :] = tail[t]
@@ -607,11 +629,12 @@
         cost_estimate=cost(1),
         name="edges",
     )(features)
-    west, east = shift_both(*edges, "lon", True)
     for k, group in enumerate(groups):
         parts = [swap(gathered, mask) for mask in group]
+        if k == min(1, len(groups) - 1):
+            west, east = shift_both(*edges, "lon", True)
         if k == max(0, len(groups) - 2):
-            west, east, _, upstream = lax.optimization_barrier((west, east, parts[0], upstream))
+            west, east, _, upstream = lax.optimization_barrier((west, east, gathered, upstream))
             wides = pl.pallas_call(
                 lambda *refs: wide_kernel(rows, cols, *refs),
                 out_shape=(shape((RAD, cols + 2 * RAD, C), BF16),) * 2,
@@ -637,6 +660,8 @@
                 name="inner",
             )(features, west, east, upstream)
         gathered = jnp.concatenate([gathered, *parts], axis=0)
+        if k == 0:
+            edges, _ = lax.optimization_barrier((edges, gathered))
         if k == max(0, len(groups) - 2):
             gathered, inner_data = lax.optimization_barrier((gathered, inner_data))
 
@@ -749,18 +774,20 @@
 
     early = (inner[0][1] + 1) // 2
     for k, group in enumerate(groups[::-1]):
+        if k > 2:
+            values, piece = lax.optimization_barrier((values, piece))
         if k == min(1, len(groups) - 1):
             values, west, east = lax.optimization_barrier((values, west, east))
         part = values.shape[0] // (len(group) + 1)
-        received = [
-            swap(values[(i + 1) * part : (i + 2) * part].astype(BF16), mask)
-            for i, mask in enumerate(group)
-        ]
+        sent = [values[(i + 1) * part : (i + 2) * part].astype(BF16) for i in range(len(group))]
         if k == min(1, len(groups) - 1):
+
             def wide(at):
                 return jnp.concatenate([west[at], gconv[at, :cols, :C], east[at]], axis=1)
 
             wides = (wide(slice(0, RAD)), wide(slice(rows - RAD, rows)))
+        received = [swap(one, mask) for one, mask in zip(sent, group)]
+        if k == min(1, len(groups) - 1):
             piece, _ = field_piece([(margin, early)], (), None, None, False)
         if k == min(2, len(groups) - 1):
             lat_halos = shift_both(*wides, "lat", False)
@@ -768,13 +795,13 @@
             at = margin * conv_rows
             late = [(margin + early, inner[0][1] - early)]
             piece, field = field_piece(late, (), (at, piece), None, False)
-            at = (margin + early) * conv_rows
-            _, field = field_piece(outer, lat_halos, (at, piece), field, True)
         values = values[:part].astype(F32)
         for other in received:
             values = values + other.astype(F32)
         if k == 1 and len(groups) > 2:
             values, wides = lax.optimization_barrier((values, wides))
+    at = (margin + early) * conv_rows
+    _, field = field_piece(outer, lat_halos, (at, piece), field, True)
     summed = lax.dynamic_slice(values.reshape(-1), (offset,), (length,))
     new_params = params - STEP_SIZE * summed + NOISE_COEF * langevin_noise
     return (output, field, new_params)

time: 70.5 us -> 67.6 us (0.959)
  the two profiles are of different devices: /device:TPU:1 before, /device:TPU:0 now
where the time goes in v8:
time: 67.6 us; the launch traced here: 66.3 us
  Pallas kernels  30 us (44%)
  starting transfers between devices  26.4 us (39%)
  waiting for transfers between devices  4.81 us (7%)
  local copies, waits for them, and re-layouts  2.57 us (4%)
  other arithmetic  1.41 us (2%)
  between operations  1.08 us (2%)
    ppermute x12, starting transfers between devices, swap(): return lax.ppermute(values, ('lon', 'lat'), pairs)  18.2 us
    pallas_call x1, Pallas kernels, body(): pl.pallas_call(lambda *refs: layer_kernel(*static, *refs), out_shape=(sha...  13.2 us
    pallas_call x3, Pallas kernels, field_piece(): pl.pallas_call(lambda *refs: field_kernel(ranges, rows, cols, lon_pad, co...  8.39 us
    ppermute x4, starting transfers between devices, send_edges(): far = lax.ppermute(jnp.where(even, low_edge, high_edge), axis, far)  6.45 us
    pallas_call x1, Pallas kernels, body(): pl.pallas_call(lambda *refs: taps_kernel(*static, *refs), out_shape=(shap...  4.11 us
    pallas_call x1, Pallas kernels, body(): pl.pallas_call(lambda *refs: inner_kernel(inner, rows, cols, conv_rows, *...  2.94 us
    ppermute x12, waiting for transfers between devices, swap(): return lax.ppermute(values, ('lon', 'lat'), pairs)  2.62 us
    ppermute x4, waiting for transfers between devices, send_edges(): far = lax.ppermute(jnp.where(even, low_edge, high_edge), axis, far)  2.18 us
  transfers between devices with their start and end apart: 20, of which 7 were waited for; matrix products, arithmetic and copies ran while one was open for 1% of the time, Pallas kernels for 25%

profile of v8, /device:TPU:0, one launch (start us, length us, event | category | flops | bytes accessed | tf_op | source)
XLA Modules:
  0.0 66.3 jit_solution(6021487214057805359)
XLA Ops:
  0.7 0.9 %fusion = bf16[10240]{0:T(1024)(128)(2,1)S(1)} fusion(s32[]{:T(128)S(6)} %select_n.106, f32[9568]{0:T(1024)} %param.5), kind=kLoop, calls=%fused_computation.24 | loop fusion | bytes 58756 | tf_op jit(solution)/shard_map/convert_element_type | solution.py:615
  1.5 4.1 %collective-permute-start = (bf16[1,40,256]{2,1,0:T(8,128)(2,1)S(1)}, bf16[1,40,256]{2,1,0:T(8,128)(2,1)S(1)}, u32[]{:S(2)}, u32[]{:S(2)}) collective-permute-start(bf16[1,40,256]{2,1,0:T(8,128)(2,1)S(1)} %reshape.16), channel_id=1, source_target_pairs={{0,16},{1,17},{2,18},{3,19},{4,20},{5,21},{6,22},{7,23},{8,24},{9,... | collective-permute-start | bytes 61448 | tf_op jit(solution)/shard_map/ppermute | solution.py:60
  5.7 1.2 %copy-done.1 = bf16[45,45,192]{2,1,0:T(8,128)(2,1)S(1)} copy-done((bf16[45,45,192]{2,1,0:T(8,128)(2,1)S(1)}, bf16[45,45,192]{2,1,0:T(8,128)(2,1)}, u32[]{:S(2)}) %copy-start.1) | copy-done | bytes 777624
  6.9 0.2 edges.1
  7.2 0.2 collective-permute-done
  7.4 1.9 %collective-permute-start.1 = (bf16[2,40,256]{2,1,0:T(8,128)(2,1)S(1)}, bf16[2,40,256]{2,1,0:T(8,128)(2,1)S(1)}, u32[]{:S(2)}, u32[]{:S(2)}) collective-permute-start(bf16[2,40,256]{2,1,0:T(8,128)(2,1)S(1)} %get-tuple-element.98), channel_id=1, source_target_pairs={{0,8},{1,9},{2,10},{3,11},{4,12},{5,13},{6,14},{7,15},{8,0},{9,1},... | collective-permute-start | bytes 122888 | tf_op jit(solution)/shard_map/ppermute | solution.py:60
  9.3 0.1 broadcast_select_fusion.6
  9.4 1.6 %collective-permute-start.6 = (bf16[45,3,192]{2,1,0:T(4,128)(2,1)S(1)}, bf16[45,3,192]{2,1,0:T(4,128)(2,1)S(1)}, u32[]{:S(2)}, u32[]{:S(2)}) collective-permute-start(bf16[45,3,192]{2,1,0:T(4,128)(2,1)S(1)} %get-tuple-element.80), channel_id=1, source_target_pairs={{0,4},{4,0},{8,12},{12,8},{16,20},{20,16},{24,28},{28,24},{1,5},{5... | collective-permute-start | bytes 155528 | tf_op jit(solution)/shard_map/ppermute | solution.py:69
  11.0 2.5 %collective-permute-start.5 = (bf16[45,3,192]{2,1,0:T(4,128)(2,1)S(1)}, bf16[45,3,192]{2,1,0:T(4,128)(2,1)S(1)}, u32[]{:S(2)}, u32[]{:S(2)}) collective-permute-start(bf16[45,3,192]{2,1,0:T(4,128)(2,1)S(1)} %get-tuple-element.81), channel_id=1, source_target_pairs={{4,8},{12,16},{20,24},{28,0},{8,4},{16,12},{24,20},{0,28},{5,9},{1... | collective-permute-start | bytes 155528 | tf_op jit(solution)/shard_map/ppermute | solution.py:70
  13.4 0.0 collective-permute-done.1
  13.4 0.9 %collective-permute-start.4 = (bf16[4,40,256]{2,1,0:T(8,128)(2,1)S(1)}, bf16[4,40,256]{2,1,0:T(8,128)(2,1)S(1)}, u32[]{:S(2)}, u32[]{:S(2)}) collective-permute-start(bf16[4,40,256]{2,1,0:T(8,128)(2,1)S(1)} %get-tuple-element.94), channel_id=1, source_target_pairs={{0,6},{1,7},{2,4},{3,5},{4,2},{5,3},{6,0},{7,1},{8,14},{9,15},{10,... | collective-permute-start | bytes 245768 | tf_op jit(solution)/shard_map/ppermute | solution.py:60
  14.3 0.8 %collective-permute-start.3 = (bf16[4,40,256]{2,1,0:T(8,128)(2,1)S(1)}, bf16[4,40,256]{2,1,0:T(8,128)(2,1)S(1)}, u32[]{:S(2)}, u32[]{:S(2)}) collective-permute-start(bf16[4,40,256]{2,1,0:T(8,128)(2,1)S(1)} %get-tuple-element.94), channel_id=1, source_target_pairs={{0,2},{1,3},{2,0},{3,1},{4,6},{5,7},{6,4},{7,5},{8,10},{9,11},{10,... | collective-permute-start | bytes 245768 | tf_op jit(solution)/shard_map/ppermute | solution.py:60
  15.1 1.9 %collective-permute-start.2 = (bf16[4,40,256]{2,1,0:T(8,128)(2,1)S(1)}, bf16[4,40,256]{2,1,0:T(8,128)(2,1)S(1)}, u32[]{:S(2)}, u32[]{:S(2)}) collective-permute-start(bf16[4,40,256]{2,1,0:T(8,128)(2,1)S(1)} %get-tuple-element.94), channel_id=1, source_target_pairs={{0,4},{1,5},{2,6},{3,7},{4,0},{5,1},{6,2},{7,3},{8,12},{9,13},{10,... | collective-permute-start | bytes 245768 | tf_op jit(solution)/shard_map/ppermute | solution.py:60
  17.0 0.0 collective-permute-done.6
  17.0 1.3 %collective-permute-done.5 = bf16[45,3,192]{2,1,0:T(4,128)(2,1)S(1)} collective-permute-done((bf16[45,3,192]{2,1,0:T(4,128)(2,1)S(1)}, bf16[45,3,192]{2,1,0:T(4,128)(2,1)S(1)}, u32[]{:S(2)}, u32[]{:S(2)}) %collective-permute-start.5) | collective-permute-done | bytes 51872 | tf_op jit(solution)/shard_map/ppermute | solution.py:70
  18.3 0.1 broadcast_select_fusion.4
  18.4 0.0 copy-done.2
  18.4 0.0 copy-start
  18.5 0.1 collective-permute-start.9
  18.6 0.8 %collective-permute-start.8 = (bf16[3,51,192]{2,1,0:T(8,128)(2,1)S(1)}, bf16[3,51,192]{2,1,0:T(8,128)(2,1)S(1)}, u32[]{:S(2)}, u32[]{:S(2)}) collective-permute-start(bf16[3,51,192]{2,1,0:T(8,128)(2,1)S(1)} %get-tuple-element.89), channel_id=1, source_target_pairs={{1,2},{2,1},{5,6},{6,5},{9,10},{10,9},{13,14},{14,13},{17,18},{18,... | collective-permute-start | bytes 176264 | tf_op jit(solution)/shard_map/ppermute | solution.py:70
  19.4 0.3 copy-done
  19.7 2.9 %inner.1 = (f32[2,77,56,128]{3,2,1,0:T(8,128)S(1)}, bf16[45,48,256]{2,1,0:T(8,128)(2,1)S(1)}, bf16[45,48,256]{2,1,0:T(8,128)(2,1)S(1)}) custom-call(bf16[45,45,192]{2,1,0:T(8,128)(2,1)S(1)} %copy-done.2, bf16[45,3,192]{2,1,0:T(4,128)(2,1)S(1)} %get-tuple-element.40.refs_1_, bf16[45,3,192]{2,1,0:T(4,128)(2,1)S(1)} %get-tuple-element.41.refs_2_, ...), custom_call_target="tpu_custom_call" | custom-call | flops 2750000128 | tf_op jit(solution)/shard_map/inner/pallas_call | solution.py:648
  22.6 0.0 collective-permute-done.2
  22.6 0.0 collective-permute-done.3
  22.6 0.0 collective-permute-done.4
  22.7 2.7 %collective-permute-start.7 = (bf16[16,40,256]{2,1,0:T(8,128)(2,1)S(1)}, bf16[16,40,256]{2,1,0:T(8,128)(2,1)S(1)}, u32[]{:S(2)}, u32[]{:S(2)}) collective-permute-start(bf16[16,40,256]{2,1,0:T(8,128)(2,1)S(1)} %constant_dynamic-update-slice_fusion.5), channel_id=1, source_target_pairs={{0,1},{1,0},{2,3},{3,2},{4,5},{5,4},{6,7},{7,6},{8,9},{9,8},{10,11... | collective-permute-start | bytes 983048 | tf_op jit(solution)/shard_map/ppermute | solution.py:60
  25.4 0.0 collective-permute-done.9
  25.4 0.0 collective-permute-done.8
  25.4 1.0 %outer.1.refs_3_ = f32[2,22,56,128]{3,2,1,0:T(8,128)S(1)} custom-call(bf16[45,45,192]{2,1,0:T(8,128)(2,1)S(1)} %copy-done.2, bf16[45,3,192]{2,1,0:T(4,128)(2,1)S(1)} %get-tuple-element.40.refs_1_, bf16[45,3,192]{2,1,0:T(4,128)(2,1)S(1)} %get-tuple-element.41.refs_2_, bf16[3,51,192]{2,1,0:T(8,128)(2,1)S(1)} %get-tuple-element.87.refs_3_, ...), custom_call_target="tpu_custom_call" | custom-call | flops 1100000000 | tf_op jit(solution)/shard_map/outer/pallas_call | solution.py:668
  26.4 0.2 collective-permute-done.7
  26.6 0.1 pad_maximum_fusion.refs_1_
  26.7 13.2 %layer.1 = (bf16[45,45,192]{2,1,0:T(8,128)(2,1)S(1)}, bf16[45,48,256]{2,1,0:T(8,128)(2,1)S(1)}, f32[256,768]{1,0:T(8,128)S(1)}, f32[256,768]{1,0:T(8,128)S(1)}, ...) custom-call(s32[1]{0:T(128)} %bitcast.refs_0_, bf16[32,40,256]{2,1,0:T(8,128)(2,1)S(1)} %pad_maximum_fusion.refs_1_, ...), custom_call_target="tpu_custom_call" | custom-call | flops 24199999488 | tf_op jit(solution)/shard_map/layer/pallas_call | solution.py:680
  39.9 0.1 broadcast_select_fusion.2
  40.0 0.1 collective-permute-start.12
  40.1 2.5 %collective-permute-start.11 = (bf16[45,3,192]{2,1,0:T(4,128)(2,1)S(1)}, bf16[45,3,192]{2,1,0:T(4,128)(2,1)S(1)}, u32[]{:S(2)}, u32[]{:S(2)}) collective-permute-start(bf16[45,3,192]{2,1,0:T(4,128)(2,1)S(1)} %get-tuple-element.72), channel_id=1, source_target_pairs={{4,8},{12,16},{20,24},{28,0},{8,4},{16,12},{24,20},{0,28},{5,9},{1... | collective-permute-start | bytes 155528 | tf_op jit(solution)/shard_map/ppermute | solution.py:70
  42.7 4.1 %taps.1 = (bf16[32,40,256]{2,1,0:T(8,128)(2,1)S(1)}, bf16[45,45,192]{2,1,0:T(8,128)(2,1)}) custom-call(s32[1]{0:T(128)} %bitcast.refs_0_, bf16[45,48,256]{2,1,0:T(8,128)(2,1)S(1)} %get-tuple-element.50.refs_1_.refs_2_, f32[2,77,56,128]{3,2,1,0:T(8,128)S(1)} %get-tuple-element.45.refs_2_, f32[2,22,56,128]{3,2,1,0:T(8,128)S(1)} %outer.1.refs_3_, ...), custom_call_target="tpu_custom_call" | custom-call | flops 12099999744 | tf_op jit(solution)/shard_map/taps/pallas_call | solution.py:708
  46.8 0.1 collective-permute-start.10
  47.0 0.0 collective-permute-done.12
  47.0 0.8 %collective-permute-done.11 = bf16[45,3,192]{2,1,0:T(4,128)(2,1)S(1)} collective-permute-done((bf16[45,3,192]{2,1,0:T(4,128)(2,1)S(1)}, bf16[45,3,192]{2,1,0:T(4,128)(2,1)S(1)}, u32[]{:S(2)}, u32[]{:S(2)}) %collective-permute-start.11) | collective-permute-done | bytes 51872 | tf_op jit(solution)/shard_map/ppermute | solution.py:70
  47.8 0.1 broadcast_select_fusion
  47.9 0.6 collective-permute-done.10
  48.5 0.1 convert_add_fusion
  48.6 0.1 collective-permute-start.13
  48.7 2.2 %collective-permute-start.15 = (bf16[4,40,256]{2,1,0:T(8,128)(2,1)S(1)}, bf16[4,40,256]{2,1,0:T(8,128)(2,1)S(1)}, u32[]{:S(2)}, u32[]{:S(2)}) collective-permute-start(bf16[4,40,256]{2,1,0:T(8,128)(2,1)S(1)} %get-tuple-element.74), channel_id=1, source_target_pairs={{0,6},{1,7},{2,4},{3,5},{4,2},{5,3},{6,0},{7,1},{8,14},{9,15},{10,... | collective-permute-start | bytes 245768 | tf_op jit(solution)/shard_map/ppermute | solution.py:60
  50.9 1.3 %collective-permute-start.14 = (bf16[4,40,256]{2,1,0:T(8,128)(2,1)S(1)}, bf16[4,40,256]{2,1,0:T(8,128)(2,1)S(1)}, u32[]{:S(2)}, u32[]{:S(2)}) collective-permute-start(bf16[4,40,256]{2,1,0:T(8,128)(2,1)S(1)} %get-tuple-element.75), channel_id=1, source_target_pairs={{0,2},{1,3},{2,0},{3,1},{4,6},{5,7},{6,4},{7,5},{8,10},{9,11},{10,... | collective-permute-start | bytes 245768 | tf_op jit(solution)/shard_map/ppermute | solution.py:60
  52.2 3.2 %field.3.refs_5_ = bf16[20,45,192]{2,1,0:T(8,128)(2,1)S(1)} custom-call(f32[2,11,8,128]{3,2,1,0:T(8,128)S(1)} %get-tuple-element.56.refs_0_, bf16[45,48,256]{2,1,0:T(8,128)(2,1)S(1)} %get-tuple-element.49.refs_5_.refs_1_, bf16[45,48,256]{2,1,0:T(8,128)(2,1)S(1)} %get-tuple-element.50.refs_1_.refs_2_, bf16[45,3,192]{2,1,0:T(4,128)(2,1)S(1)} %get-tuple-element.58.refs_3_, ...), custom_call_target="tpu_custom_call" | custom-call | flops 4840000000 | tf_op jit(solution)/shard_map/field/pallas_call | solution.py:752
  55.5 0.0 collective-permute-done.13
  55.5 0.0 collective-permute-done.15
  55.5 0.8 %collective-permute-done.14 = bf16[4,40,256]{2,1,0:T(8,128)(2,1)S(1)} collective-permute-done((bf16[4,40,256]{2,1,0:T(8,128)(2,1)S(1)}, bf16[4,40,256]{2,1,0:T(8,128)(2,1)S(1)}, u32[]{:S(2)}, u32[]{:S(2)}) %collective-permute-start.14) | collective-permute-done | bytes 81952 | tf_op jit(solution)/shard_map/ppermute | solution.py:60
  56.4 1.0 %collective-permute-start.18 = (bf16[2,40,256]{2,1,0:T(8,128)(2,1)S(1)}, bf16[2,40,256]{2,1,0:T(8,128)(2,1)S(1)}, u32[]{:S(2)}, u32[]{:S(2)}) collective-permute-start(bf16[2,40,256]{2,1,0:T(8,128)(2,1)S(1)} %slice.92), channel_id=1, source_target_pairs={{0,8},{1,9},{2,10},{3,11},{4,12},{5,13},{6,14},{7,15},{8,0},{9,1},... | collective-permute-start | bytes 122888 | tf_op jit(solution)/shard_map/ppermute | solution.py:60
  57.4 0.1 collective-permute-start.17
  57.5 0.7 %collective-permute-start.16 = (bf16[3,51,192]{2,1,0:T(8,128)(2,1)S(1)}, bf16[3,51,192]{2,1,0:T(8,128)(2,1)S(1)}, u32[]{:S(2)}, u32[]{:S(2)}) collective-permute-start(bf16[3,51,192]{2,1,0:T(8,128)(2,1)S(1)} %get-tuple-element.85), channel_id=1, source_target_pairs={{1,2},{2,1},{5,6},{6,5},{9,10},{10,9},{13,14},{14,13},{17,18},{18,... | collective-permute-start | bytes 176264 | tf_op jit(solution)/shard_map/ppermute | solution.py:70
  58.2 2.5 %field.4 = (bf16[45,45,192]{2,1,0:T(8,128)(2,1)}, bf16[15,45,192]{2,1,0:T(8,128)(2,1)S(1)}) custom-call(f32[2,11,8,128]{3,2,1,0:T(8,128)S(1)} %get-tuple-element.56.refs_0_, bf16[45,48,256]{2,1,0:T(8,128)(2,1)S(1)} %get-tuple-element.49.refs_5_.refs_1_, bf16[45,48,256]{2,1,0:T(8,128)(2,1)S(1)} %get-tuple-element.50.refs_1_.refs_2_, ...), custom_call_target="tpu_custom_call" | custom-call | flops 3630000128 | tf_op jit(solution)/shard_map/field/pallas_call | solution.py:752
  60.7 0.0 collective-permute-done.18
  60.8 1.3 %collective-permute-start.19 = (bf16[1,40,256]{2,1,0:T(8,128)(2,1)S(1)}, bf16[1,40,256]{2,1,0:T(8,128)(2,1)S(1)}, u32[]{:S(2)}, u32[]{:S(2)}) collective-permute-start(bf16[1,40,256]{2,1,0:T(8,128)(2,1)S(1)} %slice.93), channel_id=1, source_target_pairs={{0,16},{1,17},{2,18},{3,19},{4,20},{5,21},{6,22},{7,23},{8,24},{9,... | collective-permute-start | bytes 61448 | tf_op jit(solution)/shard_map/ppermute | solution.py:60
  62.0 0.0 collective-permute-done.17
  62.0 0.0 collective-permute-done.16
  62.0 0.0 copy-start.3
  62.1 0.0 copy-start.4
  62.1 2.6 %field.5 = bf16[45,45,192]{2,1,0:T(8,128)(2,1)} custom-call(f32[2,11,8,128]{3,2,1,0:T(8,128)S(1)} %get-tuple-element.56.refs_0_, bf16[45,48,256]{2,1,0:T(8,128)(2,1)S(1)} %get-tuple-element.49.refs_5_.refs_1_, bf16[45,48,256]{2,1,0:T(8,128)(2,1)S(1)} %get-tuple-element.50.refs_1_.refs_2_, ...), custom_call_target="tpu_custom_call", output_to_operand_aliasing={{}: (8, {})} | custom-call | flops 2420000000 | tf_op jit(solution)/shard_map/field/pallas_call | solution.py:752
  64.7 0.8 %collective-permute-done.19 = bf16[1,40,256]{2,1,0:T(8,128)(2,1)S(1)} collective-permute-done((bf16[1,40,256]{2,1,0:T(8,128)(2,1)S(1)}, bf16[1,40,256]{2,1,0:T(8,128)(2,1)S(1)}, u32[]{:S(2)}, u32[]{:S(2)}) %collective-permute-start.19) | collective-permute-done | bytes 20512 | tf_op jit(solution)/shard_map/ppermute | solution.py:60
  65.5 0.0 copy-done.3
  65.5 0.0 copy-done.4
  65.6 0.7 %multiply_add_fusion = f32[9568]{0:T(1024)} fusion(f32[9568]{0:T(1024)S(1)} %copy-done.4, f32[9568]{0:T(1024)S(1)} %copy-done.3, f32[10240]{0:T(1024)S(1)} %bitcast.4, s32[]{:T(128)S(6)} %select_n.127), kind=kLoop, calls=%fused_computation.26 | loop fusion | flops 38272 | bytes 153092 | tf_op jit(solution)/shard_map/add | solution.py:806
  (27 shorter events, 0.4 us)
Async XLA Ops:
  1.5 5.9 %collective-permute-start = (bf16[1,40,256]{2,1,0:T(8,128)(2,1)S(1)}, bf16[1,40,256]{2,1,0:T(8,128)(2,1)S(1)}, u32[]{:S(2)}, u32[]{:S(2)}) collective-permute-start(bf16[1,40,256]{2,1,0:T(8,128)(2,1)S(1)} %reshape.16), channel_id=1, source_target_pairs={{0,16},{1,17},{2,18},{3,19},{4,20},{5,21},{6,22},{7,23},{8,24},{9,... | collective-permute-start | bytes 61448 | tf_op jit(solution)/shard_map/ppermute | solution.py:60
  5.7 1.2 %copy-start.1 = (bf16[45,45,192]{2,1,0:T(8,128)(2,1)S(1)}, bf16[45,45,192]{2,1,0:T(8,128)(2,1)}, u32[]{:S(2)}) copy-start(bf16[45,45,192]{2,1,0:T(8,128)(2,1)} %refs_0_.7) | copy-start | bytes 2332804
  6.9 11.5 %copy-start.2 = (bf16[45,45,192]{2,1,0:T(8,128)(2,1)S(1)}, bf16[45,45,192]{2,1,0:T(8,128)(2,1)}, u32[]{:S(2)}) copy-start(bf16[45,45,192]{2,1,0:T(8,128)(2,1)} %refs_0_.7) | copy-start | bytes 2332804
  7.4 6.0 %collective-permute-start.1 = (bf16[2,40,256]{2,1,0:T(8,128)(2,1)S(1)}, bf16[2,40,256]{2,1,0:T(8,128)(2,1)S(1)}, u32[]{:S(2)}, u32[]{:S(2)}) collective-permute-start(bf16[2,40,256]{2,1,0:T(8,128)(2,1)S(1)} %get-tuple-element.98), channel_id=1, source_target_pairs={{0,8},{1,9},{2,10},{3,11},{4,12},{5,13},{6,14},{7,15},{8,0},{9,1},... | collective-permute-start | bytes 122888 | tf_op jit(solution)/shard_map/ppermute | solution.py:60
  9.4 7.6 %collective-permute-start.6 = (bf16[45,3,192]{2,1,0:T(4,128)(2,1)S(1)}, bf16[45,3,192]{2,1,0:T(4,128)(2,1)S(1)}, u32[]{:S(2)}, u32[]{:S(2)}) collective-permute-start(bf16[45,3,192]{2,1,0:T(4,128)(2,1)S(1)} %get-tuple-element.80), channel_id=1, source_target_pairs={{0,4},{4,0},{8,12},{12,8},{16,20},{20,16},{24,28},{28,24},{1,5},{5... | collective-permute-start | bytes 155528 | tf_op jit(solution)/shard_map/ppermute | solution.py:69
  11.0 7.4 %collective-permute-start.5 = (bf16[45,3,192]{2,1,0:T(4,128)(2,1)S(1)}, bf16[45,3,192]{2,1,0:T(4,128)(2,1)S(1)}, u32[]{:S(2)}, u32[]{:S(2)}) collective-permute-start(bf16[45,3,192]{2,1,0:T(4,128)(2,1)S(1)} %get-tuple-element.81), channel_id=1, source_target_pairs={{4,8},{12,16},{20,24},{28,0},{8,4},{16,12},{24,20},{0,28},{5,9},{1... | collective-permute-start | bytes 155528 | tf_op jit(solution)/shard_map/ppermute | solution.py:70
  13.4 9.2 %collective-permute-start.4 = (bf16[4,40,256]{2,1,0:T(8,128)(2,1)S(1)}, bf16[4,40,256]{2,1,0:T(8,128)(2,1)S(1)}, u32[]{:S(2)}, u32[]{:S(2)}) collective-permute-start(bf16[4,40,256]{2,1,0:T(8,128)(2,1)S(1)} %get-tuple-element.94), channel_id=1, source_target_pairs={{0,6},{1,7},{2,4},{3,5},{4,2},{5,3},{6,0},{7,1},{8,14},{9,15},{10,... | collective-permute-start | bytes 245768 | tf_op jit(solution)/shard_map/ppermute | solution.py:60
  14.3 8.3 %collective-permute-start.3 = (bf16[4,40,256]{2,1,0:T(8,128)(2,1)S(1)}, bf16[4,40,256]{2,1,0:T(8,128)(2,1)S(1)}, u32[]{:S(2)}, u32[]{:S(2)}) collective-permute-start(bf16[4,40,256]{2,1,0:T(8,128)(2,1)S(1)} %get-tuple-element.94), channel_id=1, source_target_pairs={{0,2},{1,3},{2,0},{3,1},{4,6},{5,7},{6,4},{7,5},{8,10},{9,11},{10,... | collective-permute-start | bytes 245768 | tf_op jit(solution)/shard_map/ppermute | solution.py:60
  15.1 7.5 %collective-permute-start.2 = (bf16[4,40,256]{2,1,0:T(8,128)(2,1)S(1)}, bf16[4,40,256]{2,1,0:T(8,128)(2,1)S(1)}, u32[]{:S(2)}, u32[]{:S(2)}) collective-permute-start(bf16[4,40,256]{2,1,0:T(8,128)(2,1)S(1)} %get-tuple-element.94), channel_id=1, source_target_pairs={{0,4},{1,5},{2,6},{3,7},{4,0},{5,1},{6,2},{7,3},{8,12},{9,13},{10,... | collective-permute-start | bytes 245768 | tf_op jit(solution)/shard_map/ppermute | solution.py:60
  18.4 1.2 %copy-start = (bf16[45,45,192]{2,1,0:T(8,128)(2,1)S(1)}, bf16[45,45,192]{2,1,0:T(8,128)(2,1)}, u32[]{:S(2)}) copy-start(bf16[45,45,192]{2,1,0:T(8,128)(2,1)} %refs_3_) | copy-start | bytes 2332804
  18.5 6.9 %collective-permute-start.9 = (bf16[3,51,192]{2,1,0:T(8,128)(2,1)S(1)}, bf16[3,51,192]{2,1,0:T(8,128)(2,1)S(1)}, u32[]{:S(2)}, u32[]{:S(2)}) collective-permute-start(bf16[3,51,192]{2,1,0:T(8,128)(2,1)S(1)} %get-tuple-element.88), channel_id=1, source_target_pairs={{0,1},{1,0},{2,3},{3,2},{4,5},{5,4},{6,7},{7,6},{8,9},{9,8},{10,11... | collective-permute-start | bytes 176264 | tf_op jit(solution)/shard_map/ppermute | solution.py:69
  18.6 6.8 %collective-permute-start.8 = (bf16[3,51,192]{2,1,0:T(8,128)(2,1)S(1)}, bf16[3,51,192]{2,1,0:T(8,128)(2,1)S(1)}, u32[]{:S(2)}, u32[]{:S(2)}) collective-permute-start(bf16[3,51,192]{2,1,0:T(8,128)(2,1)S(1)} %get-tuple-element.89), channel_id=1, source_target_pairs={{1,2},{2,1},{5,6},{6,5},{9,10},{10,9},{13,14},{14,13},{17,18},{18,... | collective-permute-start | bytes 176264 | tf_op jit(solution)/shard_map/ppermute | solution.py:70
  22.7 3.9 %collective-permute-start.7 = (bf16[16,40,256]{2,1,0:T(8,128)(2,1)S(1)}, bf16[16,40,256]{2,1,0:T(8,128)(2,1)S(1)}, u32[]{:S(2)}, u32[]{:S(2)}) collective-permute-start(bf16[16,40,256]{2,1,0:T(8,128)(2,1)S(1)} %constant_dynamic-update-slice_fusion.5), channel_id=1, source_target_pairs={{0,1},{1,0},{2,3},{3,2},{4,5},{5,4},{6,7},{7,6},{8,9},{9,8},{10,11... | collective-permute-start | bytes 983048 | tf_op jit(solution)/shard_map/ppermute | solution.py:60
  40.0 6.9 %collective-permute-start.12 = (bf16[45,3,192]{2,1,0:T(4,128)(2,1)S(1)}, bf16[45,3,192]{2,1,0:T(4,128)(2,1)S(1)}, u32[]{:S(2)}, u32[]{:S(2)}) collective-permute-start(bf16[45,3,192]{2,1,0:T(4,128)(2,1)S(1)} %get-tuple-element.71), channel_id=1, source_target_pairs={{0,4},{4,0},{8,12},{12,8},{16,20},{20,16},{24,28},{28,24},{1,5},{5... | collective-permute-start | bytes 155528 | tf_op jit(solution)/shard_map/ppermute | solution.py:69
  40.1 7.7 %collective-permute-start.11 = (bf16[45,3,192]{2,1,0:T(4,128)(2,1)S(1)}, bf16[45,3,192]{2,1,0:T(4,128)(2,1)S(1)}, u32[]{:S(2)}, u32[]{:S(2)}) collective-permute-start(bf16[45,3,192]{2,1,0:T(4,128)(2,1)S(1)} %get-tuple-element.72), channel_id=1, source_target_pairs={{4,8},{12,16},{20,24},{28,0},{8,4},{16,12},{24,20},{0,28},{5,9},{1... | collective-permute-start | bytes 155528 | tf_op jit(solution)/shard_map/ppermute | solution.py:70
  46.8 1.7 %collective-permute-start.10 = (bf16[16,40,256]{2,1,0:T(8,128)(2,1)S(1)}, bf16[16,40,256]{2,1,0:T(8,128)(2,1)S(1)}, u32[]{:S(2)}, u32[]{:S(2)}) collective-permute-start(bf16[16,40,256]{2,1,0:T(8,128)(2,1)S(1)} %slice.60), channel_id=1, source_target_pairs={{0,1},{1,0},{2,3},{3,2},{4,5},{5,4},{6,7},{7,6},{8,9},{9,8},{10,11... | collective-permute-start | bytes 983048 | tf_op jit(solution)/shard_map/ppermute | solution.py:60
  48.6 6.9 %collective-permute-start.13 = (bf16[4,40,256]{2,1,0:T(8,128)(2,1)S(1)}, bf16[4,40,256]{2,1,0:T(8,128)(2,1)S(1)}, u32[]{:S(2)}, u32[]{:S(2)}) collective-permute-start(bf16[4,40,256]{2,1,0:T(8,128)(2,1)S(1)} %get-tuple-element.73), channel_id=1, source_target_pairs={{0,4},{1,5},{2,6},{3,7},{4,0},{5,1},{6,2},{7,3},{8,12},{9,13},{10,... | collective-permute-start | bytes 245768 | tf_op jit(solution)/shard_map/ppermute | solution.py:60
  48.7 6.8 %collective-permute-start.15 = (bf16[4,40,256]{2,1,0:T(8,128)(2,1)S(1)}, bf16[4,40,256]{2,1,0:T(8,128)(2,1)S(1)}, u32[]{:S(2)}, u32[]{:S(2)}) collective-permute-start(bf16[4,40,256]{2,1,0:T(8,128)(2,1)S(1)} %get-tuple-element.74), channel_id=1, source_target_pairs={{0,6},{1,7},{2,4},{3,5},{4,2},{5,3},{6,0},{7,1},{8,14},{9,15},{10,... | collective-permute-start | bytes 245768 | tf_op jit(solution)/shard_map/ppermute | solution.py:60
  50.9 5.4 %collective-permute-start.14 = (bf16[4,40,256]{2,1,0:T(8,128)(2,1)S(1)}, bf16[4,40,256]{2,1,0:T(8,128)(2,1)S(1)}, u32[]{:S(2)}, u32[]{:S(2)}) collective-permute-start(bf16[4,40,256]{2,1,0:T(8,128)(2,1)S(1)} %get-tuple-element.75), channel_id=1, source_target_pairs={{0,2},{1,3},{2,0},{3,1},{4,6},{5,7},{6,4},{7,5},{8,10},{9,11},{10,... | collective-permute-start | bytes 245768 | tf_op jit(solution)/shard_map/ppermute | solution.py:60
  56.4 4.3 %collective-permute-start.18 = (bf16[2,40,256]{2,1,0:T(8,128)(2,1)S(1)}, bf16[2,40,256]{2,1,0:T(8,128)(2,1)S(1)}, u32[]{:S(2)}, u32[]{:S(2)}) collective-permute-start(bf16[2,40,256]{2,1,0:T(8,128)(2,1)S(1)} %slice.92), channel_id=1, source_target_pairs={{0,8},{1,9},{2,10},{3,11},{4,12},{5,13},{6,14},{7,15},{8,0},{9,1},... | collective-permute-start | bytes 122888 | tf_op jit(solution)/shard_map/ppermute | solution.py:60
  57.4 4.6 %collective-permute-start.17 = (bf16[3,51,192]{2,1,0:T(8,128)(2,1)S(1)}, bf16[3,51,192]{2,1,0:T(8,128)(2,1)S(1)}, u32[]{:S(2)}, u32[]{:S(2)}) collective-permute-start(bf16[3,51,192]{2,1,0:T(8,128)(2,1)S(1)} %get-tuple-element.84), channel_id=1, source_target_pairs={{0,1},{1,0},{2,3},{3,2},{4,5},{5,4},{6,7},{7,6},{8,9},{9,8},{10,11... | collective-permute-start | bytes 176264 | tf_op jit(solution)/shard_map/ppermute | solution.py:69
  57.5 4.5 %collective-permute-start.16 = (bf16[3,51,192]{2,1,0:T(8,128)(2,1)S(1)}, bf16[3,51,192]{2,1,0:T(8,128)(2,1)S(1)}, u32[]{:S(2)}, u32[]{:S(2)}) collective-permute-start(bf16[3,51,192]{2,1,0:T(8,128)(2,1)S(1)} %get-tuple-element.85), channel_id=1, source_target_pairs={{1,2},{2,1},{5,6},{6,5},{9,10},{10,9},{13,14},{14,13},{17,18},{18,... | collective-permute-start | bytes 176264 | tf_op jit(solution)/shard_map/ppermute | solution.py:70
  60.8 4.7 %collective-permute-start.19 = (bf16[1,40,256]{2,1,0:T(8,128)(2,1)S(1)}, bf16[1,40,256]{2,1,0:T(8,128)(2,1)S(1)}, u32[]{:S(2)}, u32[]{:S(2)}) collective-permute-start(bf16[1,40,256]{2,1,0:T(8,128)(2,1)S(1)} %slice.93), channel_id=1, source_target_pairs={{0,16},{1,17},{2,18},{3,19},{4,20},{5,21},{6,22},{7,23},{8,24},{9,... | collective-permute-start | bytes 61448 | tf_op jit(solution)/shard_map/ppermute | solution.py:60
  62.0 3.5 %copy-start.3 = (f32[9568]{0:T(1024)S(1)}, f32[9568]{0:T(1024)}, u32[]{:S(2)}) copy-start(f32[9568]{0:T(1024)} %param.5) | copy-start | bytes 114820
  62.1 3.5 %copy-start.4 = (f32[9568]{0:T(1024)S(1)}, f32[9568]{0:T(1024)}, u32[]{:S(2)}) copy-start(f32[9568]{0:T(1024)} %param.6) | copy-start | bytes 114820

commit v9 on v8

--- a/solution.py
+++ b/solution.py
@@ -30,6 +30,7 @@
 TILES = H // LANES
 SHARE_LANES = 256
 CHUNK = 256
+GIN_ROWS = C + 8
 ALL = ((1,), (1,)), ((), ())
 OVER = ((0,), (0,)), ((), ())
 VMEM = 28 << 20
@@ -287,7 +288,7 @@
                 v_ref[tile, (done + k) * count + i, lon, :] = value
             return carry
 
-        return lax.fori_loop(0, blocks, block, carry, unroll=blocks <= 4)
+        return lax.fori_loop(0, blocks, block, carry, unroll=True)
 
     lax.fori_loop(0, 2 * lon_regs, body, 0)
 
@@ -301,7 +302,7 @@
             )
 
 
-def depthwise_block(v_ref, u_ref, block, out_rows, lon_pad, store, flip):
+def depthwise_block(v_ref, u_ref, block, out_rows, lon_pad, store, flip, unroll):
     pairs, filters = points_for(out_rows)
     count = len(filters)
     chunk = lon_pad
@@ -331,7 +332,7 @@
         store(tile, lon, chunk, sums)
         return carry
 
-    lax.fori_loop(0, 2 * (lon_pad // chunk), body, 0)
+    lax.fori_loop(0, 2 * (lon_pad // chunk), body, 0, unroll=unroll)
 
 
 def layer_kernel(order, starts, rows, lon_pad, block_rows, conv_rows, inner, outer,
@@ -397,7 +398,7 @@
                 for r in range(conv_rows):
                     conv_ref[tile, block * conv_rows + r, pl.ds(lon, chunk), :] = sums[r]
 
-            depthwise_block(v_ref, u_ref, place, conv_rows, lon_pad, store, False)
+            depthwise_block(v_ref, u_ref, place, conv_rows, lon_pad, store, False, False)
 
         over_blocks(ranges, conv_step)
 
@@ -432,8 +433,12 @@
         gpre = gpre_ref[...]
         branch = jnp.dot(act, wout_ref[...], preferred_element_type=F32)
         gnormed = lax.dot_general(gpre, win_ref[...], ALL, preferred_element_type=F32)
-        gin_ref[...] += lax.dot_general(normed, gpre, OVER, preferred_element_type=F32)
-        gout_ref[...] += lax.dot_general(gbranch, act, OVER, preferred_element_type=F32)
+        gin_ref[...] += lax.dot_general(
+            normed[:, :GIN_ROWS], gpre, OVER, preferred_element_type=F32
+        )
+        gout_ref[...] += lax.dot_general(
+            gbranch[:, :C], act, OVER, preferred_element_type=F32
+        )
         outs = []
         gs = []
         gn = []
@@ -493,7 +498,7 @@
                         acc_ref[tile, k, b] += term.reshape(lon_pad // 8, 8, LANES).sum(axis=0)
                 return carry
 
-            lax.fori_loop(0, 2, side, 0)
+            lax.fori_loop(0, 2, side, 0, unroll=True)
 
         over_blocks(ranges, step)
 
@@ -505,7 +510,8 @@
             small_ref[t, pl.ds(a * KS, KS), :] = weighted([f[a] for f in filters], totals)
         for at, k in ((TAPS, 0), (TAPS + 1, 1), (TAPS + 2, 2), (TAPS + 7, 3), (TAPS + 8, 4)):
             small_ref[t, pl.ds(at, 1), :] = jnp.sum(sums_ref[k, t], axis=0, keepdims=True)
-        wo32_ref[t] = gout_ref[pl.ds(t * LANES, LANES), :].T
+        width = min(C, (t + 1) * LANES) - t * LANES
+        wo32_ref[t, :, 0:width] = gout_ref[pl.ds(t * LANES, width), :].T
     outs = join_quarters(
         [[wo32_ref[t, pl.ds(q, C, stride=4), :] for t in range(2)] for q in range(4)]
     )
@@ -556,7 +562,7 @@
                 total = sums[r] + up_ref[row + r, pl.ds(lon, chunk), lanes].astype(F32)
                 sum_ref[r, pl.ds(lon, chunk), lanes] = total
 
-        depthwise_block(v_ref, u_ref, place, conv_rows, lon_pad, store, True)
+        depthwise_block(v_ref, u_ref, place, conv_rows, lon_pad, store, True, True)
         out_ref[pl.ds(place * conv_rows, conv_rows)] = sum_ref[:, 0:cols, 0:C].astype(BF16)
         if last:
             out_copy(place, block).start()
@@ -682,8 +688,8 @@
         out_shape=(
             shape((rows, cols, C), BF16),
             shape((rows, lon_pad, CP), BF16),
-            shape((CP, H), F32),
-            shape((CP, H), F32),
+            shape((GIN_ROWS, H), F32),
+            shape((C, H), F32),
             shape((5, 2, 8, LANES), F32),
             shape((2, points, 8, LANES), F32),
         ),

time: 67.6 us -> 66.3 us (0.981)
  Pallas kernels: 30 us -> 27.8 us
  waiting for transfers between devices: 4.81 us -> 6.31 us
    ppermute x12, waiting for transfers between devices: 2.62 us -> 4.09 us  [swap(): return lax.ppermute(values, ('lon', 'lat'), pairs)]
    pallas_call x3, Pallas kernels: 8.39 us -> 7.14 us  [field_piece(): pl.pallas_call(lambda *refs: field_kernel(ranges, rows, cols, lon_pad, co...]
    pallas_call x1, Pallas kernels: 2.94 us -> 2.25 us  [body(): pl.pallas_call(lambda *refs: inner_kernel(inner, rows, cols, conv_rows, *...]
  transfers between devices with their start and end apart: 20 -> 20, of which waited for: 7 -> 9; matrix products, arithmetic and copies ran while one was open for 1% -> 1% of each run, Pallas kernels for 25% -> 23%
where the time goes in v9:
time: 66.3 us; the launch traced here: 65.5 us
  Pallas kernels  27.8 us (42%)
  starting transfers between devices  26.3 us (40%)
  waiting for transfers between devices  6.31 us (10%)
  local copies, waits for them, and re-layouts  2.57 us (4%)
  other arithmetic  1.41 us (2%)
  between operations  1.06 us (2%)
    ppermute x12, starting transfers between devices, swap(): return lax.ppermute(values, ('lon', 'lat'), pairs)  18.1 us
    pallas_call x1, Pallas kernels, body(): pl.pallas_call(lambda *refs: layer_kernel(*static, *refs), out_shape=(sha...  13 us
    pallas_call x3, Pallas kernels, field_piece(): pl.pallas_call(lambda *refs: field_kernel(ranges, rows, cols, lon_pad, co...  7.14 us
    ppermute x4, starting transfers between devices, send_edges(): far = lax.ppermute(jnp.where(even, low_edge, high_edge), axis, far)  6.45 us
    pallas_call x1, Pallas kernels, body(): pl.pallas_call(lambda *refs: taps_kernel(*static, *refs), out_shape=(shap...  4.09 us
    ppermute x12, waiting for transfers between devices, swap(): return lax.ppermute(values, ('lon', 'lat'), pairs)  4.09 us
    pallas_call x1, Pallas kernels, body(): pl.pallas_call(lambda *refs: inner_kernel(inner, rows, cols, conv_rows, *...  2.25 us
    ppermute x4, waiting for transfers between devices, send_edges(): far = lax.ppermute(jnp.where(even, low_edge, high_edge), axis, far)  2.21 us
  transfers between devices with their start and end apart: 20, of which 9 were waited for; matrix products, arithmetic and copies ran while one was open for 1% of the time, Pallas kernels for 23%

profile of v9, /device:TPU:0, one launch (start us, length us, event | category | flops | bytes accessed | tf_op | source)
XLA Modules:
  0.0 65.5 jit_solution(14784340825857784101)
XLA Ops:
  0.7 0.9 %fusion = bf16[10240]{0:T(1024)(128)(2,1)S(1)} fusion(s32[]{:T(128)S(6)} %select_n.106, f32[9568]{0:T(1024)} %param.5), kind=kLoop, calls=%fused_computation.24 | loop fusion | bytes 58756 | tf_op jit(solution)/shard_map/convert_element_type | solution.py:621
  1.5 4.1 %collective-permute-start = (bf16[1,40,256]{2,1,0:T(8,128)(2,1)S(1)}, bf16[1,40,256]{2,1,0:T(8,128)(2,1)S(1)}, u32[]{:S(2)}, u32[]{:S(2)}) collective-permute-start(bf16[1,40,256]{2,1,0:T(8,128)(2,1)S(1)} %reshape.16), channel_id=1, source_target_pairs={{0,16},{1,17},{2,18},{3,19},{4,20},{5,21},{6,22},{7,23},{8,24},{9,... | collective-permute-start | bytes 61448 | tf_op jit(solution)/shard_map/ppermute | solution.py:61
  5.7 1.2 %copy-done.1 = bf16[45,45,192]{2,1,0:T(8,128)(2,1)S(1)} copy-done((bf16[45,45,192]{2,1,0:T(8,128)(2,1)S(1)}, bf16[45,45,192]{2,1,0:T(8,128)(2,1)}, u32[]{:S(2)}) %copy-start.1) | copy-done | bytes 777624
  6.9 0.2 edges.1
  7.2 0.2 collective-permute-done
  7.4 1.9 %collective-permute-start.1 = (bf16[2,40,256]{2,1,0:T(8,128)(2,1)S(1)}, bf16[2,40,256]{2,1,0:T(8,128)(2,1)S(1)}, u32[]{:S(2)}, u32[]{:S(2)}) collective-permute-start(bf16[2,40,256]{2,1,0:T(8,128)(2,1)S(1)} %get-tuple-element.98), channel_id=1, source_target_pairs={{0,8},{1,9},{2,10},{3,11},{4,12},{5,13},{6,14},{7,15},{8,0},{9,1},... | collective-permute-start | bytes 122888 | tf_op jit(solution)/shard_map/ppermute | solution.py:61
  9.3 0.1 broadcast_select_fusion.6
  9.4 1.6 %collective-permute-start.6 = (bf16[45,3,192]{2,1,0:T(4,128)(2,1)S(1)}, bf16[45,3,192]{2,1,0:T(4,128)(2,1)S(1)}, u32[]{:S(2)}, u32[]{:S(2)}) collective-permute-start(bf16[45,3,192]{2,1,0:T(4,128)(2,1)S(1)} %get-tuple-element.80), channel_id=1, source_target_pairs={{0,4},{4,0},{8,12},{12,8},{16,20},{20,16},{24,28},{28,24},{1,5},{5... | collective-permute-start | bytes 155528 | tf_op jit(solution)/shard_map/ppermute | solution.py:70
  11.0 2.5 %collective-permute-start.5 = (bf16[45,3,192]{2,1,0:T(4,128)(2,1)S(1)}, bf16[45,3,192]{2,1,0:T(4,128)(2,1)S(1)}, u32[]{:S(2)}, u32[]{:S(2)}) collective-permute-start(bf16[45,3,192]{2,1,0:T(4,128)(2,1)S(1)} %get-tuple-element.81), channel_id=1, source_target_pairs={{4,8},{12,16},{20,24},{28,0},{8,4},{16,12},{24,20},{0,28},{5,9},{1... | collective-permute-start | bytes 155528 | tf_op jit(solution)/shard_map/ppermute | solution.py:71
  13.4 0.0 collective-permute-done.1
  13.4 0.9 %collective-permute-start.4 = (bf16[4,40,256]{2,1,0:T(8,128)(2,1)S(1)}, bf16[4,40,256]{2,1,0:T(8,128)(2,1)S(1)}, u32[]{:S(2)}, u32[]{:S(2)}) collective-permute-start(bf16[4,40,256]{2,1,0:T(8,128)(2,1)S(1)} %get-tuple-element.94), channel_id=1, source_target_pairs={{0,6},{1,7},{2,4},{3,5},{4,2},{5,3},{6,0},{7,1},{8,14},{9,15},{10,... | collective-permute-start | bytes 245768 | tf_op jit(solution)/shard_map/ppermute | solution.py:61
  14.3 0.8 %collective-permute-start.3 = (bf16[4,40,256]{2,1,0:T(8,128)(2,1)S(1)}, bf16[4,40,256]{2,1,0:T(8,128)(2,1)S(1)}, u32[]{:S(2)}, u32[]{:S(2)}) collective-permute-start(bf16[4,40,256]{2,1,0:T(8,128)(2,1)S(1)} %get-tuple-element.94), channel_id=1, source_target_pairs={{0,2},{1,3},{2,0},{3,1},{4,6},{5,7},{6,4},{7,5},{8,10},{9,11},{10,... | collective-permute-start | bytes 245768 | tf_op jit(solution)/shard_map/ppermute | solution.py:61
  15.1 1.9 %collective-permute-start.2 = (bf16[4,40,256]{2,1,0:T(8,128)(2,1)S(1)}, bf16[4,40,256]{2,1,0:T(8,128)(2,1)S(1)}, u32[]{:S(2)}, u32[]{:S(2)}) collective-permute-start(bf16[4,40,256]{2,1,0:T(8,128)(2,1)S(1)} %get-tuple-element.94), channel_id=1, source_target_pairs={{0,4},{1,5},{2,6},{3,7},{4,0},{5,1},{6,2},{7,3},{8,12},{9,13},{10,... | collective-permute-start | bytes 245768 | tf_op jit(solution)/shard_map/ppermute | solution.py:61
  17.0 0.0 collective-permute-done.6
  17.0 1.3 %collective-permute-done.5 = bf16[45,3,192]{2,1,0:T(4,128)(2,1)S(1)} collective-permute-done((bf16[45,3,192]{2,1,0:T(4,128)(2,1)S(1)}, bf16[45,3,192]{2,1,0:T(4,128)(2,1)S(1)}, u32[]{:S(2)}, u32[]{:S(2)}) %collective-permute-start.5) | collective-permute-done | bytes 51872 | tf_op jit(solution)/shard_map/ppermute | solution.py:71
  18.3 0.1 broadcast_select_fusion.4
  18.4 0.0 copy-done.2
  18.4 0.0 copy-start
  18.5 0.1 collective-permute-start.9
  18.6 0.8 %collective-permute-start.8 = (bf16[3,51,192]{2,1,0:T(8,128)(2,1)S(1)}, bf16[3,51,192]{2,1,0:T(8,128)(2,1)S(1)}, u32[]{:S(2)}, u32[]{:S(2)}) collective-permute-start(bf16[3,51,192]{2,1,0:T(8,128)(2,1)S(1)} %get-tuple-element.89), channel_id=1, source_target_pairs={{1,2},{2,1},{5,6},{6,5},{9,10},{10,9},{13,14},{14,13},{17,18},{18,... | collective-permute-start | bytes 176264 | tf_op jit(solution)/shard_map/ppermute | solution.py:71
  19.4 0.3 copy-done
  19.7 2.3 %inner.1 = (f32[2,77,56,128]{3,2,1,0:T(8,128)S(1)}, bf16[45,48,256]{2,1,0:T(8,128)(2,1)S(1)}, bf16[45,48,256]{2,1,0:T(8,128)(2,1)S(1)}) custom-call(bf16[45,45,192]{2,1,0:T(8,128)(2,1)S(1)} %copy-done.2, bf16[45,3,192]{2,1,0:T(4,128)(2,1)S(1)} %get-tuple-element.40.refs_1_, bf16[45,3,192]{2,1,0:T(4,128)(2,1)S(1)} %get-tuple-element.41.refs_2_, ...), custom_call_target="tpu_custom_call" | custom-call | flops 2750000128 | tf_op jit(solution)/shard_map/inner/pallas_call | solution.py:654
  21.9 0.0 collective-permute-done.2
  21.9 0.0 collective-permute-done.3
  22.0 0.0 collective-permute-done.4
  22.0 2.7 %collective-permute-start.7 = (bf16[16,40,256]{2,1,0:T(8,128)(2,1)S(1)}, bf16[16,40,256]{2,1,0:T(8,128)(2,1)S(1)}, u32[]{:S(2)}, u32[]{:S(2)}) collective-permute-start(bf16[16,40,256]{2,1,0:T(8,128)(2,1)S(1)} %constant_dynamic-update-slice_fusion.5), channel_id=1, source_target_pairs={{0,1},{1,0},{2,3},{3,2},{4,5},{5,4},{6,7},{7,6},{8,9},{9,8},{10,11... | collective-permute-start | bytes 983048 | tf_op jit(solution)/shard_map/ppermute | solution.py:61
  24.7 0.0 collective-permute-done.9
  24.7 0.0 collective-permute-done.8
  24.7 1.0 %outer.1.refs_3_ = f32[2,22,56,128]{3,2,1,0:T(8,128)S(1)} custom-call(bf16[45,45,192]{2,1,0:T(8,128)(2,1)S(1)} %copy-done.2, bf16[45,3,192]{2,1,0:T(4,128)(2,1)S(1)} %get-tuple-element.40.refs_1_, bf16[45,3,192]{2,1,0:T(4,128)(2,1)S(1)} %get-tuple-element.41.refs_2_, bf16[3,51,192]{2,1,0:T(8,128)(2,1)S(1)} %get-tuple-element.87.refs_3_, ...), custom_call_target="tpu_custom_call" | custom-call | flops 1100000000 | tf_op jit(solution)/shard_map/outer/pallas_call | solution.py:674
  25.7 0.2 collective-permute-done.7
  25.9 0.1 pad_maximum_fusion.refs_1_
  26.0 13.0 %layer.1 = (bf16[45,45,192]{2,1,0:T(8,128)(2,1)S(1)}, bf16[45,48,256]{2,1,0:T(8,128)(2,1)S(1)}, f32[200,768]{1,0:T(8,128)S(1)}, f32[192,768]{1,0:T(8,128)S(1)}, ...) custom-call(s32[1]{0:T(128)} %bitcast.refs_0_, bf16[32,40,256]{2,1,0:T(8,128)(2,1)S(1)} %pad_maximum_fusion.refs_1_, ...), custom_call_target="tpu_custom_call" | custom-call | flops 24199999488 | tf_op jit(solution)/shard_map/layer/pallas_call | solution.py:686
  39.0 0.1 broadcast_select_fusion.2
  39.1 0.1 collective-permute-start.12
  39.2 2.5 %collective-permute-start.11 = (bf16[45,3,192]{2,1,0:T(4,128)(2,1)S(1)}, bf16[45,3,192]{2,1,0:T(4,128)(2,1)S(1)}, u32[]{:S(2)}, u32[]{:S(2)}) collective-permute-start(bf16[45,3,192]{2,1,0:T(4,128)(2,1)S(1)} %get-tuple-element.72), channel_id=1, source_target_pairs={{4,8},{12,16},{20,24},{28,0},{8,4},{16,12},{24,20},{0,28},{5,9},{1... | collective-permute-start | bytes 155528 | tf_op jit(solution)/shard_map/ppermute | solution.py:71
  41.7 4.1 %taps.1 = (bf16[32,40,256]{2,1,0:T(8,128)(2,1)S(1)}, bf16[45,45,192]{2,1,0:T(8,128)(2,1)}) custom-call(s32[1]{0:T(128)} %bitcast.refs_0_, bf16[45,48,256]{2,1,0:T(8,128)(2,1)S(1)} %get-tuple-element.50.refs_1_.refs_2_, f32[2,77,56,128]{3,2,1,0:T(8,128)S(1)} %get-tuple-element.45.refs_2_, f32[2,22,56,128]{3,2,1,0:T(8,128)S(1)} %outer.1.refs_3_, ...), custom_call_target="tpu_custom_call" | custom-call | flops 12099999744 | tf_op jit(solution)/shard_map/taps/pallas_call | solution.py:714
  45.9 0.1 collective-permute-start.10
  46.0 0.0 collective-permute-done.12
  46.0 0.9 %collective-permute-done.11 = bf16[45,3,192]{2,1,0:T(4,128)(2,1)S(1)} collective-permute-done((bf16[45,3,192]{2,1,0:T(4,128)(2,1)S(1)}, bf16[45,3,192]{2,1,0:T(4,128)(2,1)S(1)}, u32[]{:S(2)}, u32[]{:S(2)}) %collective-permute-start.11) | collective-permute-done | bytes 51872 | tf_op jit(solution)/shard_map/ppermute | solution.py:71
  46.9 0.1 broadcast_select_fusion
  47.0 0.6 collective-permute-done.10
  47.6 0.1 convert_add_fusion
  47.7 0.1 collective-permute-start.13
  47.8 2.6 %collective-permute-start.15 = (bf16[4,40,256]{2,1,0:T(8,128)(2,1)S(1)}, bf16[4,40,256]{2,1,0:T(8,128)(2,1)S(1)}, u32[]{:S(2)}, u32[]{:S(2)}) collective-permute-start(bf16[4,40,256]{2,1,0:T(8,128)(2,1)S(1)} %get-tuple-element.74), channel_id=1, source_target_pairs={{0,6},{1,7},{2,4},{3,5},{4,2},{5,3},{6,0},{7,1},{8,14},{9,15},{10,... | collective-permute-start | bytes 245768 | tf_op jit(solution)/shard_map/ppermute | solution.py:61
  50.4 0.9 %collective-permute-start.14 = (bf16[4,40,256]{2,1,0:T(8,128)(2,1)S(1)}, bf16[4,40,256]{2,1,0:T(8,128)(2,1)S(1)}, u32[]{:S(2)}, u32[]{:S(2)}) collective-permute-start(bf16[4,40,256]{2,1,0:T(8,128)(2,1)S(1)} %get-tuple-element.75), channel_id=1, source_target_pairs={{0,2},{1,3},{2,0},{3,1},{4,6},{5,7},{6,4},{7,5},{8,10},{9,11},{10,... | collective-permute-start | bytes 245768 | tf_op jit(solution)/shard_map/ppermute | solution.py:61
  51.3 2.7 %field.3.refs_5_ = bf16[20,45,192]{2,1,0:T(8,128)(2,1)S(1)} custom-call(f32[2,11,8,128]{3,2,1,0:T(8,128)S(1)} %get-tuple-element.56.refs_0_, bf16[45,48,256]{2,1,0:T(8,128)(2,1)S(1)} %get-tuple-element.49.refs_5_.refs_1_, bf16[45,48,256]{2,1,0:T(8,128)(2,1)S(1)} %get-tuple-element.50.refs_1_.refs_2_, bf16[45,3,192]{2,1,0:T(4,128)(2,1)S(1)} %get-tuple-element.58.refs_3_, ...), custom_call_target="tpu_custom_call" | custom-call | flops 4840000000 | tf_op jit(solution)/shard_map/field/pallas_call | solution.py:758
  54.0 0.0 collective-permute-done.13
  54.1 0.6 collective-permute-done.15
  54.7 1.1 %collective-permute-done.14 = bf16[4,40,256]{2,1,0:T(8,128)(2,1)S(1)} collective-permute-done((bf16[4,40,256]{2,1,0:T(8,128)(2,1)S(1)}, bf16[4,40,256]{2,1,0:T(8,128)(2,1)S(1)}, u32[]{:S(2)}, u32[]{:S(2)}) %collective-permute-start.14) | collective-permute-done | bytes 81952 | tf_op jit(solution)/shard_map/ppermute | solution.py:61
  55.9 1.0 %collective-permute-start.18 = (bf16[2,40,256]{2,1,0:T(8,128)(2,1)S(1)}, bf16[2,40,256]{2,1,0:T(8,128)(2,1)S(1)}, u32[]{:S(2)}, u32[]{:S(2)}) collective-permute-start(bf16[2,40,256]{2,1,0:T(8,128)(2,1)S(1)} %slice.92), channel_id=1, source_target_pairs={{0,8},{1,9},{2,10},{3,11},{4,12},{5,13},{6,14},{7,15},{8,0},{9,1},... | collective-permute-start | bytes 122888 | tf_op jit(solution)/shard_map/ppermute | solution.py:61
  56.9 0.1 collective-permute-start.17
  57.0 0.7 %collective-permute-start.16 = (bf16[3,51,192]{2,1,0:T(8,128)(2,1)S(1)}, bf16[3,51,192]{2,1,0:T(8,128)(2,1)S(1)}, u32[]{:S(2)}, u32[]{:S(2)}) collective-permute-start(bf16[3,51,192]{2,1,0:T(8,128)(2,1)S(1)} %get-tuple-element.85), channel_id=1, source_target_pairs={{1,2},{2,1},{5,6},{6,5},{9,10},{10,9},{13,14},{14,13},{17,18},{18,... | collective-permute-start | bytes 176264 | tf_op jit(solution)/shard_map/ppermute | solution.py:71
  57.7 2.1 %field.4 = (bf16[45,45,192]{2,1,0:T(8,128)(2,1)}, bf16[15,45,192]{2,1,0:T(8,128)(2,1)S(1)}) custom-call(f32[2,11,8,128]{3,2,1,0:T(8,128)S(1)} %get-tuple-element.56.refs_0_, bf16[45,48,256]{2,1,0:T(8,128)(2,1)S(1)} %get-tuple-element.49.refs_5_.refs_1_, bf16[45,48,256]{2,1,0:T(8,128)(2,1)S(1)} %get-tuple-element.50.refs_1_.refs_2_, ...), custom_call_target="tpu_custom_call" | custom-call | flops 3630000128 | tf_op jit(solution)/shard_map/field/pallas_call | solution.py:758
  59.7 0.2 collective-permute-done.18
  60.0 1.2 %collective-permute-start.19 = (bf16[1,40,256]{2,1,0:T(8,128)(2,1)S(1)}, bf16[1,40,256]{2,1,0:T(8,128)(2,1)S(1)}, u32[]{:S(2)}, u32[]{:S(2)}) collective-permute-start(bf16[1,40,256]{2,1,0:T(8,128)(2,1)S(1)} %slice.93), channel_id=1, source_target_pairs={{0,16},{1,17},{2,18},{3,19},{4,20},{5,21},{6,22},{7,23},{8,24},{9,... | collective-permute-start | bytes 61448 | tf_op jit(solution)/shard_map/ppermute | solution.py:61
  61.1 0.0 collective-permute-done.17
  61.1 0.0 collective-permute-done.16
  61.2 0.0 copy-start.3
  61.2 0.0 copy-start.4
  61.2 2.4 %field.5 = bf16[45,45,192]{2,1,0:T(8,128)(2,1)} custom-call(f32[2,11,8,128]{3,2,1,0:T(8,128)S(1)} %get-tuple-element.56.refs_0_, bf16[45,48,256]{2,1,0:T(8,128)(2,1)S(1)} %get-tuple-element.49.refs_5_.refs_1_, bf16[45,48,256]{2,1,0:T(8,128)(2,1)S(1)} %get-tuple-element.50.refs_1_.refs_2_, ...), custom_call_target="tpu_custom_call", output_to_operand_aliasing={{}: (8, {})} | custom-call | flops 2420000000 | tf_op jit(solution)/shard_map/field/pallas_call | solution.py:758
  63.6 1.1 %collective-permute-done.19 = bf16[1,40,256]{2,1,0:T(8,128)(2,1)S(1)} collective-permute-done((bf16[1,40,256]{2,1,0:T(8,128)(2,1)S(1)}, bf16[1,40,256]{2,1,0:T(8,128)(2,1)S(1)}, u32[]{:S(2)}, u32[]{:S(2)}) %collective-permute-start.19) | collective-permute-done | bytes 20512 | tf_op jit(solution)/shard_map/ppermute | solution.py:61
  64.7 0.0 copy-done.3
  64.8 0.0 copy-done.4
  64.8 0.7 %multiply_add_fusion = f32[9568]{0:T(1024)} fusion(f32[9568]{0:T(1024)S(1)} %copy-done.4, f32[9568]{0:T(1024)S(1)} %copy-done.3, f32[10240]{0:T(1024)S(1)} %bitcast.4, s32[]{:T(128)S(6)} %select_n.127), kind=kLoop, calls=%fused_computation.26 | loop fusion | flops 38272 | bytes 153092 | tf_op jit(solution)/shard_map/add | solution.py:812
  (27 shorter events, 0.4 us)
Async XLA Ops:
  1.5 5.9 %collective-permute-start = (bf16[1,40,256]{2,1,0:T(8,128)(2,1)S(1)}, bf16[1,40,256]{2,1,0:T(8,128)(2,1)S(1)}, u32[]{:S(2)}, u32[]{:S(2)}) collective-permute-start(bf16[1,40,256]{2,1,0:T(8,128)(2,1)S(1)} %reshape.16), channel_id=1, source_target_pairs={{0,16},{1,17},{2,18},{3,19},{4,20},{5,21},{6,22},{7,23},{8,24},{9,... | collective-permute-start | bytes 61448 | tf_op jit(solution)/shard_map/ppermute | solution.py:61
  5.7 1.2 %copy-start.1 = (bf16[45,45,192]{2,1,0:T(8,128)(2,1)S(1)}, bf16[45,45,192]{2,1,0:T(8,128)(2,1)}, u32[]{:S(2)}) copy-start(bf16[45,45,192]{2,1,0:T(8,128)(2,1)} %refs_0_.7) | copy-start | bytes 2332804
  6.9 11.5 %copy-start.2 = (bf16[45,45,192]{2,1,0:T(8,128)(2,1)S(1)}, bf16[45,45,192]{2,1,0:T(8,128)(2,1)}, u32[]{:S(2)}) copy-start(bf16[45,45,192]{2,1,0:T(8,128)(2,1)} %refs_0_.7) | copy-start | bytes 2332804
  7.4 6.0 %collective-permute-start.1 = (bf16[2,40,256]{2,1,0:T(8,128)(2,1)S(1)}, bf16[2,40,256]{2,1,0:T(8,128)(2,1)S(1)}, u32[]{:S(2)}, u32[]{:S(2)}) collective-permute-start(bf16[2,40,256]{2,1,0:T(8,128)(2,1)S(1)} %get-tuple-element.98), channel_id=1, source_target_pairs={{0,8},{1,9},{2,10},{3,11},{4,12},{5,13},{6,14},{7,15},{8,0},{9,1},... | collective-permute-start | bytes 122888 | tf_op jit(solution)/shard_map/ppermute | solution.py:61
  9.4 7.6 %collective-permute-start.6 = (bf16[45,3,192]{2,1,0:T(4,128)(2,1)S(1)}, bf16[45,3,192]{2,1,0:T(4,128)(2,1)S(1)}, u32[]{:S(2)}, u32[]{:S(2)}) collective-permute-start(bf16[45,3,192]{2,1,0:T(4,128)(2,1)S(1)} %get-tuple-element.80), channel_id=1, source_target_pairs={{0,4},{4,0},{8,12},{12,8},{16,20},{20,16},{24,28},{28,24},{1,5},{5... | collective-permute-start | bytes 155528 | tf_op jit(solution)/shard_map/ppermute | solution.py:70
  11.0 7.4 %collective-permute-start.5 = (bf16[45,3,192]{2,1,0:T(4,128)(2,1)S(1)}, bf16[45,3,192]{2,1,0:T(4,128)(2,1)S(1)}, u32[]{:S(2)}, u32[]{:S(2)}) collective-permute-start(bf16[45,3,192]{2,1,0:T(4,128)(2,1)S(1)} %get-tuple-element.81), channel_id=1, source_target_pairs={{4,8},{12,16},{20,24},{28,0},{8,4},{16,12},{24,20},{0,28},{5,9},{1... | collective-permute-start | bytes 155528 | tf_op jit(solution)/shard_map/ppermute | solution.py:71
  13.4 8.5 %collective-permute-start.4 = (bf16[4,40,256]{2,1,0:T(8,128)(2,1)S(1)}, bf16[4,40,256]{2,1,0:T(8,128)(2,1)S(1)}, u32[]{:S(2)}, u32[]{:S(2)}) collective-permute-start(bf16[4,40,256]{2,1,0:T(8,128)(2,1)S(1)} %get-tuple-element.94), channel_id=1, source_target_pairs={{0,6},{1,7},{2,4},{3,5},{4,2},{5,3},{6,0},{7,1},{8,14},{9,15},{10,... | collective-permute-start | bytes 245768 | tf_op jit(solution)/shard_map/ppermute | solution.py:61
  14.3 7.6 %collective-permute-start.3 = (bf16[4,40,256]{2,1,0:T(8,128)(2,1)S(1)}, bf16[4,40,256]{2,1,0:T(8,128)(2,1)S(1)}, u32[]{:S(2)}, u32[]{:S(2)}) collective-permute-start(bf16[4,40,256]{2,1,0:T(8,128)(2,1)S(1)} %get-tuple-element.94), channel_id=1, source_target_pairs={{0,2},{1,3},{2,0},{3,1},{4,6},{5,7},{6,4},{7,5},{8,10},{9,11},{10,... | collective-permute-start | bytes 245768 | tf_op jit(solution)/shard_map/ppermute | solution.py:61
  15.1 6.8 %collective-permute-start.2 = (bf16[4,40,256]{2,1,0:T(8,128)(2,1)S(1)}, bf16[4,40,256]{2,1,0:T(8,128)(2,1)S(1)}, u32[]{:S(2)}, u32[]{:S(2)}) collective-permute-start(bf16[4,40,256]{2,1,0:T(8,128)(2,1)S(1)} %get-tuple-element.94), channel_id=1, source_target_pairs={{0,4},{1,5},{2,6},{3,7},{4,0},{5,1},{6,2},{7,3},{8,12},{9,13},{10,... | collective-permute-start | bytes 245768 | tf_op jit(solution)/shard_map/ppermute | solution.py:61
  18.4 1.2 %copy-start = (bf16[45,45,192]{2,1,0:T(8,128)(2,1)S(1)}, bf16[45,45,192]{2,1,0:T(8,128)(2,1)}, u32[]{:S(2)}) copy-start(bf16[45,45,192]{2,1,0:T(8,128)(2,1)} %refs_3_) | copy-start | bytes 2332804
  18.5 6.2 %collective-permute-start.9 = (bf16[3,51,192]{2,1,0:T(8,128)(2,1)S(1)}, bf16[3,51,192]{2,1,0:T(8,128)(2,1)S(1)}, u32[]{:S(2)}, u32[]{:S(2)}) collective-permute-start(bf16[3,51,192]{2,1,0:T(8,128)(2,1)S(1)} %get-tuple-element.88), channel_id=1, source_target_pairs={{0,1},{1,0},{2,3},{3,2},{4,5},{5,4},{6,7},{7,6},{8,9},{9,8},{10,11... | collective-permute-start | bytes 176264 | tf_op jit(solution)/shard_map/ppermute | solution.py:70
  18.6 6.1 %collective-permute-start.8 = (bf16[3,51,192]{2,1,0:T(8,128)(2,1)S(1)}, bf16[3,51,192]{2,1,0:T(8,128)(2,1)S(1)}, u32[]{:S(2)}, u32[]{:S(2)}) collective-permute-start(bf16[3,51,192]{2,1,0:T(8,128)(2,1)S(1)} %get-tuple-element.89), channel_id=1, source_target_pairs={{1,2},{2,1},{5,6},{6,5},{9,10},{10,9},{13,14},{14,13},{17,18},{18,... | collective-permute-start | bytes 176264 | tf_op jit(solution)/shard_map/ppermute | solution.py:71
  22.0 3.9 %collective-permute-start.7 = (bf16[16,40,256]{2,1,0:T(8,128)(2,1)S(1)}, bf16[16,40,256]{2,1,0:T(8,128)(2,1)S(1)}, u32[]{:S(2)}, u32[]{:S(2)}) collective-permute-start(bf16[16,40,256]{2,1,0:T(8,128)(2,1)S(1)} %constant_dynamic-update-slice_fusion.5), channel_id=1, source_target_pairs={{0,1},{1,0},{2,3},{3,2},{4,5},{5,4},{6,7},{7,6},{8,9},{9,8},{10,11... | collective-permute-start | bytes 983048 | tf_op jit(solution)/shard_map/ppermute | solution.py:61
  39.1 6.9 %collective-permute-start.12 = (bf16[45,3,192]{2,1,0:T(4,128)(2,1)S(1)}, bf16[45,3,192]{2,1,0:T(4,128)(2,1)S(1)}, u32[]{:S(2)}, u32[]{:S(2)}) collective-permute-start(bf16[45,3,192]{2,1,0:T(4,128)(2,1)S(1)} %get-tuple-element.71), channel_id=1, source_target_pairs={{0,4},{4,0},{8,12},{12,8},{16,20},{20,16},{24,28},{28,24},{1,5},{5... | collective-permute-start | bytes 155528 | tf_op jit(solution)/shard_map/ppermute | solution.py:70
  39.2 7.7 %collective-permute-start.11 = (bf16[45,3,192]{2,1,0:T(4,128)(2,1)S(1)}, bf16[45,3,192]{2,1,0:T(4,128)(2,1)S(1)}, u32[]{:S(2)}, u32[]{:S(2)}) collective-permute-start(bf16[45,3,192]{2,1,0:T(4,128)(2,1)S(1)} %get-tuple-element.72), channel_id=1, source_target_pairs={{4,8},{12,16},{20,24},{28,0},{8,4},{16,12},{24,20},{0,28},{5,9},{1... | collective-permute-start | bytes 155528 | tf_op jit(solution)/shard_map/ppermute | solution.py:71
  45.9 1.7 %collective-permute-start.10 = (bf16[16,40,256]{2,1,0:T(8,128)(2,1)S(1)}, bf16[16,40,256]{2,1,0:T(8,128)(2,1)S(1)}, u32[]{:S(2)}, u32[]{:S(2)}) collective-permute-start(bf16[16,40,256]{2,1,0:T(8,128)(2,1)S(1)} %slice.60), channel_id=1, source_target_pairs={{0,1},{1,0},{2,3},{3,2},{4,5},{5,4},{6,7},{7,6},{8,9},{9,8},{10,11... | collective-permute-start | bytes 983048 | tf_op jit(solution)/shard_map/ppermute | solution.py:61
  47.7 6.3 %collective-permute-start.13 = (bf16[4,40,256]{2,1,0:T(8,128)(2,1)S(1)}, bf16[4,40,256]{2,1,0:T(8,128)(2,1)S(1)}, u32[]{:S(2)}, u32[]{:S(2)}) collective-permute-start(bf16[4,40,256]{2,1,0:T(8,128)(2,1)S(1)} %get-tuple-element.73), channel_id=1, source_target_pairs={{0,4},{1,5},{2,6},{3,7},{4,0},{5,1},{6,2},{7,3},{8,12},{9,13},{10,... | collective-permute-start | bytes 245768 | tf_op jit(solution)/shard_map/ppermute | solution.py:61
  47.8 6.9 %collective-permute-start.15 = (bf16[4,40,256]{2,1,0:T(8,128)(2,1)S(1)}, bf16[4,40,256]{2,1,0:T(8,128)(2,1)S(1)}, u32[]{:S(2)}, u32[]{:S(2)}) collective-permute-start(bf16[4,40,256]{2,1,0:T(8,128)(2,1)S(1)} %get-tuple-element.74), channel_id=1, source_target_pairs={{0,6},{1,7},{2,4},{3,5},{4,2},{5,3},{6,0},{7,1},{8,14},{9,15},{10,... | collective-permute-start | bytes 245768 | tf_op jit(solution)/shard_map/ppermute | solution.py:61
  50.4 5.4 %collective-permute-start.14 = (bf16[4,40,256]{2,1,0:T(8,128)(2,1)S(1)}, bf16[4,40,256]{2,1,0:T(8,128)(2,1)S(1)}, u32[]{:S(2)}, u32[]{:S(2)}) collective-permute-start(bf16[4,40,256]{2,1,0:T(8,128)(2,1)S(1)} %get-tuple-element.75), channel_id=1, source_target_pairs={{0,2},{1,3},{2,0},{3,1},{4,6},{5,7},{6,4},{7,5},{8,10},{9,11},{10,... | collective-permute-start | bytes 245768 | tf_op jit(solution)/shard_map/ppermute | solution.py:61
  55.9 4.1 %collective-permute-start.18 = (bf16[2,40,256]{2,1,0:T(8,128)(2,1)S(1)}, bf16[2,40,256]{2,1,0:T(8,128)(2,1)S(1)}, u32[]{:S(2)}, u32[]{:S(2)}) collective-permute-start(bf16[2,40,256]{2,1,0:T(8,128)(2,1)S(1)} %slice.92), channel_id=1, source_target_pairs={{0,8},{1,9},{2,10},{3,11},{4,12},{5,13},{6,14},{7,15},{8,0},{9,1},... | collective-permute-start | bytes 122888 | tf_op jit(solution)/shard_map/ppermute | solution.py:61
  56.9 4.2 %collective-permute-start.17 = (bf16[3,51,192]{2,1,0:T(8,128)(2,1)S(1)}, bf16[3,51,192]{2,1,0:T(8,128)(2,1)S(1)}, u32[]{:S(2)}, u32[]{:S(2)}) collective-permute-start(bf16[3,51,192]{2,1,0:T(8,128)(2,1)S(1)} %get-tuple-element.84), channel_id=1, source_target_pairs={{0,1},{1,0},{2,3},{3,2},{4,5},{5,4},{6,7},{7,6},{8,9},{9,8},{10,11... | collective-permute-start | bytes 176264 | tf_op jit(solution)/shard_map/ppermute | solution.py:70
  57.0 4.1 %collective-permute-start.16 = (bf16[3,51,192]{2,1,0:T(8,128)(2,1)S(1)}, bf16[3,51,192]{2,1,0:T(8,128)(2,1)S(1)}, u32[]{:S(2)}, u32[]{:S(2)}) collective-permute-start(bf16[3,51,192]{2,1,0:T(8,128)(2,1)S(1)} %get-tuple-element.85), channel_id=1, source_target_pairs={{1,2},{2,1},{5,6},{6,5},{9,10},{10,9},{13,14},{14,13},{17,18},{18,... | collective-permute-start | bytes 176264 | tf_op jit(solution)/shard_map/ppermute | solution.py:71
  60.0 4.7 %collective-permute-start.19 = (bf16[1,40,256]{2,1,0:T(8,128)(2,1)S(1)}, bf16[1,40,256]{2,1,0:T(8,128)(2,1)S(1)}, u32[]{:S(2)}, u32[]{:S(2)}) collective-permute-start(bf16[1,40,256]{2,1,0:T(8,128)(2,1)S(1)} %slice.93), channel_id=1, source_target_pairs={{0,16},{1,17},{2,18},{3,19},{4,20},{5,21},{6,22},{7,23},{8,24},{9,... | collective-permute-start | bytes 61448 | tf_op jit(solution)/shard_map/ppermute | solution.py:61
  61.2 3.6 %copy-start.3 = (f32[9568]{0:T(1024)S(1)}, f32[9568]{0:T(1024)}, u32[]{:S(2)}) copy-start(f32[9568]{0:T(1024)} %param.5) | copy-start | bytes 114820
  61.2 3.6 %copy-start.4 = (f32[9568]{0:T(1024)S(1)}, f32[9568]{0:T(1024)}, u32[]{:S(2)}) copy-start(f32[9568]{0:T(1024)} %param.6) | copy-start | bytes 114820

commit v10 on v9

--- a/solution.py
+++ b/solution.py
@@ -30,6 +30,7 @@
 TILES = H // LANES
 SHARE_LANES = 256
 CHUNK = 256
+UNROLL = True
 GIN_ROWS = C + 8
 ALL = ((1,), (1,)), ((), ())
 OVER = ((0,), (0,)), ((), ())
@@ -335,10 +336,9 @@
     lax.fori_loop(0, 2 * (lon_pad // chunk), body, 0, unroll=unroll)
 
 
-def layer_kernel(order, starts, rows, lon_pad, block_rows, conv_rows, inner, outer,
-                 me_ref, gathered_ref, inner_ref, outer_ref, feat_ref, up_ref,
-                 out_ref, gconv_ref, gin_ref, gout_ref, sums_ref, flipped_ref,
-                 u_ref, taps_ref, w_ref, win_ref, wout_ref, wo32_ref, conv_ref, act_ref, gpre_ref):
+def conv_kernel(order, starts, rows, lon_pad, block_rows, conv_rows, inner, outer,
+                me_ref, gathered_ref, inner_ref, outer_ref,
+                conv_ref, win_ref, wout_ref, taps_ref, flipped_ref, u_ref, w_ref, wo32_ref, sum_ref):
     me = me_ref[0]
     window = gathered_ref.shape[1]
     w_ref[:, 0:8, :] = jnp.zeros_like(w_ref[:, 0:8, :])
@@ -368,12 +368,28 @@
     for t in range(2):
         wout_ref[:, t * LANES : (t + 1) * LANES] = wo32_ref[t].astype(BF16)
 
+    filter_points(taps_ref, conv_rows, u_ref, False)
+    filter_points(taps_ref, conv_rows, flipped_ref, True)
+    for v_ref, ranges in ((inner_ref, inner), (outer_ref, outer)):
+
+        def conv_step(place, block, v_ref=v_ref):
+            def store(tile, lon, chunk, sums):
+                for r in range(conv_rows):
+                    sum_ref[tile, r, pl.ds(lon, chunk), :] = sums[r]
+
+            depthwise_block(v_ref, u_ref, place, conv_rows, lon_pad, store, False, UNROLL)
+            conv_ref[:, pl.ds(block * conv_rows, conv_rows)] = sum_ref[...]
+
+        over_blocks(ranges, conv_step)
+
+
+def layer_kernel(rows, lon_pad, block_rows, conv_ref, win_ref, wout_ref, taps_ref, feat_ref, up_ref,
+                 out_ref, gconv_ref, gin_ref, gout_ref, sums_ref, *hidden_refs):
+    act_refs, gpre_refs = hidden_refs[:2], hidden_refs[2:]
     def vector(row, quarter):
         at = (row - ROW_TAPS) * 4 + quarter
         return [taps_ref[t, pl.ds(at, 1), :] for t in range(2)]
 
-    filter_points(taps_ref, conv_rows, u_ref, False)
-    filter_points(taps_ref, conv_rows, flipped_ref, True)
     cbias = vector(ROW_NORM, 1)
     gain = vector(ROW_NORM, 2)
     shift = vector(ROW_NORM, 3)
@@ -391,18 +407,7 @@
     def partial(values):
         return values.reshape(cells // 8, 8, LANES).sum(axis=0)
 
-    for v_ref, ranges in ((inner_ref, inner), (outer_ref, outer)):
-
-        def conv_step(place, block, v_ref=v_ref):
-            def store(tile, lon, chunk, sums):
-                for r in range(conv_rows):
-                    conv_ref[tile, block * conv_rows + r, pl.ds(lon, chunk), :] = sums[r]
-
-            depthwise_block(v_ref, u_ref, place, conv_rows, lon_pad, store, False, False)
-
-        over_blocks(ranges, conv_step)
-
-    def body(block, carry):
+    def normalise(block):
         row = block * block_rows
         conv = [
             conv_ref[t, pl.ds(row, block_rows)].reshape(cells, LANES) + cbias[t] for t in range(2)
@@ -419,6 +424,10 @@
         ups = [upstream[:, t * LANES : (t + 1) * LANES].astype(F32) for t in range(2)]
         grad_branch = [(scale[t] * ups[t]).astype(BF16) for t in range(2)]
         gbranch = jnp.concatenate(grad_branch, axis=1)
+        return standard, inv_std, normed, ups, grad_branch, gbranch
+
+    def hidden_units(block, state):
+        normed, gbranch = state[2], state[5]
         for h in range(0, H, CHUNK):
             hidden = slice(h, h + CHUNK)
             pre = jnp.dot(normed, win_ref[:, hidden], preferred_element_type=F32)
@@ -427,10 +436,14 @@
             half = 0.5 + 0.5 * jnp.tanh(pre * (GELU_A + GELU_B * square))
             act = pre * half
             slope = half + act * (1.0 - half) * (2.0 * GELU_A + 6.0 * GELU_B * square)
-            act_ref[:, hidden] = act.astype(BF16)
-            gpre_ref[:, hidden] = (gact * slope).astype(BF16)
-        act = act_ref[...]
-        gpre = gpre_ref[...]
+            act_refs[block % 2][:, hidden] = act.astype(BF16)
+            gpre_refs[block % 2][:, hidden] = (gact * slope).astype(BF16)
+
+    def finish(block, state):
+        row = block * block_rows
+        standard, inv_std, normed, ups, grad_branch, gbranch = state
+        act = act_refs[block % 2][...]
+        gpre = gpre_refs[block % 2][...]
         branch = jnp.dot(act, wout_ref[...], preferred_element_type=F32)
         gnormed = lax.dot_general(gpre, win_ref[...], ALL, preferred_element_type=F32)
         gin_ref[...] += lax.dot_general(
@@ -466,9 +479,14 @@
         )
         out = jnp.concatenate(outs, axis=1).reshape(block_rows, lon_pad, CP)
         out_ref[pl.ds(row, block_rows)] = out[:, : out_ref.shape[1], :C]
-        return carry
-
-    lax.fori_loop(0, rows // block_rows, body, 0)
+
+    states = [normalise(0)]
+    hidden_units(0, states[0])
+    for block in range(rows // block_rows):
+        if block + 1 < rows // block_rows:
+            states.append(normalise(block + 1))
+            hidden_units(block + 1, states[block + 1])
+        finish(block, states[block])
 
 
 def taps_kernel(order, starts, rows, lon_pad, block_rows, conv_rows, inner, outer,
@@ -683,33 +701,43 @@
     )(features, west, east, south, north)
 
     static = (order, starts, rows, lon_pad, block_rows, conv_rows, inner, outer)
-    output, gconv, gin, gout, sums, flipped = pl.pallas_call(
-        lambda *refs: layer_kernel(*static, *refs),
+    *weights, flipped = pl.pallas_call(
+        lambda *refs: conv_kernel(*static, *refs),
+        out_shape=(
+            shape((2, rows, lon_pad, LANES), F32),
+            shape((CP, H), BF16),
+            shape((H, CP), BF16),
+            shape((2, 64, LANES), F32),
+            shape((2, points, 8, LANES), F32),
+        ),
+        in_specs=smem + whole(3),
+        out_specs=tuple(whole(5)),
+        scratch_shapes=[
+            pltpu.VMEM((2, points, 8, LANES), F32),
+            pltpu.VMEM((2, flat_rows, LANES), F32),
+            pltpu.VMEM((2, H, LANES), F32),
+            pltpu.VMEM((2, conv_rows, lon_pad, LANES), F32),
+        ],
+        compiler_params=compiler_params,
+        cost_estimate=cost(6),
+        name="conv",
+    )(place, gathered, inner_data, outer_data)
+    output, gconv, gin, gout, sums = pl.pallas_call(
+        lambda *refs: layer_kernel(rows, lon_pad, block_rows, *refs),
         out_shape=(
             shape((rows, cols, C), BF16),
             shape((rows, lon_pad, CP), BF16),
             shape((GIN_ROWS, H), F32),
             shape((C, H), F32),
             shape((5, 2, 8, LANES), F32),
-            shape((2, points, 8, LANES), F32),
         ),
-        in_specs=smem + whole(5),
-        out_specs=tuple(whole(6)),
-        scratch_shapes=[
-            pltpu.VMEM((2, points, 8, LANES), F32),
-            pltpu.VMEM((2, 64, LANES), F32),
-            pltpu.VMEM((2, flat_rows, LANES), F32),
-            pltpu.VMEM((CP, H), BF16),
-            pltpu.VMEM((H, CP), BF16),
-            pltpu.VMEM((2, H, LANES), F32),
-            pltpu.VMEM((2, rows, lon_pad, LANES), F32),
-            pltpu.VMEM((block_rows * lon_pad, H), BF16),
-            pltpu.VMEM((block_rows * lon_pad, H), BF16),
-        ],
+        in_specs=whole(6),
+        out_specs=tuple(whole(5)),
+        scratch_shapes=[pltpu.VMEM((block_rows * lon_pad, H), BF16)] * 4,
         compiler_params=compiler_params,
-        cost_estimate=cost(22),
+        cost_estimate=cost(16),
         name="layer",
-    )(place, gathered, inner_data, outer_data, feats, ups)
+    )(*weights, feats, ups)
 
     values, output = pl.pallas_call(
         lambda *refs: taps_kernel(*static, *refs),

time: 66.3 us -> 64.7 us (0.976)
  Pallas kernels: 27.8 us -> 26.2 us
    pallas_call x1 -> x2, Pallas kernels: 13 us -> 11.3 us  [the longest x1 7.73 us: body(): pl.pallas_call(lambda *refs: layer_kernel(rows, lon_pad, block_rows, *ref...]
where the time goes in v10:
time: 64.7 us; the launch traced here: 63.9 us
  starting transfers between devices  26.3 us (41%)
  Pallas kernels  26.2 us (40%)
  waiting for transfers between devices  6.28 us (10%)
  local copies, waits for them, and re-layouts  2.57 us (4%)
  other arithmetic  1.42 us (2%)
  between operations  1.06 us (2%)
    ppermute x12, starting transfers between devices, swap(): return lax.ppermute(values, ('lon', 'lat'), pairs)  18.1 us
    pallas_call x1, Pallas kernels, body(): pl.pallas_call(lambda *refs: layer_kernel(rows, lon_pad, block_rows, *ref...  7.73 us
    pallas_call x3, Pallas kernels, field_piece(): pl.pallas_call(lambda *refs: field_kernel(ranges, rows, cols, lon_pad, co...  7.17 us
    ppermute x4, starting transfers between devices, send_edges(): far = lax.ppermute(jnp.where(even, low_edge, high_edge), axis, far)  6.45 us
    pallas_call x1, Pallas kernels, body(): pl.pallas_call(lambda *refs: taps_kernel(*static, *refs), out_shape=(shap...  4.23 us
    ppermute x12, waiting for transfers between devices, swap(): return lax.ppermute(values, ('lon', 'lat'), pairs)  4.2 us
    pallas_call x1, Pallas kernels, body(): pl.pallas_call(lambda *refs: conv_kernel(*static, *refs), out_shape=(shap...  3.52 us
    pallas_call x1, Pallas kernels, body(): pl.pallas_call(lambda *refs: inner_kernel(inner, rows, cols, conv_rows, *...  2.26 us
  transfers between devices with their start and end apart: 20, of which 9 were waited for; matrix products, arithmetic and copies ran while one was open for 1% of the time, Pallas kernels for 23%

profile of v10, /device:TPU:0, one launch (start us, length us, event | category | flops | bytes accessed | tf_op | source)
XLA Modules:
  0.0 63.9 jit_solution(11621847702979773960)
XLA Ops:
  0.7 0.9 %fusion = bf16[10240]{0:T(1024)(128)(2,1)S(1)} fusion(s32[]{:T(128)S(6)} %select_n.106, f32[9568]{0:T(1024)} %param.5), kind=kLoop, calls=%fused_computation.24 | loop fusion | bytes 58756 | tf_op jit(solution)/shard_map/convert_element_type | solution.py:639
  1.5 4.1 %collective-permute-start = (bf16[1,40,256]{2,1,0:T(8,128)(2,1)S(1)}, bf16[1,40,256]{2,1,0:T(8,128)(2,1)S(1)}, u32[]{:S(2)}, u32[]{:S(2)}) collective-permute-start(bf16[1,40,256]{2,1,0:T(8,128)(2,1)S(1)} %reshape.16), channel_id=1, source_target_pairs={{0,16},{1,17},{2,18},{3,19},{4,20},{5,21},{6,22},{7,23},{8,24},{9,... | collective-permute-start | bytes 61448 | tf_op jit(solution)/shard_map/ppermute | solution.py:62
  5.7 1.2 %copy-done.1 = bf16[45,45,192]{2,1,0:T(8,128)(2,1)S(1)} copy-done((bf16[45,45,192]{2,1,0:T(8,128)(2,1)S(1)}, bf16[45,45,192]{2,1,0:T(8,128)(2,1)}, u32[]{:S(2)}) %copy-start.1) | copy-done | bytes 777624
  6.9 0.2 edges.1
  7.2 0.2 collective-permute-done
  7.4 1.9 %collective-permute-start.1 = (bf16[2,40,256]{2,1,0:T(8,128)(2,1)S(1)}, bf16[2,40,256]{2,1,0:T(8,128)(2,1)S(1)}, u32[]{:S(2)}, u32[]{:S(2)}) collective-permute-start(bf16[2,40,256]{2,1,0:T(8,128)(2,1)S(1)} %get-tuple-element.106), channel_id=1, source_target_pairs={{0,8},{1,9},{2,10},{3,11},{4,12},{5,13},{6,14},{7,15},{8,0},{9,1},... | collective-permute-start | bytes 122888 | tf_op jit(solution)/shard_map/ppermute | solution.py:62
  9.3 0.1 broadcast_select_fusion.6
  9.4 1.6 %collective-permute-start.6 = (bf16[45,3,192]{2,1,0:T(4,128)(2,1)S(1)}, bf16[45,3,192]{2,1,0:T(4,128)(2,1)S(1)}, u32[]{:S(2)}, u32[]{:S(2)}) collective-permute-start(bf16[45,3,192]{2,1,0:T(4,128)(2,1)S(1)} %get-tuple-element.88), channel_id=1, source_target_pairs={{0,4},{4,0},{8,12},{12,8},{16,20},{20,16},{24,28},{28,24},{1,5},{5... | collective-permute-start | bytes 155528 | tf_op jit(solution)/shard_map/ppermute | solution.py:71
  11.0 2.5 %collective-permute-start.5 = (bf16[45,3,192]{2,1,0:T(4,128)(2,1)S(1)}, bf16[45,3,192]{2,1,0:T(4,128)(2,1)S(1)}, u32[]{:S(2)}, u32[]{:S(2)}) collective-permute-start(bf16[45,3,192]{2,1,0:T(4,128)(2,1)S(1)} %get-tuple-element.89), channel_id=1, source_target_pairs={{4,8},{12,16},{20,24},{28,0},{8,4},{16,12},{24,20},{0,28},{5,9},{1... | collective-permute-start | bytes 155528 | tf_op jit(solution)/shard_map/ppermute | solution.py:72
  13.4 0.0 collective-permute-done.1
  13.4 0.9 %collective-permute-start.4 = (bf16[4,40,256]{2,1,0:T(8,128)(2,1)S(1)}, bf16[4,40,256]{2,1,0:T(8,128)(2,1)S(1)}, u32[]{:S(2)}, u32[]{:S(2)}) collective-permute-start(bf16[4,40,256]{2,1,0:T(8,128)(2,1)S(1)} %get-tuple-element.102), channel_id=1, source_target_pairs={{0,6},{1,7},{2,4},{3,5},{4,2},{5,3},{6,0},{7,1},{8,14},{9,15},{10,... | collective-permute-start | bytes 245768 | tf_op jit(solution)/shard_map/ppermute | solution.py:62
  14.3 0.8 %collective-permute-start.3 = (bf16[4,40,256]{2,1,0:T(8,128)(2,1)S(1)}, bf16[4,40,256]{2,1,0:T(8,128)(2,1)S(1)}, u32[]{:S(2)}, u32[]{:S(2)}) collective-permute-start(bf16[4,40,256]{2,1,0:T(8,128)(2,1)S(1)} %get-tuple-element.102), channel_id=1, source_target_pairs={{0,2},{1,3},{2,0},{3,1},{4,6},{5,7},{6,4},{7,5},{8,10},{9,11},{10,... | collective-permute-start | bytes 245768 | tf_op jit(solution)/shard_map/ppermute | solution.py:62
  15.1 1.9 %collective-permute-start.2 = (bf16[4,40,256]{2,1,0:T(8,128)(2,1)S(1)}, bf16[4,40,256]{2,1,0:T(8,128)(2,1)S(1)}, u32[]{:S(2)}, u32[]{:S(2)}) collective-permute-start(bf16[4,40,256]{2,1,0:T(8,128)(2,1)S(1)} %get-tuple-element.102), channel_id=1, source_target_pairs={{0,4},{1,5},{2,6},{3,7},{4,0},{5,1},{6,2},{7,3},{8,12},{9,13},{10,... | collective-permute-start | bytes 245768 | tf_op jit(solution)/shard_map/ppermute | solution.py:62
  17.0 0.0 collective-permute-done.6
  17.0 1.3 %collective-permute-done.5 = bf16[45,3,192]{2,1,0:T(4,128)(2,1)S(1)} collective-permute-done((bf16[45,3,192]{2,1,0:T(4,128)(2,1)S(1)}, bf16[45,3,192]{2,1,0:T(4,128)(2,1)S(1)}, u32[]{:S(2)}, u32[]{:S(2)}) %collective-permute-start.5) | collective-permute-done | bytes 51872 | tf_op jit(solution)/shard_map/ppermute | solution.py:72
  18.3 0.1 broadcast_select_fusion.4
  18.4 0.0 copy-done.2
  18.4 0.0 copy-start
  18.5 0.1 collective-permute-start.9
  18.6 0.8 %collective-permute-start.8 = (bf16[3,51,192]{2,1,0:T(8,128)(2,1)S(1)}, bf16[3,51,192]{2,1,0:T(8,128)(2,1)S(1)}, u32[]{:S(2)}, u32[]{:S(2)}) collective-permute-start(bf16[3,51,192]{2,1,0:T(8,128)(2,1)S(1)} %get-tuple-element.97), channel_id=1, source_target_pairs={{1,2},{2,1},{5,6},{6,5},{9,10},{10,9},{13,14},{14,13},{17,18},{18,... | collective-permute-start | bytes 176264 | tf_op jit(solution)/shard_map/ppermute | solution.py:72
  19.4 0.3 copy-done
  19.7 2.3 %inner.1 = (f32[2,77,56,128]{3,2,1,0:T(8,128)S(1)}, bf16[45,48,256]{2,1,0:T(8,128)(2,1)S(1)}, bf16[45,48,256]{2,1,0:T(8,128)(2,1)S(1)}) custom-call(bf16[45,45,192]{2,1,0:T(8,128)(2,1)S(1)} %copy-done.2, bf16[45,3,192]{2,1,0:T(4,128)(2,1)S(1)} %get-tuple-element.44.refs_1_, bf16[45,3,192]{2,1,0:T(4,128)(2,1)S(1)} %get-tuple-element.45.refs_2_, ...), custom_call_target="tpu_custom_call" | custom-call | flops 2750000128 | tf_op jit(solution)/shard_map/inner/pallas_call | solution.py:672
  21.9 0.0 collective-permute-done.2
  21.9 0.0 collective-permute-done.3
  22.0 0.0 collective-permute-done.4
  22.0 2.7 %collective-permute-start.7 = (bf16[16,40,256]{2,1,0:T(8,128)(2,1)S(1)}, bf16[16,40,256]{2,1,0:T(8,128)(2,1)S(1)}, u32[]{:S(2)}, u32[]{:S(2)}) collective-permute-start(bf16[16,40,256]{2,1,0:T(8,128)(2,1)S(1)} %constant_dynamic-update-slice_fusion.5), channel_id=1, source_target_pairs={{0,1},{1,0},{2,3},{3,2},{4,5},{5,4},{6,7},{7,6},{8,9},{9,8},{10,11... | collective-permute-start | bytes 983048 | tf_op jit(solution)/shard_map/ppermute | solution.py:62
  24.7 0.0 collective-permute-done.9
  24.7 0.0 collective-permute-done.8
  24.7 1.0 %outer.1.refs_3_ = f32[2,22,56,128]{3,2,1,0:T(8,128)S(1)} custom-call(bf16[45,45,192]{2,1,0:T(8,128)(2,1)S(1)} %copy-done.2, bf16[45,3,192]{2,1,0:T(4,128)(2,1)S(1)} %get-tuple-element.44.refs_1_, bf16[45,3,192]{2,1,0:T(4,128)(2,1)S(1)} %get-tuple-element.45.refs_2_, bf16[3,51,192]{2,1,0:T(8,128)(2,1)S(1)} %get-tuple-element.95.refs_3_, ...), custom_call_target="tpu_custom_call" | custom-call | flops 1100000000 | tf_op jit(solution)/shard_map/outer/pallas_call | solution.py:692
  25.7 0.2 collective-permute-done.7
  25.9 0.1 pad_maximum_fusion.refs_1_
  26.0 3.5 %conv.1 = (f32[2,45,48,128]{3,2,1,0:T(8,128)S(1)}, bf16[256,768]{1,0:T(8,128)(2,1)S(1)}, bf16[768,256]{1,0:T(8,128)(2,1)S(1)}, f32[2,64,128]{2,1,0:T(8,128)S(1)}, f32[2,11,8,128]{3,2,1,0:T(8,128)S(1)}) custom-call(s32[1]{0:T(128)} %bitcast.refs_0_, bf16[32,40,256]{2,1,0:T(8,128)(2,1)S(1)} %pad_maximum_fusion.refs_1_, ...), custom_call_target="tpu_custom_call" | custom-call | flops 6600000000 | tf_op jit(solution)/shard_map/conv/pallas_call | solution.py:704
  29.5 7.7 %layer.1 = (bf16[45,45,192]{2,1,0:T(8,128)(2,1)S(1)}, bf16[45,48,256]{2,1,0:T(8,128)(2,1)S(1)}, f32[200,768]{1,0:T(8,128)S(1)}, f32[192,768]{1,0:T(8,128)S(1)}, f32[5,2,8,128]{3,2,1,0:T(8,128)S(1)}) custom-call(f32[2,45,48,128]{3,2,1,0:T(8,128)S(1)} %get-tuple-element.52.refs_0_, bf16[256,768]{1,0:T(8,128)(2,1)S(1)} %get-tuple-element.53.refs_1_, ...), custom_call_target="tpu_custom_call" | custom-call | flops 17600000000 | tf_op jit(solution)/shard_map/layer/pallas_call | solution.py:725
  37.3 0.1 broadcast_select_fusion.2
  37.4 0.1 collective-permute-start.12
  37.5 2.5 %collective-permute-start.11 = (bf16[45,3,192]{2,1,0:T(4,128)(2,1)S(1)}, bf16[45,3,192]{2,1,0:T(4,128)(2,1)S(1)}, u32[]{:S(2)}, u32[]{:S(2)}) collective-permute-start(bf16[45,3,192]{2,1,0:T(4,128)(2,1)S(1)} %get-tuple-element.80), channel_id=1, source_target_pairs={{4,8},{12,16},{20,24},{28,0},{8,4},{16,12},{24,20},{0,28},{5,9},{1... | collective-permute-start | bytes 155528 | tf_op jit(solution)/shard_map/ppermute | solution.py:72
  40.0 4.2 %taps.1 = (bf16[32,40,256]{2,1,0:T(8,128)(2,1)S(1)}, bf16[45,45,192]{2,1,0:T(8,128)(2,1)}) custom-call(s32[1]{0:T(128)} %bitcast.refs_0_, bf16[45,48,256]{2,1,0:T(8,128)(2,1)S(1)} %get-tuple-element.58.refs_1_.refs_2_, f32[2,77,56,128]{3,2,1,0:T(8,128)S(1)} %get-tuple-element.49.refs_2_, f32[2,22,56,128]{3,2,1,0:T(8,128)S(1)} %outer.1.refs_3_, ...), custom_call_target="tpu_custom_call" | custom-call | flops 12099999744 | tf_op jit(solution)/shard_map/taps/pallas_call | solution.py:742
  44.3 0.1 collective-permute-start.10
  44.4 0.0 collective-permute-done.12
  44.4 0.7 %collective-permute-done.11 = bf16[45,3,192]{2,1,0:T(4,128)(2,1)S(1)} collective-permute-done((bf16[45,3,192]{2,1,0:T(4,128)(2,1)S(1)}, bf16[45,3,192]{2,1,0:T(4,128)(2,1)S(1)}, u32[]{:S(2)}, u32[]{:S(2)}) %collective-permute-start.11) | collective-permute-done | bytes 51872 | tf_op jit(solution)/shard_map/ppermute | solution.py:72
  45.2 0.1 broadcast_select_fusion
  45.2 0.7 %collective-permute-done.10 = bf16[16,40,256]{2,1,0:T(8,128)(2,1)S(1)} collective-permute-done((bf16[16,40,256]{2,1,0:T(8,128)(2,1)S(1)}, bf16[16,40,256]{2,1,0:T(8,128)(2,1)S(1)}, u32[]{:S(2)}, u32[]{:S(2)}) %collective-permute-start.10) | collective-permute-done | bytes 327712 | tf_op jit(solution)/shard_map/ppermute | solution.py:62
  46.0 0.1 convert_add_fusion
  46.1 0.1 collective-permute-start.13
  46.2 2.6 %collective-permute-start.15 = (bf16[4,40,256]{2,1,0:T(8,128)(2,1)S(1)}, bf16[4,40,256]{2,1,0:T(8,128)(2,1)S(1)}, u32[]{:S(2)}, u32[]{:S(2)}) collective-permute-start(bf16[4,40,256]{2,1,0:T(8,128)(2,1)S(1)} %get-tuple-element.82), channel_id=1, source_target_pairs={{0,6},{1,7},{2,4},{3,5},{4,2},{5,3},{6,0},{7,1},{8,14},{9,15},{10,... | collective-permute-start | bytes 245768 | tf_op jit(solution)/shard_map/ppermute | solution.py:62
  48.8 0.9 %collective-permute-start.14 = (bf16[4,40,256]{2,1,0:T(8,128)(2,1)S(1)}, bf16[4,40,256]{2,1,0:T(8,128)(2,1)S(1)}, u32[]{:S(2)}, u32[]{:S(2)}) collective-permute-start(bf16[4,40,256]{2,1,0:T(8,128)(2,1)S(1)} %get-tuple-element.83), channel_id=1, source_target_pairs={{0,2},{1,3},{2,0},{3,1},{4,6},{5,7},{6,4},{7,5},{8,10},{9,11},{10,... | collective-permute-start | bytes 245768 | tf_op jit(solution)/shard_map/ppermute | solution.py:62
  49.7 2.7 %field.3.refs_5_ = bf16[20,45,192]{2,1,0:T(8,128)(2,1)S(1)} custom-call(f32[2,11,8,128]{3,2,1,0:T(8,128)S(1)} %get-tuple-element.64.refs_0_, bf16[45,48,256]{2,1,0:T(8,128)(2,1)S(1)} %get-tuple-element.57.refs_5_.refs_1_, bf16[45,48,256]{2,1,0:T(8,128)(2,1)S(1)} %get-tuple-element.58.refs_1_.refs_2_, bf16[45,3,192]{2,1,0:T(4,128)(2,1)S(1)} %get-tuple-element.66.refs_3_, ...), custom_call_target="tpu_custom_call" | custom-call | flops 4840000000 | tf_op jit(solution)/shard_map/field/pallas_call | solution.py:786
  52.4 0.0 collective-permute-done.13
  52.5 0.6 %collective-permute-done.15 = bf16[4,40,256]{2,1,0:T(8,128)(2,1)S(1)} collective-permute-done((bf16[4,40,256]{2,1,0:T(8,128)(2,1)S(1)}, bf16[4,40,256]{2,1,0:T(8,128)(2,1)S(1)}, u32[]{:S(2)}, u32[]{:S(2)}) %collective-permute-start.15) | collective-permute-done | bytes 81952 | tf_op jit(solution)/shard_map/ppermute | solution.py:62
  53.1 1.1 %collective-permute-done.14 = bf16[4,40,256]{2,1,0:T(8,128)(2,1)S(1)} collective-permute-done((bf16[4,40,256]{2,1,0:T(8,128)(2,1)S(1)}, bf16[4,40,256]{2,1,0:T(8,128)(2,1)S(1)}, u32[]{:S(2)}, u32[]{:S(2)}) %collective-permute-start.14) | collective-permute-done | bytes 81952 | tf_op jit(solution)/shard_map/ppermute | solution.py:62
  54.3 1.0 %collective-permute-start.18 = (bf16[2,40,256]{2,1,0:T(8,128)(2,1)S(1)}, bf16[2,40,256]{2,1,0:T(8,128)(2,1)S(1)}, u32[]{:S(2)}, u32[]{:S(2)}) collective-permute-start(bf16[2,40,256]{2,1,0:T(8,128)(2,1)S(1)} %slice.92), channel_id=1, source_target_pairs={{0,8},{1,9},{2,10},{3,11},{4,12},{5,13},{6,14},{7,15},{8,0},{9,1},... | collective-permute-start | bytes 122888 | tf_op jit(solution)/shard_map/ppermute | solution.py:62
  55.3 0.1 collective-permute-start.17
  55.4 0.7 %collective-permute-start.16 = (bf16[3,51,192]{2,1,0:T(8,128)(2,1)S(1)}, bf16[3,51,192]{2,1,0:T(8,128)(2,1)S(1)}, u32[]{:S(2)}, u32[]{:S(2)}) collective-permute-start(bf16[3,51,192]{2,1,0:T(8,128)(2,1)S(1)} %get-tuple-element.93), channel_id=1, source_target_pairs={{1,2},{2,1},{5,6},{6,5},{9,10},{10,9},{13,14},{14,13},{17,18},{18,... | collective-permute-start | bytes 176264 | tf_op jit(solution)/shard_map/ppermute | solution.py:72
  56.0 2.1 %field.4 = (bf16[45,45,192]{2,1,0:T(8,128)(2,1)}, bf16[15,45,192]{2,1,0:T(8,128)(2,1)S(1)}) custom-call(f32[2,11,8,128]{3,2,1,0:T(8,128)S(1)} %get-tuple-element.64.refs_0_, bf16[45,48,256]{2,1,0:T(8,128)(2,1)S(1)} %get-tuple-element.57.refs_5_.refs_1_, bf16[45,48,256]{2,1,0:T(8,128)(2,1)S(1)} %get-tuple-element.58.refs_1_.refs_2_, ...), custom_call_target="tpu_custom_call" | custom-call | flops 3630000128 | tf_op jit(solution)/shard_map/field/pallas_call | solution.py:786
  58.2 0.2 collective-permute-done.18
  58.4 1.2 %collective-permute-start.19 = (bf16[1,40,256]{2,1,0:T(8,128)(2,1)S(1)}, bf16[1,40,256]{2,1,0:T(8,128)(2,1)S(1)}, u32[]{:S(2)}, u32[]{:S(2)}) collective-permute-start(bf16[1,40,256]{2,1,0:T(8,128)(2,1)S(1)} %slice.93), channel_id=1, source_target_pairs={{0,16},{1,17},{2,18},{3,19},{4,20},{5,21},{6,22},{7,23},{8,24},{9,... | collective-permute-start | bytes 61448 | tf_op jit(solution)/shard_map/ppermute | solution.py:62
  59.5 0.0 collective-permute-done.17
  59.5 0.0 collective-permute-done.16
  59.5 0.0 copy-start.3
  59.6 0.0 copy-start.4
  59.6 2.4 %field.5 = bf16[45,45,192]{2,1,0:T(8,128)(2,1)} custom-call(f32[2,11,8,128]{3,2,1,0:T(8,128)S(1)} %get-tuple-element.64.refs_0_, bf16[45,48,256]{2,1,0:T(8,128)(2,1)S(1)} %get-tuple-element.57.refs_5_.refs_1_, bf16[45,48,256]{2,1,0:T(8,128)(2,1)S(1)} %get-tuple-element.58.refs_1_.refs_2_, ...), custom_call_target="tpu_custom_call", output_to_operand_aliasing={{}: (8, {})} | custom-call | flops 2420000000 | tf_op jit(solution)/shard_map/field/pallas_call | solution.py:786
  62.0 1.1 %collective-permute-done.19 = bf16[1,40,256]{2,1,0:T(8,128)(2,1)S(1)} collective-permute-done((bf16[1,40,256]{2,1,0:T(8,128)(2,1)S(1)}, bf16[1,40,256]{2,1,0:T(8,128)(2,1)S(1)}, u32[]{:S(2)}, u32[]{:S(2)}) %collective-permute-start.19) | collective-permute-done | bytes 20512 | tf_op jit(solution)/shard_map/ppermute | solution.py:62
  63.1 0.0 copy-done.3
  63.2 0.7 %multiply_add_fusion = f32[9568]{0:T(1024)} fusion(f32[9568]{0:T(1024)S(1)} %copy-done.4, f32[9568]{0:T(1024)S(1)} %copy-done.3, f32[10240]{0:T(1024)S(1)} %bitcast.4, s32[]{:T(128)S(6)} %select_n.127), kind=kLoop, calls=%fused_computation.26 | loop fusion | flops 38272 | bytes 153092 | tf_op jit(solution)/shard_map/add | solution.py:840
  (28 shorter events, 0.4 us)
Async XLA Ops:
  1.5 5.9 %collective-permute-start = (bf16[1,40,256]{2,1,0:T(8,128)(2,1)S(1)}, bf16[1,40,256]{2,1,0:T(8,128)(2,1)S(1)}, u32[]{:S(2)}, u32[]{:S(2)}) collective-permute-start(bf16[1,40,256]{2,1,0:T(8,128)(2,1)S(1)} %reshape.16), channel_id=1, source_target_pairs={{0,16},{1,17},{2,18},{3,19},{4,20},{5,21},{6,22},{7,23},{8,24},{9,... | collective-permute-start | bytes 61448 | tf_op jit(solution)/shard_map/ppermute | solution.py:62
  5.7 1.2 %copy-start.1 = (bf16[45,45,192]{2,1,0:T(8,128)(2,1)S(1)}, bf16[45,45,192]{2,1,0:T(8,128)(2,1)}, u32[]{:S(2)}) copy-start(bf16[45,45,192]{2,1,0:T(8,128)(2,1)} %refs_0_.7) | copy-start | bytes 2332804
  6.9 11.5 %copy-start.2 = (bf16[45,45,192]{2,1,0:T(8,128)(2,1)S(1)}, bf16[45,45,192]{2,1,0:T(8,128)(2,1)}, u32[]{:S(2)}) copy-start(bf16[45,45,192]{2,1,0:T(8,128)(2,1)} %refs_0_.7) | copy-start | bytes 2332804
  7.4 6.0 %collective-permute-start.1 = (bf16[2,40,256]{2,1,0:T(8,128)(2,1)S(1)}, bf16[2,40,256]{2,1,0:T(8,128)(2,1)S(1)}, u32[]{:S(2)}, u32[]{:S(2)}) collective-permute-start(bf16[2,40,256]{2,1,0:T(8,128)(2,1)S(1)} %get-tuple-element.106), channel_id=1, source_target_pairs={{0,8},{1,9},{2,10},{3,11},{4,12},{5,13},{6,14},{7,15},{8,0},{9,1},... | collective-permute-start | bytes 122888 | tf_op jit(solution)/shard_map/ppermute | solution.py:62
  9.4 7.6 %collective-permute-start.6 = (bf16[45,3,192]{2,1,0:T(4,128)(2,1)S(1)}, bf16[45,3,192]{2,1,0:T(4,128)(2,1)S(1)}, u32[]{:S(2)}, u32[]{:S(2)}) collective-permute-start(bf16[45,3,192]{2,1,0:T(4,128)(2,1)S(1)} %get-tuple-element.88), channel_id=1, source_target_pairs={{0,4},{4,0},{8,12},{12,8},{16,20},{20,16},{24,28},{28,24},{1,5},{5... | collective-permute-start | bytes 155528 | tf_op jit(solution)/shard_map/ppermute | solution.py:71
  11.0 7.4 %collective-permute-start.5 = (bf16[45,3,192]{2,1,0:T(4,128)(2,1)S(1)}, bf16[45,3,192]{2,1,0:T(4,128)(2,1)S(1)}, u32[]{:S(2)}, u32[]{:S(2)}) collective-permute-start(bf16[45,3,192]{2,1,0:T(4,128)(2,1)S(1)} %get-tuple-element.89), channel_id=1, source_target_pairs={{4,8},{12,16},{20,24},{28,0},{8,4},{16,12},{24,20},{0,28},{5,9},{1... | collective-permute-start | bytes 155528 | tf_op jit(solution)/shard_map/ppermute | solution.py:72
  13.4 8.5 %collective-permute-start.4 = (bf16[4,40,256]{2,1,0:T(8,128)(2,1)S(1)}, bf16[4,40,256]{2,1,0:T(8,128)(2,1)S(1)}, u32[]{:S(2)}, u32[]{:S(2)}) collective-permute-start(bf16[4,40,256]{2,1,0:T(8,128)(2,1)S(1)} %get-tuple-element.102), channel_id=1, source_target_pairs={{0,6},{1,7},{2,4},{3,5},{4,2},{5,3},{6,0},{7,1},{8,14},{9,15},{10,... | collective-permute-start | bytes 245768 | tf_op jit(solution)/shard_map/ppermute | solution.py:62
  14.3 7.6 %collective-permute-start.3 = (bf16[4,40,256]{2,1,0:T(8,128)(2,1)S(1)}, bf16[4,40,256]{2,1,0:T(8,128)(2,1)S(1)}, u32[]{:S(2)}, u32[]{:S(2)}) collective-permute-start(bf16[4,40,256]{2,1,0:T(8,128)(2,1)S(1)} %get-tuple-element.102), channel_id=1, source_target_pairs={{0,2},{1,3},{2,0},{3,1},{4,6},{5,7},{6,4},{7,5},{8,10},{9,11},{10,... | collective-permute-start | bytes 245768 | tf_op jit(solution)/shard_map/ppermute | solution.py:62
  15.1 6.8 %collective-permute-start.2 = (bf16[4,40,256]{2,1,0:T(8,128)(2,1)S(1)}, bf16[4,40,256]{2,1,0:T(8,128)(2,1)S(1)}, u32[]{:S(2)}, u32[]{:S(2)}) collective-permute-start(bf16[4,40,256]{2,1,0:T(8,128)(2,1)S(1)} %get-tuple-element.102), channel_id=1, source_target_pairs={{0,4},{1,5},{2,6},{3,7},{4,0},{5,1},{6,2},{7,3},{8,12},{9,13},{10,... | collective-permute-start | bytes 245768 | tf_op jit(solution)/shard_map/ppermute | solution.py:62
  18.4 1.2 %copy-start = (bf16[45,45,192]{2,1,0:T(8,128)(2,1)S(1)}, bf16[45,45,192]{2,1,0:T(8,128)(2,1)}, u32[]{:S(2)}) copy-start(bf16[45,45,192]{2,1,0:T(8,128)(2,1)} %refs_3_) | copy-start | bytes 2332804
  18.5 6.2 %collective-permute-start.9 = (bf16[3,51,192]{2,1,0:T(8,128)(2,1)S(1)}, bf16[3,51,192]{2,1,0:T(8,128)(2,1)S(1)}, u32[]{:S(2)}, u32[]{:S(2)}) collective-permute-start(bf16[3,51,192]{2,1,0:T(8,128)(2,1)S(1)} %get-tuple-element.96), channel_id=1, source_target_pairs={{0,1},{1,0},{2,3},{3,2},{4,5},{5,4},{6,7},{7,6},{8,9},{9,8},{10,11... | collective-permute-start | bytes 176264 | tf_op jit(solution)/shard_map/ppermute | solution.py:71
  18.6 6.1 %collective-permute-start.8 = (bf16[3,51,192]{2,1,0:T(8,128)(2,1)S(1)}, bf16[3,51,192]{2,1,0:T(8,128)(2,1)S(1)}, u32[]{:S(2)}, u32[]{:S(2)}) collective-permute-start(bf16[3,51,192]{2,1,0:T(8,128)(2,1)S(1)} %get-tuple-element.97), channel_id=1, source_target_pairs={{1,2},{2,1},{5,6},{6,5},{9,10},{10,9},{13,14},{14,13},{17,18},{18,... | collective-permute-start | bytes 176264 | tf_op jit(solution)/shard_map/ppermute | solution.py:72
  22.0 3.9 %collective-permute-start.7 = (bf16[16,40,256]{2,1,0:T(8,128)(2,1)S(1)}, bf16[16,40,256]{2,1,0:T(8,128)(2,1)S(1)}, u32[]{:S(2)}, u32[]{:S(2)}) collective-permute-start(bf16[16,40,256]{2,1,0:T(8,128)(2,1)S(1)} %constant_dynamic-update-slice_fusion.5), channel_id=1, source_target_pairs={{0,1},{1,0},{2,3},{3,2},{4,5},{5,4},{6,7},{7,6},{8,9},{9,8},{10,11... | collective-permute-start | bytes 983048 | tf_op jit(solution)/shard_map/ppermute | solution.py:62
  37.4 7.0 %collective-permute-start.12 = (bf16[45,3,192]{2,1,0:T(4,128)(2,1)S(1)}, bf16[45,3,192]{2,1,0:T(4,128)(2,1)S(1)}, u32[]{:S(2)}, u32[]{:S(2)}) collective-permute-start(bf16[45,3,192]{2,1,0:T(4,128)(2,1)S(1)} %get-tuple-element.79), channel_id=1, source_target_pairs={{0,4},{4,0},{8,12},{12,8},{16,20},{20,16},{24,28},{28,24},{1,5},{5... | collective-permute-start | bytes 155528 | tf_op jit(solution)/shard_map/ppermute | solution.py:71
  37.5 7.7 %collective-permute-start.11 = (bf16[45,3,192]{2,1,0:T(4,128)(2,1)S(1)}, bf16[45,3,192]{2,1,0:T(4,128)(2,1)S(1)}, u32[]{:S(2)}, u32[]{:S(2)}) collective-permute-start(bf16[45,3,192]{2,1,0:T(4,128)(2,1)S(1)} %get-tuple-element.80), channel_id=1, source_target_pairs={{4,8},{12,16},{20,24},{28,0},{8,4},{16,12},{24,20},{0,28},{5,9},{1... | collective-permute-start | bytes 155528 | tf_op jit(solution)/shard_map/ppermute | solution.py:72
  44.3 1.7 %collective-permute-start.10 = (bf16[16,40,256]{2,1,0:T(8,128)(2,1)S(1)}, bf16[16,40,256]{2,1,0:T(8,128)(2,1)S(1)}, u32[]{:S(2)}, u32[]{:S(2)}) collective-permute-start(bf16[16,40,256]{2,1,0:T(8,128)(2,1)S(1)} %slice.60), channel_id=1, source_target_pairs={{0,1},{1,0},{2,3},{3,2},{4,5},{5,4},{6,7},{7,6},{8,9},{9,8},{10,11... | collective-permute-start | bytes 983048 | tf_op jit(solution)/shard_map/ppermute | solution.py:62
  46.1 6.3 %collective-permute-start.13 = (bf16[4,40,256]{2,1,0:T(8,128)(2,1)S(1)}, bf16[4,40,256]{2,1,0:T(8,128)(2,1)S(1)}, u32[]{:S(2)}, u32[]{:S(2)}) collective-permute-start(bf16[4,40,256]{2,1,0:T(8,128)(2,1)S(1)} %get-tuple-element.81), channel_id=1, source_target_pairs={{0,4},{1,5},{2,6},{3,7},{4,0},{5,1},{6,2},{7,3},{8,12},{9,13},{10,... | collective-permute-start | bytes 245768 | tf_op jit(solution)/shard_map/ppermute | solution.py:62
  46.2 6.9 %collective-permute-start.15 = (bf16[4,40,256]{2,1,0:T(8,128)(2,1)S(1)}, bf16[4,40,256]{2,1,0:T(8,128)(2,1)S(1)}, u32[]{:S(2)}, u32[]{:S(2)}) collective-permute-start(bf16[4,40,256]{2,1,0:T(8,128)(2,1)S(1)} %get-tuple-element.82), channel_id=1, source_target_pairs={{0,6},{1,7},{2,4},{3,5},{4,2},{5,3},{6,0},{7,1},{8,14},{9,15},{10,... | collective-permute-start | bytes 245768 | tf_op jit(solution)/shard_map/ppermute | solution.py:62
  48.8 5.4 %collective-permute-start.14 = (bf16[4,40,256]{2,1,0:T(8,128)(2,1)S(1)}, bf16[4,40,256]{2,1,0:T(8,128)(2,1)S(1)}, u32[]{:S(2)}, u32[]{:S(2)}) collective-permute-start(bf16[4,40,256]{2,1,0:T(8,128)(2,1)S(1)} %get-tuple-element.83), channel_id=1, source_target_pairs={{0,2},{1,3},{2,0},{3,1},{4,6},{5,7},{6,4},{7,5},{8,10},{9,11},{10,... | collective-permute-start | bytes 245768 | tf_op jit(solution)/shard_map/ppermute | solution.py:62
  54.3 4.1 %collective-permute-start.18 = (bf16[2,40,256]{2,1,0:T(8,128)(2,1)S(1)}, bf16[2,40,256]{2,1,0:T(8,128)(2,1)S(1)}, u32[]{:S(2)}, u32[]{:S(2)}) collective-permute-start(bf16[2,40,256]{2,1,0:T(8,128)(2,1)S(1)} %slice.92), channel_id=1, source_target_pairs={{0,8},{1,9},{2,10},{3,11},{4,12},{5,13},{6,14},{7,15},{8,0},{9,1},... | collective-permute-start | bytes 122888 | tf_op jit(solution)/shard_map/ppermute | solution.py:62
  55.3 4.2 %collective-permute-start.17 = (bf16[3,51,192]{2,1,0:T(8,128)(2,1)S(1)}, bf16[3,51,192]{2,1,0:T(8,128)(2,1)S(1)}, u32[]{:S(2)}, u32[]{:S(2)}) collective-permute-start(bf16[3,51,192]{2,1,0:T(8,128)(2,1)S(1)} %get-tuple-element.92), channel_id=1, source_target_pairs={{0,1},{1,0},{2,3},{3,2},{4,5},{5,4},{6,7},{7,6},{8,9},{9,8},{10,11... | collective-permute-start | bytes 176264 | tf_op jit(solution)/shard_map/ppermute | solution.py:71
  55.4 4.1 %collective-permute-start.16 = (bf16[3,51,192]{2,1,0:T(8,128)(2,1)S(1)}, bf16[3,51,192]{2,1,0:T(8,128)(2,1)S(1)}, u32[]{:S(2)}, u32[]{:S(2)}) collective-permute-start(bf16[3,51,192]{2,1,0:T(8,128)(2,1)S(1)} %get-tuple-element.93), channel_id=1, source_target_pairs={{1,2},{2,1},{5,6},{6,5},{9,10},{10,9},{13,14},{14,13},{17,18},{18,... | collective-permute-start | bytes 176264 | tf_op jit(solution)/shard_map/ppermute | solution.py:72
  58.4 4.7 %collective-permute-start.19 = (bf16[1,40,256]{2,1,0:T(8,128)(2,1)S(1)}, bf16[1,40,256]{2,1,0:T(8,128)(2,1)S(1)}, u32[]{:S(2)}, u32[]{:S(2)}) collective-permute-start(bf16[1,40,256]{2,1,0:T(8,128)(2,1)S(1)} %slice.93), channel_id=1, source_target_pairs={{0,16},{1,17},{2,18},{3,19},{4,20},{5,21},{6,22},{7,23},{8,24},{9,... | collective-permute-start | bytes 61448 | tf_op jit(solution)/shard_map/ppermute | solution.py:62
  59.5 3.6 %copy-start.3 = (f32[9568]{0:T(1024)S(1)}, f32[9568]{0:T(1024)}, u32[]{:S(2)}) copy-start(f32[9568]{0:T(1024)} %param.5) | copy-start | bytes 114820
  59.6 3.6 %copy-start.4 = (f32[9568]{0:T(1024)S(1)}, f32[9568]{0:T(1024)}, u32[]{:S(2)}) copy-start(f32[9568]{0:T(1024)} %param.6) | copy-start | bytes 114820

commit v11 on v10

--- a/solution.py
+++ b/solution.py
@@ -279,19 +279,13 @@
     count = len(filters)
     lon_regs = x_ref.shape[2] // 8
 
-    def body(step, carry):
+    for step in range(2 * lon_regs):
         tile = step // lon_regs
-        lon = pl.ds(pl.multiple_of(step % lon_regs * 8, 8), 8)
-
-        def block(k, carry):
+        lon = pl.ds(step % lon_regs * 8, 8)
+        for k in range(blocks):
             rows = [x_ref[tile, base + k * out_rows + r, lon, :] for r in range(count)]
             for i, value in enumerate(data_points(pairs, rows)):
                 v_ref[tile, (done + k) * count + i, lon, :] = value
-            return carry
-
-        return lax.fori_loop(0, blocks, block, carry, unroll=True)
-
-    lax.fori_loop(0, 2 * lon_regs, body, 0)
 
 
 def filter_points(taps_ref, out_rows, u_ref, flip):

time: 64.7 us -> 64.4 us (level)
  Pallas kernels: 26.2 us -> 24.8 us
  waiting for transfers between devices: 6.28 us -> 7.46 us
    ppermute x12, waiting for transfers between devices: 4.2 us -> 5.43 us  [swap(): return lax.ppermute(values, ('lon', 'lat'), pairs)]
    pallas_call x3, Pallas kernels: 7.17 us -> 6.18 us  [field_piece(): pl.pallas_call(lambda *refs: field_kernel(ranges, rows, cols, lon_pad, co...]
  transfers between devices with their start and end apart: 20 -> 20, of which waited for: 9 -> 9; matrix products, arithmetic and copies ran while one was open for 1% -> 1% of each run, Pallas kernels for 23% -> 21%
where the time goes in v11:
time: 64.4 us; the launch traced here: 63.6 us
  starting transfers between devices  26.3 us (41%)
  Pallas kernels  24.8 us (39%)
  waiting for transfers between devices  7.46 us (12%)
  local copies, waits for them, and re-layouts  2.57 us (4%)
  other arithmetic  1.42 us (2%)
  between operations  1.06 us (2%)
    ppermute x12, starting transfers between devices, swap(): return lax.ppermute(values, ('lon', 'lat'), pairs)  18.1 us
    pallas_call x1, Pallas kernels, body(): pl.pallas_call(lambda *refs: layer_kernel(rows, lon_pad, block_rows, *ref...  7.73 us
    ppermute x4, starting transfers between devices, send_edges(): far = lax.ppermute(jnp.where(even, low_edge, high_edge), axis, far)  6.45 us
    pallas_call x3, Pallas kernels, field_piece(): pl.pallas_call(lambda *refs: field_kernel(ranges, rows, cols, lon_pad, co...  6.18 us
    ppermute x12, waiting for transfers between devices, swap(): return lax.ppermute(values, ('lon', 'lat'), pairs)  5.43 us
    pallas_call x1, Pallas kernels, body(): pl.pallas_call(lambda *refs: taps_kernel(*static, *refs), out_shape=(shap...  4.27 us
    pallas_call x1, Pallas kernels, body(): pl.pallas_call(lambda *refs: conv_kernel(*static, *refs), out_shape=(shap...  3.7 us
    pallas_call x1, Pallas kernels, body(): pl.pallas_call(lambda *refs: inner_kernel(inner, rows, cols, conv_rows, *...  2.08 us
  transfers between devices with their start and end apart: 20, of which 9 were waited for; matrix products, arithmetic and copies ran while one was open for 1% of the time, Pallas kernels for 21%

profile of v11, /device:TPU:0, one launch (start us, length us, event | category | flops | bytes accessed | tf_op | source)
XLA Modules:
  0.0 63.6 jit_solution(13651557956655318985)
XLA Ops:
  0.7 0.9 %fusion = bf16[10240]{0:T(1024)(128)(2,1)S(1)} fusion(s32[]{:T(128)S(6)} %select_n.106, f32[9568]{0:T(1024)} %param.5), kind=kLoop, calls=%fused_computation.24 | loop fusion | bytes 58756 | tf_op jit(solution)/shard_map/convert_element_type | solution.py:633
  1.5 4.1 %collective-permute-start = (bf16[1,40,256]{2,1,0:T(8,128)(2,1)S(1)}, bf16[1,40,256]{2,1,0:T(8,128)(2,1)S(1)}, u32[]{:S(2)}, u32[]{:S(2)}) collective-permute-start(bf16[1,40,256]{2,1,0:T(8,128)(2,1)S(1)} %reshape.16), channel_id=1, source_target_pairs={{0,16},{1,17},{2,18},{3,19},{4,20},{5,21},{6,22},{7,23},{8,24},{9,... | collective-permute-start | bytes 61448 | tf_op jit(solution)/shard_map/ppermute | solution.py:62
  5.7 1.2 %copy-done.1 = bf16[45,45,192]{2,1,0:T(8,128)(2,1)S(1)} copy-done((bf16[45,45,192]{2,1,0:T(8,128)(2,1)S(1)}, bf16[45,45,192]{2,1,0:T(8,128)(2,1)}, u32[]{:S(2)}) %copy-start.1) | copy-done | bytes 777624
  6.9 0.2 edges.1
  7.2 0.2 collective-permute-done
  7.4 1.9 %collective-permute-start.1 = (bf16[2,40,256]{2,1,0:T(8,128)(2,1)S(1)}, bf16[2,40,256]{2,1,0:T(8,128)(2,1)S(1)}, u32[]{:S(2)}, u32[]{:S(2)}) collective-permute-start(bf16[2,40,256]{2,1,0:T(8,128)(2,1)S(1)} %get-tuple-element.106), channel_id=1, source_target_pairs={{0,8},{1,9},{2,10},{3,11},{4,12},{5,13},{6,14},{7,15},{8,0},{9,1},... | collective-permute-start | bytes 122888 | tf_op jit(solution)/shard_map/ppermute | solution.py:62
  9.3 0.1 broadcast_select_fusion.6
  9.4 1.6 %collective-permute-start.6 = (bf16[45,3,192]{2,1,0:T(4,128)(2,1)S(1)}, bf16[45,3,192]{2,1,0:T(4,128)(2,1)S(1)}, u32[]{:S(2)}, u32[]{:S(2)}) collective-permute-start(bf16[45,3,192]{2,1,0:T(4,128)(2,1)S(1)} %get-tuple-element.88), channel_id=1, source_target_pairs={{0,4},{4,0},{8,12},{12,8},{16,20},{20,16},{24,28},{28,24},{1,5},{5... | collective-permute-start | bytes 155528 | tf_op jit(solution)/shard_map/ppermute | solution.py:71
  11.0 2.5 %collective-permute-start.5 = (bf16[45,3,192]{2,1,0:T(4,128)(2,1)S(1)}, bf16[45,3,192]{2,1,0:T(4,128)(2,1)S(1)}, u32[]{:S(2)}, u32[]{:S(2)}) collective-permute-start(bf16[45,3,192]{2,1,0:T(4,128)(2,1)S(1)} %get-tuple-element.89), channel_id=1, source_target_pairs={{4,8},{12,16},{20,24},{28,0},{8,4},{16,12},{24,20},{0,28},{5,9},{1... | collective-permute-start | bytes 155528 | tf_op jit(solution)/shard_map/ppermute | solution.py:72
  13.4 0.0 collective-permute-done.1
  13.4 0.9 %collective-permute-start.4 = (bf16[4,40,256]{2,1,0:T(8,128)(2,1)S(1)}, bf16[4,40,256]{2,1,0:T(8,128)(2,1)S(1)}, u32[]{:S(2)}, u32[]{:S(2)}) collective-permute-start(bf16[4,40,256]{2,1,0:T(8,128)(2,1)S(1)} %get-tuple-element.102), channel_id=1, source_target_pairs={{0,6},{1,7},{2,4},{3,5},{4,2},{5,3},{6,0},{7,1},{8,14},{9,15},{10,... | collective-permute-start | bytes 245768 | tf_op jit(solution)/shard_map/ppermute | solution.py:62
  14.3 0.8 %collective-permute-start.3 = (bf16[4,40,256]{2,1,0:T(8,128)(2,1)S(1)}, bf16[4,40,256]{2,1,0:T(8,128)(2,1)S(1)}, u32[]{:S(2)}, u32[]{:S(2)}) collective-permute-start(bf16[4,40,256]{2,1,0:T(8,128)(2,1)S(1)} %get-tuple-element.102), channel_id=1, source_target_pairs={{0,2},{1,3},{2,0},{3,1},{4,6},{5,7},{6,4},{7,5},{8,10},{9,11},{10,... | collective-permute-start | bytes 245768 | tf_op jit(solution)/shard_map/ppermute | solution.py:62
  15.1 1.9 %collective-permute-start.2 = (bf16[4,40,256]{2,1,0:T(8,128)(2,1)S(1)}, bf16[4,40,256]{2,1,0:T(8,128)(2,1)S(1)}, u32[]{:S(2)}, u32[]{:S(2)}) collective-permute-start(bf16[4,40,256]{2,1,0:T(8,128)(2,1)S(1)} %get-tuple-element.102), channel_id=1, source_target_pairs={{0,4},{1,5},{2,6},{3,7},{4,0},{5,1},{6,2},{7,3},{8,12},{9,13},{10,... | collective-permute-start | bytes 245768 | tf_op jit(solution)/shard_map/ppermute | solution.py:62
  17.0 0.0 collective-permute-done.6
  17.0 1.3 %collective-permute-done.5 = bf16[45,3,192]{2,1,0:T(4,128)(2,1)S(1)} collective-permute-done((bf16[45,3,192]{2,1,0:T(4,128)(2,1)S(1)}, bf16[45,3,192]{2,1,0:T(4,128)(2,1)S(1)}, u32[]{:S(2)}, u32[]{:S(2)}) %collective-permute-start.5) | collective-permute-done | bytes 51872 | tf_op jit(solution)/shard_map/ppermute | solution.py:72
  18.3 0.1 broadcast_select_fusion.4
  18.4 0.0 copy-done.2
  18.4 0.0 copy-start
  18.5 0.1 collective-permute-start.9
  18.6 0.8 %collective-permute-start.8 = (bf16[3,51,192]{2,1,0:T(8,128)(2,1)S(1)}, bf16[3,51,192]{2,1,0:T(8,128)(2,1)S(1)}, u32[]{:S(2)}, u32[]{:S(2)}) collective-permute-start(bf16[3,51,192]{2,1,0:T(8,128)(2,1)S(1)} %get-tuple-element.97), channel_id=1, source_target_pairs={{1,2},{2,1},{5,6},{6,5},{9,10},{10,9},{13,14},{14,13},{17,18},{18,... | collective-permute-start | bytes 176264 | tf_op jit(solution)/shard_map/ppermute | solution.py:72
  19.4 0.3 copy-done
  19.7 2.1 %inner.1 = (f32[2,77,56,128]{3,2,1,0:T(8,128)S(1)}, bf16[45,48,256]{2,1,0:T(8,128)(2,1)S(1)}, bf16[45,48,256]{2,1,0:T(8,128)(2,1)S(1)}) custom-call(bf16[45,45,192]{2,1,0:T(8,128)(2,1)S(1)} %copy-done.2, bf16[45,3,192]{2,1,0:T(4,128)(2,1)S(1)} %get-tuple-element.44.refs_1_, bf16[45,3,192]{2,1,0:T(4,128)(2,1)S(1)} %get-tuple-element.45.refs_2_, ...), custom_call_target="tpu_custom_call" | custom-call | flops 2750000128 | tf_op jit(solution)/shard_map/inner/pallas_call | solution.py:666
  21.7 0.0 collective-permute-done.2
  21.8 0.0 collective-permute-done.3
  21.8 0.0 collective-permute-done.4
  21.8 2.7 %collective-permute-start.7 = (bf16[16,40,256]{2,1,0:T(8,128)(2,1)S(1)}, bf16[16,40,256]{2,1,0:T(8,128)(2,1)S(1)}, u32[]{:S(2)}, u32[]{:S(2)}) collective-permute-start(bf16[16,40,256]{2,1,0:T(8,128)(2,1)S(1)} %constant_dynamic-update-slice_fusion.5), channel_id=1, source_target_pairs={{0,1},{1,0},{2,3},{3,2},{4,5},{5,4},{6,7},{7,6},{8,9},{9,8},{10,11... | collective-permute-start | bytes 983048 | tf_op jit(solution)/shard_map/ppermute | solution.py:62
  24.5 0.0 collective-permute-done.9
  24.5 0.0 collective-permute-done.8
  24.5 0.5 outer.1.refs_3_
  25.1 0.7 %collective-permute-done.7 = bf16[16,40,256]{2,1,0:T(8,128)(2,1)S(1)} collective-permute-done((bf16[16,40,256]{2,1,0:T(8,128)(2,1)S(1)}, bf16[16,40,256]{2,1,0:T(8,128)(2,1)S(1)}, u32[]{:S(2)}, u32[]{:S(2)}) %collective-permute-start.7) | collective-permute-done | bytes 327712 | tf_op jit(solution)/shard_map/ppermute | solution.py:62
  25.7 0.1 pad_maximum_fusion.refs_1_
  25.8 3.7 %conv.1 = (f32[2,45,48,128]{3,2,1,0:T(8,128)S(1)}, bf16[256,768]{1,0:T(8,128)(2,1)S(1)}, bf16[768,256]{1,0:T(8,128)(2,1)S(1)}, f32[2,64,128]{2,1,0:T(8,128)S(1)}, f32[2,11,8,128]{3,2,1,0:T(8,128)S(1)}) custom-call(s32[1]{0:T(128)} %bitcast.refs_0_, bf16[32,40,256]{2,1,0:T(8,128)(2,1)S(1)} %pad_maximum_fusion.refs_1_, ...), custom_call_target="tpu_custom_call" | custom-call | flops 6600000000 | tf_op jit(solution)/shard_map/conv/pallas_call | solution.py:698
  29.5 7.7 %layer.1 = (bf16[45,45,192]{2,1,0:T(8,128)(2,1)S(1)}, bf16[45,48,256]{2,1,0:T(8,128)(2,1)S(1)}, f32[200,768]{1,0:T(8,128)S(1)}, f32[192,768]{1,0:T(8,128)S(1)}, f32[5,2,8,128]{3,2,1,0:T(8,128)S(1)}) custom-call(f32[2,45,48,128]{3,2,1,0:T(8,128)S(1)} %get-tuple-element.52.refs_0_, bf16[256,768]{1,0:T(8,128)(2,1)S(1)} %get-tuple-element.53.refs_1_, ...), custom_call_target="tpu_custom_call" | custom-call | flops 17600000000 | tf_op jit(solution)/shard_map/layer/pallas_call | solution.py:719
  37.3 0.1 broadcast_select_fusion.2
  37.4 0.1 collective-permute-start.12
  37.4 2.5 %collective-permute-start.11 = (bf16[45,3,192]{2,1,0:T(4,128)(2,1)S(1)}, bf16[45,3,192]{2,1,0:T(4,128)(2,1)S(1)}, u32[]{:S(2)}, u32[]{:S(2)}) collective-permute-start(bf16[45,3,192]{2,1,0:T(4,128)(2,1)S(1)} %get-tuple-element.80), channel_id=1, source_target_pairs={{4,8},{12,16},{20,24},{28,0},{8,4},{16,12},{24,20},{0,28},{5,9},{1... | collective-permute-start | bytes 155528 | tf_op jit(solution)/shard_map/ppermute | solution.py:72
  40.0 4.3 %taps.1 = (bf16[32,40,256]{2,1,0:T(8,128)(2,1)S(1)}, bf16[45,45,192]{2,1,0:T(8,128)(2,1)}) custom-call(s32[1]{0:T(128)} %bitcast.refs_0_, bf16[45,48,256]{2,1,0:T(8,128)(2,1)S(1)} %get-tuple-element.58.refs_1_.refs_2_, f32[2,77,56,128]{3,2,1,0:T(8,128)S(1)} %get-tuple-element.49.refs_2_, f32[2,22,56,128]{3,2,1,0:T(8,128)S(1)} %outer.1.refs_3_, ...), custom_call_target="tpu_custom_call" | custom-call | flops 12099999744 | tf_op jit(solution)/shard_map/taps/pallas_call | solution.py:736
  44.3 0.1 collective-permute-start.10
  44.4 0.0 collective-permute-done.12
  44.5 0.7 %collective-permute-done.11 = bf16[45,3,192]{2,1,0:T(4,128)(2,1)S(1)} collective-permute-done((bf16[45,3,192]{2,1,0:T(4,128)(2,1)S(1)}, bf16[45,3,192]{2,1,0:T(4,128)(2,1)S(1)}, u32[]{:S(2)}, u32[]{:S(2)}) %collective-permute-start.11) | collective-permute-done | bytes 51872 | tf_op jit(solution)/shard_map/ppermute | solution.py:72
  45.1 0.1 broadcast_select_fusion
  45.2 0.8 %collective-permute-done.10 = bf16[16,40,256]{2,1,0:T(8,128)(2,1)S(1)} collective-permute-done((bf16[16,40,256]{2,1,0:T(8,128)(2,1)S(1)}, bf16[16,40,256]{2,1,0:T(8,128)(2,1)S(1)}, u32[]{:S(2)}, u32[]{:S(2)}) %collective-permute-start.10) | collective-permute-done | bytes 327712 | tf_op jit(solution)/shard_map/ppermute | solution.py:62
  46.0 0.1 convert_add_fusion
  46.1 0.1 collective-permute-start.13
  46.2 2.3 %collective-permute-start.15 = (bf16[4,40,256]{2,1,0:T(8,128)(2,1)S(1)}, bf16[4,40,256]{2,1,0:T(8,128)(2,1)S(1)}, u32[]{:S(2)}, u32[]{:S(2)}) collective-permute-start(bf16[4,40,256]{2,1,0:T(8,128)(2,1)S(1)} %get-tuple-element.82), channel_id=1, source_target_pairs={{0,6},{1,7},{2,4},{3,5},{4,2},{5,3},{6,0},{7,1},{8,14},{9,15},{10,... | collective-permute-start | bytes 245768 | tf_op jit(solution)/shard_map/ppermute | solution.py:62
  48.5 1.2 %collective-permute-start.14 = (bf16[4,40,256]{2,1,0:T(8,128)(2,1)S(1)}, bf16[4,40,256]{2,1,0:T(8,128)(2,1)S(1)}, u32[]{:S(2)}, u32[]{:S(2)}) collective-permute-start(bf16[4,40,256]{2,1,0:T(8,128)(2,1)S(1)} %get-tuple-element.83), channel_id=1, source_target_pairs={{0,2},{1,3},{2,0},{3,1},{4,6},{5,7},{6,4},{7,5},{8,10},{9,11},{10,... | collective-permute-start | bytes 245768 | tf_op jit(solution)/shard_map/ppermute | solution.py:62
  49.7 2.4 %field.3.refs_5_ = bf16[20,45,192]{2,1,0:T(8,128)(2,1)S(1)} custom-call(f32[2,11,8,128]{3,2,1,0:T(8,128)S(1)} %get-tuple-element.64.refs_0_, bf16[45,48,256]{2,1,0:T(8,128)(2,1)S(1)} %get-tuple-element.57.refs_5_.refs_1_, bf16[45,48,256]{2,1,0:T(8,128)(2,1)S(1)} %get-tuple-element.58.refs_1_.refs_2_, bf16[45,3,192]{2,1,0:T(4,128)(2,1)S(1)} %get-tuple-element.66.refs_3_, ...), custom_call_target="tpu_custom_call" | custom-call | flops 4840000000 | tf_op jit(solution)/shard_map/field/pallas_call | solution.py:780
  52.2 0.0 collective-permute-done.13
  52.2 0.6 collective-permute-done.15
  52.8 1.1 %collective-permute-done.14 = bf16[4,40,256]{2,1,0:T(8,128)(2,1)S(1)} collective-permute-done((bf16[4,40,256]{2,1,0:T(8,128)(2,1)S(1)}, bf16[4,40,256]{2,1,0:T(8,128)(2,1)S(1)}, u32[]{:S(2)}, u32[]{:S(2)}) %collective-permute-start.14) | collective-permute-done | bytes 81952 | tf_op jit(solution)/shard_map/ppermute | solution.py:62
  54.0 1.0 %collective-permute-start.18 = (bf16[2,40,256]{2,1,0:T(8,128)(2,1)S(1)}, bf16[2,40,256]{2,1,0:T(8,128)(2,1)S(1)}, u32[]{:S(2)}, u32[]{:S(2)}) collective-permute-start(bf16[2,40,256]{2,1,0:T(8,128)(2,1)S(1)} %slice.92), channel_id=1, source_target_pairs={{0,8},{1,9},{2,10},{3,11},{4,12},{5,13},{6,14},{7,15},{8,0},{9,1},... | collective-permute-start | bytes 122888 | tf_op jit(solution)/shard_map/ppermute | solution.py:62
  55.0 0.1 collective-permute-start.17
  55.1 0.7 %collective-permute-start.16 = (bf16[3,51,192]{2,1,0:T(8,128)(2,1)S(1)}, bf16[3,51,192]{2,1,0:T(8,128)(2,1)S(1)}, u32[]{:S(2)}, u32[]{:S(2)}) collective-permute-start(bf16[3,51,192]{2,1,0:T(8,128)(2,1)S(1)} %get-tuple-element.93), channel_id=1, source_target_pairs={{1,2},{2,1},{5,6},{6,5},{9,10},{10,9},{13,14},{14,13},{17,18},{18,... | collective-permute-start | bytes 176264 | tf_op jit(solution)/shard_map/ppermute | solution.py:72
  55.8 1.9 %field.4 = (bf16[45,45,192]{2,1,0:T(8,128)(2,1)}, bf16[15,45,192]{2,1,0:T(8,128)(2,1)S(1)}) custom-call(f32[2,11,8,128]{3,2,1,0:T(8,128)S(1)} %get-tuple-element.64.refs_0_, bf16[45,48,256]{2,1,0:T(8,128)(2,1)S(1)} %get-tuple-element.57.refs_5_.refs_1_, bf16[45,48,256]{2,1,0:T(8,128)(2,1)S(1)} %get-tuple-element.58.refs_1_.refs_2_, ...), custom_call_target="tpu_custom_call" | custom-call | flops 3630000128 | tf_op jit(solution)/shard_map/field/pallas_call | solution.py:780
  57.6 0.4 collective-permute-done.18
  58.1 1.2 %collective-permute-start.19 = (bf16[1,40,256]{2,1,0:T(8,128)(2,1)S(1)}, bf16[1,40,256]{2,1,0:T(8,128)(2,1)S(1)}, u32[]{:S(2)}, u32[]{:S(2)}) collective-permute-start(bf16[1,40,256]{2,1,0:T(8,128)(2,1)S(1)} %slice.93), channel_id=1, source_target_pairs={{0,16},{1,17},{2,18},{3,19},{4,20},{5,21},{6,22},{7,23},{8,24},{9,... | collective-permute-start | bytes 61448 | tf_op jit(solution)/shard_map/ppermute | solution.py:62
  59.2 0.0 collective-permute-done.17
  59.2 0.0 collective-permute-done.16
  59.3 0.0 copy-start.3
  59.3 0.0 copy-start.4
  59.3 1.9 %field.5 = bf16[45,45,192]{2,1,0:T(8,128)(2,1)} custom-call(f32[2,11,8,128]{3,2,1,0:T(8,128)S(1)} %get-tuple-element.64.refs_0_, bf16[45,48,256]{2,1,0:T(8,128)(2,1)S(1)} %get-tuple-element.57.refs_5_.refs_1_, bf16[45,48,256]{2,1,0:T(8,128)(2,1)S(1)} %get-tuple-element.58.refs_1_.refs_2_, ...), custom_call_target="tpu_custom_call", output_to_operand_aliasing={{}: (8, {})} | custom-call | flops 2420000000 | tf_op jit(solution)/shard_map/field/pallas_call | solution.py:780
  61.2 1.6 %collective-permute-done.19 = bf16[1,40,256]{2,1,0:T(8,128)(2,1)S(1)} collective-permute-done((bf16[1,40,256]{2,1,0:T(8,128)(2,1)S(1)}, bf16[1,40,256]{2,1,0:T(8,128)(2,1)S(1)}, u32[]{:S(2)}, u32[]{:S(2)}) %collective-permute-start.19) | collective-permute-done | bytes 20512 | tf_op jit(solution)/shard_map/ppermute | solution.py:62
  62.9 0.0 copy-done.3
  62.9 0.7 %multiply_add_fusion = f32[9568]{0:T(1024)} fusion(f32[9568]{0:T(1024)S(1)} %copy-done.4, f32[9568]{0:T(1024)S(1)} %copy-done.3, f32[10240]{0:T(1024)S(1)} %bitcast.4, s32[]{:T(128)S(6)} %select_n.127), kind=kLoop, calls=%fused_computation.26 | loop fusion | flops 38272 | bytes 153092 | tf_op jit(solution)/shard_map/add | solution.py:834
  (28 shorter events, 0.4 us)
Async XLA Ops:
  1.5 5.9 %collective-permute-start = (bf16[1,40,256]{2,1,0:T(8,128)(2,1)S(1)}, bf16[1,40,256]{2,1,0:T(8,128)(2,1)S(1)}, u32[]{:S(2)}, u32[]{:S(2)}) collective-permute-start(bf16[1,40,256]{2,1,0:T(8,128)(2,1)S(1)} %reshape.16), channel_id=1, source_target_pairs={{0,16},{1,17},{2,18},{3,19},{4,20},{5,21},{6,22},{7,23},{8,24},{9,... | collective-permute-start | bytes 61448 | tf_op jit(solution)/shard_map/ppermute | solution.py:62
  5.7 1.2 %copy-start.1 = (bf16[45,45,192]{2,1,0:T(8,128)(2,1)S(1)}, bf16[45,45,192]{2,1,0:T(8,128)(2,1)}, u32[]{:S(2)}) copy-start(bf16[45,45,192]{2,1,0:T(8,128)(2,1)} %refs_0_.7) | copy-start | bytes 2332804
  6.9 11.5 %copy-start.2 = (bf16[45,45,192]{2,1,0:T(8,128)(2,1)S(1)}, bf16[45,45,192]{2,1,0:T(8,128)(2,1)}, u32[]{:S(2)}) copy-start(bf16[45,45,192]{2,1,0:T(8,128)(2,1)} %refs_0_.7) | copy-start | bytes 2332804
  7.4 6.0 %collective-permute-start.1 = (bf16[2,40,256]{2,1,0:T(8,128)(2,1)S(1)}, bf16[2,40,256]{2,1,0:T(8,128)(2,1)S(1)}, u32[]{:S(2)}, u32[]{:S(2)}) collective-permute-start(bf16[2,40,256]{2,1,0:T(8,128)(2,1)S(1)} %get-tuple-element.106), channel_id=1, source_target_pairs={{0,8},{1,9},{2,10},{3,11},{4,12},{5,13},{6,14},{7,15},{8,0},{9,1},... | collective-permute-start | bytes 122888 | tf_op jit(solution)/shard_map/ppermute | solution.py:62
  9.4 7.6 %collective-permute-start.6 = (bf16[45,3,192]{2,1,0:T(4,128)(2,1)S(1)}, bf16[45,3,192]{2,1,0:T(4,128)(2,1)S(1)}, u32[]{:S(2)}, u32[]{:S(2)}) collective-permute-start(bf16[45,3,192]{2,1,0:T(4,128)(2,1)S(1)} %get-tuple-element.88), channel_id=1, source_target_pairs={{0,4},{4,0},{8,12},{12,8},{16,20},{20,16},{24,28},{28,24},{1,5},{5... | collective-permute-start | bytes 155528 | tf_op jit(solution)/shard_map/ppermute | solution.py:71
  11.0 7.4 %collective-permute-start.5 = (bf16[45,3,192]{2,1,0:T(4,128)(2,1)S(1)}, bf16[45,3,192]{2,1,0:T(4,128)(2,1)S(1)}, u32[]{:S(2)}, u32[]{:S(2)}) collective-permute-start(bf16[45,3,192]{2,1,0:T(4,128)(2,1)S(1)} %get-tuple-element.89), channel_id=1, source_target_pairs={{4,8},{12,16},{20,24},{28,0},{8,4},{16,12},{24,20},{0,28},{5,9},{1... | collective-permute-start | bytes 155528 | tf_op jit(solution)/shard_map/ppermute | solution.py:72
  13.4 8.4 %collective-permute-start.4 = (bf16[4,40,256]{2,1,0:T(8,128)(2,1)S(1)}, bf16[4,40,256]{2,1,0:T(8,128)(2,1)S(1)}, u32[]{:S(2)}, u32[]{:S(2)}) collective-permute-start(bf16[4,40,256]{2,1,0:T(8,128)(2,1)S(1)} %get-tuple-element.102), channel_id=1, source_target_pairs={{0,6},{1,7},{2,4},{3,5},{4,2},{5,3},{6,0},{7,1},{8,14},{9,15},{10,... | collective-permute-start | bytes 245768 | tf_op jit(solution)/shard_map/ppermute | solution.py:62
  14.3 7.5 %collective-permute-start.3 = (bf16[4,40,256]{2,1,0:T(8,128)(2,1)S(1)}, bf16[4,40,256]{2,1,0:T(8,128)(2,1)S(1)}, u32[]{:S(2)}, u32[]{:S(2)}) collective-permute-start(bf16[4,40,256]{2,1,0:T(8,128)(2,1)S(1)} %get-tuple-element.102), channel_id=1, source_target_pairs={{0,2},{1,3},{2,0},{3,1},{4,6},{5,7},{6,4},{7,5},{8,10},{9,11},{10,... | collective-permute-start | bytes 245768 | tf_op jit(solution)/shard_map/ppermute | solution.py:62
  15.1 6.6 %collective-permute-start.2 = (bf16[4,40,256]{2,1,0:T(8,128)(2,1)S(1)}, bf16[4,40,256]{2,1,0:T(8,128)(2,1)S(1)}, u32[]{:S(2)}, u32[]{:S(2)}) collective-permute-start(bf16[4,40,256]{2,1,0:T(8,128)(2,1)S(1)} %get-tuple-element.102), channel_id=1, source_target_pairs={{0,4},{1,5},{2,6},{3,7},{4,0},{5,1},{6,2},{7,3},{8,12},{9,13},{10,... | collective-permute-start | bytes 245768 | tf_op jit(solution)/shard_map/ppermute | solution.py:62
  18.4 1.2 %copy-start = (bf16[45,45,192]{2,1,0:T(8,128)(2,1)S(1)}, bf16[45,45,192]{2,1,0:T(8,128)(2,1)}, u32[]{:S(2)}) copy-start(bf16[45,45,192]{2,1,0:T(8,128)(2,1)} %refs_3_) | copy-start | bytes 2332804
  18.5 6.0 %collective-permute-start.9 = (bf16[3,51,192]{2,1,0:T(8,128)(2,1)S(1)}, bf16[3,51,192]{2,1,0:T(8,128)(2,1)S(1)}, u32[]{:S(2)}, u32[]{:S(2)}) collective-permute-start(bf16[3,51,192]{2,1,0:T(8,128)(2,1)S(1)} %get-tuple-element.96), channel_id=1, source_target_pairs={{0,1},{1,0},{2,3},{3,2},{4,5},{5,4},{6,7},{7,6},{8,9},{9,8},{10,11... | collective-permute-start | bytes 176264 | tf_op jit(solution)/shard_map/ppermute | solution.py:71
  18.6 5.9 %collective-permute-start.8 = (bf16[3,51,192]{2,1,0:T(8,128)(2,1)S(1)}, bf16[3,51,192]{2,1,0:T(8,128)(2,1)S(1)}, u32[]{:S(2)}, u32[]{:S(2)}) collective-permute-start(bf16[3,51,192]{2,1,0:T(8,128)(2,1)S(1)} %get-tuple-element.97), channel_id=1, source_target_pairs={{1,2},{2,1},{5,6},{6,5},{9,10},{10,9},{13,14},{14,13},{17,18},{18,... | collective-permute-start | bytes 176264 | tf_op jit(solution)/shard_map/ppermute | solution.py:72
  21.8 3.9 %collective-permute-start.7 = (bf16[16,40,256]{2,1,0:T(8,128)(2,1)S(1)}, bf16[16,40,256]{2,1,0:T(8,128)(2,1)S(1)}, u32[]{:S(2)}, u32[]{:S(2)}) collective-permute-start(bf16[16,40,256]{2,1,0:T(8,128)(2,1)S(1)} %constant_dynamic-update-slice_fusion.5), channel_id=1, source_target_pairs={{0,1},{1,0},{2,3},{3,2},{4,5},{5,4},{6,7},{7,6},{8,9},{9,8},{10,11... | collective-permute-start | bytes 983048 | tf_op jit(solution)/shard_map/ppermute | solution.py:62
  37.4 7.1 %collective-permute-start.12 = (bf16[45,3,192]{2,1,0:T(4,128)(2,1)S(1)}, bf16[45,3,192]{2,1,0:T(4,128)(2,1)S(1)}, u32[]{:S(2)}, u32[]{:S(2)}) collective-permute-start(bf16[45,3,192]{2,1,0:T(4,128)(2,1)S(1)} %get-tuple-element.79), channel_id=1, source_target_pairs={{0,4},{4,0},{8,12},{12,8},{16,20},{20,16},{24,28},{28,24},{1,5},{5... | collective-permute-start | bytes 155528 | tf_op jit(solution)/shard_map/ppermute | solution.py:71
  37.4 7.7 %collective-permute-start.11 = (bf16[45,3,192]{2,1,0:T(4,128)(2,1)S(1)}, bf16[45,3,192]{2,1,0:T(4,128)(2,1)S(1)}, u32[]{:S(2)}, u32[]{:S(2)}) collective-permute-start(bf16[45,3,192]{2,1,0:T(4,128)(2,1)S(1)} %get-tuple-element.80), channel_id=1, source_target_pairs={{4,8},{12,16},{20,24},{28,0},{8,4},{16,12},{24,20},{0,28},{5,9},{1... | collective-permute-start | bytes 155528 | tf_op jit(solution)/shard_map/ppermute | solution.py:72
  44.3 1.7 %collective-permute-start.10 = (bf16[16,40,256]{2,1,0:T(8,128)(2,1)S(1)}, bf16[16,40,256]{2,1,0:T(8,128)(2,1)S(1)}, u32[]{:S(2)}, u32[]{:S(2)}) collective-permute-start(bf16[16,40,256]{2,1,0:T(8,128)(2,1)S(1)} %slice.60), channel_id=1, source_target_pairs={{0,1},{1,0},{2,3},{3,2},{4,5},{5,4},{6,7},{7,6},{8,9},{9,8},{10,11... | collective-permute-start | bytes 983048 | tf_op jit(solution)/shard_map/ppermute | solution.py:62
  46.1 6.1 %collective-permute-start.13 = (bf16[4,40,256]{2,1,0:T(8,128)(2,1)S(1)}, bf16[4,40,256]{2,1,0:T(8,128)(2,1)S(1)}, u32[]{:S(2)}, u32[]{:S(2)}) collective-permute-start(bf16[4,40,256]{2,1,0:T(8,128)(2,1)S(1)} %get-tuple-element.81), channel_id=1, source_target_pairs={{0,4},{1,5},{2,6},{3,7},{4,0},{5,1},{6,2},{7,3},{8,12},{9,13},{10,... | collective-permute-start | bytes 245768 | tf_op jit(solution)/shard_map/ppermute | solution.py:62
  46.2 6.6 %collective-permute-start.15 = (bf16[4,40,256]{2,1,0:T(8,128)(2,1)S(1)}, bf16[4,40,256]{2,1,0:T(8,128)(2,1)S(1)}, u32[]{:S(2)}, u32[]{:S(2)}) collective-permute-start(bf16[4,40,256]{2,1,0:T(8,128)(2,1)S(1)} %get-tuple-element.82), channel_id=1, source_target_pairs={{0,6},{1,7},{2,4},{3,5},{4,2},{5,3},{6,0},{7,1},{8,14},{9,15},{10,... | collective-permute-start | bytes 245768 | tf_op jit(solution)/shard_map/ppermute | solution.py:62
  48.5 5.4 %collective-permute-start.14 = (bf16[4,40,256]{2,1,0:T(8,128)(2,1)S(1)}, bf16[4,40,256]{2,1,0:T(8,128)(2,1)S(1)}, u32[]{:S(2)}, u32[]{:S(2)}) collective-permute-start(bf16[4,40,256]{2,1,0:T(8,128)(2,1)S(1)} %get-tuple-element.83), channel_id=1, source_target_pairs={{0,2},{1,3},{2,0},{3,1},{4,6},{5,7},{6,4},{7,5},{8,10},{9,11},{10,... | collective-permute-start | bytes 245768 | tf_op jit(solution)/shard_map/ppermute | solution.py:62
  54.0 4.1 %collective-permute-start.18 = (bf16[2,40,256]{2,1,0:T(8,128)(2,1)S(1)}, bf16[2,40,256]{2,1,0:T(8,128)(2,1)S(1)}, u32[]{:S(2)}, u32[]{:S(2)}) collective-permute-start(bf16[2,40,256]{2,1,0:T(8,128)(2,1)S(1)} %slice.92), channel_id=1, source_target_pairs={{0,8},{1,9},{2,10},{3,11},{4,12},{5,13},{6,14},{7,15},{8,0},{9,1},... | collective-permute-start | bytes 122888 | tf_op jit(solution)/shard_map/ppermute | solution.py:62
  55.0 4.2 %collective-permute-start.17 = (bf16[3,51,192]{2,1,0:T(8,128)(2,1)S(1)}, bf16[3,51,192]{2,1,0:T(8,128)(2,1)S(1)}, u32[]{:S(2)}, u32[]{:S(2)}) collective-permute-start(bf16[3,51,192]{2,1,0:T(8,128)(2,1)S(1)} %get-tuple-element.92), channel_id=1, source_target_pairs={{0,1},{1,0},{2,3},{3,2},{4,5},{5,4},{6,7},{7,6},{8,9},{9,8},{10,11... | collective-permute-start | bytes 176264 | tf_op jit(solution)/shard_map/ppermute | solution.py:71
  55.1 4.2 %collective-permute-start.16 = (bf16[3,51,192]{2,1,0:T(8,128)(2,1)S(1)}, bf16[3,51,192]{2,1,0:T(8,128)(2,1)S(1)}, u32[]{:S(2)}, u32[]{:S(2)}) collective-permute-start(bf16[3,51,192]{2,1,0:T(8,128)(2,1)S(1)} %get-tuple-element.93), channel_id=1, source_target_pairs={{1,2},{2,1},{5,6},{6,5},{9,10},{10,9},{13,14},{14,13},{17,18},{18,... | collective-permute-start | bytes 176264 | tf_op jit(solution)/shard_map/ppermute | solution.py:72
  58.1 4.7 %collective-permute-start.19 = (bf16[1,40,256]{2,1,0:T(8,128)(2,1)S(1)}, bf16[1,40,256]{2,1,0:T(8,128)(2,1)S(1)}, u32[]{:S(2)}, u32[]{:S(2)}) collective-permute-start(bf16[1,40,256]{2,1,0:T(8,128)(2,1)S(1)} %slice.93), channel_id=1, source_target_pairs={{0,16},{1,17},{2,18},{3,19},{4,20},{5,21},{6,22},{7,23},{8,24},{9,... | collective-permute-start | bytes 61448 | tf_op jit(solution)/shard_map/ppermute | solution.py:62
  59.3 3.6 %copy-start.3 = (f32[9568]{0:T(1024)S(1)}, f32[9568]{0:T(1024)}, u32[]{:S(2)}) copy-start(f32[9568]{0:T(1024)} %param.5) | copy-start | bytes 114820
  59.3 3.6 %copy-start.4 = (f32[9568]{0:T(1024)S(1)}, f32[9568]{0:T(1024)}, u32[]{:S(2)}) copy-start(f32[9568]{0:T(1024)} %param.6) | copy-start | bytes 114820

commit v12 on v11

--- a/solution.py
+++ b/solution.py
@@ -800,7 +800,7 @@
         )(*operands)
         return (None if last else results[-1]), (results[0] if out_shape[0] is not own else None)
 
-    early = (inner[0][1] + 1) // 2
+    early = (2 * inner[0][1] + 2) // 3
     for k, group in enumerate(groups[::-1]):
         if k > 2:
             values, piece = lax.optimization_barrier((values, piece))

time: 64.4 us -> 63.9 us (level)
  transfers between devices with their start and end apart: 20 -> 20, of which waited for: 9 -> 8; matrix products, arithmetic and copies ran while one was open for 1% -> 1% of each run, Pallas kernels for 21% -> 21%
where the time goes in v12:
time: 63.9 us; the launch traced here: 63.6 us
  starting transfers between devices  26.3 us (41%)
  Pallas kernels  24.7 us (39%)
  waiting for transfers between devices  7.48 us (12%)
  local copies, waits for them, and re-layouts  2.57 us (4%)
  other arithmetic  1.42 us (2%)
  between operations  1.06 us (2%)
    ppermute x12, starting transfers between devices, swap(): return lax.ppermute(values, ('lon', 'lat'), pairs)  18.1 us
    pallas_call x1, Pallas kernels, body(): pl.pallas_call(lambda *refs: layer_kernel(rows, lon_pad, block_rows, *ref...  7.73 us
    ppermute x4, starting transfers between devices, send_edges(): far = lax.ppermute(jnp.where(even, low_edge, high_edge), axis, far)  6.45 us
    pallas_call x3, Pallas kernels, field_piece(): pl.pallas_call(lambda *refs: field_kernel(ranges, rows, cols, lon_pad, co...  6.15 us
    ppermute x12, waiting for transfers between devices, swap(): return lax.ppermute(values, ('lon', 'lat'), pairs)  5.45 us
    pallas_call x1, Pallas kernels, body(): pl.pallas_call(lambda *refs: taps_kernel(*static, *refs), out_shape=(shap...  4.27 us
    pallas_call x1, Pallas kernels, body(): pl.pallas_call(lambda *refs: conv_kernel(*static, *refs), out_shape=(shap...  3.7 us
    pallas_call x1, Pallas kernels, body(): pl.pallas_call(lambda *refs: inner_kernel(inner, rows, cols, conv_rows, *...  2.08 us
  transfers between devices with their start and end apart: 20, of which 8 were waited for; matrix products, arithmetic and copies ran while one was open for 1% of the time, Pallas kernels for 21%

profile of v12, /device:TPU:0, one launch (start us, length us, event | category | flops | bytes accessed | tf_op | source)
XLA Modules:
  0.0 63.6 jit_solution(15652964659474069260)
XLA Ops:
  0.7 0.9 %fusion = bf16[10240]{0:T(1024)(128)(2,1)S(1)} fusion(s32[]{:T(128)S(6)} %select_n.106, f32[9568]{0:T(1024)} %param.5), kind=kLoop, calls=%fused_computation.24 | loop fusion | bytes 58756 | tf_op jit(solution)/shard_map/convert_element_type | solution.py:633
  1.5 4.1 %collective-permute-start = (bf16[1,40,256]{2,1,0:T(8,128)(2,1)S(1)}, bf16[1,40,256]{2,1,0:T(8,128)(2,1)S(1)}, u32[]{:S(2)}, u32[]{:S(2)}) collective-permute-start(bf16[1,40,256]{2,1,0:T(8,128)(2,1)S(1)} %reshape.16), channel_id=1, source_target_pairs={{0,16},{1,17},{2,18},{3,19},{4,20},{5,21},{6,22},{7,23},{8,24},{9,... | collective-permute-start | bytes 61448 | tf_op jit(solution)/shard_map/ppermute | solution.py:62
  5.7 1.2 %copy-done.1 = bf16[45,45,192]{2,1,0:T(8,128)(2,1)S(1)} copy-done((bf16[45,45,192]{2,1,0:T(8,128)(2,1)S(1)}, bf16[45,45,192]{2,1,0:T(8,128)(2,1)}, u32[]{:S(2)}) %copy-start.1) | copy-done | bytes 777624
  6.9 0.2 edges.1
  7.2 0.2 collective-permute-done
  7.4 1.9 %collective-permute-start.1 = (bf16[2,40,256]{2,1,0:T(8,128)(2,1)S(1)}, bf16[2,40,256]{2,1,0:T(8,128)(2,1)S(1)}, u32[]{:S(2)}, u32[]{:S(2)}) collective-permute-start(bf16[2,40,256]{2,1,0:T(8,128)(2,1)S(1)} %get-tuple-element.106), channel_id=1, source_target_pairs={{0,8},{1,9},{2,10},{3,11},{4,12},{5,13},{6,14},{7,15},{8,0},{9,1},... | collective-permute-start | bytes 122888 | tf_op jit(solution)/shard_map/ppermute | solution.py:62
  9.3 0.1 broadcast_select_fusion.6
  9.4 1.6 %collective-permute-start.6 = (bf16[45,3,192]{2,1,0:T(4,128)(2,1)S(1)}, bf16[45,3,192]{2,1,0:T(4,128)(2,1)S(1)}, u32[]{:S(2)}, u32[]{:S(2)}) collective-permute-start(bf16[45,3,192]{2,1,0:T(4,128)(2,1)S(1)} %get-tuple-element.88), channel_id=1, source_target_pairs={{0,4},{4,0},{8,12},{12,8},{16,20},{20,16},{24,28},{28,24},{1,5},{5... | collective-permute-start | bytes 155528 | tf_op jit(solution)/shard_map/ppermute | solution.py:71
  11.0 2.5 %collective-permute-start.5 = (bf16[45,3,192]{2,1,0:T(4,128)(2,1)S(1)}, bf16[45,3,192]{2,1,0:T(4,128)(2,1)S(1)}, u32[]{:S(2)}, u32[]{:S(2)}) collective-permute-start(bf16[45,3,192]{2,1,0:T(4,128)(2,1)S(1)} %get-tuple-element.89), channel_id=1, source_target_pairs={{4,8},{12,16},{20,24},{28,0},{8,4},{16,12},{24,20},{0,28},{5,9},{1... | collective-permute-start | bytes 155528 | tf_op jit(solution)/shard_map/ppermute | solution.py:72
  13.4 0.0 collective-permute-done.1
  13.4 0.9 %collective-permute-start.4 = (bf16[4,40,256]{2,1,0:T(8,128)(2,1)S(1)}, bf16[4,40,256]{2,1,0:T(8,128)(2,1)S(1)}, u32[]{:S(2)}, u32[]{:S(2)}) collective-permute-start(bf16[4,40,256]{2,1,0:T(8,128)(2,1)S(1)} %get-tuple-element.102), channel_id=1, source_target_pairs={{0,6},{1,7},{2,4},{3,5},{4,2},{5,3},{6,0},{7,1},{8,14},{9,15},{10,... | collective-permute-start | bytes 245768 | tf_op jit(solution)/shard_map/ppermute | solution.py:62
  14.3 0.8 %collective-permute-start.3 = (bf16[4,40,256]{2,1,0:T(8,128)(2,1)S(1)}, bf16[4,40,256]{2,1,0:T(8,128)(2,1)S(1)}, u32[]{:S(2)}, u32[]{:S(2)}) collective-permute-start(bf16[4,40,256]{2,1,0:T(8,128)(2,1)S(1)} %get-tuple-element.102), channel_id=1, source_target_pairs={{0,2},{1,3},{2,0},{3,1},{4,6},{5,7},{6,4},{7,5},{8,10},{9,11},{10,... | collective-permute-start | bytes 245768 | tf_op jit(solution)/shard_map/ppermute | solution.py:62
  15.1 1.9 %collective-permute-start.2 = (bf16[4,40,256]{2,1,0:T(8,128)(2,1)S(1)}, bf16[4,40,256]{2,1,0:T(8,128)(2,1)S(1)}, u32[]{:S(2)}, u32[]{:S(2)}) collective-permute-start(bf16[4,40,256]{2,1,0:T(8,128)(2,1)S(1)} %get-tuple-element.102), channel_id=1, source_target_pairs={{0,4},{1,5},{2,6},{3,7},{4,0},{5,1},{6,2},{7,3},{8,12},{9,13},{10,... | collective-permute-start | bytes 245768 | tf_op jit(solution)/shard_map/ppermute | solution.py:62
  17.0 0.0 collective-permute-done.6
  17.0 1.3 %collective-permute-done.5 = bf16[45,3,192]{2,1,0:T(4,128)(2,1)S(1)} collective-permute-done((bf16[45,3,192]{2,1,0:T(4,128)(2,1)S(1)}, bf16[45,3,192]{2,1,0:T(4,128)(2,1)S(1)}, u32[]{:S(2)}, u32[]{:S(2)}) %collective-permute-start.5) | collective-permute-done | bytes 51872 | tf_op jit(solution)/shard_map/ppermute | solution.py:72
  18.3 0.1 broadcast_select_fusion.4
  18.4 0.0 copy-done.2
  18.4 0.0 copy-start
  18.5 0.1 collective-permute-start.9
  18.6 0.8 %collective-permute-start.8 = (bf16[3,51,192]{2,1,0:T(8,128)(2,1)S(1)}, bf16[3,51,192]{2,1,0:T(8,128)(2,1)S(1)}, u32[]{:S(2)}, u32[]{:S(2)}) collective-permute-start(bf16[3,51,192]{2,1,0:T(8,128)(2,1)S(1)} %get-tuple-element.97), channel_id=1, source_target_pairs={{1,2},{2,1},{5,6},{6,5},{9,10},{10,9},{13,14},{14,13},{17,18},{18,... | collective-permute-start | bytes 176264 | tf_op jit(solution)/shard_map/ppermute | solution.py:72
  19.4 0.3 copy-done
  19.7 2.1 %inner.1 = (f32[2,77,56,128]{3,2,1,0:T(8,128)S(1)}, bf16[45,48,256]{2,1,0:T(8,128)(2,1)S(1)}, bf16[45,48,256]{2,1,0:T(8,128)(2,1)S(1)}) custom-call(bf16[45,45,192]{2,1,0:T(8,128)(2,1)S(1)} %copy-done.2, bf16[45,3,192]{2,1,0:T(4,128)(2,1)S(1)} %get-tuple-element.44.refs_1_, bf16[45,3,192]{2,1,0:T(4,128)(2,1)S(1)} %get-tuple-element.45.refs_2_, ...), custom_call_target="tpu_custom_call" | custom-call | flops 2750000128 | tf_op jit(solution)/shard_map/inner/pallas_call | solution.py:666
  21.7 0.0 collective-permute-done.2
  21.8 0.0 collective-permute-done.3
  21.8 0.0 collective-permute-done.4
  21.8 2.7 %collective-permute-start.7 = (bf16[16,40,256]{2,1,0:T(8,128)(2,1)S(1)}, bf16[16,40,256]{2,1,0:T(8,128)(2,1)S(1)}, u32[]{:S(2)}, u32[]{:S(2)}) collective-permute-start(bf16[16,40,256]{2,1,0:T(8,128)(2,1)S(1)} %constant_dynamic-update-slice_fusion.5), channel_id=1, source_target_pairs={{0,1},{1,0},{2,3},{3,2},{4,5},{5,4},{6,7},{7,6},{8,9},{9,8},{10,11... | collective-permute-start | bytes 983048 | tf_op jit(solution)/shard_map/ppermute | solution.py:62
  24.5 0.0 collective-permute-done.9
  24.5 0.0 collective-permute-done.8
  24.5 0.5 outer.1.refs_3_
  25.1 0.7 %collective-permute-done.7 = bf16[16,40,256]{2,1,0:T(8,128)(2,1)S(1)} collective-permute-done((bf16[16,40,256]{2,1,0:T(8,128)(2,1)S(1)}, bf16[16,40,256]{2,1,0:T(8,128)(2,1)S(1)}, u32[]{:S(2)}, u32[]{:S(2)}) %collective-permute-start.7) | collective-permute-done | bytes 327712 | tf_op jit(solution)/shard_map/ppermute | solution.py:62
  25.7 0.1 pad_maximum_fusion.refs_1_
  25.8 3.7 %conv.1 = (f32[2,45,48,128]{3,2,1,0:T(8,128)S(1)}, bf16[256,768]{1,0:T(8,128)(2,1)S(1)}, bf16[768,256]{1,0:T(8,128)(2,1)S(1)}, f32[2,64,128]{2,1,0:T(8,128)S(1)}, f32[2,11,8,128]{3,2,1,0:T(8,128)S(1)}) custom-call(s32[1]{0:T(128)} %bitcast.refs_0_, bf16[32,40,256]{2,1,0:T(8,128)(2,1)S(1)} %pad_maximum_fusion.refs_1_, ...), custom_call_target="tpu_custom_call" | custom-call | flops 6600000000 | tf_op jit(solution)/shard_map/conv/pallas_call | solution.py:698
  29.5 7.7 %layer.1 = (bf16[45,45,192]{2,1,0:T(8,128)(2,1)S(1)}, bf16[45,48,256]{2,1,0:T(8,128)(2,1)S(1)}, f32[200,768]{1,0:T(8,128)S(1)}, f32[192,768]{1,0:T(8,128)S(1)}, f32[5,2,8,128]{3,2,1,0:T(8,128)S(1)}) custom-call(f32[2,45,48,128]{3,2,1,0:T(8,128)S(1)} %get-tuple-element.52.refs_0_, bf16[256,768]{1,0:T(8,128)(2,1)S(1)} %get-tuple-element.53.refs_1_, ...), custom_call_target="tpu_custom_call" | custom-call | flops 17600000000 | tf_op jit(solution)/shard_map/layer/pallas_call | solution.py:719
  37.3 0.1 broadcast_select_fusion.2
  37.4 0.1 collective-permute-start.12
  37.4 2.5 %collective-permute-start.11 = (bf16[45,3,192]{2,1,0:T(4,128)(2,1)S(1)}, bf16[45,3,192]{2,1,0:T(4,128)(2,1)S(1)}, u32[]{:S(2)}, u32[]{:S(2)}) collective-permute-start(bf16[45,3,192]{2,1,0:T(4,128)(2,1)S(1)} %get-tuple-element.80), channel_id=1, source_target_pairs={{4,8},{12,16},{20,24},{28,0},{8,4},{16,12},{24,20},{0,28},{5,9},{1... | collective-permute-start | bytes 155528 | tf_op jit(solution)/shard_map/ppermute | solution.py:72
  40.0 4.3 %taps.1 = (bf16[32,40,256]{2,1,0:T(8,128)(2,1)S(1)}, bf16[45,45,192]{2,1,0:T(8,128)(2,1)}) custom-call(s32[1]{0:T(128)} %bitcast.refs_0_, bf16[45,48,256]{2,1,0:T(8,128)(2,1)S(1)} %get-tuple-element.58.refs_1_.refs_2_, f32[2,77,56,128]{3,2,1,0:T(8,128)S(1)} %get-tuple-element.49.refs_2_, f32[2,22,56,128]{3,2,1,0:T(8,128)S(1)} %outer.1.refs_3_, ...), custom_call_target="tpu_custom_call" | custom-call | flops 12099999744 | tf_op jit(solution)/shard_map/taps/pallas_call | solution.py:736
  44.3 0.1 collective-permute-start.10
  44.4 0.0 collective-permute-done.12
  44.5 0.7 %collective-permute-done.11 = bf16[45,3,192]{2,1,0:T(4,128)(2,1)S(1)} collective-permute-done((bf16[45,3,192]{2,1,0:T(4,128)(2,1)S(1)}, bf16[45,3,192]{2,1,0:T(4,128)(2,1)S(1)}, u32[]{:S(2)}, u32[]{:S(2)}) %collective-permute-start.11) | collective-permute-done | bytes 51872 | tf_op jit(solution)/shard_map/ppermute | solution.py:72
  45.1 0.1 broadcast_select_fusion
  45.2 0.8 %collective-permute-done.10 = bf16[16,40,256]{2,1,0:T(8,128)(2,1)S(1)} collective-permute-done((bf16[16,40,256]{2,1,0:T(8,128)(2,1)S(1)}, bf16[16,40,256]{2,1,0:T(8,128)(2,1)S(1)}, u32[]{:S(2)}, u32[]{:S(2)}) %collective-permute-start.10) | collective-permute-done | bytes 327712 | tf_op jit(solution)/shard_map/ppermute | solution.py:62
  46.0 0.1 convert_add_fusion
  46.1 0.1 collective-permute-start.13
  46.2 2.3 %collective-permute-start.15 = (bf16[4,40,256]{2,1,0:T(8,128)(2,1)S(1)}, bf16[4,40,256]{2,1,0:T(8,128)(2,1)S(1)}, u32[]{:S(2)}, u32[]{:S(2)}) collective-permute-start(bf16[4,40,256]{2,1,0:T(8,128)(2,1)S(1)} %get-tuple-element.82), channel_id=1, source_target_pairs={{0,6},{1,7},{2,4},{3,5},{4,2},{5,3},{6,0},{7,1},{8,14},{9,15},{10,... | collective-permute-start | bytes 245768 | tf_op jit(solution)/shard_map/ppermute | solution.py:62
  48.5 1.2 %collective-permute-start.14 = (bf16[4,40,256]{2,1,0:T(8,128)(2,1)S(1)}, bf16[4,40,256]{2,1,0:T(8,128)(2,1)S(1)}, u32[]{:S(2)}, u32[]{:S(2)}) collective-permute-start(bf16[4,40,256]{2,1,0:T(8,128)(2,1)S(1)} %get-tuple-element.83), channel_id=1, source_target_pairs={{0,2},{1,3},{2,0},{3,1},{4,6},{5,7},{6,4},{7,5},{8,10},{9,11},{10,... | collective-permute-start | bytes 245768 | tf_op jit(solution)/shard_map/ppermute | solution.py:62
  49.7 3.0 %field.3.refs_5_ = bf16[25,45,192]{2,1,0:T(8,128)(2,1)S(1)} custom-call(f32[2,11,8,128]{3,2,1,0:T(8,128)S(1)} %get-tuple-element.64.refs_0_, bf16[45,48,256]{2,1,0:T(8,128)(2,1)S(1)} %get-tuple-element.57.refs_5_.refs_1_, bf16[45,48,256]{2,1,0:T(8,128)(2,1)S(1)} %get-tuple-element.58.refs_1_.refs_2_, bf16[45,3,192]{2,1,0:T(4,128)(2,1)S(1)} %get-tuple-element.66.refs_3_, ...), custom_call_target="tpu_custom_call" | custom-call | flops 6049999872 | tf_op jit(solution)/shard_map/field/pallas_call | solution.py:780
  52.8 0.0 collective-permute-done.13
  52.8 0.0 collective-permute-done.15
  52.9 1.1 %collective-permute-done.14 = bf16[4,40,256]{2,1,0:T(8,128)(2,1)S(1)} collective-permute-done((bf16[4,40,256]{2,1,0:T(8,128)(2,1)S(1)}, bf16[4,40,256]{2,1,0:T(8,128)(2,1)S(1)}, u32[]{:S(2)}, u32[]{:S(2)}) %collective-permute-start.14) | collective-permute-done | bytes 81952 | tf_op jit(solution)/shard_map/ppermute | solution.py:62
  54.0 1.0 %collective-permute-start.18 = (bf16[2,40,256]{2,1,0:T(8,128)(2,1)S(1)}, bf16[2,40,256]{2,1,0:T(8,128)(2,1)S(1)}, u32[]{:S(2)}, u32[]{:S(2)}) collective-permute-start(bf16[2,40,256]{2,1,0:T(8,128)(2,1)S(1)} %slice.92), channel_id=1, source_target_pairs={{0,8},{1,9},{2,10},{3,11},{4,12},{5,13},{6,14},{7,15},{8,0},{9,1},... | collective-permute-start | bytes 122888 | tf_op jit(solution)/shard_map/ppermute | solution.py:62
  55.0 0.1 collective-permute-start.17
  55.1 0.7 %collective-permute-start.16 = (bf16[3,51,192]{2,1,0:T(8,128)(2,1)S(1)}, bf16[3,51,192]{2,1,0:T(8,128)(2,1)S(1)}, u32[]{:S(2)}, u32[]{:S(2)}) collective-permute-start(bf16[3,51,192]{2,1,0:T(8,128)(2,1)S(1)} %get-tuple-element.93), channel_id=1, source_target_pairs={{1,2},{2,1},{5,6},{6,5},{9,10},{10,9},{13,14},{14,13},{17,18},{18,... | collective-permute-start | bytes 176264 | tf_op jit(solution)/shard_map/ppermute | solution.py:72
  55.8 1.2 %field.4 = (bf16[45,45,192]{2,1,0:T(8,128)(2,1)}, bf16[10,45,192]{2,1,0:T(8,128)(2,1)S(1)}) custom-call(f32[2,11,8,128]{3,2,1,0:T(8,128)S(1)} %get-tuple-element.64.refs_0_, bf16[45,48,256]{2,1,0:T(8,128)(2,1)S(1)} %get-tuple-element.57.refs_5_.refs_1_, bf16[45,48,256]{2,1,0:T(8,128)(2,1)S(1)} %get-tuple-element.58.refs_1_.refs_2_, ...), custom_call_target="tpu_custom_call" | custom-call | flops 2420000000 | tf_op jit(solution)/shard_map/field/pallas_call | solution.py:780
  57.0 1.1 %collective-permute-done.18 = bf16[2,40,256]{2,1,0:T(8,128)(2,1)S(1)} collective-permute-done((bf16[2,40,256]{2,1,0:T(8,128)(2,1)S(1)}, bf16[2,40,256]{2,1,0:T(8,128)(2,1)S(1)}, u32[]{:S(2)}, u32[]{:S(2)}) %collective-permute-start.18) | collective-permute-done | bytes 40992 | tf_op jit(solution)/shard_map/ppermute | solution.py:62
  58.1 1.2 %collective-permute-start.19 = (bf16[1,40,256]{2,1,0:T(8,128)(2,1)S(1)}, bf16[1,40,256]{2,1,0:T(8,128)(2,1)S(1)}, u32[]{:S(2)}, u32[]{:S(2)}) collective-permute-start(bf16[1,40,256]{2,1,0:T(8,128)(2,1)S(1)} %slice.93), channel_id=1, source_target_pairs={{0,16},{1,17},{2,18},{3,19},{4,20},{5,21},{6,22},{7,23},{8,24},{9,... | collective-permute-start | bytes 61448 | tf_op jit(solution)/shard_map/ppermute | solution.py:62
  59.2 0.0 collective-permute-done.17
  59.2 0.0 collective-permute-done.16
  59.3 0.0 copy-start.3
  59.3 0.0 copy-start.4
  59.3 1.9 %field.5 = bf16[45,45,192]{2,1,0:T(8,128)(2,1)} custom-call(f32[2,11,8,128]{3,2,1,0:T(8,128)S(1)} %get-tuple-element.64.refs_0_, bf16[45,48,256]{2,1,0:T(8,128)(2,1)S(1)} %get-tuple-element.57.refs_5_.refs_1_, bf16[45,48,256]{2,1,0:T(8,128)(2,1)S(1)} %get-tuple-element.58.refs_1_.refs_2_, ...), custom_call_target="tpu_custom_call", output_to_operand_aliasing={{}: (8, {})} | custom-call | flops 2420000000 | tf_op jit(solution)/shard_map/field/pallas_call | solution.py:780
  61.2 1.6 %collective-permute-done.19 = bf16[1,40,256]{2,1,0:T(8,128)(2,1)S(1)} collective-permute-done((bf16[1,40,256]{2,1,0:T(8,128)(2,1)S(1)}, bf16[1,40,256]{2,1,0:T(8,128)(2,1)S(1)}, u32[]{:S(2)}, u32[]{:S(2)}) %collective-permute-start.19) | collective-permute-done | bytes 20512 | tf_op jit(solution)/shard_map/ppermute | solution.py:62
  62.9 0.0 copy-done.3
  62.9 0.7 %multiply_add_fusion = f32[9568]{0:T(1024)} fusion(f32[9568]{0:T(1024)S(1)} %copy-done.4, f32[9568]{0:T(1024)S(1)} %copy-done.3, f32[10240]{0:T(1024)S(1)} %bitcast.4, s32[]{:T(128)S(6)} %select_n.127), kind=kLoop, calls=%fused_computation.26 | loop fusion | flops 38272 | bytes 153092 | tf_op jit(solution)/shard_map/add | solution.py:834
  (28 shorter events, 0.4 us)
Async XLA Ops:
  1.5 5.9 %collective-permute-start = (bf16[1,40,256]{2,1,0:T(8,128)(2,1)S(1)}, bf16[1,40,256]{2,1,0:T(8,128)(2,1)S(1)}, u32[]{:S(2)}, u32[]{:S(2)}) collective-permute-start(bf16[1,40,256]{2,1,0:T(8,128)(2,1)S(1)} %reshape.16), channel_id=1, source_target_pairs={{0,16},{1,17},{2,18},{3,19},{4,20},{5,21},{6,22},{7,23},{8,24},{9,... | collective-permute-start | bytes 61448 | tf_op jit(solution)/shard_map/ppermute | solution.py:62
  5.7 1.2 %copy-start.1 = (bf16[45,45,192]{2,1,0:T(8,128)(2,1)S(1)}, bf16[45,45,192]{2,1,0:T(8,128)(2,1)}, u32[]{:S(2)}) copy-start(bf16[45,45,192]{2,1,0:T(8,128)(2,1)} %refs_0_.7) | copy-start | bytes 2332804
  6.9 11.5 %copy-start.2 = (bf16[45,45,192]{2,1,0:T(8,128)(2,1)S(1)}, bf16[45,45,192]{2,1,0:T(8,128)(2,1)}, u32[]{:S(2)}) copy-start(bf16[45,45,192]{2,1,0:T(8,128)(2,1)} %refs_0_.7) | copy-start | bytes 2332804
  7.4 6.0 %collective-permute-start.1 = (bf16[2,40,256]{2,1,0:T(8,128)(2,1)S(1)}, bf16[2,40,256]{2,1,0:T(8,128)(2,1)S(1)}, u32[]{:S(2)}, u32[]{:S(2)}) collective-permute-start(bf16[2,40,256]{2,1,0:T(8,128)(2,1)S(1)} %get-tuple-element.106), channel_id=1, source_target_pairs={{0,8},{1,9},{2,10},{3,11},{4,12},{5,13},{6,14},{7,15},{8,0},{9,1},... | collective-permute-start | bytes 122888 | tf_op jit(solution)/shard_map/ppermute | solution.py:62
  9.4 7.6 %collective-permute-start.6 = (bf16[45,3,192]{2,1,0:T(4,128)(2,1)S(1)}, bf16[45,3,192]{2,1,0:T(4,128)(2,1)S(1)}, u32[]{:S(2)}, u32[]{:S(2)}) collective-permute-start(bf16[45,3,192]{2,1,0:T(4,128)(2,1)S(1)} %get-tuple-element.88), channel_id=1, source_target_pairs={{0,4},{4,0},{8,12},{12,8},{16,20},{20,16},{24,28},{28,24},{1,5},{5... | collective-permute-start | bytes 155528 | tf_op jit(solution)/shard_map/ppermute | solution.py:71
  11.0 7.4 %collective-permute-start.5 = (bf16[45,3,192]{2,1,0:T(4,128)(2,1)S(1)}, bf16[45,3,192]{2,1,0:T(4,128)(2,1)S(1)}, u32[]{:S(2)}, u32[]{:S(2)}) collective-permute-start(bf16[45,3,192]{2,1,0:T(4,128)(2,1)S(1)} %get-tuple-element.89), channel_id=1, source_target_pairs={{4,8},{12,16},{20,24},{28,0},{8,4},{16,12},{24,20},{0,28},{5,9},{1... | collective-permute-start | bytes 155528 | tf_op jit(solution)/shard_map/ppermute | solution.py:72
  13.4 8.4 %collective-permute-start.4 = (bf16[4,40,256]{2,1,0:T(8,128)(2,1)S(1)}, bf16[4,40,256]{2,1,0:T(8,128)(2,1)S(1)}, u32[]{:S(2)}, u32[]{:S(2)}) collective-permute-start(bf16[4,40,256]{2,1,0:T(8,128)(2,1)S(1)} %get-tuple-element.102), channel_id=1, source_target_pairs={{0,6},{1,7},{2,4},{3,5},{4,2},{5,3},{6,0},{7,1},{8,14},{9,15},{10,... | collective-permute-start | bytes 245768 | tf_op jit(solution)/shard_map/ppermute | solution.py:62
  14.3 7.5 %collective-permute-start.3 = (bf16[4,40,256]{2,1,0:T(8,128)(2,1)S(1)}, bf16[4,40,256]{2,1,0:T(8,128)(2,1)S(1)}, u32[]{:S(2)}, u32[]{:S(2)}) collective-permute-start(bf16[4,40,256]{2,1,0:T(8,128)(2,1)S(1)} %get-tuple-element.102), channel_id=1, source_target_pairs={{0,2},{1,3},{2,0},{3,1},{4,6},{5,7},{6,4},{7,5},{8,10},{9,11},{10,... | collective-permute-start | bytes 245768 | tf_op jit(solution)/shard_map/ppermute | solution.py:62
  15.1 6.6 %collective-permute-start.2 = (bf16[4,40,256]{2,1,0:T(8,128)(2,1)S(1)}, bf16[4,40,256]{2,1,0:T(8,128)(2,1)S(1)}, u32[]{:S(2)}, u32[]{:S(2)}) collective-permute-start(bf16[4,40,256]{2,1,0:T(8,128)(2,1)S(1)} %get-tuple-element.102), channel_id=1, source_target_pairs={{0,4},{1,5},{2,6},{3,7},{4,0},{5,1},{6,2},{7,3},{8,12},{9,13},{10,... | collective-permute-start | bytes 245768 | tf_op jit(solution)/shard_map/ppermute | solution.py:62
  18.4 1.2 %copy-start = (bf16[45,45,192]{2,1,0:T(8,128)(2,1)S(1)}, bf16[45,45,192]{2,1,0:T(8,128)(2,1)}, u32[]{:S(2)}) copy-start(bf16[45,45,192]{2,1,0:T(8,128)(2,1)} %refs_3_) | copy-start | bytes 2332804
  18.5 6.0 %collective-permute-start.9 = (bf16[3,51,192]{2,1,0:T(8,128)(2,1)S(1)}, bf16[3,51,192]{2,1,0:T(8,128)(2,1)S(1)}, u32[]{:S(2)}, u32[]{:S(2)}) collective-permute-start(bf16[3,51,192]{2,1,0:T(8,128)(2,1)S(1)} %get-tuple-element.96), channel_id=1, source_target_pairs={{0,1},{1,0},{2,3},{3,2},{4,5},{5,4},{6,7},{7,6},{8,9},{9,8},{10,11... | collective-permute-start | bytes 176264 | tf_op jit(solution)/shard_map/ppermute | solution.py:71
  18.6 5.9 %collective-permute-start.8 = (bf16[3,51,192]{2,1,0:T(8,128)(2,1)S(1)}, bf16[3,51,192]{2,1,0:T(8,128)(2,1)S(1)}, u32[]{:S(2)}, u32[]{:S(2)}) collective-permute-start(bf16[3,51,192]{2,1,0:T(8,128)(2,1)S(1)} %get-tuple-element.97), channel_id=1, source_target_pairs={{1,2},{2,1},{5,6},{6,5},{9,10},{10,9},{13,14},{14,13},{17,18},{18,... | collective-permute-start | bytes 176264 | tf_op jit(solution)/shard_map/ppermute | solution.py:72
  21.8 3.9 %collective-permute-start.7 = (bf16[16,40,256]{2,1,0:T(8,128)(2,1)S(1)}, bf16[16,40,256]{2,1,0:T(8,128)(2,1)S(1)}, u32[]{:S(2)}, u32[]{:S(2)}) collective-permute-start(bf16[16,40,256]{2,1,0:T(8,128)(2,1)S(1)} %constant_dynamic-update-slice_fusion.5), channel_id=1, source_target_pairs={{0,1},{1,0},{2,3},{3,2},{4,5},{5,4},{6,7},{7,6},{8,9},{9,8},{10,11... | collective-permute-start | bytes 983048 | tf_op jit(solution)/shard_map/ppermute | solution.py:62
  37.4 7.1 %collective-permute-start.12 = (bf16[45,3,192]{2,1,0:T(4,128)(2,1)S(1)}, bf16[45,3,192]{2,1,0:T(4,128)(2,1)S(1)}, u32[]{:S(2)}, u32[]{:S(2)}) collective-permute-start(bf16[45,3,192]{2,1,0:T(4,128)(2,1)S(1)} %get-tuple-element.79), channel_id=1, source_target_pairs={{0,4},{4,0},{8,12},{12,8},{16,20},{20,16},{24,28},{28,24},{1,5},{5... | collective-permute-start | bytes 155528 | tf_op jit(solution)/shard_map/ppermute | solution.py:71
  37.4 7.7 %collective-permute-start.11 = (bf16[45,3,192]{2,1,0:T(4,128)(2,1)S(1)}, bf16[45,3,192]{2,1,0:T(4,128)(2,1)S(1)}, u32[]{:S(2)}, u32[]{:S(2)}) collective-permute-start(bf16[45,3,192]{2,1,0:T(4,128)(2,1)S(1)} %get-tuple-element.80), channel_id=1, source_target_pairs={{4,8},{12,16},{20,24},{28,0},{8,4},{16,12},{24,20},{0,28},{5,9},{1... | collective-permute-start | bytes 155528 | tf_op jit(solution)/shard_map/ppermute | solution.py:72
  44.3 1.7 %collective-permute-start.10 = (bf16[16,40,256]{2,1,0:T(8,128)(2,1)S(1)}, bf16[16,40,256]{2,1,0:T(8,128)(2,1)S(1)}, u32[]{:S(2)}, u32[]{:S(2)}) collective-permute-start(bf16[16,40,256]{2,1,0:T(8,128)(2,1)S(1)} %slice.60), channel_id=1, source_target_pairs={{0,1},{1,0},{2,3},{3,2},{4,5},{5,4},{6,7},{7,6},{8,9},{9,8},{10,11... | collective-permute-start | bytes 983048 | tf_op jit(solution)/shard_map/ppermute | solution.py:62
  46.1 6.7 %collective-permute-start.13 = (bf16[4,40,256]{2,1,0:T(8,128)(2,1)S(1)}, bf16[4,40,256]{2,1,0:T(8,128)(2,1)S(1)}, u32[]{:S(2)}, u32[]{:S(2)}) collective-permute-start(bf16[4,40,256]{2,1,0:T(8,128)(2,1)S(1)} %get-tuple-element.81), channel_id=1, source_target_pairs={{0,4},{1,5},{2,6},{3,7},{4,0},{5,1},{6,2},{7,3},{8,12},{9,13},{10,... | collective-permute-start | bytes 245768 | tf_op jit(solution)/shard_map/ppermute | solution.py:62
  46.2 6.6 %collective-permute-start.15 = (bf16[4,40,256]{2,1,0:T(8,128)(2,1)S(1)}, bf16[4,40,256]{2,1,0:T(8,128)(2,1)S(1)}, u32[]{:S(2)}, u32[]{:S(2)}) collective-permute-start(bf16[4,40,256]{2,1,0:T(8,128)(2,1)S(1)} %get-tuple-element.82), channel_id=1, source_target_pairs={{0,6},{1,7},{2,4},{3,5},{4,2},{5,3},{6,0},{7,1},{8,14},{9,15},{10,... | collective-permute-start | bytes 245768 | tf_op jit(solution)/shard_map/ppermute | solution.py:62
  48.5 5.4 %collective-permute-start.14 = (bf16[4,40,256]{2,1,0:T(8,128)(2,1)S(1)}, bf16[4,40,256]{2,1,0:T(8,128)(2,1)S(1)}, u32[]{:S(2)}, u32[]{:S(2)}) collective-permute-start(bf16[4,40,256]{2,1,0:T(8,128)(2,1)S(1)} %get-tuple-element.83), channel_id=1, source_target_pairs={{0,2},{1,3},{2,0},{3,1},{4,6},{5,7},{6,4},{7,5},{8,10},{9,11},{10,... | collective-permute-start | bytes 245768 | tf_op jit(solution)/shard_map/ppermute | solution.py:62
  54.0 4.1 %collective-permute-start.18 = (bf16[2,40,256]{2,1,0:T(8,128)(2,1)S(1)}, bf16[2,40,256]{2,1,0:T(8,128)(2,1)S(1)}, u32[]{:S(2)}, u32[]{:S(2)}) collective-permute-start(bf16[2,40,256]{2,1,0:T(8,128)(2,1)S(1)} %slice.92), channel_id=1, source_target_pairs={{0,8},{1,9},{2,10},{3,11},{4,12},{5,13},{6,14},{7,15},{8,0},{9,1},... | collective-permute-start | bytes 122888 | tf_op jit(solution)/shard_map/ppermute | solution.py:62
  55.0 4.2 %collective-permute-start.17 = (bf16[3,51,192]{2,1,0:T(8,128)(2,1)S(1)}, bf16[3,51,192]{2,1,0:T(8,128)(2,1)S(1)}, u32[]{:S(2)}, u32[]{:S(2)}) collective-permute-start(bf16[3,51,192]{2,1,0:T(8,128)(2,1)S(1)} %get-tuple-element.92), channel_id=1, source_target_pairs={{0,1},{1,0},{2,3},{3,2},{4,5},{5,4},{6,7},{7,6},{8,9},{9,8},{10,11... | collective-permute-start | bytes 176264 | tf_op jit(solution)/shard_map/ppermute | solution.py:71
  55.1 4.2 %collective-permute-start.16 = (bf16[3,51,192]{2,1,0:T(8,128)(2,1)S(1)}, bf16[3,51,192]{2,1,0:T(8,128)(2,1)S(1)}, u32[]{:S(2)}, u32[]{:S(2)}) collective-permute-start(bf16[3,51,192]{2,1,0:T(8,128)(2,1)S(1)} %get-tuple-element.93), channel_id=1, source_target_pairs={{1,2},{2,1},{5,6},{6,5},{9,10},{10,9},{13,14},{14,13},{17,18},{18,... | collective-permute-start | bytes 176264 | tf_op jit(solution)/shard_map/ppermute | solution.py:72
  58.1 4.7 %collective-permute-start.19 = (bf16[1,40,256]{2,1,0:T(8,128)(2,1)S(1)}, bf16[1,40,256]{2,1,0:T(8,128)(2,1)S(1)}, u32[]{:S(2)}, u32[]{:S(2)}) collective-permute-start(bf16[1,40,256]{2,1,0:T(8,128)(2,1)S(1)} %slice.93), channel_id=1, source_target_pairs={{0,16},{1,17},{2,18},{3,19},{4,20},{5,21},{6,22},{7,23},{8,24},{9,... | collective-permute-start | bytes 61448 | tf_op jit(solution)/shard_map/ppermute | solution.py:62
  59.3 3.6 %copy-start.3 = (f32[9568]{0:T(1024)S(1)}, f32[9568]{0:T(1024)}, u32[]{:S(2)}) copy-start(f32[9568]{0:T(1024)} %param.5) | copy-start | bytes 114820
  59.3 3.6 %copy-start.4 = (f32[9568]{0:T(1024)S(1)}, f32[9568]{0:T(1024)}, u32[]{:S(2)}) copy-start(f32[9568]{0:T(1024)} %param.6) | copy-start | bytes 114820
